TPU v7x, 512 devices: a whole 4x8x8 slice. The times are simulated.
512 devices in a mesh: dp: 64 (over y, z), tensor: 8 (over x, core).
Axes of the slice: x: 4, y: 8, z: 8, core: 2. Of those that a mesh axis runs over, the one named last changes fastest.
Arguments:
- features: bfloat16 [8192, 4096], P('dp', 'tensor'), may hold values from -6 to 6
- gate_pre: bfloat16 [8192, 7168], P('dp', 'tensor'), may hold values from -6 to 6
- up_pre: bfloat16 [8192, 7168], P('dp', 'tensor'), may hold values from -6 to 6
- hidden_grad: bfloat16 [8192, 7168], P('dp', 'tensor'), may hold values from -8 to 8
- lengths: int32 [64], replicated, may hold values from 1 to 128, as said below
- momentum: float32 [4096, 7168], P('dp', 'tensor'), may hold values from -6 to 6
Outputs:
- update: bfloat16 [8, 896, 4096], P('tensor', 'dp')
- new_momentum: float32 [4096, 7168], P('dp', 'tensor')
Inputs may be any that keep to these rules, and one draw needn't show every extreme that they name: `lengths`: a whole number of trained tokens at the start of each sequence; some sequence has all 128 trained.
All inputs are finite; a program needn't handle non-finite values.
Results may differ from a plain program's by a relative error of at most 0.0058.
Values may be sent and summed in bfloat16 or wider, within the bound.
No kernel may reach another device: no remote copies, remote signals or barrier semaphores. Data moves between devices by JAX's collectives and lax.ppermute only.
A program may use at most 64 MiB of HBM per device.

v0:
```python
import math

import jax
import jax.numpy as jnp
from jax import lax
from jax.sharding import PartitionSpec as P

HID = 7168
SEQ_LEN = 128
BLK = 64
ITERS = 5


momentum_decay = 0.95
linear_coeff = 3.4445
cubic_coeff = -4.775
quintic_coeff = 2.0315
norm_epsilon = 1e-07
update_gain = 0.2


def gate_cotangent(gate_pre, up_pre, hidden_grad, lengths):
    token_count = gate_pre.shape[0]
    position = lax.axis_index("dp") * token_count + jnp.arange(token_count, dtype=jnp.int32)
    sequence = position // SEQ_LEN
    columns = jnp.arange(lengths.shape[0], dtype=jnp.int32)
    token_limit = jnp.sum(
        jnp.where(sequence[:, None] == columns[None, :], lengths[None, :], 0), axis=1
    )
    trained = position % SEQ_LEN < token_limit
    gate_value = gate_pre.astype(jnp.float32)
    up_value = up_pre.astype(jnp.float32)
    cotangent = hidden_grad.astype(jnp.float32)
    sigmoid_gate = jax.nn.sigmoid(gate_value)
    gate_grad = cotangent * up_value * sigmoid_gate * (1.0 + gate_value * (1.0 - sigmoid_gate))
    return jnp.where(trained[:, None], gate_grad, 0.0).astype(jnp.bfloat16)


def block_gram(orthogonal):
    return jnp.einsum("kbr,kcr->kbc", orthogonal, orthogonal, precision=lax.Precision.HIGHEST)


def newton_step(orthogonal, gram_matrix):
    highest = lax.Precision.HIGHEST
    square = jnp.einsum("kbc,kcd->kbd", gram_matrix, gram_matrix, precision=highest)
    polynomial = cubic_coeff * gram_matrix + quintic_coeff * square
    return linear_coeff * orthogonal + jnp.einsum(
        "kbc,kcr->kbr", polynomial, orthogonal, precision=highest
    )


def per_device(features, gate_pre, up_pre, hidden_grad, lengths, momentum):
    gate_grad = gate_cotangent(gate_pre, up_pre, hidden_grad, lengths)
    whole_inputs = lax.all_gather(features, "tensor", axis=1, tiled=True)
    contract = (((0,), (0,)), ((), ()))
    partial_value = lax.dot_general(
        whole_inputs, gate_grad, contract, preferred_element_type=jnp.float32
    ).astype(jnp.bfloat16)
    n_dp = lax.axis_size("dp")
    own_cols = momentum.shape[0]
    shard_rows = momentum.shape[1]
    pieces = partial_value.reshape(n_dp, own_cols, shard_rows)
    received = lax.all_to_all(pieces, "dp", split_axis=0, concat_axis=0, tiled=True)
    grad_block = jnp.sum(received, axis=0, dtype=jnp.float32)
    new_moment = momentum_decay * momentum + grad_block
    nesterov = grad_block + momentum_decay * new_moment
    stacked = nesterov.reshape(own_cols // BLK, BLK, shard_rows)
    squares = lax.psum(jnp.sum(stacked * stacked, axis=(1, 2)), "tensor")
    orthogonal = stacked / (jnp.sqrt(squares) + norm_epsilon)[:, None, None]
    for iteration in range(ITERS):
        gram_matrix = lax.psum(block_gram(orthogonal), "tensor")
        orthogonal = newton_step(orthogonal, gram_matrix)
    update_block = (
        (update_gain * math.sqrt(HID) * orthogonal)
        .astype(jnp.bfloat16)
        .reshape(own_cols, shard_rows)
    )
    update_rows = lax.all_to_all(update_block.T, "dp", split_axis=0, concat_axis=1, tiled=True)
    return (update_rows.reshape(1, update_rows.shape[0], update_rows.shape[1]), new_moment)


def solution(mesh):
    placed = (
        P("dp", "tensor"),
        P("dp", "tensor"),
        P("dp", "tensor"),
        P("dp", "tensor"),
        P(),
        P("dp", "tensor"),
    )
    return jax.shard_map(
        per_device,
        mesh=mesh,
        in_specs=placed,
        out_specs=(P("tensor", "dp", None), P("dp", "tensor")),
        check_vma=False,
    )
```

profile of v0, /device:TPU:8, one launch (start us, length us, event | category | flops | bytes accessed | tf_op | source)
XLA Modules:
  0.0 439.8 jit_solution(9352633690207851949)
XLA Ops:
  7.2 0.0 all-gather.2.cloned.1.call-start
  7.2 0.7 all-gather.2.cloned.1.call-update
  7.9 0.7 select_reduce_fusion
  8.7 34.7 %all-gather.2.cloned.1.call-done = bf16[128,4096]{1,0:T(8,128)(2,1)} async-done(((bf16[128,512]{1,0:T(8,128)(2,1)}), bf16[128,4096]{1,0:T(8,128)(2,1)}) %all-gather.2.cloned.1.call-update) | async-done | bytes 1048592 | tf_op jit(solution)/shard_map/all_gather | solution.py:54
  43.4 6.8 %convert_bitcast_fusion = bf16[4096,896]{0,1:T(8,128)(2,1)} fusion(bf16[128,4096]{1,0:T(8,128)(2,1)} %all-gather.2.cloned.1.call-done, bf16[128,896]{1,0:T(8,128)(2,1)} %param.7, bf16[128,896]{1,0:T(8,128)(2,1)} %param.8, bf16[128,896]{1,0:T(8,128)(2,1)} %param.9, pred[128]{0:T(512)(128)(4,1)S(1)} %fusion.34), kind=kOutput, calls=%fused_computation.1 | convolution fusion | flops 944799744 | bytes 9076864 | tf_op jit(solution)/shard_map/dot_general | solution.py:56
  50.2 10.8 %copy.14 = bf16[4096,896]{1,0:T(8,128)(2,1)} copy(bf16[4096,896]{0,1:T(8,128)(2,1)} %convert_bitcast_fusion) | data formatting | bytes 14680064 | tf_op jit(solution)/shard_map/convert_element_type | solution.py:58
  61.0 200.3 %all_to_all.21 = bf16[64,64,896]{2,1,0:T(8,128)(2,1)S(1)} all-to-all(bf16[64,64,896]{2,1,0:T(8,128)(2,1)} %bitcast.91), channel_id=1, replica_groups=mesh['dp'=64,'tensor'=8] {'dp'}, dimensions={0} | all-to-all | bytes 14680064 | tf_op jit(solution)/shard_map/all_to_all | solution.py:63
  261.4 0.0 copy-start
  261.4 1.2 convert_reduce_fusion
  262.5 0.0 copy-done
  262.5 0.7 multiply_reduce_fusion
  263.2 0.0 copy-start.1
  263.2 13.8 %psum.42 = f32[1]{0:T(128)} all-reduce(f32[1]{0:T(128)} %bitcast.2), channel_id=1, replica_groups=mesh['dp'=64,'tensor'=8] {'tensor'}, use_global_device_ids=true, to_apply=%region_3.4 | all-reduce | flops 1 | bytes 8 | tf_op jit(solution)/shard_map/psum | solution.py:68
  277.7 0.4 convolution_bitcast_fusion.4
  278.1 23.6 %psum.43 = f32[1,64,64]{2,1,0:T(8,128)S(1)} all-reduce(f32[1,64,64]{2,1,0:T(8,128)S(1)} %convolution_bitcast_fusion.4), channel_id=1, replica_groups=mesh['dp'=64,'tensor'=8] {'tensor'}, use_global_device_ids=true, to_apply=%region_4.5 | all-reduce | flops 4096 | bytes 32768 | tf_op jit(solution)/shard_map/psum | solution.py:71
  301.7 0.2 fusion.9
  301.8 0.3 convolution_add_fusion.4
  302.2 0.4 convolution_bitcast_fusion.3
  302.6 23.6 %psum.44 = f32[1,64,64]{2,1,0:T(8,128)S(1)} all-reduce(f32[1,64,64]{2,1,0:T(8,128)S(1)} %convolution_bitcast_fusion.3), channel_id=1, replica_groups=mesh['dp'=64,'tensor'=8] {'tensor'}, use_global_device_ids=true, to_apply=%region_5.6 | all-reduce | flops 4096 | bytes 32768 | tf_op jit(solution)/shard_map/psum | solution.py:71
  326.1 0.2 fusion.11
  326.3 0.3 convolution_add_fusion.3
  326.7 0.4 convolution_bitcast_fusion.2
  327.0 23.6 %psum.45 = f32[1,64,64]{2,1,0:T(8,128)S(1)} all-reduce(f32[1,64,64]{2,1,0:T(8,128)S(1)} %convolution_bitcast_fusion.2), channel_id=1, replica_groups=mesh['dp'=64,'tensor'=8] {'tensor'}, use_global_device_ids=true, to_apply=%region_6.7 | all-reduce | flops 4096 | bytes 32768 | tf_op jit(solution)/shard_map/psum | solution.py:71
  350.6 0.2 fusion.13
  350.8 0.3 convolution_add_fusion.2
  351.1 0.4 convolution_bitcast_fusion.1
  351.5 23.6 %psum.46 = f32[1,64,64]{2,1,0:T(8,128)S(1)} all-reduce(f32[1,64,64]{2,1,0:T(8,128)S(1)} %convolution_bitcast_fusion.1), channel_id=1, replica_groups=mesh['dp'=64,'tensor'=8] {'tensor'}, use_global_device_ids=true, to_apply=%region_7.8 | all-reduce | flops 4096 | bytes 32768 | tf_op jit(solution)/shard_map/psum | solution.py:71
  375.1 0.2 fusion.15
  375.2 0.3 convolution_add_fusion.1
  375.6 0.3 convolution_bitcast_fusion
  375.9 23.6 %psum.47 = f32[1,64,64]{2,1,0:T(8,128)S(1)} all-reduce(f32[1,64,64]{2,1,0:T(8,128)S(1)} %convolution_bitcast_fusion), channel_id=1, replica_groups=mesh['dp'=64,'tensor'=8] {'tensor'}, use_global_device_ids=true, to_apply=%region_8.9 | all-reduce | flops 4096 | bytes 32768 | tf_op jit(solution)/shard_map/psum | solution.py:71
  399.5 0.2 fusion.17
  399.7 0.3 fusion.2
  400.1 0.2 copy.15
  400.2 0.1 all_to_all.16
  400.3 0.2 reshape.168
  400.5 31.3 %all_to_all.22 = bf16[64,2,448]{2,1,0:T(2,128)(2,1)S(1)} all-to-all(bf16[64,2,448]{2,1,0:T(2,128)(2,1)S(1)} %reshape.168), channel_id=1, replica_groups=mesh['dp'=64,'tensor'=8] {'dp'}, dimensions={0} | all-to-all | bytes 229376 | tf_op jit(solution)/shard_map/all_to_all | solution.py:78
  431.8 0.2 reshape.169
  432.0 0.1 copy.16
  432.1 0.9 reshape.167
  433.0 0.0 copy-done.1
  (2 shorter events, 0.0 us)
Async XLA Ops:
  7.2 36.2 %all-gather.2.cloned.1.call-start = ((), (), s32[]{:S(2)}) async-start(), calls=%async_computation.2 | async-start | bytes 1179648 | tf_op jit(solution)/shard_map/all_gather | solution.py:54
  261.4 1.2 copy-start
  263.2 169.8 %copy-start.1 = (f32[64,896]{1,0:T(8,128)}, f32[64,896]{1,0:T(8,128)S(1)}, u32[]{:S(2)}) copy-start(f32[64,896]{1,0:T(8,128)S(1)} %get-tuple-element.3) | copy-start | bytes 688132
Sparse Core Ops, SparseCore 0:
  10.1 33.2 all-gather.1
where the time goes:
time: 440 us
  blocking collectives  363 us (82%)
  waiting for transfers between devices  35.4 us (8%)
  between operations  14.9 us (3%)
  local copies, waits for them, and re-layouts  12.4 us (3%)
  matrix products  11 us (2%)
    all_to_all x1, blocking collectives, per_device(): lax.all_to_all(pieces, 'dp', split_axis=0, concat_axis=0, tiled=True)  200 us
    psum x5, blocking collectives, per_device(): gram_matrix = lax.psum(block_gram(orthogonal), 'tensor')  118 us
    all_gather x1, waiting for transfers between devices, per_device(): whole_inputs = lax.all_gather(features, 'tensor', axis=1, tiled=True)  34.7 us
    all_to_all x1, blocking collectives, per_device(): lax.all_to_all(update_block.T, 'dp', split_axis=0, concat_axis=1, tiled=T...  31.3 us
    psum x1, blocking collectives, per_device(): squares = lax.psum(jnp.sum(stacked * stacked, axis=(1, 2)), 'tensor')  13.8 us
    convert_element_type x1, local copies, waits for them, and re-layouts, per_device(): partial_value = lax.dot_general(whole_inputs, gate_grad, contract, prefer...  10.8 us
  transfers between devices with their start and end apart: 1, of which 1 were waited for; matrix products, arithmetic and copies ran while one was open for 0% of the time, Pallas kernels for 0%

commit v1 on v0

v1 whole, which is shorter than its diff:
```python
import functools
import math

import jax
import jax.numpy as jnp
from jax import lax
from jax.experimental import pallas as pl
from jax.experimental.pallas import tpu as pltpu
from jax.sharding import Mesh
from jax.sharding import PartitionSpec as P

HID = 7168
SEQ_LEN = 128
BLK = 64
ITERS = 5
NY = 8
NZ = 8
NT = 8

momentum_decay = 0.95
linear_coeff = 3.4445
cubic_coeff = -4.775
quintic_coeff = 2.0315
norm_epsilon = 1e-07
update_gain = 0.2

HIGHEST = lax.Precision.HIGHEST


def gate_cotangent(gate_pre, up_pre, hidden_grad, trained_tokens):
    position = lax.broadcasted_iota(jnp.int32, gate_pre.shape, 0)
    gate_value = gate_pre.astype(jnp.float32)
    up_value = up_pre.astype(jnp.float32)
    cotangent = hidden_grad.astype(jnp.float32)
    sigmoid_gate = jax.nn.sigmoid(gate_value)
    gate_grad = cotangent * up_value * sigmoid_gate * (1.0 + gate_value * (1.0 - sigmoid_gate))
    return jnp.where(position < trained_tokens, gate_grad, 0.0).astype(jnp.bfloat16)


def partial_kernel(own_ref, *refs):
    feature_refs, grad_ref, out_ref, joined = refs[:NT], refs[NT], refs[NT + 1], refs[NT + 2]
    own = own_ref[0]
    tokens = feature_refs[0].shape[0]
    for shift in range(NT):
        group = lax.rem(own + NT - shift, NT)
        joined[pl.ds(pl.multiple_of(group * tokens, tokens), tokens), :] = feature_refs[shift][...]
    rows = out_ref.shape[0]
    step = 128
    for start in range(0, rows, step):
        product = lax.dot_general(
            joined[:, start : start + step],
            grad_ref[...],
            (((0,), (0,)), ((), ())),
            preferred_element_type=jnp.float32,
        )
        out_ref[start : start + step, :] = product.astype(out_ref.dtype)


def partial_product(own, feature_blocks, grads):
    tokens, rows = feature_blocks[0].shape
    columns = grads.shape[1]
    vmem = pl.BlockSpec(memory_space=pltpu.VMEM)
    return pl.pallas_call(
        partial_kernel,
        out_shape=jax.ShapeDtypeStruct((rows, columns), jnp.bfloat16),
        in_specs=[pl.BlockSpec(memory_space=pltpu.SMEM)] + [vmem] * (NT + 1),
        out_specs=vmem,
        scratch_shapes=[pltpu.VMEM((NT * tokens, rows), jnp.bfloat16)],
        compiler_params=pltpu.CompilerParams(vmem_limit_bytes=32 * 1024 * 1024),
        cost_estimate=pl.CostEstimate(
            flops=2 * NT * tokens * rows * columns, bytes_accessed=6_000_000, transcendentals=0
        ),
        name="partial_product",
    )(jnp.reshape(own, (1,)), *feature_blocks, grads)


def polar_map(gram_total):
    mul = functools.partial(jnp.dot, precision=HIGHEST, preferred_element_type=jnp.float32)
    size = gram_total.shape[0]
    eye = jnp.eye(size, dtype=jnp.float32)
    squares = jnp.sum(gram_total * eye)
    inverse = 1.0 / (jnp.sqrt(squares) + norm_epsilon)
    gram = gram_total * inverse * inverse
    mapping = eye
    for iteration in range(ITERS):
        square = mul(gram, gram)
        poly = linear_coeff * eye + cubic_coeff * gram + quintic_coeff * square
        mapping = poly if iteration == 0 else mul(poly, mapping)
        if iteration < ITERS - 1:
            gram = mul(mul(poly, gram), poly)
    return mapping * (inverse * (update_gain * math.sqrt(HID)))


def per_device(features, gate_pre, up_pre, hidden_grad, lengths, momentum):
    y, z, t = (lax.axis_index(name) for name in ("y", "z", "t"))
    swap = [(a * NT + b, b * NT + a) for a in range(NY) for b in range(NT)]
    own_features = lax.ppermute(features, ("y", "t"), swap)
    feature_blocks = [own_features] + [
        lax.ppermute(own_features, "t", [(i, (i + s) % NT) for i in range(NT)]) for s in range(1, NT)
    ]
    trained_tokens = lax.dynamic_index_in_dim(lengths, y * NZ + z, 0, keepdims=False)
    gate_grad = gate_cotangent(gate_pre, up_pre, hidden_grad, trained_tokens)
    grads = lax.all_gather(gate_grad, "y", axis=0, tiled=True)
    partial_value = partial_product(t, feature_blocks, grads)
    pieces = partial_value.reshape(NZ, BLK, partial_value.shape[1])
    received = lax.all_to_all(pieces, "z", split_axis=0, concat_axis=0, tiled=True)
    grad_block = jnp.sum(received.astype(jnp.float32), axis=0)
    new_moment = momentum_decay * momentum + grad_block
    nesterov = grad_block + momentum_decay * new_moment
    gram_own = lax.dot_general(
        nesterov, nesterov, (((1,), (1,)), ((), ())), precision=HIGHEST, preferred_element_type=jnp.float32
    )
    gram_total = gram_own
    for s in range(1, NT):
        gram_total = gram_total + lax.ppermute(gram_own, "t", [(i, (i + s) % NT) for i in range(NT)])
    mapping = polar_map(gram_total)
    update = lax.dot_general(
        nesterov, mapping, (((0,), (1,)), ((), ())), precision=HIGHEST, preferred_element_type=jnp.float32
    ).astype(jnp.bfloat16)
    unit_count = update.shape[0] // (NY * NZ)
    by_y = update.reshape(NY, NZ * unit_count, BLK)
    by_y = lax.all_to_all(by_y, "y", split_axis=0, concat_axis=0, tiled=True)
    by_z = by_y.reshape(NY, NZ, unit_count, BLK)
    by_z = lax.all_to_all(by_z, "z", split_axis=1, concat_axis=1, tiled=True)
    result = by_z.transpose(2, 0, 1, 3).reshape(1, unit_count, NY * NZ * BLK)
    return result, new_moment


def solution(mesh):
    fine = Mesh(mesh.devices.reshape(NY, NZ, NT), ("y", "z", "t"))
    split = P(("y", "z"), "t")
    return jax.shard_map(
        per_device,
        mesh=fine,
        in_specs=(split, split, split, split, P(), split),
        out_specs=(P("t", ("y", "z"), None), split),
        check_vma=False,
    )
```

time: 440 us -> 150 us (0.34)
  blocking collectives: 363 us -> 52.3 us
  starting transfers between devices: 0.04 us -> 46.5 us
  waiting for transfers between devices: 35.4 us -> 22.6 us
  local copies, waits for them, and re-layouts: 12.4 us -> 4.46 us
  matrix products: 11 us -> 3.46 us
    all_to_all x2 -> x3, blocking collectives: 232 us -> 52.3 us  [the longest x1 28.6 us: per_device(): lax.all_to_all(pieces, 'z', split_axis=0, concat_axis=0, tiled=True)]
    psum x6 -> x0, blocking collectives: 132 us -> none  [the longest x5 118 us: per_device(): gram_matrix = lax.psum(block_gram(orthogonal), 'tensor')]
    ppermute x0 -> x15, starting transfers between devices: none -> 46.4 us  [the longest x7 27.4 us: per_device(): lax.ppermute(own_features, 't', [(i, (i + s) % NT) for i in range(NT)])]
    all_gather x1, waiting for transfers between devices: 34.7 us -> 6.13 us  [per_device(): grads = lax.all_gather(gate_grad, 'y', axis=0, tiled=True)]
    ppermute x0 -> x15, waiting for transfers between devices: none -> 16.5 us  [the longest x7 7.65 us: per_device(): lax.ppermute(own_features, 't', [(i, (i + s) % NT) for i in range(NT)])]
    convert_element_type x1 -> x0, local copies, waits for them, and re-layouts: 10.8 us -> none  [per_device(): partial_value = lax.dot_general(whole_inputs, gate_grad, contract, prefer...]
    dot_general x16 -> x19, matrix products: 11 us -> 3.46 us  [the longest x8 1.29 us: polar_map(): gram = mul(mul(poly, gram), poly)]
  transfers between devices with their start and end apart: 1 -> 16, of which waited for: 1 -> 8; matrix products, arithmetic and copies ran while one was open for 0% -> 0% of each run, Pallas kernels for 0% -> 0%
where the time goes in v1:
time: 150 us; the launch traced here: 149 us
  blocking collectives  52.3 us (35%)
  starting transfers between devices  46.5 us (31%)
  waiting for transfers between devices  22.6 us (15%)
  between operations  15.1 us (10%)
  local copies, waits for them, and re-layouts  4.46 us (3%)
  other arithmetic  3.49 us (2%)
  matrix products  3.46 us (2%)
    all_to_all x1, blocking collectives, per_device(): lax.all_to_all(pieces, 'z', split_axis=0, concat_axis=0, tiled=True)  28.6 us
    ppermute x7, starting transfers between devices, per_device(): lax.ppermute(own_features, 't', [(i, (i + s) % NT) for i in range(NT)])  27.4 us
    ppermute x7, starting transfers between devices, per_device(): lax.ppermute(gram_own, 't', [(i, (i + s) % NT) for i in range(NT)])  17.1 us
    all_to_all x1, blocking collectives, per_device(): by_y = lax.all_to_all(by_y, 'y', split_axis=0, concat_axis=0, tiled=True)  12.4 us
    all_to_all x1, blocking collectives, per_device(): by_z = lax.all_to_all(by_z, 'z', split_axis=1, concat_axis=1, tiled=True)  11.3 us
    ppermute x7, waiting for transfers between devices, per_device(): lax.ppermute(own_features, 't', [(i, (i + s) % NT) for i in range(NT)])  7.65 us
    all_gather x1, waiting for transfers between devices, per_device(): grads = lax.all_gather(gate_grad, 'y', axis=0, tiled=True)  6.13 us
    ppermute x1, waiting for transfers between devices, per_device(): own_features = lax.ppermute(features, ('y', 't'), swap)  4.57 us
  transfers between devices with their start and end apart: 16, of which 8 were waited for; matrix products, arithmetic and copies ran while one was open for 0% of the time, Pallas kernels for 0%

profile of v1, /device:TPU:8, one launch (start us, length us, event | category | flops | bytes accessed | tf_op | source)
XLA Modules:
  0.0 149.3 jit_solution(13374377504926740879)
XLA Ops:
  7.2 0.0 all-gather.2.cloned.1.call-start
  7.2 1.2 dynamic_slice.4
  8.5 0.6 iota_compare_fusion.1
  9.1 2.1 %fusion.10 = bf16[128,896]{1,0:T(8,128)(2,1)} fusion(bf16[128,896]{1,0:T(8,128)(2,1)} %param.7, bf16[128,896]{1,0:T(8,128)(2,1)} %param.8, bf16[128,896]{1,0:T(8,128)(2,1)} %param.9, pred[128]{0:T(512)(128)(4,1)S(1)} %iota_compare_fusion.1), kind=kLoop, calls=%fused_computation.20 | loop fusion | flops 1605632 | bytes 917632 | tf_op jit(solution)/shard_map/convert_element_type | solution.py:37
  11.2 0.0 all-gather.2.cloned.1.call-update
  11.2 1.9 %collective-permute-start = (bf16[128,512]{1,0:T(8,128)(2,1)}, bf16[128,512]{1,0:T(8,128)(2,1)S(1)}, u32[]{:S(2)}, u32[]{:S(2)}) collective-permute-start(bf16[128,512]{1,0:T(8,128)(2,1)} %param.6), channel_id=1, source_target_pairs={{0,0},{1,64},{2,128},{3,192},{4,256},{5,320},{6,384},{7,448},{64,1... | collective-permute-start | bytes 393224 | tf_op jit(solution)/shard_map/ppermute | solution.py:97
  13.1 4.6 %collective-permute-done.refs_0_ = bf16[128,512]{1,0:T(8,128)(2,1)S(1)} collective-permute-done((bf16[128,512]{1,0:T(8,128)(2,1)}, bf16[128,512]{1,0:T(8,128)(2,1)S(1)}, u32[]{:S(2)}, u32[]{:S(2)}) %collective-permute-start) | collective-permute-done | bytes 131104 | tf_op jit(solution)/shard_map/ppermute | solution.py:97
  17.7 12.4 %collective-permute-start.7 = (bf16[128,512]{1,0:T(8,128)(2,1)S(1)}, bf16[128,512]{1,0:T(8,128)(2,1)S(1)}, u32[]{:S(2)}, u32[]{:S(2)}) collective-permute-start(bf16[128,512]{1,0:T(8,128)(2,1)S(1)} %collective-permute-done.refs_0_), channel_id=1, source_target_pairs={{0,7},{1,0},{2,1},{3,2},{4,3},{5,4},{6,5},{7,6},{8,15},{9,8},{10,9... | collective-permute-start | bytes 393224 | tf_op jit(solution)/shard_map/ppermute | solution.py:99
  30.1 1.9 %collective-permute-start.6 = (bf16[128,512]{1,0:T(8,128)(2,1)S(1)}, bf16[128,512]{1,0:T(8,128)(2,1)S(1)}, u32[]{:S(2)}, u32[]{:S(2)}) collective-permute-start(bf16[128,512]{1,0:T(8,128)(2,1)S(1)} %collective-permute-done.refs_0_), channel_id=1, source_target_pairs={{0,6},{1,7},{2,0},{3,1},{4,2},{5,3},{6,4},{7,5},{8,14},{9,15},{10,... | collective-permute-start | bytes 393224 | tf_op jit(solution)/shard_map/ppermute | solution.py:99
  32.1 1.9 %collective-permute-start.5 = (bf16[128,512]{1,0:T(8,128)(2,1)S(1)}, bf16[128,512]{1,0:T(8,128)(2,1)S(1)}, u32[]{:S(2)}, u32[]{:S(2)}) collective-permute-start(bf16[128,512]{1,0:T(8,128)(2,1)S(1)} %collective-permute-done.refs_0_), channel_id=1, source_target_pairs={{0,5},{1,6},{2,7},{3,0},{4,1},{5,2},{6,3},{7,4},{8,13},{9,14},{10,... | collective-permute-start | bytes 393224 | tf_op jit(solution)/shard_map/ppermute | solution.py:99
  34.0 5.1 %collective-permute-start.4 = (bf16[128,512]{1,0:T(8,128)(2,1)S(1)}, bf16[128,512]{1,0:T(8,128)(2,1)S(1)}, u32[]{:S(2)}, u32[]{:S(2)}) collective-permute-start(bf16[128,512]{1,0:T(8,128)(2,1)S(1)} %collective-permute-done.refs_0_), channel_id=1, source_target_pairs={{0,4},{1,5},{2,6},{3,7},{4,0},{5,1},{6,2},{7,3},{8,12},{9,13},{10,... | collective-permute-start | bytes 393224 | tf_op jit(solution)/shard_map/ppermute | solution.py:99
  39.1 1.9 %collective-permute-start.3 = (bf16[128,512]{1,0:T(8,128)(2,1)S(1)}, bf16[128,512]{1,0:T(8,128)(2,1)S(1)}, u32[]{:S(2)}, u32[]{:S(2)}) collective-permute-start(bf16[128,512]{1,0:T(8,128)(2,1)S(1)} %collective-permute-done.refs_0_), channel_id=1, source_target_pairs={{0,3},{1,4},{2,5},{3,6},{4,7},{5,0},{6,1},{7,2},{8,11},{9,12},{10,... | collective-permute-start | bytes 393224 | tf_op jit(solution)/shard_map/ppermute | solution.py:99
  41.1 0.0 collective-permute-done.7.refs_7_
  41.1 2.4 %collective-permute-start.2 = (bf16[128,512]{1,0:T(8,128)(2,1)S(1)}, bf16[128,512]{1,0:T(8,128)(2,1)S(1)}, u32[]{:S(2)}, u32[]{:S(2)}) collective-permute-start(bf16[128,512]{1,0:T(8,128)(2,1)S(1)} %collective-permute-done.refs_0_), channel_id=1, source_target_pairs={{0,2},{1,3},{2,4},{3,5},{4,6},{5,7},{6,0},{7,1},{8,10},{9,11},{10,... | collective-permute-start | bytes 393224 | tf_op jit(solution)/shard_map/ppermute | solution.py:99
  43.5 0.0 collective-permute-done.6.refs_6_
  43.5 1.6 %collective-permute-start.1 = (bf16[128,512]{1,0:T(8,128)(2,1)S(1)}, bf16[128,512]{1,0:T(8,128)(2,1)S(1)}, u32[]{:S(2)}, u32[]{:S(2)}) collective-permute-start(bf16[128,512]{1,0:T(8,128)(2,1)S(1)} %collective-permute-done.refs_0_), channel_id=1, source_target_pairs={{0,1},{1,2},{2,3},{3,4},{4,5},{5,6},{6,7},{7,0},{8,9},{9,10},{10,1... | collective-permute-start | bytes 393224 | tf_op jit(solution)/shard_map/ppermute | solution.py:99
  45.2 2.7 %collective-permute-done.3.refs_3_ = bf16[128,512]{1,0:T(8,128)(2,1)S(1)} collective-permute-done((bf16[128,512]{1,0:T(8,128)(2,1)S(1)}, bf16[128,512]{1,0:T(8,128)(2,1)S(1)}, u32[]{:S(2)}, u32[]{:S(2)}) %collective-permute-start.3) | collective-permute-done | bytes 131104 | tf_op jit(solution)/shard_map/ppermute | solution.py:99
  47.8 4.2 %collective-permute-done.2.refs_2_ = bf16[128,512]{1,0:T(8,128)(2,1)S(1)} collective-permute-done((bf16[128,512]{1,0:T(8,128)(2,1)S(1)}, bf16[128,512]{1,0:T(8,128)(2,1)S(1)}, u32[]{:S(2)}, u32[]{:S(2)}) %collective-permute-start.2) | collective-permute-done | bytes 131104 | tf_op jit(solution)/shard_map/ppermute | solution.py:99
  52.1 0.7 collective-permute-done.1.refs_1_
  52.8 6.1 %all-gather.2.cloned.1.call-done.refs_8_ = bf16[1024,896]{1,0:T(8,128)(2,1)} async-done(((bf16[128,896]{1,0:T(8,128)(2,1)}), bf16[1024,896]{1,0:T(8,128)(2,1)}) %all-gather.2.cloned.1.call-update) | async-done | bytes 1835024 | tf_op jit(solution)/shard_map/all_gather | solution.py:103
  58.9 1.5 %copy-done = bf16[1024,896]{1,0:T(8,128)(2,1)S(1)} copy-done((bf16[1024,896]{1,0:T(8,128)(2,1)S(1)}, bf16[1024,896]{1,0:T(8,128)(2,1)}, u32[]{:S(2)}) %copy-start) | copy-done | bytes 1835032
  60.4 1.4 partial_product.1
  61.8 0.0 copy-start.2
  61.9 28.6 %all_to_all.15 = bf16[8,64,896]{2,1,0:T(8,128)(2,1)S(1)} all-to-all(bf16[8,64,896]{2,1,0:T(8,128)(2,1)S(1)} %bitcast.45), channel_id=1, replica_groups=mesh['y'=8,'z'=8,'t'=8] {'z'}, dimensions={0} | all-to-all | bytes 1835008 | tf_op jit(solution)/shard_map/all_to_all | solution.py:106
  90.4 0.1 convert_reduce_fusion
  90.6 0.0 copy-start.1
  90.6 0.4 fusion.11
  91.0 0.0 collective-permute-start.14
  91.0 4.9 %collective-permute-start.13 = (f32[64,64]{1,0:T(8,128)S(1)}, f32[64,64]{1,0:T(8,128)S(1)}, u32[]{:S(2)}, u32[]{:S(2)}) collective-permute-start(f32[64,64]{1,0:T(8,128)S(1)} %fusion.11), channel_id=1, source_target_pairs={{0,6},{1,7},{2,0},{3,1},{4,2},{5,3},{6,4},{7,5},{8,14},{9,15},{10,... | collective-permute-start | bytes 49160 | tf_op jit(solution)/shard_map/ppermute | solution.py:115
  95.9 2.3 %collective-permute-start.12 = (f32[64,64]{1,0:T(8,128)S(1)}, f32[64,64]{1,0:T(8,128)S(1)}, u32[]{:S(2)}, u32[]{:S(2)}) collective-permute-start(f32[64,64]{1,0:T(8,128)S(1)} %fusion.11), channel_id=1, source_target_pairs={{0,5},{1,6},{2,7},{3,0},{4,1},{5,2},{6,3},{7,4},{8,13},{9,14},{10,... | collective-permute-start | bytes 49160 | tf_op jit(solution)/shard_map/ppermute | solution.py:115
  98.2 4.9 %collective-permute-start.11 = (f32[64,64]{1,0:T(8,128)S(1)}, f32[64,64]{1,0:T(8,128)S(1)}, u32[]{:S(2)}, u32[]{:S(2)}) collective-permute-start(f32[64,64]{1,0:T(8,128)S(1)} %fusion.11), channel_id=1, source_target_pairs={{0,4},{1,5},{2,6},{3,7},{4,0},{5,1},{6,2},{7,3},{8,12},{9,13},{10,... | collective-permute-start | bytes 49160 | tf_op jit(solution)/shard_map/ppermute | solution.py:115
  103.0 1.9 %collective-permute-start.10 = (f32[64,64]{1,0:T(8,128)S(1)}, f32[64,64]{1,0:T(8,128)S(1)}, u32[]{:S(2)}, u32[]{:S(2)}) collective-permute-start(f32[64,64]{1,0:T(8,128)S(1)} %fusion.11), channel_id=1, source_target_pairs={{0,3},{1,4},{2,5},{3,6},{4,7},{5,0},{6,1},{7,2},{8,11},{9,12},{10,... | collective-permute-start | bytes 49160 | tf_op jit(solution)/shard_map/ppermute | solution.py:115
  105.0 2.1 %collective-permute-start.9 = (f32[64,64]{1,0:T(8,128)S(1)}, f32[64,64]{1,0:T(8,128)S(1)}, u32[]{:S(2)}, u32[]{:S(2)}) collective-permute-start(f32[64,64]{1,0:T(8,128)S(1)} %fusion.11), channel_id=1, source_target_pairs={{0,2},{1,3},{2,4},{3,5},{4,6},{5,7},{6,0},{7,1},{8,10},{9,11},{10,... | collective-permute-start | bytes 49160 | tf_op jit(solution)/shard_map/ppermute | solution.py:115
  107.1 1.1 collective-permute-start.8
  108.2 1.6 %collective-permute-done.10 = f32[64,64]{1,0:T(8,128)S(1)} collective-permute-done((f32[64,64]{1,0:T(8,128)S(1)}, f32[64,64]{1,0:T(8,128)S(1)}, u32[]{:S(2)}, u32[]{:S(2)}) %collective-permute-start.10) | collective-permute-done | bytes 16416 | tf_op jit(solution)/shard_map/ppermute | solution.py:115
  109.8 2.6 %collective-permute-done.9 = f32[64,64]{1,0:T(8,128)S(1)} collective-permute-done((f32[64,64]{1,0:T(8,128)S(1)}, f32[64,64]{1,0:T(8,128)S(1)}, u32[]{:S(2)}, u32[]{:S(2)}) %collective-permute-start.9) | collective-permute-done | bytes 16416 | tf_op jit(solution)/shard_map/ppermute | solution.py:115
  112.3 0.1 collective-permute-done.8
  112.4 0.6 select_reduce_fusion
  113.8 0.2 fusion.12
  113.9 0.2 fusion.13
  114.1 0.2 fusion.18
  114.3 0.2 fusion.3
  114.4 0.2 fusion.25
  114.6 0.2 fusion.19
  114.8 0.2 fusion.20
  114.9 0.2 fusion.2
  115.1 0.2 fusion.21
  115.3 0.2 fusion.26
  115.5 0.2 fusion.22
  115.6 0.2 fusion.1
  115.8 0.2 fusion.23
  116.0 0.2 fusion.27
  116.1 0.2 fusion.24
  116.3 0.2 fusion
  116.5 0.2 convolution_multiply_fusion
  116.6 0.4 convolution_convert_fusion
  117.0 0.2 reshape.21
  117.2 12.4 %all_to_all.16 = bf16[8,112,64]{1,2,0:T(8,128)(2,1)S(1)} all-to-all(bf16[8,112,64]{1,2,0:T(8,128)(2,1)S(1)} %copy.12), channel_id=1, replica_groups=mesh['y'=8,'z'=8,'t'=8] {'y'}, dimensions={0} | all-to-all | bytes 229376 | tf_op jit(solution)/shard_map/all_to_all | solution.py:122
  129.6 0.2 copy.13
  129.8 0.2 reshape.24
  130.0 11.3 %all_to_all.17 = bf16[8,2,3584]{2,1,0:T(2,128)(2,1)S(1)} all-to-all(bf16[8,2,3584]{2,1,0:T(2,128)(2,1)S(1)} %reshape.24), channel_id=1, replica_groups=mesh['y'=8,'z'=8,'t'=8] {'z'}, dimensions={0} | all-to-all | bytes 229376 | tf_op jit(solution)/shard_map/all_to_all | solution.py:124
  141.3 0.2 reshape.25
  141.5 0.1 copy.14
  141.6 0.9 reshape.23
  (12 shorter events, 0.1 us)
Async XLA Ops:
  7.2 51.8 %all-gather.2.cloned.1.call-start = ((), (), s32[]{:S(2)}) async-start(), calls=%async_computation.3 | async-start | bytes 2064384 | tf_op jit(solution)/shard_map/all_gather | solution.py:103
  11.2 6.5 %collective-permute-start = (bf16[128,512]{1,0:T(8,128)(2,1)}, bf16[128,512]{1,0:T(8,128)(2,1)S(1)}, u32[]{:S(2)}, u32[]{:S(2)}) collective-permute-start(bf16[128,512]{1,0:T(8,128)(2,1)} %param.6), channel_id=1, source_target_pairs={{0,0},{1,64},{2,128},{3,192},{4,256},{5,320},{6,384},{7,448},{64,1... | collective-permute-start | bytes 393224 | tf_op jit(solution)/shard_map/ppermute | solution.py:97
  17.7 23.3 %collective-permute-start.7 = (bf16[128,512]{1,0:T(8,128)(2,1)S(1)}, bf16[128,512]{1,0:T(8,128)(2,1)S(1)}, u32[]{:S(2)}, u32[]{:S(2)}) collective-permute-start(bf16[128,512]{1,0:T(8,128)(2,1)S(1)} %collective-permute-done.refs_0_), channel_id=1, source_target_pairs={{0,7},{1,0},{2,1},{3,2},{4,3},{5,4},{6,5},{7,6},{8,15},{9,8},{10,9... | collective-permute-start | bytes 393224 | tf_op jit(solution)/shard_map/ppermute | solution.py:99
  30.1 13.4 %collective-permute-start.6 = (bf16[128,512]{1,0:T(8,128)(2,1)S(1)}, bf16[128,512]{1,0:T(8,128)(2,1)S(1)}, u32[]{:S(2)}, u32[]{:S(2)}) collective-permute-start(bf16[128,512]{1,0:T(8,128)(2,1)S(1)} %collective-permute-done.refs_0_), channel_id=1, source_target_pairs={{0,6},{1,7},{2,0},{3,1},{4,2},{5,3},{6,4},{7,5},{8,14},{9,15},{10,... | collective-permute-start | bytes 393224 | tf_op jit(solution)/shard_map/ppermute | solution.py:99
  32.1 13.1 %collective-permute-start.5 = (bf16[128,512]{1,0:T(8,128)(2,1)S(1)}, bf16[128,512]{1,0:T(8,128)(2,1)S(1)}, u32[]{:S(2)}, u32[]{:S(2)}) collective-permute-start(bf16[128,512]{1,0:T(8,128)(2,1)S(1)} %collective-permute-done.refs_0_), channel_id=1, source_target_pairs={{0,5},{1,6},{2,7},{3,0},{4,1},{5,2},{6,3},{7,4},{8,13},{9,14},{10,... | collective-permute-start | bytes 393224 | tf_op jit(solution)/shard_map/ppermute | solution.py:99
  34.0 11.2 %collective-permute-start.4 = (bf16[128,512]{1,0:T(8,128)(2,1)S(1)}, bf16[128,512]{1,0:T(8,128)(2,1)S(1)}, u32[]{:S(2)}, u32[]{:S(2)}) collective-permute-start(bf16[128,512]{1,0:T(8,128)(2,1)S(1)} %collective-permute-done.refs_0_), channel_id=1, source_target_pairs={{0,4},{1,5},{2,6},{3,7},{4,0},{5,1},{6,2},{7,3},{8,12},{9,13},{10,... | collective-permute-start | bytes 393224 | tf_op jit(solution)/shard_map/ppermute | solution.py:99
  39.1 8.7 %collective-permute-start.3 = (bf16[128,512]{1,0:T(8,128)(2,1)S(1)}, bf16[128,512]{1,0:T(8,128)(2,1)S(1)}, u32[]{:S(2)}, u32[]{:S(2)}) collective-permute-start(bf16[128,512]{1,0:T(8,128)(2,1)S(1)} %collective-permute-done.refs_0_), channel_id=1, source_target_pairs={{0,3},{1,4},{2,5},{3,6},{4,7},{5,0},{6,1},{7,2},{8,11},{9,12},{10,... | collective-permute-start | bytes 393224 | tf_op jit(solution)/shard_map/ppermute | solution.py:99
  41.1 11.0 %collective-permute-start.2 = (bf16[128,512]{1,0:T(8,128)(2,1)S(1)}, bf16[128,512]{1,0:T(8,128)(2,1)S(1)}, u32[]{:S(2)}, u32[]{:S(2)}) collective-permute-start(bf16[128,512]{1,0:T(8,128)(2,1)S(1)} %collective-permute-done.refs_0_), channel_id=1, source_target_pairs={{0,2},{1,3},{2,4},{3,5},{4,6},{5,7},{6,0},{7,1},{8,10},{9,11},{10,... | collective-permute-start | bytes 393224 | tf_op jit(solution)/shard_map/ppermute | solution.py:99
  43.5 9.3 %collective-permute-start.1 = (bf16[128,512]{1,0:T(8,128)(2,1)S(1)}, bf16[128,512]{1,0:T(8,128)(2,1)S(1)}, u32[]{:S(2)}, u32[]{:S(2)}) collective-permute-start(bf16[128,512]{1,0:T(8,128)(2,1)S(1)} %collective-permute-done.refs_0_), channel_id=1, source_target_pairs={{0,1},{1,2},{2,3},{3,4},{4,5},{5,6},{6,7},{7,0},{8,9},{9,10},{10,1... | collective-permute-start | bytes 393224 | tf_op jit(solution)/shard_map/ppermute | solution.py:99
  58.9 1.5 %copy-start = (bf16[1024,896]{1,0:T(8,128)(2,1)S(1)}, bf16[1024,896]{1,0:T(8,128)(2,1)}, u32[]{:S(2)}) copy-start(bf16[1024,896]{1,0:T(8,128)(2,1)} %all-gather.2.cloned.1.call-done.refs_8_) | copy-start | bytes 5505028
  61.8 28.7 %copy-start.2 = (f32[64,896]{1,0:T(8,128)S(1)}, f32[64,896]{1,0:T(8,128)}, u32[]{:S(2)}) copy-start(f32[64,896]{1,0:T(8,128)} %param.11) | copy-start | bytes 688132
  90.6 39.0 %copy-start.1 = (f32[64,896]{1,0:T(8,128)}, f32[64,896]{1,0:T(8,128)S(1)}, u32[]{:S(2)}) copy-start(f32[64,896]{1,0:T(8,128)S(1)} %multiply_add_fusion.1) | copy-start | bytes 688132
  91.0 14.0 %collective-permute-start.14 = (f32[64,64]{1,0:T(8,128)S(1)}, f32[64,64]{1,0:T(8,128)S(1)}, u32[]{:S(2)}, u32[]{:S(2)}) collective-permute-start(f32[64,64]{1,0:T(8,128)S(1)} %fusion.11), channel_id=1, source_target_pairs={{0,7},{1,0},{2,1},{3,2},{4,3},{5,4},{6,5},{7,6},{8,15},{9,8},{10,9... | collective-permute-start | bytes 49160 | tf_op jit(solution)/shard_map/ppermute | solution.py:115
  91.0 16.1 %collective-permute-start.13 = (f32[64,64]{1,0:T(8,128)S(1)}, f32[64,64]{1,0:T(8,128)S(1)}, u32[]{:S(2)}, u32[]{:S(2)}) collective-permute-start(f32[64,64]{1,0:T(8,128)S(1)} %fusion.11), channel_id=1, source_target_pairs={{0,6},{1,7},{2,0},{3,1},{4,2},{5,3},{6,4},{7,5},{8,14},{9,15},{10,... | collective-permute-start | bytes 49160 | tf_op jit(solution)/shard_map/ppermute | solution.py:115
  95.9 12.3 %collective-permute-start.12 = (f32[64,64]{1,0:T(8,128)S(1)}, f32[64,64]{1,0:T(8,128)S(1)}, u32[]{:S(2)}, u32[]{:S(2)}) collective-permute-start(f32[64,64]{1,0:T(8,128)S(1)} %fusion.11), channel_id=1, source_target_pairs={{0,5},{1,6},{2,7},{3,0},{4,1},{5,2},{6,3},{7,4},{8,13},{9,14},{10,... | collective-permute-start | bytes 49160 | tf_op jit(solution)/shard_map/ppermute | solution.py:115
  98.2 10.0 %collective-permute-start.11 = (f32[64,64]{1,0:T(8,128)S(1)}, f32[64,64]{1,0:T(8,128)S(1)}, u32[]{:S(2)}, u32[]{:S(2)}) collective-permute-start(f32[64,64]{1,0:T(8,128)S(1)} %fusion.11), channel_id=1, source_target_pairs={{0,4},{1,5},{2,6},{3,7},{4,0},{5,1},{6,2},{7,3},{8,12},{9,13},{10,... | collective-permute-start | bytes 49160 | tf_op jit(solution)/shard_map/ppermute | solution.py:115
  103.0 6.7 %collective-permute-start.10 = (f32[64,64]{1,0:T(8,128)S(1)}, f32[64,64]{1,0:T(8,128)S(1)}, u32[]{:S(2)}, u32[]{:S(2)}) collective-permute-start(f32[64,64]{1,0:T(8,128)S(1)} %fusion.11), channel_id=1, source_target_pairs={{0,3},{1,4},{2,5},{3,6},{4,7},{5,0},{6,1},{7,2},{8,11},{9,12},{10,... | collective-permute-start | bytes 49160 | tf_op jit(solution)/shard_map/ppermute | solution.py:115
  105.0 7.4 %collective-permute-start.9 = (f32[64,64]{1,0:T(8,128)S(1)}, f32[64,64]{1,0:T(8,128)S(1)}, u32[]{:S(2)}, u32[]{:S(2)}) collective-permute-start(f32[64,64]{1,0:T(8,128)S(1)} %fusion.11), channel_id=1, source_target_pairs={{0,2},{1,3},{2,4},{3,5},{4,6},{5,7},{6,0},{7,1},{8,10},{9,11},{10,... | collective-permute-start | bytes 49160 | tf_op jit(solution)/shard_map/ppermute | solution.py:115
  107.1 5.3 %collective-permute-start.8 = (f32[64,64]{1,0:T(8,128)S(1)}, f32[64,64]{1,0:T(8,128)S(1)}, u32[]{:S(2)}, u32[]{:S(2)}) collective-permute-start(f32[64,64]{1,0:T(8,128)S(1)} %fusion.11), channel_id=1, source_target_pairs={{0,1},{1,2},{2,3},{3,4},{4,5},{5,6},{6,7},{7,0},{8,9},{9,10},{10,1... | collective-permute-start | bytes 49160 | tf_op jit(solution)/shard_map/ppermute | solution.py:115
Sparse Core Ops, SparseCore 0:
  11.3 47.5 all-gather.1

commit v2 on v1

v2 whole, which is shorter than its diff:
```python
import functools
import math

import jax
import jax.numpy as jnp
from jax import lax
from jax.experimental import pallas as pl
from jax.experimental.pallas import tpu as pltpu
from jax.sharding import Mesh
from jax.sharding import PartitionSpec as P

HID = 7168
SEQ_LEN = 128
BLK = 64
ITERS = 5
NY = 8
NZ = 8
NT = 8

momentum_decay = 0.95
linear_coeff = 3.4445
cubic_coeff = -4.775
quintic_coeff = 2.0315
norm_epsilon = 1e-07
update_gain = 0.2

HIGHEST = lax.Precision.HIGHEST


def gate_kernel(place_ref, lengths_ref, gate_ref, up_ref, cotangent_ref, out_ref):
    rows = gate_ref.shape[0]
    position = lax.broadcasted_iota(jnp.int32, gate_ref.shape, 0) + pl.program_id(0) * rows
    gate_value = gate_ref[...].astype(jnp.float32)
    up_value = up_ref[...].astype(jnp.float32)
    cotangent = cotangent_ref[...].astype(jnp.float32)
    sigmoid_gate = jax.nn.sigmoid(gate_value)
    gate_grad = cotangent * up_value * sigmoid_gate * (1.0 + gate_value * (1.0 - sigmoid_gate))
    trained = position < lengths_ref[place_ref[0]]
    out_ref[...] = jnp.where(trained, gate_grad, 0.0).astype(out_ref.dtype)


def gate_cotangent(place, lengths, gate_pre, up_pre, hidden_grad):
    tokens, columns = gate_pre.shape
    rows = tokens // 2
    block = pl.BlockSpec((rows, columns), lambda i: (i, 0))
    smem = pl.BlockSpec(memory_space=pltpu.SMEM)
    return pl.pallas_call(
        gate_kernel,
        grid=(tokens // rows,),
        out_shape=jax.ShapeDtypeStruct((tokens, columns), jnp.bfloat16),
        in_specs=[smem, smem, block, block, block],
        out_specs=block,
        compiler_params=pltpu.CompilerParams(vmem_limit_bytes=16 * 1024 * 1024),
        cost_estimate=pl.CostEstimate(
            flops=12 * tokens * columns, bytes_accessed=8 * tokens * columns, transcendentals=tokens * columns
        ),
        name="gate_cotangent",
    )(jnp.reshape(place, (1,)), lengths, gate_pre, up_pre, hidden_grad)


def partial_kernel(feature_offsets, grad_offsets, y_ref, t_ref, *refs):
    feature_refs, grad_refs = refs[:2], refs[2 : 2 + NY]
    out_ref, features, grads = refs[2 + NY :]
    tokens = grad_refs[0].shape[0]
    y, t = y_ref[0], t_ref[0]

    def place(group):
        return pl.ds(pl.multiple_of(group * tokens, tokens), tokens)

    blocks = [
        (ref, start) for ref in feature_refs for start in range(0, ref.shape[0], tokens)
    ]
    for offset, (ref, start) in zip(feature_offsets, blocks):
        features[place(lax.bitwise_xor(t, offset)), :] = ref[start : start + tokens, :]
    for offset, ref in zip(grad_offsets, grad_refs):
        grads[place(lax.rem(y + (NY + offset), NY)), :] = ref[...]
    rows = out_ref.shape[0]
    step = 128
    for start in range(0, rows, step):
        product = lax.dot_general(
            features[:, start : start + step],
            grads[...],
            (((0,), (0,)), ((), ())),
            preferred_element_type=jnp.float32,
        )
        out_ref[start : start + step, :] = product.astype(out_ref.dtype)


def partial_product(y, t, feature_offsets, grad_offsets, feature_halves, grad_blocks):
    tokens, columns = grad_blocks[0].shape
    rows = feature_halves[0].shape[1]
    vmem = pl.BlockSpec(memory_space=pltpu.VMEM)
    smem = pl.BlockSpec(memory_space=pltpu.SMEM)
    return pl.pallas_call(
        functools.partial(partial_kernel, tuple(feature_offsets), tuple(grad_offsets)),
        out_shape=jax.ShapeDtypeStruct((rows, columns), jnp.bfloat16),
        in_specs=[smem, smem] + [vmem] * (2 + NY),
        out_specs=vmem,
        scratch_shapes=[
            pltpu.VMEM((NY * tokens, rows), jnp.bfloat16),
            pltpu.VMEM((NY * tokens, columns), jnp.bfloat16),
        ],
        compiler_params=pltpu.CompilerParams(vmem_limit_bytes=32 * 1024 * 1024),
        cost_estimate=pl.CostEstimate(
            flops=2 * NY * tokens * rows * columns, bytes_accessed=6_000_000, transcendentals=0
        ),
        name="partial_product",
    )(jnp.reshape(y, (1,)), jnp.reshape(t, (1,)), *feature_halves, *grad_blocks)


def momentum_kernel(parts_ref, momentum_ref, moment_ref, nesterov_ref, grams_ref):
    grad = parts_ref[0].astype(jnp.float32)
    for part in range(1, parts_ref.shape[0]):
        grad = grad + parts_ref[part].astype(jnp.float32)
    new_moment = momentum_decay * momentum_ref[...] + grad
    moment_ref[...] = new_moment
    nesterov = grad + momentum_decay * new_moment
    nesterov_ref[...] = nesterov
    gram = lax.dot_general(
        nesterov, nesterov, (((1,), (1,)), ((), ())), precision=HIGHEST, preferred_element_type=jnp.float32
    )
    half = gram.shape[0] // 2
    packed = jnp.concatenate([gram[:half], gram[half:]], axis=1)
    for part in range(grams_ref.shape[0]):
        grams_ref[part] = packed


def momentum_step(parts, momentum):
    size, columns = momentum.shape
    vmem = pl.BlockSpec(memory_space=pltpu.VMEM)
    return pl.pallas_call(
        momentum_kernel,
        out_shape=(
            jax.ShapeDtypeStruct((size, columns), jnp.float32),
            jax.ShapeDtypeStruct((size, columns), jnp.float32),
            jax.ShapeDtypeStruct((NT, size // 2, 2 * size), jnp.float32),
        ),
        in_specs=[vmem, vmem],
        out_specs=(vmem, vmem, vmem),
        compiler_params=pltpu.CompilerParams(vmem_limit_bytes=16 * 1024 * 1024),
        cost_estimate=pl.CostEstimate(flops=60_000_000, bytes_accessed=1_700_000, transcendentals=0),
        name="momentum_step",
    )(parts, momentum)


def polar_kernel(grams_ref, block_ref, out_ref):
    mul = functools.partial(jnp.dot, precision=HIGHEST, preferred_element_type=jnp.float32)
    packed = grams_ref[0]
    for part in range(1, grams_ref.shape[0]):
        packed = packed + grams_ref[part]
    size = packed.shape[1] // 2
    total = jnp.concatenate([packed[:, :size], packed[:, size:]], axis=0)
    shape = (size, size)
    diagonal = lax.broadcasted_iota(jnp.int32, shape, 0) == lax.broadcasted_iota(jnp.int32, shape, 1)
    eye = jnp.where(diagonal, 1.0, 0.0).astype(jnp.float32)
    squares = jnp.sum(jnp.sum(total * eye, axis=1, keepdims=True), axis=0, keepdims=True)
    inverse = 1.0 / (jnp.sqrt(squares) + norm_epsilon)
    gram = total * inverse * inverse
    mapping = None
    for iteration in range(ITERS):
        square = mul(gram, gram)
        poly = linear_coeff * eye + cubic_coeff * gram + quintic_coeff * square
        mapping = poly if iteration == 0 else mul(poly, mapping)
        if iteration < ITERS - 1:
            gram = mul(mul(poly, gram), poly)
    mapping = mapping * (inverse * (update_gain * math.sqrt(HID)))
    units = out_ref.shape[2]
    rows = mul(mapping, block_ref[...]).astype(out_ref.dtype)
    for part in range(out_ref.shape[0]):
        out_ref[part] = rows[:, part * units : (part + 1) * units]


def polar_update(grams, block):
    size, columns = block.shape
    vmem = pl.BlockSpec(memory_space=pltpu.VMEM)
    return pl.pallas_call(
        polar_kernel,
        out_shape=jax.ShapeDtypeStruct((NY, size, columns // NY), jnp.bfloat16),
        in_specs=[vmem, vmem],
        out_specs=vmem,
        compiler_params=pltpu.CompilerParams(vmem_limit_bytes=16 * 1024 * 1024),
        cost_estimate=pl.CostEstimate(flops=100_000_000, bytes_accessed=600_000, transcendentals=0),
        name="polar_update",
    )(grams, block)


def per_device(features, gate_pre, up_pre, hidden_grad, lengths, momentum):
    y, z, t = (lax.axis_index(name) for name in ("y", "z", "t"))
    swap = [(a * NT + b, b * NT + a) for a in range(NY) for b in range(NT)]
    held = lax.ppermute(features, ("y", "t"), swap)
    gate_grad = gate_cotangent(y * NZ + z, lengths, gate_pre, up_pre, hidden_grad)

    offsets = [0]
    halves = None
    for mask in [m for m in (1, 2, 6) if m < NT]:
        arrived = lax.ppermute(held, "t", [(i, i ^ mask) for i in range(NT)])
        halves = (held, arrived)
        offsets = offsets + [o ^ mask for o in offsets]
        held = jnp.concatenate(halves, axis=0)

    grad_blocks, grad_offsets = [gate_grad], [0]
    up, down = gate_grad, gate_grad
    for step in range(1, NY // 2 + 1):
        up = lax.ppermute(up, "y", [(i, (i + 1) % NY) for i in range(NY)])
        grad_blocks.append(up)
        grad_offsets.append(-step)
        if 2 * step < NY:
            down = lax.ppermute(down, "y", [(i, (i + NY - 1) % NY) for i in range(NY)])
            grad_blocks.append(down)
            grad_offsets.append(step)

    partial_value = partial_product(y, t, offsets, grad_offsets, halves, grad_blocks)
    pieces = partial_value.reshape(NZ, BLK, partial_value.shape[1])
    received = lax.all_to_all(pieces, "z", split_axis=0, concat_axis=0, tiled=True)
    new_moment, nesterov, grams = momentum_step(received, momentum)
    grams = lax.all_to_all(grams, "t", split_axis=0, concat_axis=0, tiled=True)
    by_y = polar_update(grams, nesterov)
    by_y = lax.all_to_all(by_y, "y", split_axis=0, concat_axis=0, tiled=True)
    unit_count = by_y.shape[2] // NZ
    by_z = by_y.reshape(NY, BLK, NZ, unit_count).transpose(2, 3, 0, 1)
    by_z = lax.all_to_all(by_z, "z", split_axis=0, concat_axis=0, tiled=True)
    result = by_z.transpose(1, 2, 0, 3).reshape(1, unit_count, NY * NZ * BLK)
    return result, new_moment


def solution(mesh):
    fine = Mesh(mesh.devices.reshape(NY, NZ, NT), ("y", "z", "t"))
    split = P(("y", "z"), "t")
    return jax.shard_map(
        per_device,
        mesh=fine,
        in_specs=(split, split, split, split, P(), split),
        out_specs=(P("t", ("y", "z"), None), split),
        check_vma=False,
    )
```

time: 150 us -> 139 us (0.927)
  the two profiles are of different devices: /device:TPU:8 before, /device:TPU:2 now
where the time goes in v2:
time: 139 us; the launch traced here: 138 us
  blocking collectives  68.2 us (49%)
  starting transfers between devices  36.3 us (26%)
  waiting for transfers between devices  21.5 us (15%)
  Pallas kernels  6.16 us (4%)
  local copies, waits for them, and re-layouts  5 us (4%)
    all_to_all x1, blocking collectives, per_device(): lax.all_to_all(pieces, 'z', split_axis=0, concat_axis=0, tiled=True)  33.3 us
    ppermute x3, starting transfers between devices, per_device(): down = lax.ppermute(down, 'y', [(i, (i + NY - 1) % NY) for i in range(NY)])  15.6 us
    all_to_all x1, blocking collectives, per_device(): by_y = lax.all_to_all(by_y, 'y', split_axis=0, concat_axis=0, tiled=True)  14.1 us
    all_to_all x1, blocking collectives, per_device(): by_z = lax.all_to_all(by_z, 'z', split_axis=0, concat_axis=0, tiled=True)  11.3 us
    ppermute x1, waiting for transfers between devices, per_device(): held = lax.ppermute(features, ('y', 't'), swap)  11 us
    all_to_all x1, blocking collectives, per_device(): grams = lax.all_to_all(grams, 't', split_axis=0, concat_axis=0, tiled=True)  9.61 us
    ppermute x4, starting transfers between devices, per_device(): up = lax.ppermute(up, 'y', [(i, (i + 1) % NY) for i in range(NY)])  8.19 us
    ppermute x3, starting transfers between devices, per_device(): arrived = lax.ppermute(held, 't', [(i, i ^ mask) for i in range(NT)])  8.11 us
  transfers between devices with their start and end apart: 11, of which 5 were waited for; matrix products, arithmetic and copies ran while one was open for 0% of the time, Pallas kernels for 1%

profile of v2, /device:TPU:2, one launch (start us, length us, event | category | flops | bytes accessed | tf_op | source)
XLA Modules:
  0.0 138.1 jit_solution(14097269027863699283)
XLA Ops:
  0.6 4.5 %collective-permute-start = (bf16[128,512]{1,0:T(8,128)(2,1)}, bf16[128,512]{1,0:T(8,128)(2,1)S(1)}, u32[]{:S(2)}, u32[]{:S(2)}) collective-permute-start(bf16[128,512]{1,0:T(8,128)(2,1)} %param.6), channel_id=1, source_target_pairs={{0,0},{1,64},{2,128},{3,192},{4,256},{5,320},{6,384},{7,448},{64,1... | collective-permute-start | bytes 393224 | tf_op jit(solution)/shard_map/ppermute | solution.py:190
  5.1 11.0 %collective-permute-done = bf16[128,512]{1,0:T(8,128)(2,1)S(1)} collective-permute-done((bf16[128,512]{1,0:T(8,128)(2,1)}, bf16[128,512]{1,0:T(8,128)(2,1)S(1)}, u32[]{:S(2)}, u32[]{:S(2)}) %collective-permute-start) | collective-permute-done | bytes 131104 | tf_op jit(solution)/shard_map/ppermute | solution.py:190
  16.1 1.9 %collective-permute-start.1 = (bf16[128,512]{1,0:T(8,128)(2,1)S(1)}, bf16[128,512]{1,0:T(8,128)(2,1)S(1)}, u32[]{:S(2)}, u32[]{:S(2)}) collective-permute-start(bf16[128,512]{1,0:T(8,128)(2,1)S(1)} %collective-permute-done), channel_id=1, source_target_pairs={{0,1},{1,0},{2,3},{3,2},{4,5},{5,4},{6,7},{7,6},{8,9},{9,8},{10,11... | collective-permute-start | bytes 393224 | tf_op jit(solution)/shard_map/ppermute | solution.py:196
  18.0 0.0 copy-start.4
  18.0 0.6 copy-done.4
  18.6 0.0 copy-start
  18.6 0.9 copy-done
  19.6 0.0 copy-start.1
  19.6 0.9 copy-done.1
  20.5 0.0 copy-start.2
  20.5 0.9 copy-done.2
  21.5 0.8 gate_cotangent.1.refs_2_
  22.3 2.1 %collective-permute-start.4 = (bf16[128,896]{1,0:T(8,128)(2,1)S(1)}, bf16[128,896]{1,0:T(8,128)(2,1)S(1)}, u32[]{:S(2)}, u32[]{:S(2)}) collective-permute-start(bf16[128,896]{1,0:T(8,128)(2,1)S(1)} %gate_cotangent.1.refs_2_), channel_id=1, source_target_pairs={{0,64},{64,128},{128,192},{192,256},{256,320},{320,384},{384,448},... | collective-permute-start | bytes 688136 | tf_op jit(solution)/shard_map/ppermute | solution.py:204
  24.4 0.0 collective-permute-done.1
  24.4 1.9 %collective-permute-start.2 = (bf16[256,512]{1,0:T(8,128)(2,1)S(1)}, bf16[256,512]{1,0:T(8,128)(2,1)S(1)}, u32[]{:S(2)}, u32[]{:S(2)}) collective-permute-start(bf16[256,512]{1,0:T(8,128)(2,1)S(1)} %pad_maximum_fusion), channel_id=1, source_target_pairs={{0,2},{1,3},{2,0},{3,1},{4,6},{5,7},{6,4},{7,5},{8,10},{9,11},{10,... | collective-permute-start | bytes 786440 | tf_op jit(solution)/shard_map/ppermute | solution.py:196
  26.3 6.6 %collective-permute-start.5 = (bf16[128,896]{1,0:T(8,128)(2,1)S(1)}, bf16[128,896]{1,0:T(8,128)(2,1)S(1)}, u32[]{:S(2)}, u32[]{:S(2)}) collective-permute-start(bf16[128,896]{1,0:T(8,128)(2,1)S(1)} %gate_cotangent.1.refs_2_), channel_id=1, source_target_pairs={{0,448},{64,0},{128,64},{192,128},{256,192},{320,256},{384,320},{4... | collective-permute-start | bytes 688136 | tf_op jit(solution)/shard_map/ppermute | solution.py:208
  33.0 0.4 collective-permute-done.4.refs_3_
  33.4 1.9 %collective-permute-start.6 = (bf16[128,896]{1,0:T(8,128)(2,1)S(1)}, bf16[128,896]{1,0:T(8,128)(2,1)S(1)}, u32[]{:S(2)}, u32[]{:S(2)}) collective-permute-start(bf16[128,896]{1,0:T(8,128)(2,1)S(1)} %collective-permute-done.4.refs_3_), channel_id=1, source_target_pairs={{0,64},{64,128},{128,192},{192,256},{256,320},{320,384},{384,448},... | collective-permute-start | bytes 688136 | tf_op jit(solution)/shard_map/ppermute | solution.py:204
  35.3 0.0 collective-permute-done.2
  35.3 4.3 %collective-permute-start.3 = (bf16[512,512]{1,0:T(8,128)(2,1)S(1)}, bf16[512,512]{1,0:T(8,128)(2,1)S(1)}, u32[]{:S(2)}, u32[]{:S(2)}) collective-permute-start(bf16[512,512]{1,0:T(8,128)(2,1)S(1)} %constant_dynamic-update-slice_fusion.refs_0_), channel_id=1, source_target_pairs={{0,6},{1,7},{2,4},{3,5},{4,2},{5,3},{6,0},{7,1},{8,14},{9,15},{10,... | collective-permute-start | bytes 1572872 | tf_op jit(solution)/shard_map/ppermute | solution.py:196
  39.6 0.0 collective-permute-done.5.refs_4_
  39.6 4.3 %collective-permute-start.7 = (bf16[128,896]{1,0:T(8,128)(2,1)S(1)}, bf16[128,896]{1,0:T(8,128)(2,1)S(1)}, u32[]{:S(2)}, u32[]{:S(2)}) collective-permute-start(bf16[128,896]{1,0:T(8,128)(2,1)S(1)} %collective-permute-done.5.refs_4_), channel_id=1, source_target_pairs={{0,448},{64,0},{128,64},{192,128},{256,192},{320,256},{384,320},{4... | collective-permute-start | bytes 688136 | tf_op jit(solution)/shard_map/ppermute | solution.py:208
  43.9 0.0 collective-permute-done.6.refs_5_
  43.9 2.2 %collective-permute-start.8 = (bf16[128,896]{1,0:T(8,128)(2,1)S(1)}, bf16[128,896]{1,0:T(8,128)(2,1)S(1)}, u32[]{:S(2)}, u32[]{:S(2)}) collective-permute-start(bf16[128,896]{1,0:T(8,128)(2,1)S(1)} %collective-permute-done.6.refs_5_), channel_id=1, source_target_pairs={{0,64},{64,128},{128,192},{192,256},{256,320},{320,384},{384,448},... | collective-permute-start | bytes 688136 | tf_op jit(solution)/shard_map/ppermute | solution.py:204
  46.2 2.9 %collective-permute-done.7.refs_6_ = bf16[128,896]{1,0:T(8,128)(2,1)S(1)} collective-permute-done((bf16[128,896]{1,0:T(8,128)(2,1)S(1)}, bf16[128,896]{1,0:T(8,128)(2,1)S(1)}, u32[]{:S(2)}, u32[]{:S(2)}) %collective-permute-start.7) | collective-permute-done | bytes 229408 | tf_op jit(solution)/shard_map/ppermute | solution.py:208
  49.1 4.7 %collective-permute-start.9 = (bf16[128,896]{1,0:T(8,128)(2,1)S(1)}, bf16[128,896]{1,0:T(8,128)(2,1)S(1)}, u32[]{:S(2)}, u32[]{:S(2)}) collective-permute-start(bf16[128,896]{1,0:T(8,128)(2,1)S(1)} %collective-permute-done.7.refs_6_), channel_id=1, source_target_pairs={{0,448},{64,0},{128,64},{192,128},{256,192},{320,256},{384,320},{4... | collective-permute-start | bytes 688136 | tf_op jit(solution)/shard_map/ppermute | solution.py:208
  53.8 0.0 collective-permute-done.8.refs_7_
  53.8 1.9 %collective-permute-start.10 = (bf16[128,896]{1,0:T(8,128)(2,1)S(1)}, bf16[128,896]{1,0:T(8,128)(2,1)S(1)}, u32[]{:S(2)}, u32[]{:S(2)}) collective-permute-start(bf16[128,896]{1,0:T(8,128)(2,1)S(1)} %collective-permute-done.8.refs_7_), channel_id=1, source_target_pairs={{0,64},{64,128},{128,192},{192,256},{256,320},{320,384},{384,448},... | collective-permute-start | bytes 688136 | tf_op jit(solution)/shard_map/ppermute | solution.py:204
  55.7 1.6 %collective-permute-done.9.refs_8_ = bf16[128,896]{1,0:T(8,128)(2,1)S(1)} collective-permute-done((bf16[128,896]{1,0:T(8,128)(2,1)S(1)}, bf16[128,896]{1,0:T(8,128)(2,1)S(1)}, u32[]{:S(2)}, u32[]{:S(2)}) %collective-permute-start.9) | collective-permute-done | bytes 229408 | tf_op jit(solution)/shard_map/ppermute | solution.py:208
  57.3 5.6 %collective-permute-done.10.refs_9_ = bf16[128,896]{1,0:T(8,128)(2,1)S(1)} collective-permute-done((bf16[128,896]{1,0:T(8,128)(2,1)S(1)}, bf16[128,896]{1,0:T(8,128)(2,1)S(1)}, u32[]{:S(2)}, u32[]{:S(2)}) %collective-permute-start.10) | collective-permute-done | bytes 229408 | tf_op jit(solution)/shard_map/ppermute | solution.py:204
  62.9 0.0 collective-permute-done.3.refs_1_
  62.9 1.5 %partial_product.1 = bf16[512,896]{1,0:T(8,128)(2,1)S(1)} custom-call(s32[1]{0:T(128)} %bitcast.y_ref, s32[1]{0:T(128)} %bitcast.1.t_ref, bf16[512,512]{1,0:T(8,128)(2,1)S(1)} %constant_dynamic-update-slice_fusion.refs_0_, bf16[512,512]{1,0:T(8,128)(2,1)S(1)} %collective-permute-done.3.refs_1_, bf16[128,896]{1,0:T(8,128)(2,1)S(1)} %gate_cotangent.1.refs_2_, ...), custom_call_target="tpu_custom_call" | custom-call | flops 939524096 | bytes 6000000 | tf_op jit(solution)/shard_map/partial_product/pallas_call | solution.py:94
  64.4 0.0 copy-start.3
  64.4 33.3 %all_to_all.20.parts_ref = bf16[8,64,896]{2,1,0:T(8,128)(2,1)S(1)} all-to-all(bf16[8,64,896]{2,1,0:T(8,128)(2,1)S(1)} %bitcast.10), channel_id=1, replica_groups=mesh['y'=8,'z'=8,'t'=8] {'z'}, dimensions={0} | all-to-all | bytes 1835008 | tf_op jit(solution)/shard_map/all_to_all | solution.py:214
  97.7 0.0 copy-done.3
  97.7 0.9 momentum_step.1
  98.6 9.6 %all_to_all.21.grams_ref = f32[8,32,128]{2,1,0:T(8,128)S(1)} all-to-all(f32[8,32,128]{2,1,0:T(8,128)S(1)} %get-tuple-element.5), channel_id=1, replica_groups=mesh['y'=8,'z'=8,'t'=8] {'t'}, dimensions={0} | all-to-all | bytes 262144 | tf_op jit(solution)/shard_map/all_to_all | solution.py:216
  108.2 3.0 %polar_update.1 = bf16[8,64,112]{2,1,0:T(8,128)(2,1)S(1)} custom-call(f32[8,32,128]{2,1,0:T(8,128)S(1)} %all_to_all.21.grams_ref, f32[64,896]{1,0:T(8,128)S(1)} %get-tuple-element.6.block_ref), custom_call_target="tpu_custom_call" | custom-call | flops 100000000 | bytes 600000 | tf_op jit(solution)/shard_map/polar_update/pallas_call | solution.py:176
  111.2 14.1 %all_to_all.22 = bf16[8,64,112]{2,1,0:T(8,128)(2,1)S(1)} all-to-all(bf16[8,64,112]{2,1,0:T(8,128)(2,1)S(1)} %polar_update.1), channel_id=1, replica_groups=mesh['y'=8,'z'=8,'t'=8] {'y'}, dimensions={0} | all-to-all | bytes 229376 | tf_op jit(solution)/shard_map/all_to_all | solution.py:218
  125.3 0.2 copy.10
  125.5 0.2 reshape.28
  125.6 11.3 %all_to_all.23 = bf16[8,2,3584]{2,1,0:T(2,128)(2,1)S(1)} all-to-all(bf16[8,2,3584]{2,1,0:T(2,128)(2,1)S(1)} %reshape.28), channel_id=1, replica_groups=mesh['y'=8,'z'=8,'t'=8] {'z'}, dimensions={0} | all-to-all | bytes 229376 | tf_op jit(solution)/shard_map/all_to_all | solution.py:221
  136.9 0.2 reshape.29
  137.1 0.1 copy.11
  137.2 0.9 reshape.27
  (4 shorter events, 0.1 us)
Async XLA Ops:
  0.6 15.4 %collective-permute-start = (bf16[128,512]{1,0:T(8,128)(2,1)}, bf16[128,512]{1,0:T(8,128)(2,1)S(1)}, u32[]{:S(2)}, u32[]{:S(2)}) collective-permute-start(bf16[128,512]{1,0:T(8,128)(2,1)} %param.6), channel_id=1, source_target_pairs={{0,0},{1,64},{2,128},{3,192},{4,256},{5,320},{6,384},{7,448},{64,1... | collective-permute-start | bytes 393224 | tf_op jit(solution)/shard_map/ppermute | solution.py:190
  16.1 8.3 %collective-permute-start.1 = (bf16[128,512]{1,0:T(8,128)(2,1)S(1)}, bf16[128,512]{1,0:T(8,128)(2,1)S(1)}, u32[]{:S(2)}, u32[]{:S(2)}) collective-permute-start(bf16[128,512]{1,0:T(8,128)(2,1)S(1)} %collective-permute-done), channel_id=1, source_target_pairs={{0,1},{1,0},{2,3},{3,2},{4,5},{5,4},{6,7},{7,6},{8,9},{9,8},{10,11... | collective-permute-start | bytes 393224 | tf_op jit(solution)/shard_map/ppermute | solution.py:196
  18.0 0.7 copy-start.4
  18.6 0.9 copy-start
  19.6 0.9 copy-start.1
  20.5 0.9 copy-start.2
  22.3 11.1 %collective-permute-start.4 = (bf16[128,896]{1,0:T(8,128)(2,1)S(1)}, bf16[128,896]{1,0:T(8,128)(2,1)S(1)}, u32[]{:S(2)}, u32[]{:S(2)}) collective-permute-start(bf16[128,896]{1,0:T(8,128)(2,1)S(1)} %gate_cotangent.1.refs_2_), channel_id=1, source_target_pairs={{0,64},{64,128},{128,192},{192,256},{256,320},{320,384},{384,448},... | collective-permute-start | bytes 688136 | tf_op jit(solution)/shard_map/ppermute | solution.py:204
  24.4 10.9 %collective-permute-start.2 = (bf16[256,512]{1,0:T(8,128)(2,1)S(1)}, bf16[256,512]{1,0:T(8,128)(2,1)S(1)}, u32[]{:S(2)}, u32[]{:S(2)}) collective-permute-start(bf16[256,512]{1,0:T(8,128)(2,1)S(1)} %pad_maximum_fusion), channel_id=1, source_target_pairs={{0,2},{1,3},{2,0},{3,1},{4,6},{5,7},{6,4},{7,5},{8,10},{9,11},{10,... | collective-permute-start | bytes 786440 | tf_op jit(solution)/shard_map/ppermute | solution.py:196
  26.3 13.3 %collective-permute-start.5 = (bf16[128,896]{1,0:T(8,128)(2,1)S(1)}, bf16[128,896]{1,0:T(8,128)(2,1)S(1)}, u32[]{:S(2)}, u32[]{:S(2)}) collective-permute-start(bf16[128,896]{1,0:T(8,128)(2,1)S(1)} %gate_cotangent.1.refs_2_), channel_id=1, source_target_pairs={{0,448},{64,0},{128,64},{192,128},{256,192},{320,256},{384,320},{4... | collective-permute-start | bytes 688136 | tf_op jit(solution)/shard_map/ppermute | solution.py:208
  33.4 10.6 %collective-permute-start.6 = (bf16[128,896]{1,0:T(8,128)(2,1)S(1)}, bf16[128,896]{1,0:T(8,128)(2,1)S(1)}, u32[]{:S(2)}, u32[]{:S(2)}) collective-permute-start(bf16[128,896]{1,0:T(8,128)(2,1)S(1)} %collective-permute-done.4.refs_3_), channel_id=1, source_target_pairs={{0,64},{64,128},{128,192},{192,256},{256,320},{320,384},{384,448},... | collective-permute-start | bytes 688136 | tf_op jit(solution)/shard_map/ppermute | solution.py:204
  35.3 27.6 %collective-permute-start.3 = (bf16[512,512]{1,0:T(8,128)(2,1)S(1)}, bf16[512,512]{1,0:T(8,128)(2,1)S(1)}, u32[]{:S(2)}, u32[]{:S(2)}) collective-permute-start(bf16[512,512]{1,0:T(8,128)(2,1)S(1)} %constant_dynamic-update-slice_fusion.refs_0_), channel_id=1, source_target_pairs={{0,6},{1,7},{2,4},{3,5},{4,2},{5,3},{6,0},{7,1},{8,14},{9,15},{10,... | collective-permute-start | bytes 1572872 | tf_op jit(solution)/shard_map/ppermute | solution.py:196
  39.6 9.5 %collective-permute-start.7 = (bf16[128,896]{1,0:T(8,128)(2,1)S(1)}, bf16[128,896]{1,0:T(8,128)(2,1)S(1)}, u32[]{:S(2)}, u32[]{:S(2)}) collective-permute-start(bf16[128,896]{1,0:T(8,128)(2,1)S(1)} %collective-permute-done.5.refs_4_), channel_id=1, source_target_pairs={{0,448},{64,0},{128,64},{192,128},{256,192},{320,256},{384,320},{4... | collective-permute-start | bytes 688136 | tf_op jit(solution)/shard_map/ppermute | solution.py:208
  43.9 9.9 %collective-permute-start.8 = (bf16[128,896]{1,0:T(8,128)(2,1)S(1)}, bf16[128,896]{1,0:T(8,128)(2,1)S(1)}, u32[]{:S(2)}, u32[]{:S(2)}) collective-permute-start(bf16[128,896]{1,0:T(8,128)(2,1)S(1)} %collective-permute-done.6.refs_5_), channel_id=1, source_target_pairs={{0,64},{64,128},{128,192},{192,256},{256,320},{320,384},{384,448},... | collective-permute-start | bytes 688136 | tf_op jit(solution)/shard_map/ppermute | solution.py:204
  49.1 8.2 %collective-permute-start.9 = (bf16[128,896]{1,0:T(8,128)(2,1)S(1)}, bf16[128,896]{1,0:T(8,128)(2,1)S(1)}, u32[]{:S(2)}, u32[]{:S(2)}) collective-permute-start(bf16[128,896]{1,0:T(8,128)(2,1)S(1)} %collective-permute-done.7.refs_6_), channel_id=1, source_target_pairs={{0,448},{64,0},{128,64},{192,128},{256,192},{320,256},{384,320},{4... | collective-permute-start | bytes 688136 | tf_op jit(solution)/shard_map/ppermute | solution.py:208
  53.8 9.1 %collective-permute-start.10 = (bf16[128,896]{1,0:T(8,128)(2,1)S(1)}, bf16[128,896]{1,0:T(8,128)(2,1)S(1)}, u32[]{:S(2)}, u32[]{:S(2)}) collective-permute-start(bf16[128,896]{1,0:T(8,128)(2,1)S(1)} %collective-permute-done.8.refs_7_), channel_id=1, source_target_pairs={{0,64},{64,128},{128,192},{192,256},{256,320},{320,384},{384,448},... | collective-permute-start | bytes 688136 | tf_op jit(solution)/shard_map/ppermute | solution.py:204
  64.4 33.3 %copy-start.3 = (f32[64,896]{1,0:T(8,128)S(1)}, f32[64,896]{1,0:T(8,128)}, u32[]{:S(2)}) copy-start(f32[64,896]{1,0:T(8,128)} %momentum_ref.1) | copy-start | bytes 688132

commit v3 on v2

--- a/solution.py
+++ b/solution.py
@@ -25,79 +25,132 @@
 update_gain = 0.2
 
 HIGHEST = lax.Precision.HIGHEST
-
-
-def gate_kernel(place_ref, lengths_ref, gate_ref, up_ref, cotangent_ref, out_ref):
-    rows = gate_ref.shape[0]
-    position = lax.broadcasted_iota(jnp.int32, gate_ref.shape, 0) + pl.program_id(0) * rows
-    gate_value = gate_ref[...].astype(jnp.float32)
-    up_value = up_ref[...].astype(jnp.float32)
-    cotangent = cotangent_ref[...].astype(jnp.float32)
+AXES = ("y", "z", "t")
+
+
+def prepare_kernel(place_ref, lengths_ref, features_in, gate_in, up_in, cotangent_in, turned_ref, grad_ref, *scratch):
+    buffers, arrived = scratch[:4], scratch[4]
+    sources = (features_in, gate_in, up_in, cotangent_in)
+    copies = [
+        pltpu.make_async_copy(source, buffer, arrived.at[i])
+        for i, (source, buffer) in enumerate(zip(sources, buffers))
+    ]
+    for copy in copies:
+        copy.start()
+    copies[0].wait()
+    turned_ref[...] = buffers[0][...].T
+    for copy in copies[1:]:
+        copy.wait()
+    gate_value, up_value, cotangent = (buffer[...].astype(jnp.float32) for buffer in buffers[1:])
     sigmoid_gate = jax.nn.sigmoid(gate_value)
     gate_grad = cotangent * up_value * sigmoid_gate * (1.0 + gate_value * (1.0 - sigmoid_gate))
+    position = lax.broadcasted_iota(jnp.int32, gate_value.shape, 0)
     trained = position < lengths_ref[place_ref[0]]
-    out_ref[...] = jnp.where(trained, gate_grad, 0.0).astype(out_ref.dtype)
-
-
-def gate_cotangent(place, lengths, gate_pre, up_pre, hidden_grad):
+    grad_ref[...] = jnp.where(trained, gate_grad, 0.0).astype(grad_ref.dtype)
+
+
+def prepare(place, lengths, features, gate_pre, up_pre, hidden_grad):
     tokens, columns = gate_pre.shape
-    rows = tokens // 2
-    block = pl.BlockSpec((rows, columns), lambda i: (i, 0))
+    rows = features.shape[1]
+    hbm = pl.BlockSpec(memory_space=pltpu.HBM)
+    vmem = pl.BlockSpec(memory_space=pltpu.VMEM)
     smem = pl.BlockSpec(memory_space=pltpu.SMEM)
-    return pl.pallas_call(
-        gate_kernel,
-        grid=(tokens // rows,),
-        out_shape=jax.ShapeDtypeStruct((tokens, columns), jnp.bfloat16),
-        in_specs=[smem, smem, block, block, block],
-        out_specs=block,
-        compiler_params=pltpu.CompilerParams(vmem_limit_bytes=16 * 1024 * 1024),
+    arrays = (features, gate_pre, up_pre, hidden_grad)
+    return pl.pallas_call(
+        prepare_kernel,
+        out_shape=(
+            jax.ShapeDtypeStruct((rows, tokens), jnp.bfloat16),
+            jax.ShapeDtypeStruct((tokens, columns), jnp.bfloat16),
+        ),
+        in_specs=[smem, smem] + [hbm] * 4,
+        out_specs=(vmem, vmem),
+        scratch_shapes=[pltpu.VMEM(array.shape, array.dtype) for array in arrays]
+        + [pltpu.SemaphoreType.DMA((4,))],
+        compiler_params=pltpu.CompilerParams(vmem_limit_bytes=60 * 1024 * 1024),
         cost_estimate=pl.CostEstimate(
             flops=12 * tokens * columns, bytes_accessed=8 * tokens * columns, transcendentals=tokens * columns
         ),
-        name="gate_cotangent",
-    )(jnp.reshape(place, (1,)), lengths, gate_pre, up_pre, hidden_grad)
-
-
-def partial_kernel(feature_offsets, grad_offsets, y_ref, t_ref, *refs):
+        name="prepare",
+    )(jnp.reshape(place, (1,)), lengths, *arrays)
+
+
+def device_number(y, z, t):
+    return (y * NZ + z) * NT + t
+
+
+def ring_pairs(step):
+    pairs = []
+    for y in range(NY):
+        for z in range(NZ):
+            for t in range(NT):
+                target = (y, (z + step) % NZ, t) if t % 2 else ((y + step) % NY, z, t)
+                pairs.append((device_number(y, z, t), device_number(*target)))
+    return pairs
+
+
+def tensor_pairs(masks):
+    return [
+        (device_number(y, z, t), device_number(y, z, t ^ masks[t % 2]))
+        for y in range(NY)
+        for z in range(NZ)
+        for t in range(NT)
+    ]
+
+
+def cross_groups():
+    along_z = [[device_number(y, z, t) for z in range(NZ)] for y in range(NY) for t in range(0, NT, 2)]
+    along_y = [[device_number(y, z, t) for y in range(NY)] for z in range(NZ) for t in range(1, NT, 2)]
+    return along_z + along_y
+
+
+def partial_kernel(orders, grad_offsets, y_ref, z_ref, t_ref, *refs):
     feature_refs, grad_refs = refs[:2], refs[2 : 2 + NY]
     out_ref, features, grads = refs[2 + NY :]
     tokens = grad_refs[0].shape[0]
-    y, t = y_ref[0], t_ref[0]
-
-    def place(group):
-        return pl.ds(pl.multiple_of(group * tokens, tokens), tokens)
-
-    blocks = [
-        (ref, start) for ref in feature_refs for start in range(0, ref.shape[0], tokens)
-    ]
-    for offset, (ref, start) in zip(feature_offsets, blocks):
-        features[place(lax.bitwise_xor(t, offset)), :] = ref[start : start + tokens, :]
+    rows = out_ref.shape[0]
+    t = t_ref[0]
+    odd = lax.rem(t, 2)
+    blocks = [(ref, start) for ref in feature_refs for start in range(0, ref.shape[0], rows)]
+
+    @pl.when(odd == 0)
+    def _():
+        for offset, (ref, start) in zip(orders[0], blocks):
+            group = lax.bitwise_xor(t, offset)
+            features[:, pl.ds(pl.multiple_of(group * tokens, tokens), tokens)] = ref[start : start + rows, :]
+
+    @pl.when(odd == 1)
+    def _():
+        for offset, (ref, start) in zip(orders[1], blocks):
+            group = lax.bitwise_xor(t, offset)
+            for z in range(NZ):
+                features[pl.ds(pl.multiple_of(group * BLK, BLK), BLK), z * tokens : (z + 1) * tokens] = ref[
+                    start + z * BLK : start + (z + 1) * BLK, :
+                ]
+
+    own = jnp.where(odd == 0, y_ref[0], z_ref[0])
     for offset, ref in zip(grad_offsets, grad_refs):
-        grads[place(lax.rem(y + (NY + offset), NY)), :] = ref[...]
-    rows = out_ref.shape[0]
+        group = lax.rem(own + (NY + offset), NY)
+        grads[pl.ds(pl.multiple_of(group * tokens, tokens), tokens), :] = ref[...]
     step = 128
     for start in range(0, rows, step):
-        product = lax.dot_general(
-            features[:, start : start + step],
-            grads[...],
-            (((0,), (0,)), ((), ())),
-            preferred_element_type=jnp.float32,
+        product = jnp.dot(
+            features[start : start + step, :], grads[...], preferred_element_type=jnp.float32
         )
         out_ref[start : start + step, :] = product.astype(out_ref.dtype)
 
 
-def partial_product(y, t, feature_offsets, grad_offsets, feature_halves, grad_blocks):
+def partial_product(y, z, t, orders, grad_offsets, feature_halves, grad_blocks):
     tokens, columns = grad_blocks[0].shape
-    rows = feature_halves[0].shape[1]
+    rows = NZ * BLK
     vmem = pl.BlockSpec(memory_space=pltpu.VMEM)
     smem = pl.BlockSpec(memory_space=pltpu.SMEM)
     return pl.pallas_call(
-        functools.partial(partial_kernel, tuple(feature_offsets), tuple(grad_offsets)),
+        functools.partial(partial_kernel, orders, tuple(grad_offsets)),
         out_shape=jax.ShapeDtypeStruct((rows, columns), jnp.bfloat16),
-        in_specs=[smem, smem] + [vmem] * (2 + NY),
+        in_specs=[smem] * 3 + [vmem] * (2 + NY),
         out_specs=vmem,
         scratch_shapes=[
-            pltpu.VMEM((NY * tokens, rows), jnp.bfloat16),
+            pltpu.VMEM((rows, NY * tokens), jnp.bfloat16),
             pltpu.VMEM((NY * tokens, columns), jnp.bfloat16),
         ],
         compiler_params=pltpu.CompilerParams(vmem_limit_bytes=32 * 1024 * 1024),
@@ -105,7 +158,7 @@
             flops=2 * NY * tokens * rows * columns, bytes_accessed=6_000_000, transcendentals=0
         ),
         name="partial_product",
-    )(jnp.reshape(y, (1,)), jnp.reshape(t, (1,)), *feature_halves, *grad_blocks)
+    )(*(jnp.reshape(i, (1,)) for i in (y, z, t)), *feature_halves, *grad_blocks)
 
 
 def momentum_kernel(parts_ref, momentum_ref, moment_ref, nesterov_ref, grams_ref):
@@ -185,33 +238,42 @@
 
 
 def per_device(features, gate_pre, up_pre, hidden_grad, lengths, momentum):
-    y, z, t = (lax.axis_index(name) for name in ("y", "z", "t"))
+    y, z, t = (lax.axis_index(name) for name in AXES)
+    turned, gate_grad = prepare(y * NZ + z, lengths, features, gate_pre, up_pre, hidden_grad)
+
     swap = [(a * NT + b, b * NT + a) for a in range(NY) for b in range(NT)]
-    held = lax.ppermute(features, ("y", "t"), swap)
-    gate_grad = gate_cotangent(y * NZ + z, lengths, gate_pre, up_pre, hidden_grad)
-
-    offsets = [0]
-    halves = None
-    for mask in [m for m in (1, 2, 6) if m < NT]:
-        arrived = lax.ppermute(held, "t", [(i, i ^ mask) for i in range(NT)])
-        halves = (held, arrived)
-        offsets = offsets + [o ^ mask for o in offsets]
-        held = jnp.concatenate(halves, axis=0)
+    by_tokens = lax.ppermute(turned, ("y", "t"), swap)
+    up, down = (lax.ppermute(gate_grad, AXES, ring_pairs(step)) for step in (1, -1))
+    by_blocks = lax.all_to_all(
+        turned.reshape(NZ, BLK, turned.shape[1]), "z", split_axis=0, concat_axis=0, tiled=True
+    ).reshape(turned.shape)
+    even = lax.rem(t, 2) == 0
+    kept = jnp.where(even, by_tokens, by_blocks)
+    given = jnp.where(even, by_blocks, by_tokens)
+    orders, halves = ([0], [0]), None
+    for masks in [m for m in ((1, 1), (2, 6), (6, 2)) if max(m) < NT]:
+        arrived = lax.ppermute(given if halves is None else kept, AXES, tensor_pairs(masks))
+        orders = tuple(order + [o ^ mask for o in order] for order, mask in zip(orders, masks))
+        halves = (kept, arrived)
+        kept = jnp.concatenate(halves, axis=0)
 
     grad_blocks, grad_offsets = [gate_grad], [0]
-    up, down = gate_grad, gate_grad
     for step in range(1, NY // 2 + 1):
-        up = lax.ppermute(up, "y", [(i, (i + 1) % NY) for i in range(NY)])
+        if step > 1:
+            up = lax.ppermute(up, AXES, ring_pairs(1))
         grad_blocks.append(up)
         grad_offsets.append(-step)
         if 2 * step < NY:
-            down = lax.ppermute(down, "y", [(i, (i + NY - 1) % NY) for i in range(NY)])
+            if step > 1:
+                down = lax.ppermute(down, AXES, ring_pairs(-1))
             grad_blocks.append(down)
             grad_offsets.append(step)
 
-    partial_value = partial_product(y, t, offsets, grad_offsets, halves, grad_blocks)
+    partial_value = partial_product(y, z, t, orders, grad_offsets, halves, grad_blocks)
     pieces = partial_value.reshape(NZ, BLK, partial_value.shape[1])
-    received = lax.all_to_all(pieces, "z", split_axis=0, concat_axis=0, tiled=True)
+    received = lax.all_to_all(
+        pieces, AXES, split_axis=0, concat_axis=0, axis_index_groups=cross_groups(), tiled=True
+    )
     new_moment, nesterov, grams = momentum_step(received, momentum)
     grams = lax.all_to_all(grams, "t", split_axis=0, concat_axis=0, tiled=True)
     by_y = polar_update(grams, nesterov)
@@ -224,7 +286,7 @@
 
 
 def solution(mesh):
-    fine = Mesh(mesh.devices.reshape(NY, NZ, NT), ("y", "z", "t"))
+    fine = Mesh(mesh.devices.reshape(NY, NZ, NT), AXES)
     split = P(("y", "z"), "t")
     return jax.shard_map(
         per_device,

time: 139 us -> 140 us (level)
  starting transfers between devices: 36.3 us -> 47.2 us
  blocking collectives: 68.2 us -> 58.6 us
  local copies, waits for them, and re-layouts: 5 us -> 1.51 us
  Pallas kernels: 6.16 us -> 8.42 us
    all_to_all x0 -> x1, starting transfers between devices: none -> 10.5 us  [per_device(): lax.all_to_all(turned.reshape(NZ, BLK, turned.shape[1]), 'z', split_axis=...]
    all_to_all x1, blocking collectives: 33.3 us -> 24.4 us  [per_device(): lax.all_to_all(pieces, AXES, split_axis=0, concat_axis=0, axis_index_grou...]
    unnamed x14 -> x8, local copies, waits for them, and re-layouts: 3.86 us -> 0.38 us
    pallas_call x2, Pallas kernels: 2.26 us -> 4.52 us  [the longest x1 2.81 us: prepare(): pl.pallas_call(prepare_kernel, out_shape=(jax.ShapeDtypeStruct((rows, tok...]
    ppermute x11, waiting for transfers between devices: 21.5 us -> 22.9 us  [the longest x1 10.7 us: per_device(): by_tokens = lax.ppermute(turned, ('y', 't'), swap)]
  transfers between devices with their start and end apart: 11 -> 12, of which waited for: 5 -> 6; matrix products, arithmetic and copies ran while one was open for 0% -> 0% of each run, Pallas kernels for 1% -> 0%
where the time goes in v3:
time: 140 us
  blocking collectives  58.6 us (42%)
  starting transfers between devices  47.2 us (34%)
  waiting for transfers between devices  22.9 us (16%)
  Pallas kernels  8.42 us (6%)
  local copies, waits for them, and re-layouts  1.51 us (1%)
    all_to_all x1, blocking collectives, per_device(): lax.all_to_all(pieces, AXES, split_axis=0, concat_axis=0, axis_index_grou...  24.4 us
    all_to_all x1, blocking collectives, per_device(): by_y = lax.all_to_all(by_y, 'y', split_axis=0, concat_axis=0, tiled=True)  13.9 us
    all_to_all x1, blocking collectives, per_device(): by_z = lax.all_to_all(by_z, 'z', split_axis=0, concat_axis=0, tiled=True)  11.3 us
    ppermute x1, waiting for transfers between devices, per_device(): by_tokens = lax.ppermute(turned, ('y', 't'), swap)  10.7 us
    all_to_all x1, starting transfers between devices, per_device(): lax.all_to_all(turned.reshape(NZ, BLK, turned.shape[1]), 'z', split_axis=...  10.5 us
    ppermute x2, starting transfers between devices, per_device(): down = lax.ppermute(down, AXES, ring_pairs(-1))  10.1 us
    ppermute x2, starting transfers between devices, per_device(): lax.ppermute(gate_grad, AXES, ring_pairs(step))  9.07 us
    all_to_all x1, blocking collectives, per_device(): grams = lax.all_to_all(grams, 't', split_axis=0, concat_axis=0, tiled=True)  8.98 us
  transfers between devices with their start and end apart: 12, of which 6 were waited for; matrix products, arithmetic and copies ran while one was open for 0% of the time, Pallas kernels for 0%

profile of v3, /device:TPU:2, one launch (start us, length us, event | category | flops | bytes accessed | tf_op | source)
XLA Modules:
  0.0 139.6 jit_solution(6535238630126104762)
XLA Ops:
  0.6 2.8 %prepare.1 = (bf16[512,128]{1,0:T(8,128)(2,1)}, bf16[128,896]{1,0:T(8,128)(2,1)}) custom-call(s32[1]{0:T(128)} %bitcast.3.place_ref, s32[64]{0:T(128)} %lengths_ref.1, bf16[128,512]{1,0:T(8,128)(2,1)} %features_in.1, bf16[128,896]{1,0:T(8,128)(2,1)} %gate_in.1, bf16[128,896]{1,0:T(8,128)(2,1)} %up_in.1, bf16[128,896]{1,0:T(8,128)(2,1)} %cotangent_in.1), custom_call_target="tpu_custom_call" | custom-call | flops 1376256 | bytes 917504 | tf_op jit(solution)/shard_map/prepare/pallas_call | solution.py:59
  3.5 0.0 copy-start.2
  3.5 10.5 %all-to-all-start = ((bf16[8,64,128]{2,1,0:T(8,128)(2,1)}), bf16[8,64,128]{2,1,0:T(8,128)(2,1)S(1)}, u32[]{:S(2)}, u32[]{:S(2)}) async-start(bf16[8,64,128]{2,1,0:T(8,128)(2,1)} %bitcast.18), calls=%async_computation | async-start | bytes 262144 | tf_op jit(solution)/shard_map/all_to_all | solution.py:247
  13.9 0.0 copy-done.2
  13.9 4.5 %collective-permute-start = (bf16[512,128]{1,0:T(8,128)(2,1)S(1)}, bf16[512,128]{1,0:T(8,128)(2,1)S(1)}, u32[]{:S(2)}, u32[]{:S(2)}) collective-permute-start(bf16[512,128]{1,0:T(8,128)(2,1)S(1)} %copy-done.2), channel_id=1, source_target_pairs={{0,0},{1,64},{2,128},{3,192},{4,256},{5,320},{6,384},{7,448},{64,1... | collective-permute-start | bytes 393224 | tf_op jit(solution)/shard_map/ppermute | solution.py:245
  18.4 10.7 %collective-permute-done = bf16[512,128]{1,0:T(8,128)(2,1)S(1)} collective-permute-done((bf16[512,128]{1,0:T(8,128)(2,1)S(1)}, bf16[512,128]{1,0:T(8,128)(2,1)S(1)}, u32[]{:S(2)}, u32[]{:S(2)}) %collective-permute-start) | collective-permute-done | bytes 131104 | tf_op jit(solution)/shard_map/ppermute | solution.py:245
  29.2 0.0 all-to-all-done
  29.2 1.9 %collective-permute-start.1 = (bf16[512,128]{1,0:T(8,128)(2,1)S(1)}, bf16[512,128]{1,0:T(8,128)(2,1)S(1)}, u32[]{:S(2)}, u32[]{:S(2)}) collective-permute-start(bf16[512,128]{1,0:T(8,128)(2,1)S(1)} %get-tuple-element.13), channel_id=1, source_target_pairs={{0,1},{1,0},{2,3},{3,2},{4,5},{5,4},{6,7},{7,6},{8,9},{9,8},{10,11... | collective-permute-start | bytes 393224 | tf_op jit(solution)/shard_map/ppermute | solution.py:255
  31.1 1.3 collective-permute-done.1
  32.4 0.0 copy-start.1
  32.5 2.1 %collective-permute-start.2 = (bf16[1024,128]{1,0:T(8,128)(2,1)S(1)}, bf16[1024,128]{1,0:T(8,128)(2,1)S(1)}, u32[]{:S(2)}, u32[]{:S(2)}) collective-permute-start(bf16[1024,128]{1,0:T(8,128)(2,1)S(1)} %pad_maximum_fusion.1), channel_id=1, source_target_pairs={{0,2},{1,7},{2,0},{3,5},{4,6},{5,3},{6,4},{7,1},{8,10},{9,15},{10,... | collective-permute-start | bytes 786440 | tf_op jit(solution)/shard_map/ppermute | solution.py:255
  34.5 0.0 copy-done.1
  34.5 2.3 %collective-permute-start.4 = (bf16[128,896]{1,0:T(8,128)(2,1)S(1)}, bf16[128,896]{1,0:T(8,128)(2,1)S(1)}, u32[]{:S(2)}, u32[]{:S(2)}) collective-permute-start(bf16[128,896]{1,0:T(8,128)(2,1)S(1)} %copy-done.1), channel_id=1, source_target_pairs={{0,64},{1,9},{2,66},{3,11},{4,68},{5,13},{6,70},{7,15},{8,72},{9,1... | collective-permute-start | bytes 688136 | tf_op jit(solution)/shard_map/ppermute | solution.py:246
  36.8 6.8 %collective-permute-start.5 = (bf16[128,896]{1,0:T(8,128)(2,1)S(1)}, bf16[128,896]{1,0:T(8,128)(2,1)S(1)}, u32[]{:S(2)}, u32[]{:S(2)}) collective-permute-start(bf16[128,896]{1,0:T(8,128)(2,1)S(1)} %copy-done.1), channel_id=1, source_target_pairs={{0,448},{1,57},{2,450},{3,59},{4,452},{5,61},{6,454},{7,63},{8,456... | collective-permute-start | bytes 688136 | tf_op jit(solution)/shard_map/ppermute | solution.py:246
  43.6 2.1 %collective-permute-done.4.refs_3_ = bf16[128,896]{1,0:T(8,128)(2,1)S(1)} collective-permute-done((bf16[128,896]{1,0:T(8,128)(2,1)S(1)}, bf16[128,896]{1,0:T(8,128)(2,1)S(1)}, u32[]{:S(2)}, u32[]{:S(2)}) %collective-permute-start.4) | collective-permute-done | bytes 229408 | tf_op jit(solution)/shard_map/ppermute | solution.py:246
  45.7 1.9 %collective-permute-start.6 = (bf16[128,896]{1,0:T(8,128)(2,1)S(1)}, bf16[128,896]{1,0:T(8,128)(2,1)S(1)}, u32[]{:S(2)}, u32[]{:S(2)}) collective-permute-start(bf16[128,896]{1,0:T(8,128)(2,1)S(1)} %collective-permute-done.4.refs_3_), channel_id=1, source_target_pairs={{0,64},{1,9},{2,66},{3,11},{4,68},{5,13},{6,70},{7,15},{8,72},{9,1... | collective-permute-start | bytes 688136 | tf_op jit(solution)/shard_map/ppermute | solution.py:263
  47.6 0.0 collective-permute-done.2
  47.6 3.4 %collective-permute-start.3 = (bf16[2048,128]{1,0:T(8,128)(2,1)S(1)}, bf16[2048,128]{1,0:T(8,128)(2,1)S(1)}, u32[]{:S(2)}, u32[]{:S(2)}) collective-permute-start(bf16[2048,128]{1,0:T(8,128)(2,1)S(1)} %pad_maximum_fusion.refs_0_), channel_id=1, source_target_pairs={{0,6},{1,3},{2,4},{3,1},{4,2},{5,7},{6,0},{7,5},{8,14},{9,11},{10,... | collective-permute-start | bytes 1572872 | tf_op jit(solution)/shard_map/ppermute | solution.py:255
  51.1 0.0 collective-permute-done.5.refs_4_
  51.1 4.5 %collective-permute-start.7 = (bf16[128,896]{1,0:T(8,128)(2,1)S(1)}, bf16[128,896]{1,0:T(8,128)(2,1)S(1)}, u32[]{:S(2)}, u32[]{:S(2)}) collective-permute-start(bf16[128,896]{1,0:T(8,128)(2,1)S(1)} %collective-permute-done.5.refs_4_), channel_id=1, source_target_pairs={{0,448},{1,57},{2,450},{3,59},{4,452},{5,61},{6,454},{7,63},{8,456... | collective-permute-start | bytes 688136 | tf_op jit(solution)/shard_map/ppermute | solution.py:268
  55.6 0.0 collective-permute-done.6.refs_5_
  55.6 1.9 %collective-permute-start.8 = (bf16[128,896]{1,0:T(8,128)(2,1)S(1)}, bf16[128,896]{1,0:T(8,128)(2,1)S(1)}, u32[]{:S(2)}, u32[]{:S(2)}) collective-permute-start(bf16[128,896]{1,0:T(8,128)(2,1)S(1)} %collective-permute-done.6.refs_5_), channel_id=1, source_target_pairs={{0,64},{1,9},{2,66},{3,11},{4,68},{5,13},{6,70},{7,15},{8,72},{9,1... | collective-permute-start | bytes 688136 | tf_op jit(solution)/shard_map/ppermute | solution.py:263
  57.5 1.6 %collective-permute-done.7.refs_6_ = bf16[128,896]{1,0:T(8,128)(2,1)S(1)} collective-permute-done((bf16[128,896]{1,0:T(8,128)(2,1)S(1)}, bf16[128,896]{1,0:T(8,128)(2,1)S(1)}, u32[]{:S(2)}, u32[]{:S(2)}) %collective-permute-start.7) | collective-permute-done | bytes 229408 | tf_op jit(solution)/shard_map/ppermute | solution.py:268
  59.1 5.6 %collective-permute-start.9 = (bf16[128,896]{1,0:T(8,128)(2,1)S(1)}, bf16[128,896]{1,0:T(8,128)(2,1)S(1)}, u32[]{:S(2)}, u32[]{:S(2)}) collective-permute-start(bf16[128,896]{1,0:T(8,128)(2,1)S(1)} %collective-permute-done.7.refs_6_), channel_id=1, source_target_pairs={{0,448},{1,57},{2,450},{3,59},{4,452},{5,61},{6,454},{7,63},{8,456... | collective-permute-start | bytes 688136 | tf_op jit(solution)/shard_map/ppermute | solution.py:268
  64.7 0.0 collective-permute-done.8.refs_7_
  64.7 1.9 %collective-permute-start.10 = (bf16[128,896]{1,0:T(8,128)(2,1)S(1)}, bf16[128,896]{1,0:T(8,128)(2,1)S(1)}, u32[]{:S(2)}, u32[]{:S(2)}) collective-permute-start(bf16[128,896]{1,0:T(8,128)(2,1)S(1)} %collective-permute-done.8.refs_7_), channel_id=1, source_target_pairs={{0,64},{1,9},{2,66},{3,11},{4,68},{5,13},{6,70},{7,15},{8,72},{9,1... | collective-permute-start | bytes 688136 | tf_op jit(solution)/shard_map/ppermute | solution.py:263
  66.7 1.6 %collective-permute-done.9.refs_8_ = bf16[128,896]{1,0:T(8,128)(2,1)S(1)} collective-permute-done((bf16[128,896]{1,0:T(8,128)(2,1)S(1)}, bf16[128,896]{1,0:T(8,128)(2,1)S(1)}, u32[]{:S(2)}, u32[]{:S(2)}) %collective-permute-start.9) | collective-permute-done | bytes 229408 | tf_op jit(solution)/shard_map/ppermute | solution.py:268
  68.2 5.6 %collective-permute-done.10.refs_9_ = bf16[128,896]{1,0:T(8,128)(2,1)S(1)} collective-permute-done((bf16[128,896]{1,0:T(8,128)(2,1)S(1)}, bf16[128,896]{1,0:T(8,128)(2,1)S(1)}, u32[]{:S(2)}, u32[]{:S(2)}) %collective-permute-start.10) | collective-permute-done | bytes 229408 | tf_op jit(solution)/shard_map/ppermute | solution.py:263
  73.9 0.0 collective-permute-done.3.refs_1_
  73.9 1.7 %partial_product.1 = bf16[512,896]{1,0:T(8,128)(2,1)S(1)} custom-call(s32[1]{0:T(128)} %bitcast.y_ref, s32[1]{0:T(128)} %bitcast.1.z_ref, s32[1]{0:T(128)} %bitcast.2.t_ref, bf16[2048,128]{1,0:T(8,128)(2,1)S(1)} %pad_maximum_fusion.refs_0_, bf16[2048,128]{1,0:T(8,128)(2,1)S(1)} %collective-permute-done.3.refs_1_, bf16[128,896]{1,0:T(8,128)(2,1)S(1)} %copy-done.1, ...), custom_call_target="tpu_custom_call" | custom-call | flops 939524096 | bytes 6000000 | tf_op jit(solution)/shard_map/partial_product/pallas_call | solution.py:147
  75.6 0.0 copy-start
  75.6 24.4 %all_to_all.25.parts_ref = bf16[8,64,896]{2,1,0:T(8,128)(2,1)S(1)} all-to-all(bf16[8,64,896]{2,1,0:T(8,128)(2,1)S(1)} %bitcast.15), channel_id=1, replica_groups={{0,8,16,24,32,40,48,56},{2,10,18,26,34,42,50,58},{4,12,20,28,36,44,52,6..., dimensions={0} | all-to-all | bytes 1835008 | tf_op jit(solution)/shard_map/all_to_all | solution.py:274
  100.0 0.0 copy-done
  100.0 0.9 momentum_step.1
  100.9 9.0 %all_to_all.26.grams_ref = f32[8,32,128]{2,1,0:T(8,128)S(1)} all-to-all(f32[8,32,128]{2,1,0:T(8,128)S(1)} %get-tuple-element.9), channel_id=1, replica_groups=mesh['y'=8,'z'=8,'t'=8] {'t'}, dimensions={0} | all-to-all | bytes 262144 | tf_op jit(solution)/shard_map/all_to_all | solution.py:278
  109.9 3.0 %polar_update.1 = bf16[8,64,112]{2,1,0:T(8,128)(2,1)S(1)} custom-call(f32[8,32,128]{2,1,0:T(8,128)S(1)} %all_to_all.26.grams_ref, f32[64,896]{1,0:T(8,128)S(1)} %get-tuple-element.10.block_ref), custom_call_target="tpu_custom_call" | custom-call | flops 100000000 | bytes 600000 | tf_op jit(solution)/shard_map/polar_update/pallas_call | solution.py:229
  112.9 13.9 %all_to_all.27 = bf16[8,64,112]{2,1,0:T(8,128)(2,1)S(1)} all-to-all(bf16[8,64,112]{2,1,0:T(8,128)(2,1)S(1)} %polar_update.1), channel_id=1, replica_groups=mesh['y'=8,'z'=8,'t'=8] {'y'}, dimensions={0} | all-to-all | bytes 229376 | tf_op jit(solution)/shard_map/all_to_all | solution.py:280
  126.8 0.2 copy.10
  127.0 0.2 reshape.40
  127.2 11.3 %all_to_all.28 = bf16[8,2,3584]{2,1,0:T(2,128)(2,1)S(1)} all-to-all(bf16[8,2,3584]{2,1,0:T(2,128)(2,1)S(1)} %reshape.40), channel_id=1, replica_groups=mesh['y'=8,'z'=8,'t'=8] {'z'}, dimensions={0} | all-to-all | bytes 229376 | tf_op jit(solution)/shard_map/all_to_all | solution.py:283
  138.5 0.2 reshape.41
  138.7 0.1 copy.11
  138.7 0.9 reshape.39
  (3 shorter events, 0.1 us)
Async XLA Ops:
  3.5 10.5 %copy-start.2 = (bf16[512,128]{1,0:T(8,128)(2,1)S(1)}, bf16[512,128]{1,0:T(8,128)(2,1)}, u32[]{:S(2)}) copy-start(bf16[512,128]{1,0:T(8,128)(2,1)} %get-tuple-element.7) | copy-start | bytes 393220
  3.5 25.7 %all-to-all-start = ((bf16[8,64,128]{2,1,0:T(8,128)(2,1)}), bf16[8,64,128]{2,1,0:T(8,128)(2,1)S(1)}, u32[]{:S(2)}, u32[]{:S(2)}) async-start(bf16[8,64,128]{2,1,0:T(8,128)(2,1)} %bitcast.18), calls=%async_computation | async-start | bytes 262144 | tf_op jit(solution)/shard_map/all_to_all | solution.py:247
  13.9 15.2 %collective-permute-start = (bf16[512,128]{1,0:T(8,128)(2,1)S(1)}, bf16[512,128]{1,0:T(8,128)(2,1)S(1)}, u32[]{:S(2)}, u32[]{:S(2)}) collective-permute-start(bf16[512,128]{1,0:T(8,128)(2,1)S(1)} %copy-done.2), channel_id=1, source_target_pairs={{0,0},{1,64},{2,128},{3,192},{4,256},{5,320},{6,384},{7,448},{64,1... | collective-permute-start | bytes 393224 | tf_op jit(solution)/shard_map/ppermute | solution.py:245
  29.2 3.2 %collective-permute-start.1 = (bf16[512,128]{1,0:T(8,128)(2,1)S(1)}, bf16[512,128]{1,0:T(8,128)(2,1)S(1)}, u32[]{:S(2)}, u32[]{:S(2)}) collective-permute-start(bf16[512,128]{1,0:T(8,128)(2,1)S(1)} %get-tuple-element.13), channel_id=1, source_target_pairs={{0,1},{1,0},{2,3},{3,2},{4,5},{5,4},{6,7},{7,6},{8,9},{9,8},{10,11... | collective-permute-start | bytes 393224 | tf_op jit(solution)/shard_map/ppermute | solution.py:255
  32.4 2.1 %copy-start.1 = (bf16[128,896]{1,0:T(8,128)(2,1)S(1)}, bf16[128,896]{1,0:T(8,128)(2,1)}, u32[]{:S(2)}) copy-start(bf16[128,896]{1,0:T(8,128)(2,1)} %get-tuple-element.8.refs_2_) | copy-start | bytes 688132
  32.5 15.1 %collective-permute-start.2 = (bf16[1024,128]{1,0:T(8,128)(2,1)S(1)}, bf16[1024,128]{1,0:T(8,128)(2,1)S(1)}, u32[]{:S(2)}, u32[]{:S(2)}) collective-permute-start(bf16[1024,128]{1,0:T(8,128)(2,1)S(1)} %pad_maximum_fusion.1), channel_id=1, source_target_pairs={{0,2},{1,7},{2,0},{3,5},{4,6},{5,3},{6,4},{7,1},{8,10},{9,15},{10,... | collective-permute-start | bytes 786440 | tf_op jit(solution)/shard_map/ppermute | solution.py:255
  34.5 11.1 %collective-permute-start.4 = (bf16[128,896]{1,0:T(8,128)(2,1)S(1)}, bf16[128,896]{1,0:T(8,128)(2,1)S(1)}, u32[]{:S(2)}, u32[]{:S(2)}) collective-permute-start(bf16[128,896]{1,0:T(8,128)(2,1)S(1)} %copy-done.1), channel_id=1, source_target_pairs={{0,64},{1,9},{2,66},{3,11},{4,68},{5,13},{6,70},{7,15},{8,72},{9,1... | collective-permute-start | bytes 688136 | tf_op jit(solution)/shard_map/ppermute | solution.py:246
  36.8 14.2 %collective-permute-start.5 = (bf16[128,896]{1,0:T(8,128)(2,1)S(1)}, bf16[128,896]{1,0:T(8,128)(2,1)S(1)}, u32[]{:S(2)}, u32[]{:S(2)}) collective-permute-start(bf16[128,896]{1,0:T(8,128)(2,1)S(1)} %copy-done.1), channel_id=1, source_target_pairs={{0,448},{1,57},{2,450},{3,59},{4,452},{5,61},{6,454},{7,63},{8,456... | collective-permute-start | bytes 688136 | tf_op jit(solution)/shard_map/ppermute | solution.py:246
  45.7 9.9 %collective-permute-start.6 = (bf16[128,896]{1,0:T(8,128)(2,1)S(1)}, bf16[128,896]{1,0:T(8,128)(2,1)S(1)}, u32[]{:S(2)}, u32[]{:S(2)}) collective-permute-start(bf16[128,896]{1,0:T(8,128)(2,1)S(1)} %collective-permute-done.4.refs_3_), channel_id=1, source_target_pairs={{0,64},{1,9},{2,66},{3,11},{4,68},{5,13},{6,70},{7,15},{8,72},{9,1... | collective-permute-start | bytes 688136 | tf_op jit(solution)/shard_map/ppermute | solution.py:263
  47.6 26.2 %collective-permute-start.3 = (bf16[2048,128]{1,0:T(8,128)(2,1)S(1)}, bf16[2048,128]{1,0:T(8,128)(2,1)S(1)}, u32[]{:S(2)}, u32[]{:S(2)}) collective-permute-start(bf16[2048,128]{1,0:T(8,128)(2,1)S(1)} %pad_maximum_fusion.refs_0_), channel_id=1, source_target_pairs={{0,6},{1,3},{2,4},{3,1},{4,2},{5,7},{6,0},{7,5},{8,14},{9,11},{10,... | collective-permute-start | bytes 1572872 | tf_op jit(solution)/shard_map/ppermute | solution.py:255
  51.1 8.1 %collective-permute-start.7 = (bf16[128,896]{1,0:T(8,128)(2,1)S(1)}, bf16[128,896]{1,0:T(8,128)(2,1)S(1)}, u32[]{:S(2)}, u32[]{:S(2)}) collective-permute-start(bf16[128,896]{1,0:T(8,128)(2,1)S(1)} %collective-permute-done.5.refs_4_), channel_id=1, source_target_pairs={{0,448},{1,57},{2,450},{3,59},{4,452},{5,61},{6,454},{7,63},{8,456... | collective-permute-start | bytes 688136 | tf_op jit(solution)/shard_map/ppermute | solution.py:268
  55.6 9.1 %collective-permute-start.8 = (bf16[128,896]{1,0:T(8,128)(2,1)S(1)}, bf16[128,896]{1,0:T(8,128)(2,1)S(1)}, u32[]{:S(2)}, u32[]{:S(2)}) collective-permute-start(bf16[128,896]{1,0:T(8,128)(2,1)S(1)} %collective-permute-done.6.refs_5_), channel_id=1, source_target_pairs={{0,64},{1,9},{2,66},{3,11},{4,68},{5,13},{6,70},{7,15},{8,72},{9,1... | collective-permute-start | bytes 688136 | tf_op jit(solution)/shard_map/ppermute | solution.py:263
  59.1 9.1 %collective-permute-start.9 = (bf16[128,896]{1,0:T(8,128)(2,1)S(1)}, bf16[128,896]{1,0:T(8,128)(2,1)S(1)}, u32[]{:S(2)}, u32[]{:S(2)}) collective-permute-start(bf16[128,896]{1,0:T(8,128)(2,1)S(1)} %collective-permute-done.7.refs_6_), channel_id=1, source_target_pairs={{0,448},{1,57},{2,450},{3,59},{4,452},{5,61},{6,454},{7,63},{8,456... | collective-permute-start | bytes 688136 | tf_op jit(solution)/shard_map/ppermute | solution.py:268
  64.7 9.1 %collective-permute-start.10 = (bf16[128,896]{1,0:T(8,128)(2,1)S(1)}, bf16[128,896]{1,0:T(8,128)(2,1)S(1)}, u32[]{:S(2)}, u32[]{:S(2)}) collective-permute-start(bf16[128,896]{1,0:T(8,128)(2,1)S(1)} %collective-permute-done.8.refs_7_), channel_id=1, source_target_pairs={{0,64},{1,9},{2,66},{3,11},{4,68},{5,13},{6,70},{7,15},{8,72},{9,1... | collective-permute-start | bytes 688136 | tf_op jit(solution)/shard_map/ppermute | solution.py:263
  75.6 24.4 %copy-start = (f32[64,896]{1,0:T(8,128)S(1)}, f32[64,896]{1,0:T(8,128)}, u32[]{:S(2)}) copy-start(f32[64,896]{1,0:T(8,128)} %momentum_ref.1) | copy-start | bytes 688132

commit v4 on v2

--- a/solution.py
+++ b/solution.py
@@ -27,35 +27,44 @@
 HIGHEST = lax.Precision.HIGHEST
 
 
-def gate_kernel(place_ref, lengths_ref, gate_ref, up_ref, cotangent_ref, out_ref):
-    rows = gate_ref.shape[0]
-    position = lax.broadcasted_iota(jnp.int32, gate_ref.shape, 0) + pl.program_id(0) * rows
-    gate_value = gate_ref[...].astype(jnp.float32)
-    up_value = up_ref[...].astype(jnp.float32)
-    cotangent = cotangent_ref[...].astype(jnp.float32)
+def gate_kernel(place_ref, lengths_ref, gate_in, up_in, cotangent_in, grad_ref, *scratch):
+    buffers, arrived = scratch[:3], scratch[3]
+    sources = (gate_in, up_in, cotangent_in)
+    copies = [
+        pltpu.make_async_copy(source, buffer, arrived.at[i])
+        for i, (source, buffer) in enumerate(zip(sources, buffers))
+    ]
+    for copy in copies:
+        copy.start()
+    for copy in copies:
+        copy.wait()
+    gate_value, up_value, cotangent = (buffer[...].astype(jnp.float32) for buffer in buffers)
     sigmoid_gate = jax.nn.sigmoid(gate_value)
     gate_grad = cotangent * up_value * sigmoid_gate * (1.0 + gate_value * (1.0 - sigmoid_gate))
+    position = lax.broadcasted_iota(jnp.int32, gate_value.shape, 0)
     trained = position < lengths_ref[place_ref[0]]
-    out_ref[...] = jnp.where(trained, gate_grad, 0.0).astype(out_ref.dtype)
+    grad_ref[...] = jnp.where(trained, gate_grad, 0.0).astype(grad_ref.dtype)
 
 
 def gate_cotangent(place, lengths, gate_pre, up_pre, hidden_grad):
     tokens, columns = gate_pre.shape
-    rows = tokens // 2
-    block = pl.BlockSpec((rows, columns), lambda i: (i, 0))
+    hbm = pl.BlockSpec(memory_space=pltpu.HBM)
+    vmem = pl.BlockSpec(memory_space=pltpu.VMEM)
     smem = pl.BlockSpec(memory_space=pltpu.SMEM)
+    arrays = (gate_pre, up_pre, hidden_grad)
     return pl.pallas_call(
         gate_kernel,
-        grid=(tokens // rows,),
         out_shape=jax.ShapeDtypeStruct((tokens, columns), jnp.bfloat16),
-        in_specs=[smem, smem, block, block, block],
-        out_specs=block,
-        compiler_params=pltpu.CompilerParams(vmem_limit_bytes=16 * 1024 * 1024),
+        in_specs=[smem, smem] + [hbm] * 3,
+        out_specs=vmem,
+        scratch_shapes=[pltpu.VMEM(array.shape, array.dtype) for array in arrays]
+        + [pltpu.SemaphoreType.DMA((3,))],
+        compiler_params=pltpu.CompilerParams(vmem_limit_bytes=60 * 1024 * 1024),
         cost_estimate=pl.CostEstimate(
             flops=12 * tokens * columns, bytes_accessed=8 * tokens * columns, transcendentals=tokens * columns
         ),
         name="gate_cotangent",
-    )(jnp.reshape(place, (1,)), lengths, gate_pre, up_pre, hidden_grad)
+    )(jnp.reshape(place, (1,)), lengths, *arrays)
 
 
 def partial_kernel(feature_offsets, grad_offsets, y_ref, t_ref, *refs):
@@ -189,10 +198,11 @@
     swap = [(a * NT + b, b * NT + a) for a in range(NY) for b in range(NT)]
     held = lax.ppermute(features, ("y", "t"), swap)
     gate_grad = gate_cotangent(y * NZ + z, lengths, gate_pre, up_pre, hidden_grad)
+    held, _ = lax.optimization_barrier((held, gate_grad))
 
     offsets = [0]
     halves = None
-    for mask in [m for m in (1, 2, 6) if m < NT]:
+    for mask in [m for m in (2, 6, 1) if m < NT]:
         arrived = lax.ppermute(held, "t", [(i, i ^ mask) for i in range(NT)])
         halves = (held, arrived)
         offsets = offsets + [o ^ mask for o in offsets]

time: 139 us -> 137 us (0.986)
  starting transfers between devices: 36.3 us -> 32.7 us
  local copies, waits for them, and re-layouts: 5 us -> 1.54 us
  blocking collectives: 68.2 us -> 70.5 us
  Pallas kernels: 6.16 us -> 8.09 us
  waiting for transfers between devices: 21.5 us -> 22.9 us
    ppermute x3, starting transfers between devices: 15.6 us -> 11.9 us  [per_device(): down = lax.ppermute(down, 'y', [(i, (i + NY - 1) % NY) for i in range(NY)])]
    all_to_all x1, blocking collectives: 9.61 us -> 13.3 us  [per_device(): grams = lax.all_to_all(grams, 't', split_axis=0, concat_axis=0, tiled=True)]
    ppermute x3, waiting for transfers between devices: 0.01 us -> 3.58 us  [per_device(): arrived = lax.ppermute(held, 't', [(i, i ^ mask) for i in range(NT)])]
    unnamed x14 -> x8, local copies, waits for them, and re-layouts: 3.86 us -> 0.4 us
    ppermute x1, waiting for transfers between devices: 11 us -> 8.3 us  [per_device(): held = lax.ppermute(features, ('y', 't'), swap)]
    pallas_call x1, Pallas kernels: 0.79 us -> 2.73 us  [gate_cotangent(): pl.pallas_call(gate_kernel, out_shape=jax.ShapeDtypeStruct((tokens, colum...]
  transfers between devices with their start and end apart: 11 -> 11, of which waited for: 5 -> 7; matrix products, arithmetic and copies ran while one was open for 0% -> 0% of each run, Pallas kernels for 1% -> 2%
where the time goes in v4:
time: 137 us
  blocking collectives  70.5 us (51%)
  starting transfers between devices  32.7 us (24%)
  waiting for transfers between devices  22.9 us (17%)
  Pallas kernels  8.09 us (6%)
  local copies, waits for them, and re-layouts  1.54 us (1%)
    all_to_all x1, blocking collectives, per_device(): lax.all_to_all(pieces, 'z', split_axis=0, concat_axis=0, tiled=True)  33.2 us
    all_to_all x1, blocking collectives, per_device(): grams = lax.all_to_all(grams, 't', split_axis=0, concat_axis=0, tiled=True)  13.3 us
    all_to_all x1, blocking collectives, per_device(): by_y = lax.all_to_all(by_y, 'y', split_axis=0, concat_axis=0, tiled=True)  12.7 us
    ppermute x3, starting transfers between devices, per_device(): down = lax.ppermute(down, 'y', [(i, (i + NY - 1) % NY) for i in range(NY)])  11.9 us
    all_to_all x1, blocking collectives, per_device(): by_z = lax.all_to_all(by_z, 'z', split_axis=0, concat_axis=0, tiled=True)  11.3 us
    ppermute x4, starting transfers between devices, per_device(): up = lax.ppermute(up, 'y', [(i, (i + 1) % NY) for i in range(NY)])  8.78 us
    ppermute x1, waiting for transfers between devices, per_device(): held = lax.ppermute(features, ('y', 't'), swap)  8.3 us
    ppermute x3, starting transfers between devices, per_device(): arrived = lax.ppermute(held, 't', [(i, i ^ mask) for i in range(NT)])  7.57 us
  transfers between devices with their start and end apart: 11, of which 7 were waited for; matrix products, arithmetic and copies ran while one was open for 0% of the time, Pallas kernels for 2%

profile of v4, /device:TPU:2, one launch (start us, length us, event | category | flops | bytes accessed | tf_op | source)
XLA Modules:
  0.0 136.6 jit_solution(15212818134733039293)
XLA Ops:
  0.6 4.5 %collective-permute-start = (bf16[128,512]{1,0:T(8,128)(2,1)}, bf16[128,512]{1,0:T(8,128)(2,1)S(1)}, u32[]{:S(2)}, u32[]{:S(2)}) collective-permute-start(bf16[128,512]{1,0:T(8,128)(2,1)} %param.6), channel_id=1, source_target_pairs={{0,0},{1,64},{2,128},{3,192},{4,256},{5,320},{6,384},{7,448},{64,1... | collective-permute-start | bytes 393224 | tf_op jit(solution)/shard_map/ppermute | solution.py:199
  5.1 2.7 %gate_cotangent.1.refs_2_ = bf16[128,896]{1,0:T(8,128)(2,1)} custom-call(s32[1]{0:T(128)} %bitcast.2.place_ref, s32[64]{0:T(128)} %lengths_ref.1, bf16[128,896]{1,0:T(8,128)(2,1)} %gate_in.1, bf16[128,896]{1,0:T(8,128)(2,1)} %up_in.1, bf16[128,896]{1,0:T(8,128)(2,1)} %cotangent_in.1), custom_call_target="tpu_custom_call" | custom-call | flops 1376256 | bytes 917504 | tf_op jit(solution)/shard_map/gate_cotangent/pallas_call | solution.py:55
  7.8 0.0 copy-start
  7.9 8.3 %collective-permute-done = bf16[128,512]{1,0:T(8,128)(2,1)S(1)} collective-permute-done((bf16[128,512]{1,0:T(8,128)(2,1)}, bf16[128,512]{1,0:T(8,128)(2,1)S(1)}, u32[]{:S(2)}, u32[]{:S(2)}) %collective-permute-start) | collective-permute-done | bytes 131104 | tf_op jit(solution)/shard_map/ppermute | solution.py:199
  16.2 1.9 %collective-permute-start.1 = (bf16[128,512]{1,0:T(8,128)(2,1)S(1)}, bf16[128,512]{1,0:T(8,128)(2,1)S(1)}, u32[]{:S(2)}, u32[]{:S(2)}) collective-permute-start(bf16[128,512]{1,0:T(8,128)(2,1)S(1)} %collective-permute-done), channel_id=1, source_target_pairs={{0,2},{1,3},{2,0},{3,1},{4,6},{5,7},{6,4},{7,5},{8,10},{9,11},{10,... | collective-permute-start | bytes 393224 | tf_op jit(solution)/shard_map/ppermute | solution.py:206
  18.1 2.0 %collective-permute-start.4 = (bf16[128,896]{1,0:T(8,128)(2,1)}, bf16[128,896]{1,0:T(8,128)(2,1)S(1)}, u32[]{:S(2)}, u32[]{:S(2)}) collective-permute-start(bf16[128,896]{1,0:T(8,128)(2,1)} %gate_cotangent.1.refs_2_), channel_id=1, source_target_pairs={{0,64},{64,128},{128,192},{192,256},{256,320},{320,384},{384,448},... | collective-permute-start | bytes 688136 | tf_op jit(solution)/shard_map/ppermute | solution.py:214
  20.1 2.9 %collective-permute-done.1 = bf16[128,512]{1,0:T(8,128)(2,1)S(1)} collective-permute-done((bf16[128,512]{1,0:T(8,128)(2,1)S(1)}, bf16[128,512]{1,0:T(8,128)(2,1)S(1)}, u32[]{:S(2)}, u32[]{:S(2)}) %collective-permute-start.1) | collective-permute-done | bytes 131104 | tf_op jit(solution)/shard_map/ppermute | solution.py:206
  23.0 3.7 %collective-permute-start.2 = (bf16[256,512]{1,0:T(8,128)(2,1)S(1)}, bf16[256,512]{1,0:T(8,128)(2,1)S(1)}, u32[]{:S(2)}, u32[]{:S(2)}) collective-permute-start(bf16[256,512]{1,0:T(8,128)(2,1)S(1)} %pad_maximum_fusion), channel_id=1, source_target_pairs={{0,6},{1,7},{2,4},{3,5},{4,2},{5,3},{6,0},{7,1},{8,14},{9,15},{10,... | collective-permute-start | bytes 786440 | tf_op jit(solution)/shard_map/ppermute | solution.py:206
  26.8 0.0 copy-done
  26.8 2.9 %collective-permute-start.5 = (bf16[128,896]{1,0:T(8,128)(2,1)S(1)}, bf16[128,896]{1,0:T(8,128)(2,1)S(1)}, u32[]{:S(2)}, u32[]{:S(2)}) collective-permute-start(bf16[128,896]{1,0:T(8,128)(2,1)S(1)} %copy-done), channel_id=1, source_target_pairs={{0,448},{64,0},{128,64},{192,128},{256,192},{320,256},{384,320},{4... | collective-permute-start | bytes 688136 | tf_op jit(solution)/shard_map/ppermute | solution.py:218
  29.7 0.0 collective-permute-done.4.refs_3_
  29.7 2.9 %collective-permute-start.6 = (bf16[128,896]{1,0:T(8,128)(2,1)S(1)}, bf16[128,896]{1,0:T(8,128)(2,1)S(1)}, u32[]{:S(2)}, u32[]{:S(2)}) collective-permute-start(bf16[128,896]{1,0:T(8,128)(2,1)S(1)} %collective-permute-done.4.refs_3_), channel_id=1, source_target_pairs={{0,64},{64,128},{128,192},{192,256},{256,320},{320,384},{384,448},... | collective-permute-start | bytes 688136 | tf_op jit(solution)/shard_map/ppermute | solution.py:214
  32.7 0.7 collective-permute-done.2
  33.4 1.9 %collective-permute-start.3 = (bf16[512,512]{1,0:T(8,128)(2,1)S(1)}, bf16[512,512]{1,0:T(8,128)(2,1)S(1)}, u32[]{:S(2)}, u32[]{:S(2)}) collective-permute-start(bf16[512,512]{1,0:T(8,128)(2,1)S(1)} %constant_dynamic-update-slice_fusion.refs_0_), channel_id=1, source_target_pairs={{0,1},{1,0},{2,3},{3,2},{4,5},{5,4},{6,7},{7,6},{8,9},{9,8},{10,11... | collective-permute-start | bytes 1572872 | tf_op jit(solution)/shard_map/ppermute | solution.py:206
  35.3 0.8 collective-permute-done.5.refs_4_
  36.1 4.2 %collective-permute-start.7 = (bf16[128,896]{1,0:T(8,128)(2,1)S(1)}, bf16[128,896]{1,0:T(8,128)(2,1)S(1)}, u32[]{:S(2)}, u32[]{:S(2)}) collective-permute-start(bf16[128,896]{1,0:T(8,128)(2,1)S(1)} %collective-permute-done.5.refs_4_), channel_id=1, source_target_pairs={{0,448},{64,0},{128,64},{192,128},{256,192},{320,256},{384,320},{4... | collective-permute-start | bytes 688136 | tf_op jit(solution)/shard_map/ppermute | solution.py:218
  40.3 0.0 collective-permute-done.6.refs_5_
  40.3 1.9 %collective-permute-start.8 = (bf16[128,896]{1,0:T(8,128)(2,1)S(1)}, bf16[128,896]{1,0:T(8,128)(2,1)S(1)}, u32[]{:S(2)}, u32[]{:S(2)}) collective-permute-start(bf16[128,896]{1,0:T(8,128)(2,1)S(1)} %collective-permute-done.6.refs_5_), channel_id=1, source_target_pairs={{0,64},{64,128},{128,192},{192,256},{256,320},{320,384},{384,448},... | collective-permute-start | bytes 688136 | tf_op jit(solution)/shard_map/ppermute | solution.py:214
  42.3 3.0 %collective-permute-done.7.refs_6_ = bf16[128,896]{1,0:T(8,128)(2,1)S(1)} collective-permute-done((bf16[128,896]{1,0:T(8,128)(2,1)S(1)}, bf16[128,896]{1,0:T(8,128)(2,1)S(1)}, u32[]{:S(2)}, u32[]{:S(2)}) %collective-permute-start.7) | collective-permute-done | bytes 229408 | tf_op jit(solution)/shard_map/ppermute | solution.py:218
  45.3 4.8 %collective-permute-start.9 = (bf16[128,896]{1,0:T(8,128)(2,1)S(1)}, bf16[128,896]{1,0:T(8,128)(2,1)S(1)}, u32[]{:S(2)}, u32[]{:S(2)}) collective-permute-start(bf16[128,896]{1,0:T(8,128)(2,1)S(1)} %collective-permute-done.7.refs_6_), channel_id=1, source_target_pairs={{0,448},{64,0},{128,64},{192,128},{256,192},{320,256},{384,320},{4... | collective-permute-start | bytes 688136 | tf_op jit(solution)/shard_map/ppermute | solution.py:218
  50.1 0.0 collective-permute-done.8.refs_7_
  50.1 1.9 %collective-permute-start.10 = (bf16[128,896]{1,0:T(8,128)(2,1)S(1)}, bf16[128,896]{1,0:T(8,128)(2,1)S(1)}, u32[]{:S(2)}, u32[]{:S(2)}) collective-permute-start(bf16[128,896]{1,0:T(8,128)(2,1)S(1)} %collective-permute-done.8.refs_7_), channel_id=1, source_target_pairs={{0,64},{64,128},{128,192},{192,256},{256,320},{320,384},{384,448},... | collective-permute-start | bytes 688136 | tf_op jit(solution)/shard_map/ppermute | solution.py:214
  52.1 1.6 %collective-permute-done.9.refs_8_ = bf16[128,896]{1,0:T(8,128)(2,1)S(1)} collective-permute-done((bf16[128,896]{1,0:T(8,128)(2,1)S(1)}, bf16[128,896]{1,0:T(8,128)(2,1)S(1)}, u32[]{:S(2)}, u32[]{:S(2)}) %collective-permute-start.9) | collective-permute-done | bytes 229408 | tf_op jit(solution)/shard_map/ppermute | solution.py:218
  53.6 5.6 %collective-permute-done.10.refs_9_ = bf16[128,896]{1,0:T(8,128)(2,1)S(1)} collective-permute-done((bf16[128,896]{1,0:T(8,128)(2,1)S(1)}, bf16[128,896]{1,0:T(8,128)(2,1)S(1)}, u32[]{:S(2)}, u32[]{:S(2)}) %collective-permute-start.10) | collective-permute-done | bytes 229408 | tf_op jit(solution)/shard_map/ppermute | solution.py:214
  59.2 0.0 collective-permute-done.3.refs_1_
  59.2 1.5 %partial_product.1 = bf16[512,896]{1,0:T(8,128)(2,1)S(1)} custom-call(s32[1]{0:T(128)} %bitcast.y_ref, s32[1]{0:T(128)} %bitcast.1.t_ref, bf16[512,512]{1,0:T(8,128)(2,1)S(1)} %constant_dynamic-update-slice_fusion.refs_0_, bf16[512,512]{1,0:T(8,128)(2,1)S(1)} %collective-permute-done.3.refs_1_, bf16[128,896]{1,0:T(8,128)(2,1)S(1)} %copy-done, ...), custom_call_target="tpu_custom_call" | custom-call | flops 939524096 | bytes 6000000 | tf_op jit(solution)/shard_map/partial_product/pallas_call | solution.py:103
  60.7 0.0 copy-start.1
  60.7 33.2 %all_to_all.20.parts_ref = bf16[8,64,896]{2,1,0:T(8,128)(2,1)S(1)} all-to-all(bf16[8,64,896]{2,1,0:T(8,128)(2,1)S(1)} %bitcast.10), channel_id=1, replica_groups=mesh['y'=8,'z'=8,'t'=8] {'z'}, dimensions={0} | all-to-all | bytes 1835008 | tf_op jit(solution)/shard_map/all_to_all | solution.py:224
  94.0 0.0 copy-done.1
  94.0 0.9 momentum_step.1
  94.9 13.3 %all_to_all.21.grams_ref = f32[8,32,128]{2,1,0:T(8,128)S(1)} all-to-all(f32[8,32,128]{2,1,0:T(8,128)S(1)} %get-tuple-element.7), channel_id=1, replica_groups=mesh['y'=8,'z'=8,'t'=8] {'t'}, dimensions={0} | all-to-all | bytes 262144 | tf_op jit(solution)/shard_map/all_to_all | solution.py:226
  108.1 3.0 %polar_update.1 = bf16[8,64,112]{2,1,0:T(8,128)(2,1)S(1)} custom-call(f32[8,32,128]{2,1,0:T(8,128)S(1)} %all_to_all.21.grams_ref, f32[64,896]{1,0:T(8,128)S(1)} %get-tuple-element.8.block_ref), custom_call_target="tpu_custom_call" | custom-call | flops 100000000 | bytes 600000 | tf_op jit(solution)/shard_map/polar_update/pallas_call | solution.py:185
  111.1 12.7 %all_to_all.22 = bf16[8,64,112]{2,1,0:T(8,128)(2,1)S(1)} all-to-all(bf16[8,64,112]{2,1,0:T(8,128)(2,1)S(1)} %polar_update.1), channel_id=1, replica_groups=mesh['y'=8,'z'=8,'t'=8] {'y'}, dimensions={0} | all-to-all | bytes 229376 | tf_op jit(solution)/shard_map/all_to_all | solution.py:228
  123.8 0.2 copy.10
  124.0 0.2 reshape.28
  124.2 11.3 %all_to_all.23 = bf16[8,2,3584]{2,1,0:T(2,128)(2,1)S(1)} all-to-all(bf16[8,2,3584]{2,1,0:T(2,128)(2,1)S(1)} %reshape.28), channel_id=1, replica_groups=mesh['y'=8,'z'=8,'t'=8] {'z'}, dimensions={0} | all-to-all | bytes 229376 | tf_op jit(solution)/shard_map/all_to_all | solution.py:231
  135.5 0.2 reshape.29
  135.7 0.1 copy.11
  135.7 0.9 reshape.27
  (4 shorter events, 0.1 us)
Async XLA Ops:
  0.6 15.5 %collective-permute-start = (bf16[128,512]{1,0:T(8,128)(2,1)}, bf16[128,512]{1,0:T(8,128)(2,1)S(1)}, u32[]{:S(2)}, u32[]{:S(2)}) collective-permute-start(bf16[128,512]{1,0:T(8,128)(2,1)} %param.6), channel_id=1, source_target_pairs={{0,0},{1,64},{2,128},{3,192},{4,256},{5,320},{6,384},{7,448},{64,1... | collective-permute-start | bytes 393224 | tf_op jit(solution)/shard_map/ppermute | solution.py:199
  7.8 18.9 %copy-start = (bf16[128,896]{1,0:T(8,128)(2,1)S(1)}, bf16[128,896]{1,0:T(8,128)(2,1)}, u32[]{:S(2)}) copy-start(bf16[128,896]{1,0:T(8,128)(2,1)} %gate_cotangent.1.refs_2_) | copy-start | bytes 688132
  16.2 6.8 %collective-permute-start.1 = (bf16[128,512]{1,0:T(8,128)(2,1)S(1)}, bf16[128,512]{1,0:T(8,128)(2,1)S(1)}, u32[]{:S(2)}, u32[]{:S(2)}) collective-permute-start(bf16[128,512]{1,0:T(8,128)(2,1)S(1)} %collective-permute-done), channel_id=1, source_target_pairs={{0,2},{1,3},{2,0},{3,1},{4,6},{5,7},{6,4},{7,5},{8,10},{9,11},{10,... | collective-permute-start | bytes 393224 | tf_op jit(solution)/shard_map/ppermute | solution.py:206
  18.1 11.7 %collective-permute-start.4 = (bf16[128,896]{1,0:T(8,128)(2,1)}, bf16[128,896]{1,0:T(8,128)(2,1)S(1)}, u32[]{:S(2)}, u32[]{:S(2)}) collective-permute-start(bf16[128,896]{1,0:T(8,128)(2,1)} %gate_cotangent.1.refs_2_), channel_id=1, source_target_pairs={{0,64},{64,128},{128,192},{192,256},{256,320},{320,384},{384,448},... | collective-permute-start | bytes 688136 | tf_op jit(solution)/shard_map/ppermute | solution.py:214
  23.0 10.3 %collective-permute-start.2 = (bf16[256,512]{1,0:T(8,128)(2,1)S(1)}, bf16[256,512]{1,0:T(8,128)(2,1)S(1)}, u32[]{:S(2)}, u32[]{:S(2)}) collective-permute-start(bf16[256,512]{1,0:T(8,128)(2,1)S(1)} %pad_maximum_fusion), channel_id=1, source_target_pairs={{0,6},{1,7},{2,4},{3,5},{4,2},{5,3},{6,0},{7,1},{8,14},{9,15},{10,... | collective-permute-start | bytes 786440 | tf_op jit(solution)/shard_map/ppermute | solution.py:206
  26.8 9.3 %collective-permute-start.5 = (bf16[128,896]{1,0:T(8,128)(2,1)S(1)}, bf16[128,896]{1,0:T(8,128)(2,1)S(1)}, u32[]{:S(2)}, u32[]{:S(2)}) collective-permute-start(bf16[128,896]{1,0:T(8,128)(2,1)S(1)} %copy-done), channel_id=1, source_target_pairs={{0,448},{64,0},{128,64},{192,128},{256,192},{320,256},{384,320},{4... | collective-permute-start | bytes 688136 | tf_op jit(solution)/shard_map/ppermute | solution.py:218
  29.7 10.6 %collective-permute-start.6 = (bf16[128,896]{1,0:T(8,128)(2,1)S(1)}, bf16[128,896]{1,0:T(8,128)(2,1)S(1)}, u32[]{:S(2)}, u32[]{:S(2)}) collective-permute-start(bf16[128,896]{1,0:T(8,128)(2,1)S(1)} %collective-permute-done.4.refs_3_), channel_id=1, source_target_pairs={{0,64},{64,128},{128,192},{192,256},{256,320},{320,384},{384,448},... | collective-permute-start | bytes 688136 | tf_op jit(solution)/shard_map/ppermute | solution.py:214
  33.4 25.9 %collective-permute-start.3 = (bf16[512,512]{1,0:T(8,128)(2,1)S(1)}, bf16[512,512]{1,0:T(8,128)(2,1)S(1)}, u32[]{:S(2)}, u32[]{:S(2)}) collective-permute-start(bf16[512,512]{1,0:T(8,128)(2,1)S(1)} %constant_dynamic-update-slice_fusion.refs_0_), channel_id=1, source_target_pairs={{0,1},{1,0},{2,3},{3,2},{4,5},{5,4},{6,7},{7,6},{8,9},{9,8},{10,11... | collective-permute-start | bytes 1572872 | tf_op jit(solution)/shard_map/ppermute | solution.py:206
  36.1 9.2 %collective-permute-start.7 = (bf16[128,896]{1,0:T(8,128)(2,1)S(1)}, bf16[128,896]{1,0:T(8,128)(2,1)S(1)}, u32[]{:S(2)}, u32[]{:S(2)}) collective-permute-start(bf16[128,896]{1,0:T(8,128)(2,1)S(1)} %collective-permute-done.5.refs_4_), channel_id=1, source_target_pairs={{0,448},{64,0},{128,64},{192,128},{256,192},{320,256},{384,320},{4... | collective-permute-start | bytes 688136 | tf_op jit(solution)/shard_map/ppermute | solution.py:218
  40.3 9.8 %collective-permute-start.8 = (bf16[128,896]{1,0:T(8,128)(2,1)S(1)}, bf16[128,896]{1,0:T(8,128)(2,1)S(1)}, u32[]{:S(2)}, u32[]{:S(2)}) collective-permute-start(bf16[128,896]{1,0:T(8,128)(2,1)S(1)} %collective-permute-done.6.refs_5_), channel_id=1, source_target_pairs={{0,64},{64,128},{128,192},{192,256},{256,320},{320,384},{384,448},... | collective-permute-start | bytes 688136 | tf_op jit(solution)/shard_map/ppermute | solution.py:214
  45.3 8.3 %collective-permute-start.9 = (bf16[128,896]{1,0:T(8,128)(2,1)S(1)}, bf16[128,896]{1,0:T(8,128)(2,1)S(1)}, u32[]{:S(2)}, u32[]{:S(2)}) collective-permute-start(bf16[128,896]{1,0:T(8,128)(2,1)S(1)} %collective-permute-done.7.refs_6_), channel_id=1, source_target_pairs={{0,448},{64,0},{128,64},{192,128},{256,192},{320,256},{384,320},{4... | collective-permute-start | bytes 688136 | tf_op jit(solution)/shard_map/ppermute | solution.py:218
  50.1 9.1 %collective-permute-start.10 = (bf16[128,896]{1,0:T(8,128)(2,1)S(1)}, bf16[128,896]{1,0:T(8,128)(2,1)S(1)}, u32[]{:S(2)}, u32[]{:S(2)}) collective-permute-start(bf16[128,896]{1,0:T(8,128)(2,1)S(1)} %collective-permute-done.8.refs_7_), channel_id=1, source_target_pairs={{0,64},{64,128},{128,192},{192,256},{256,320},{320,384},{384,448},... | collective-permute-start | bytes 688136 | tf_op jit(solution)/shard_map/ppermute | solution.py:214
  60.7 33.2 %copy-start.1 = (f32[64,896]{1,0:T(8,128)S(1)}, f32[64,896]{1,0:T(8,128)}, u32[]{:S(2)}) copy-start(f32[64,896]{1,0:T(8,128)} %momentum_ref.1) | copy-start | bytes 688132

commit v5 on v4

--- a/solution.py
+++ b/solution.py
@@ -67,54 +67,71 @@
     )(jnp.reshape(place, (1,)), lengths, *arrays)
 
 
-def partial_kernel(feature_offsets, grad_offsets, y_ref, t_ref, *refs):
-    feature_refs, grad_refs = refs[:2], refs[2 : 2 + NY]
-    out_ref, features, grads = refs[2 + NY :]
+def turn_kernel(value_in, turned_ref, buffer, arrived):
+    copy = pltpu.make_async_copy(value_in, buffer, arrived)
+    copy.start()
+    copy.wait()
+    turned_ref[...] = buffer[...].T
+
+
+def turn(value):
+    rows, columns = value.shape
+    return pl.pallas_call(
+        turn_kernel,
+        out_shape=jax.ShapeDtypeStruct((columns, rows), value.dtype),
+        in_specs=[pl.BlockSpec(memory_space=pltpu.HBM)],
+        out_specs=pl.BlockSpec(memory_space=pltpu.VMEM),
+        scratch_shapes=[pltpu.VMEM(value.shape, value.dtype), pltpu.SemaphoreType.DMA],
+        compiler_params=pltpu.CompilerParams(vmem_limit_bytes=60 * 1024 * 1024),
+        cost_estimate=pl.CostEstimate(flops=rows * columns, bytes_accessed=4 * rows * columns, transcendentals=0),
+        name="turn",
+    )(value)
+
+
+def partial_kernel(feature_offsets, grad_offsets, z_ref, t_ref, *refs):
+    feature_refs, grad_refs = refs[:2], refs[2 : 2 + NZ]
+    out_ref, features, grads = refs[2 + NZ :]
     tokens = grad_refs[0].shape[0]
-    y, t = y_ref[0], t_ref[0]
-
-    def place(group):
-        return pl.ds(pl.multiple_of(group * tokens, tokens), tokens)
-
-    blocks = [
-        (ref, start) for ref in feature_refs for start in range(0, ref.shape[0], tokens)
-    ]
+    rows = out_ref.shape[0]
+    z, t = z_ref[0], t_ref[0]
+    blocks = [(ref, start) for ref in feature_refs for start in range(0, ref.shape[0], rows)]
     for offset, (ref, start) in zip(feature_offsets, blocks):
-        features[place(lax.bitwise_xor(t, offset)), :] = ref[start : start + tokens, :]
+        block_rows = pl.ds(pl.multiple_of(lax.bitwise_xor(t, offset) * BLK, BLK), BLK)
+        for group in range(NZ):
+            features[block_rows, group * tokens : (group + 1) * tokens] = ref[
+                start + group * BLK : start + (group + 1) * BLK, :
+            ]
     for offset, ref in zip(grad_offsets, grad_refs):
-        grads[place(lax.rem(y + (NY + offset), NY)), :] = ref[...]
-    rows = out_ref.shape[0]
+        group = lax.rem(z + (NZ + offset), NZ)
+        grads[pl.ds(pl.multiple_of(group * tokens, tokens), tokens), :] = ref[...]
     step = 128
     for start in range(0, rows, step):
-        product = lax.dot_general(
-            features[:, start : start + step],
-            grads[...],
-            (((0,), (0,)), ((), ())),
-            preferred_element_type=jnp.float32,
+        product = jnp.dot(
+            features[start : start + step, :], grads[...], preferred_element_type=jnp.float32
         )
         out_ref[start : start + step, :] = product.astype(out_ref.dtype)
 
 
-def partial_product(y, t, feature_offsets, grad_offsets, feature_halves, grad_blocks):
+def partial_product(z, t, feature_offsets, grad_offsets, feature_halves, grad_blocks):
     tokens, columns = grad_blocks[0].shape
-    rows = feature_halves[0].shape[1]
+    rows = NY * BLK
     vmem = pl.BlockSpec(memory_space=pltpu.VMEM)
     smem = pl.BlockSpec(memory_space=pltpu.SMEM)
     return pl.pallas_call(
         functools.partial(partial_kernel, tuple(feature_offsets), tuple(grad_offsets)),
         out_shape=jax.ShapeDtypeStruct((rows, columns), jnp.bfloat16),
-        in_specs=[smem, smem] + [vmem] * (2 + NY),
+        in_specs=[smem] * 2 + [vmem] * (2 + NZ),
         out_specs=vmem,
         scratch_shapes=[
-            pltpu.VMEM((NY * tokens, rows), jnp.bfloat16),
-            pltpu.VMEM((NY * tokens, columns), jnp.bfloat16),
+            pltpu.VMEM((rows, NZ * tokens), jnp.bfloat16),
+            pltpu.VMEM((NZ * tokens, columns), jnp.bfloat16),
         ],
         compiler_params=pltpu.CompilerParams(vmem_limit_bytes=32 * 1024 * 1024),
         cost_estimate=pl.CostEstimate(
-            flops=2 * NY * tokens * rows * columns, bytes_accessed=6_000_000, transcendentals=0
+            flops=2 * NZ * tokens * rows * columns, bytes_accessed=6_000_000, transcendentals=0
         ),
         name="partial_product",
-    )(jnp.reshape(y, (1,)), jnp.reshape(t, (1,)), *feature_halves, *grad_blocks)
+    )(*(jnp.reshape(i, (1,)) for i in (z, t)), *feature_halves, *grad_blocks)
 
 
 def momentum_kernel(parts_ref, momentum_ref, moment_ref, nesterov_ref, grams_ref):
@@ -195,33 +212,34 @@
 
 def per_device(features, gate_pre, up_pre, hidden_grad, lengths, momentum):
     y, z, t = (lax.axis_index(name) for name in ("y", "z", "t"))
-    swap = [(a * NT + b, b * NT + a) for a in range(NY) for b in range(NT)]
-    held = lax.ppermute(features, ("y", "t"), swap)
+
+    turned = turn(features)
+    held = lax.all_to_all(
+        turned.reshape(NZ, BLK, turned.shape[1]), "z", split_axis=0, concat_axis=0, tiled=True
+    ).reshape(turned.shape)
     gate_grad = gate_cotangent(y * NZ + z, lengths, gate_pre, up_pre, hidden_grad)
     held, _ = lax.optimization_barrier((held, gate_grad))
-
-    offsets = [0]
-    halves = None
+    feature_offsets, halves = [0], None
     for mask in [m for m in (2, 6, 1) if m < NT]:
         arrived = lax.ppermute(held, "t", [(i, i ^ mask) for i in range(NT)])
         halves = (held, arrived)
-        offsets = offsets + [o ^ mask for o in offsets]
+        feature_offsets = feature_offsets + [o ^ mask for o in feature_offsets]
         held = jnp.concatenate(halves, axis=0)
 
     grad_blocks, grad_offsets = [gate_grad], [0]
     up, down = gate_grad, gate_grad
-    for step in range(1, NY // 2 + 1):
-        up = lax.ppermute(up, "y", [(i, (i + 1) % NY) for i in range(NY)])
+    for step in range(1, NZ // 2 + 1):
+        up = lax.ppermute(up, "z", [(i, (i + 1) % NZ) for i in range(NZ)])
         grad_blocks.append(up)
         grad_offsets.append(-step)
-        if 2 * step < NY:
-            down = lax.ppermute(down, "y", [(i, (i + NY - 1) % NY) for i in range(NY)])
+        if 2 * step < NZ:
+            down = lax.ppermute(down, "z", [(i, (i + NZ - 1) % NZ) for i in range(NZ)])
             grad_blocks.append(down)
             grad_offsets.append(step)
 
-    partial_value = partial_product(y, t, offsets, grad_offsets, halves, grad_blocks)
-    pieces = partial_value.reshape(NZ, BLK, partial_value.shape[1])
-    received = lax.all_to_all(pieces, "z", split_axis=0, concat_axis=0, tiled=True)
+    partial_value = partial_product(z, t, feature_offsets, grad_offsets, halves, grad_blocks)
+    pieces = partial_value.reshape(NY, BLK, partial_value.shape[1])
+    received = lax.all_to_all(pieces, "y", split_axis=0, concat_axis=0, tiled=True)
     new_moment, nesterov, grams = momentum_step(received, momentum)
     grams = lax.all_to_all(grams, "t", split_axis=0, concat_axis=0, tiled=True)
     by_y = polar_update(grams, nesterov)

time: 137 us -> 137 us (level)
  starting transfers between devices: 32.7 us -> 40.3 us
  blocking collectives: 70.5 us -> 63.8 us
  waiting for transfers between devices: 22.9 us -> 20.2 us
  Pallas kernels: 8.09 us -> 9.86 us
    all_to_all x0 -> x1, starting transfers between devices: none -> 10.3 us  [per_device(): lax.all_to_all(turned.reshape(NZ, BLK, turned.shape[1]), 'z', split_axis=...]
    ppermute x8 -> x7, waiting for transfers between devices: 19.3 us -> 11.7 us  [the longest x3 6.36 us: per_device(): down = lax.ppermute(down, 'z', [(i, (i + NZ - 1) % NZ) for i in range(NZ)])]
    all_to_all x0 -> x1, waiting for transfers between devices: none -> 6.36 us  [per_device(): lax.all_to_all(turned.reshape(NZ, BLK, turned.shape[1]), 'z', split_axis=...]
    all_to_all x1, blocking collectives: 13.3 us -> 8.48 us  [per_device(): grams = lax.all_to_all(grams, 't', split_axis=0, concat_axis=0, tiled=True)]
    ppermute x8 -> x7, starting transfers between devices: 25.2 us -> 22.1 us  [the longest x3 13.4 us: per_device(): down = lax.ppermute(down, 'z', [(i, (i + NZ - 1) % NZ) for i in range(NZ)])]
    pallas_call x0 -> x1, Pallas kernels: none -> 1.65 us  [turn(): pl.pallas_call(turn_kernel, out_shape=jax.ShapeDtypeStruct((columns, rows...]
    all_to_all x1, blocking collectives: 33.2 us -> 31.6 us  [per_device(): lax.all_to_all(pieces, 'y', split_axis=0, concat_axis=0, tiled=True)]
    ppermute x3, waiting for transfers between devices: 3.58 us -> 2.13 us  [per_device(): arrived = lax.ppermute(held, 't', [(i, i ^ mask) for i in range(NT)])]
  transfers between devices with their start and end apart: 11 -> 11, of which waited for: 7 -> 5; matrix products, arithmetic and copies ran while one was open for 0% -> 0% of each run, Pallas kernels for 2% -> 2%
where the time goes in v5:
time: 137 us
  blocking collectives  63.8 us (47%)
  starting transfers between devices  40.3 us (29%)
  waiting for transfers between devices  20.2 us (15%)
  Pallas kernels  9.86 us (7%)
  local copies, waits for them, and re-layouts  1.57 us (1%)
    all_to_all x1, blocking collectives, per_device(): lax.all_to_all(pieces, 'y', split_axis=0, concat_axis=0, tiled=True)  31.6 us
    ppermute x3, starting transfers between devices, per_device(): down = lax.ppermute(down, 'z', [(i, (i + NZ - 1) % NZ) for i in range(NZ)])  13.4 us
    all_to_all x1, blocking collectives, per_device(): by_z = lax.all_to_all(by_z, 'z', split_axis=0, concat_axis=0, tiled=True)  12.1 us
    all_to_all x1, blocking collectives, per_device(): by_y = lax.all_to_all(by_y, 'y', split_axis=0, concat_axis=0, tiled=True)  11.5 us
    all_to_all x1, starting transfers between devices, per_device(): lax.all_to_all(turned.reshape(NZ, BLK, turned.shape[1]), 'z', split_axis=...  10.3 us
    ppermute x4, starting transfers between devices, per_device(): up = lax.ppermute(up, 'z', [(i, (i + 1) % NZ) for i in range(NZ)])  8.63 us
    all_to_all x1, blocking collectives, per_device(): grams = lax.all_to_all(grams, 't', split_axis=0, concat_axis=0, tiled=True)  8.48 us
    ppermute x3, starting transfers between devices, per_device(): arrived = lax.ppermute(held, 't', [(i, i ^ mask) for i in range(NT)])  7.88 us
  transfers between devices with their start and end apart: 11, of which 5 were waited for; matrix products, arithmetic and copies ran while one was open for 0% of the time, Pallas kernels for 2%

profile of v5, /device:TPU:2, one launch (start us, length us, event | category | flops | bytes accessed | tf_op | source)
XLA Modules:
  0.0 136.6 jit_solution(14171503946934482515)
XLA Ops:
  0.6 1.7 %turn.1 = bf16[512,128]{1,0:T(8,128)(2,1)} custom-call(bf16[128,512]{1,0:T(8,128)(2,1)} %value_in.1), custom_call_target="tpu_custom_call" | custom-call | flops 65536 | bytes 262144 | tf_op jit(solution)/shard_map/turn/pallas_call | solution.py:79
  2.3 10.3 %all-to-all-start = ((bf16[8,64,128]{2,1,0:T(8,128)(2,1)}), bf16[8,64,128]{2,1,0:T(8,128)(2,1)S(1)}, u32[]{:S(2)}, u32[]{:S(2)}) async-start(bf16[8,64,128]{2,1,0:T(8,128)(2,1)} %bitcast.18), calls=%async_computation | async-start | bytes 262144 | tf_op jit(solution)/shard_map/all_to_all | solution.py:217
  12.6 2.7 %gate_cotangent.1.refs_2_ = bf16[128,896]{1,0:T(8,128)(2,1)} custom-call(s32[1]{0:T(128)} %bitcast.4.place_ref, s32[64]{0:T(128)} %lengths_ref.1, bf16[128,896]{1,0:T(8,128)(2,1)} %gate_in.1, bf16[128,896]{1,0:T(8,128)(2,1)} %up_in.1, bf16[128,896]{1,0:T(8,128)(2,1)} %cotangent_in.1), custom_call_target="tpu_custom_call" | custom-call | flops 1376256 | bytes 917504 | tf_op jit(solution)/shard_map/gate_cotangent/pallas_call | solution.py:55
  15.4 6.4 %all-to-all-done = bf16[8,64,128]{2,1,0:T(8,128)(2,1)S(1)} async-done(((bf16[8,64,128]{2,1,0:T(8,128)(2,1)}), bf16[8,64,128]{2,1,0:T(8,128)(2,1)S(1)}, u32[]{:S(2)}, u32[]{:S(2)}) %all-to-all-start) | async-done | bytes 131104 | tf_op jit(solution)/shard_map/all_to_all | solution.py:217
  21.7 0.0 copy-start
  21.7 2.6 %collective-permute-start = (bf16[512,128]{1,0:T(8,128)(2,1)S(1)}, bf16[512,128]{1,0:T(8,128)(2,1)S(1)}, u32[]{:S(2)}, u32[]{:S(2)}) collective-permute-start(bf16[512,128]{1,0:T(8,128)(2,1)S(1)} %bitcast.13), channel_id=1, source_target_pairs={{0,2},{1,3},{2,0},{3,1},{4,6},{5,7},{6,4},{7,5},{8,10},{9,11},{10,... | collective-permute-start | bytes 393224 | tf_op jit(solution)/shard_map/ppermute | solution.py:224
  24.3 2.3 %collective-permute-start.3 = (bf16[128,896]{1,0:T(8,128)(2,1)}, bf16[128,896]{1,0:T(8,128)(2,1)S(1)}, u32[]{:S(2)}, u32[]{:S(2)}) collective-permute-start(bf16[128,896]{1,0:T(8,128)(2,1)} %gate_cotangent.1.refs_2_), channel_id=1, source_target_pairs={{0,8},{8,16},{16,24},{24,32},{32,40},{40,48},{48,56},{56,0},{1,9},... | collective-permute-start | bytes 688136 | tf_op jit(solution)/shard_map/ppermute | solution.py:232
  26.6 2.1 %collective-permute-done = bf16[512,128]{1,0:T(8,128)(2,1)S(1)} collective-permute-done((bf16[512,128]{1,0:T(8,128)(2,1)S(1)}, bf16[512,128]{1,0:T(8,128)(2,1)S(1)}, u32[]{:S(2)}, u32[]{:S(2)}) %collective-permute-start) | collective-permute-done | bytes 131104 | tf_op jit(solution)/shard_map/ppermute | solution.py:224
  28.7 3.4 %collective-permute-start.1 = (bf16[1024,128]{1,0:T(8,128)(2,1)S(1)}, bf16[1024,128]{1,0:T(8,128)(2,1)S(1)}, u32[]{:S(2)}, u32[]{:S(2)}) collective-permute-start(bf16[1024,128]{1,0:T(8,128)(2,1)S(1)} %pad_maximum_fusion), channel_id=1, source_target_pairs={{0,6},{1,7},{2,4},{3,5},{4,2},{5,3},{6,0},{7,1},{8,14},{9,15},{10,... | collective-permute-start | bytes 786440 | tf_op jit(solution)/shard_map/ppermute | solution.py:224
  32.1 0.0 copy-done
  32.1 3.3 %collective-permute-start.4 = (bf16[128,896]{1,0:T(8,128)(2,1)S(1)}, bf16[128,896]{1,0:T(8,128)(2,1)S(1)}, u32[]{:S(2)}, u32[]{:S(2)}) collective-permute-start(bf16[128,896]{1,0:T(8,128)(2,1)S(1)} %copy-done), channel_id=1, source_target_pairs={{0,56},{8,0},{16,8},{24,16},{32,24},{40,32},{48,40},{56,48},{1,57}... | collective-permute-start | bytes 688136 | tf_op jit(solution)/shard_map/ppermute | solution.py:236
  35.5 0.0 collective-permute-done.3.refs_3_
  35.5 2.5 %collective-permute-start.5 = (bf16[128,896]{1,0:T(8,128)(2,1)S(1)}, bf16[128,896]{1,0:T(8,128)(2,1)S(1)}, u32[]{:S(2)}, u32[]{:S(2)}) collective-permute-start(bf16[128,896]{1,0:T(8,128)(2,1)S(1)} %collective-permute-done.3.refs_3_), channel_id=1, source_target_pairs={{0,8},{8,16},{16,24},{24,32},{32,40},{40,48},{48,56},{56,0},{1,9},... | collective-permute-start | bytes 688136 | tf_op jit(solution)/shard_map/ppermute | solution.py:232
  38.1 0.0 collective-permute-done.1
  38.1 1.9 %collective-permute-start.2 = (bf16[2048,128]{1,0:T(8,128)(2,1)S(1)}, bf16[2048,128]{1,0:T(8,128)(2,1)S(1)}, u32[]{:S(2)}, u32[]{:S(2)}) collective-permute-start(bf16[2048,128]{1,0:T(8,128)(2,1)S(1)} %constant_dynamic-update-slice_fusion.refs_0_), channel_id=1, source_target_pairs={{0,1},{1,0},{2,3},{3,2},{4,5},{5,4},{6,7},{7,6},{8,9},{9,8},{10,11... | collective-permute-start | bytes 1572872 | tf_op jit(solution)/shard_map/ppermute | solution.py:224
  40.0 0.0 collective-permute-done.4.refs_4_
  40.1 4.5 %collective-permute-start.6 = (bf16[128,896]{1,0:T(8,128)(2,1)S(1)}, bf16[128,896]{1,0:T(8,128)(2,1)S(1)}, u32[]{:S(2)}, u32[]{:S(2)}) collective-permute-start(bf16[128,896]{1,0:T(8,128)(2,1)S(1)} %collective-permute-done.4.refs_4_), channel_id=1, source_target_pairs={{0,56},{8,0},{16,8},{24,16},{32,24},{40,32},{48,40},{56,48},{1,57}... | collective-permute-start | bytes 688136 | tf_op jit(solution)/shard_map/ppermute | solution.py:236
  44.6 0.0 collective-permute-done.5.refs_5_
  44.6 1.9 %collective-permute-start.7 = (bf16[128,896]{1,0:T(8,128)(2,1)S(1)}, bf16[128,896]{1,0:T(8,128)(2,1)S(1)}, u32[]{:S(2)}, u32[]{:S(2)}) collective-permute-start(bf16[128,896]{1,0:T(8,128)(2,1)S(1)} %collective-permute-done.5.refs_5_), channel_id=1, source_target_pairs={{0,8},{8,16},{16,24},{24,32},{32,40},{40,48},{48,56},{56,0},{1,9},... | collective-permute-start | bytes 688136 | tf_op jit(solution)/shard_map/ppermute | solution.py:232
  46.5 3.6 %collective-permute-done.6.refs_6_ = bf16[128,896]{1,0:T(8,128)(2,1)S(1)} collective-permute-done((bf16[128,896]{1,0:T(8,128)(2,1)S(1)}, bf16[128,896]{1,0:T(8,128)(2,1)S(1)}, u32[]{:S(2)}, u32[]{:S(2)}) %collective-permute-start.6) | collective-permute-done | bytes 229408 | tf_op jit(solution)/shard_map/ppermute | solution.py:236
  50.1 5.6 %collective-permute-start.8 = (bf16[128,896]{1,0:T(8,128)(2,1)S(1)}, bf16[128,896]{1,0:T(8,128)(2,1)S(1)}, u32[]{:S(2)}, u32[]{:S(2)}) collective-permute-start(bf16[128,896]{1,0:T(8,128)(2,1)S(1)} %collective-permute-done.6.refs_6_), channel_id=1, source_target_pairs={{0,56},{8,0},{16,8},{24,16},{32,24},{40,32},{48,40},{56,48},{1,57}... | collective-permute-start | bytes 688136 | tf_op jit(solution)/shard_map/ppermute | solution.py:236
  55.7 0.0 collective-permute-done.7.refs_7_
  55.7 1.9 %collective-permute-start.9 = (bf16[128,896]{1,0:T(8,128)(2,1)S(1)}, bf16[128,896]{1,0:T(8,128)(2,1)S(1)}, u32[]{:S(2)}, u32[]{:S(2)}) collective-permute-start(bf16[128,896]{1,0:T(8,128)(2,1)S(1)} %collective-permute-done.7.refs_7_), channel_id=1, source_target_pairs={{0,8},{8,16},{16,24},{24,32},{32,40},{40,48},{48,56},{56,0},{1,9},... | collective-permute-start | bytes 688136 | tf_op jit(solution)/shard_map/ppermute | solution.py:232
  57.6 2.8 %collective-permute-done.8.refs_8_ = bf16[128,896]{1,0:T(8,128)(2,1)S(1)} collective-permute-done((bf16[128,896]{1,0:T(8,128)(2,1)S(1)}, bf16[128,896]{1,0:T(8,128)(2,1)S(1)}, u32[]{:S(2)}, u32[]{:S(2)}) %collective-permute-start.8) | collective-permute-done | bytes 229408 | tf_op jit(solution)/shard_map/ppermute | solution.py:236
  60.4 5.3 %collective-permute-done.9.refs_9_ = bf16[128,896]{1,0:T(8,128)(2,1)S(1)} collective-permute-done((bf16[128,896]{1,0:T(8,128)(2,1)S(1)}, bf16[128,896]{1,0:T(8,128)(2,1)S(1)}, u32[]{:S(2)}, u32[]{:S(2)}) %collective-permute-start.9) | collective-permute-done | bytes 229408 | tf_op jit(solution)/shard_map/ppermute | solution.py:232
  65.8 0.0 collective-permute-done.2.refs_1_
  65.8 1.6 %partial_product.1 = bf16[512,896]{1,0:T(8,128)(2,1)S(1)} custom-call(s32[1]{0:T(128)} %bitcast.z_ref, s32[1]{0:T(128)} %bitcast.1.t_ref, bf16[2048,128]{1,0:T(8,128)(2,1)S(1)} %constant_dynamic-update-slice_fusion.refs_0_, bf16[2048,128]{1,0:T(8,128)(2,1)S(1)} %collective-permute-done.2.refs_1_, bf16[128,896]{1,0:T(8,128)(2,1)S(1)} %copy-done, ...), custom_call_target="tpu_custom_call" | custom-call | flops 939524096 | bytes 6000000 | tf_op jit(solution)/shard_map/partial_product/pallas_call | solution.py:120
  67.3 0.0 copy-start.1
  67.4 31.6 %all_to_all.25.parts_ref = bf16[8,64,896]{2,1,0:T(8,128)(2,1)S(1)} all-to-all(bf16[8,64,896]{2,1,0:T(8,128)(2,1)S(1)} %bitcast.12), channel_id=1, replica_groups=mesh['y'=8,'z'=8,'t'=8] {'y'}, dimensions={0} | all-to-all | bytes 1835008 | tf_op jit(solution)/shard_map/all_to_all | solution.py:242
  99.0 0.0 copy-done.1
  99.0 0.9 momentum_step.1
  99.9 8.5 %all_to_all.26.grams_ref = f32[8,32,128]{2,1,0:T(8,128)S(1)} all-to-all(f32[8,32,128]{2,1,0:T(8,128)S(1)} %get-tuple-element.7), channel_id=1, replica_groups=mesh['y'=8,'z'=8,'t'=8] {'t'}, dimensions={0} | all-to-all | bytes 262144 | tf_op jit(solution)/shard_map/all_to_all | solution.py:244
  108.4 3.0 %polar_update.1 = bf16[8,64,112]{2,1,0:T(8,128)(2,1)S(1)} custom-call(f32[8,32,128]{2,1,0:T(8,128)S(1)} %all_to_all.26.grams_ref, f32[64,896]{1,0:T(8,128)S(1)} %get-tuple-element.8.block_ref), custom_call_target="tpu_custom_call" | custom-call | flops 100000000 | bytes 600000 | tf_op jit(solution)/shard_map/polar_update/pallas_call | solution.py:202
  111.4 11.5 %all_to_all.27 = bf16[8,64,112]{2,1,0:T(8,128)(2,1)S(1)} all-to-all(bf16[8,64,112]{2,1,0:T(8,128)(2,1)S(1)} %polar_update.1), channel_id=1, replica_groups=mesh['y'=8,'z'=8,'t'=8] {'y'}, dimensions={0} | all-to-all | bytes 229376 | tf_op jit(solution)/shard_map/all_to_all | solution.py:246
  122.9 0.2 copy.10
  123.1 0.2 reshape.36
  123.3 12.1 %all_to_all.28 = bf16[8,2,3584]{2,1,0:T(2,128)(2,1)S(1)} all-to-all(bf16[8,2,3584]{2,1,0:T(2,128)(2,1)S(1)} %reshape.36), channel_id=1, replica_groups=mesh['y'=8,'z'=8,'t'=8] {'z'}, dimensions={0} | all-to-all | bytes 229376 | tf_op jit(solution)/shard_map/all_to_all | solution.py:249
  135.4 0.2 reshape.37
  135.6 0.1 copy.11
  135.7 0.9 reshape.35
  (4 shorter events, 0.1 us)
Async XLA Ops:
  2.3 19.4 %all-to-all-start = ((bf16[8,64,128]{2,1,0:T(8,128)(2,1)}), bf16[8,64,128]{2,1,0:T(8,128)(2,1)S(1)}, u32[]{:S(2)}, u32[]{:S(2)}) async-start(bf16[8,64,128]{2,1,0:T(8,128)(2,1)} %bitcast.18), calls=%async_computation | async-start | bytes 262144 | tf_op jit(solution)/shard_map/all_to_all | solution.py:217
  21.7 10.4 %copy-start = (bf16[128,896]{1,0:T(8,128)(2,1)S(1)}, bf16[128,896]{1,0:T(8,128)(2,1)}, u32[]{:S(2)}) copy-start(bf16[128,896]{1,0:T(8,128)(2,1)} %gate_cotangent.1.refs_2_) | copy-start | bytes 688132
  21.7 7.0 %collective-permute-start = (bf16[512,128]{1,0:T(8,128)(2,1)S(1)}, bf16[512,128]{1,0:T(8,128)(2,1)S(1)}, u32[]{:S(2)}, u32[]{:S(2)}) collective-permute-start(bf16[512,128]{1,0:T(8,128)(2,1)S(1)} %bitcast.13), channel_id=1, source_target_pairs={{0,2},{1,3},{2,0},{3,1},{4,6},{5,7},{6,4},{7,5},{8,10},{9,11},{10,... | collective-permute-start | bytes 393224 | tf_op jit(solution)/shard_map/ppermute | solution.py:224
  24.3 11.2 %collective-permute-start.3 = (bf16[128,896]{1,0:T(8,128)(2,1)}, bf16[128,896]{1,0:T(8,128)(2,1)S(1)}, u32[]{:S(2)}, u32[]{:S(2)}) collective-permute-start(bf16[128,896]{1,0:T(8,128)(2,1)} %gate_cotangent.1.refs_2_), channel_id=1, source_target_pairs={{0,8},{8,16},{16,24},{24,32},{32,40},{40,48},{48,56},{56,0},{1,9},... | collective-permute-start | bytes 688136 | tf_op jit(solution)/shard_map/ppermute | solution.py:232
  28.7 9.3 %collective-permute-start.1 = (bf16[1024,128]{1,0:T(8,128)(2,1)S(1)}, bf16[1024,128]{1,0:T(8,128)(2,1)S(1)}, u32[]{:S(2)}, u32[]{:S(2)}) collective-permute-start(bf16[1024,128]{1,0:T(8,128)(2,1)S(1)} %pad_maximum_fusion), channel_id=1, source_target_pairs={{0,6},{1,7},{2,4},{3,5},{4,2},{5,3},{6,0},{7,1},{8,14},{9,15},{10,... | collective-permute-start | bytes 786440 | tf_op jit(solution)/shard_map/ppermute | solution.py:224
  32.1 7.9 %collective-permute-start.4 = (bf16[128,896]{1,0:T(8,128)(2,1)S(1)}, bf16[128,896]{1,0:T(8,128)(2,1)S(1)}, u32[]{:S(2)}, u32[]{:S(2)}) collective-permute-start(bf16[128,896]{1,0:T(8,128)(2,1)S(1)} %copy-done), channel_id=1, source_target_pairs={{0,56},{8,0},{16,8},{24,16},{32,24},{40,32},{48,40},{56,48},{1,57}... | collective-permute-start | bytes 688136 | tf_op jit(solution)/shard_map/ppermute | solution.py:236
  35.5 9.1 %collective-permute-start.5 = (bf16[128,896]{1,0:T(8,128)(2,1)S(1)}, bf16[128,896]{1,0:T(8,128)(2,1)S(1)}, u32[]{:S(2)}, u32[]{:S(2)}) collective-permute-start(bf16[128,896]{1,0:T(8,128)(2,1)S(1)} %collective-permute-done.3.refs_3_), channel_id=1, source_target_pairs={{0,8},{8,16},{16,24},{24,32},{32,40},{40,48},{48,56},{56,0},{1,9},... | collective-permute-start | bytes 688136 | tf_op jit(solution)/shard_map/ppermute | solution.py:232
  38.1 27.6 %collective-permute-start.2 = (bf16[2048,128]{1,0:T(8,128)(2,1)S(1)}, bf16[2048,128]{1,0:T(8,128)(2,1)S(1)}, u32[]{:S(2)}, u32[]{:S(2)}) collective-permute-start(bf16[2048,128]{1,0:T(8,128)(2,1)S(1)} %constant_dynamic-update-slice_fusion.refs_0_), channel_id=1, source_target_pairs={{0,1},{1,0},{2,3},{3,2},{4,5},{5,4},{6,7},{7,6},{8,9},{9,8},{10,11... | collective-permute-start | bytes 1572872 | tf_op jit(solution)/shard_map/ppermute | solution.py:224
  40.1 10.0 %collective-permute-start.6 = (bf16[128,896]{1,0:T(8,128)(2,1)S(1)}, bf16[128,896]{1,0:T(8,128)(2,1)S(1)}, u32[]{:S(2)}, u32[]{:S(2)}) collective-permute-start(bf16[128,896]{1,0:T(8,128)(2,1)S(1)} %collective-permute-done.4.refs_4_), channel_id=1, source_target_pairs={{0,56},{8,0},{16,8},{24,16},{32,24},{40,32},{48,40},{56,48},{1,57}... | collective-permute-start | bytes 688136 | tf_op jit(solution)/shard_map/ppermute | solution.py:236
  44.6 11.1 %collective-permute-start.7 = (bf16[128,896]{1,0:T(8,128)(2,1)S(1)}, bf16[128,896]{1,0:T(8,128)(2,1)S(1)}, u32[]{:S(2)}, u32[]{:S(2)}) collective-permute-start(bf16[128,896]{1,0:T(8,128)(2,1)S(1)} %collective-permute-done.5.refs_5_), channel_id=1, source_target_pairs={{0,8},{8,16},{16,24},{24,32},{32,40},{40,48},{48,56},{56,0},{1,9},... | collective-permute-start | bytes 688136 | tf_op jit(solution)/shard_map/ppermute | solution.py:232
  50.1 10.3 %collective-permute-start.8 = (bf16[128,896]{1,0:T(8,128)(2,1)S(1)}, bf16[128,896]{1,0:T(8,128)(2,1)S(1)}, u32[]{:S(2)}, u32[]{:S(2)}) collective-permute-start(bf16[128,896]{1,0:T(8,128)(2,1)S(1)} %collective-permute-done.6.refs_6_), channel_id=1, source_target_pairs={{0,56},{8,0},{16,8},{24,16},{32,24},{40,32},{48,40},{56,48},{1,57}... | collective-permute-start | bytes 688136 | tf_op jit(solution)/shard_map/ppermute | solution.py:236
  55.7 10.0 %collective-permute-start.9 = (bf16[128,896]{1,0:T(8,128)(2,1)S(1)}, bf16[128,896]{1,0:T(8,128)(2,1)S(1)}, u32[]{:S(2)}, u32[]{:S(2)}) collective-permute-start(bf16[128,896]{1,0:T(8,128)(2,1)S(1)} %collective-permute-done.7.refs_7_), channel_id=1, source_target_pairs={{0,8},{8,16},{16,24},{24,32},{32,40},{40,48},{48,56},{56,0},{1,9},... | collective-permute-start | bytes 688136 | tf_op jit(solution)/shard_map/ppermute | solution.py:232
  67.3 31.6 %copy-start.1 = (f32[64,896]{1,0:T(8,128)S(1)}, f32[64,896]{1,0:T(8,128)}, u32[]{:S(2)}) copy-start(f32[64,896]{1,0:T(8,128)} %momentum_ref.1) | copy-start | bytes 688132

commit v6 on v4

--- a/solution.py
+++ b/solution.py
@@ -80,7 +80,7 @@
         (ref, start) for ref in feature_refs for start in range(0, ref.shape[0], tokens)
     ]
     for offset, (ref, start) in zip(feature_offsets, blocks):
-        features[place(lax.bitwise_xor(t, offset)), :] = ref[start : start + tokens, :]
+        features[place(lax.bitwise_xor(lax.bitwise_xor(t, y), offset)), :] = ref[start : start + tokens, :]
     for offset, ref in zip(grad_offsets, grad_refs):
         grads[place(lax.rem(y + (NY + offset), NY)), :] = ref[...]
     rows = out_ref.shape[0]
@@ -195,7 +195,7 @@
 
 def per_device(features, gate_pre, up_pre, hidden_grad, lengths, momentum):
     y, z, t = (lax.axis_index(name) for name in ("y", "z", "t"))
-    swap = [(a * NT + b, b * NT + a) for a in range(NY) for b in range(NT)]
+    swap = [(a * NT + b, b * NT + (a ^ b)) for a in range(NY) for b in range(NT)]
     held = lax.ppermute(features, ("y", "t"), swap)
     gate_grad = gate_cotangent(y * NZ + z, lengths, gate_pre, up_pre, hidden_grad)
     held, _ = lax.optimization_barrier((held, gate_grad))

time: 137 us -> 138 us (level)
  starting transfers between devices: 32.7 us -> 36 us
  blocking collectives: 70.5 us -> 68.9 us
    all_to_all x1, blocking collectives: 13.3 us -> 9.81 us  [per_device(): grams = lax.all_to_all(grams, 't', split_axis=0, concat_axis=0, tiled=True)]
    ppermute x3, starting transfers between devices: 11.9 us -> 14.7 us  [per_device(): down = lax.ppermute(down, 'y', [(i, (i + NY - 1) % NY) for i in range(NY)])]
    all_to_all x1, blocking collectives: 33.2 us -> 34.8 us  [per_device(): lax.all_to_all(pieces, 'z', split_axis=0, concat_axis=0, tiled=True)]
  transfers between devices with their start and end apart: 11 -> 11, of which waited for: 7 -> 5; matrix products, arithmetic and copies ran while one was open for 0% -> 0% of each run, Pallas kernels for 2% -> 2%
where the time goes in v6:
time: 138 us
  blocking collectives  68.9 us (50%)
  starting transfers between devices  36 us (26%)
  waiting for transfers between devices  22.3 us (16%)
  Pallas kernels  8.1 us (6%)
  local copies, waits for them, and re-layouts  1.54 us (1%)
    all_to_all x1, blocking collectives, per_device(): lax.all_to_all(pieces, 'z', split_axis=0, concat_axis=0, tiled=True)  34.8 us
    ppermute x3, starting transfers between devices, per_device(): down = lax.ppermute(down, 'y', [(i, (i + NY - 1) % NY) for i in range(NY)])  14.7 us
    all_to_all x1, blocking collectives, per_device(): by_y = lax.all_to_all(by_y, 'y', split_axis=0, concat_axis=0, tiled=True)  13 us
    all_to_all x1, blocking collectives, per_device(): by_z = lax.all_to_all(by_z, 'z', split_axis=0, concat_axis=0, tiled=True)  11.3 us
    all_to_all x1, blocking collectives, per_device(): grams = lax.all_to_all(grams, 't', split_axis=0, concat_axis=0, tiled=True)  9.81 us
    ppermute x3, starting transfers between devices, per_device(): arrived = lax.ppermute(held, 't', [(i, i ^ mask) for i in range(NT)])  8.86 us
    ppermute x4, starting transfers between devices, per_device(): up = lax.ppermute(up, 'y', [(i, (i + 1) % NY) for i in range(NY)])  7.88 us
    ppermute x1, waiting for transfers between devices, per_device(): held = lax.ppermute(features, ('y', 't'), swap)  7.61 us
  transfers between devices with their start and end apart: 11, of which 5 were waited for; matrix products, arithmetic and copies ran while one was open for 0% of the time, Pallas kernels for 2%

profile of v6, /device:TPU:2, one launch (start us, length us, event | category | flops | bytes accessed | tf_op | source)
XLA Modules:
  0.0 137.7 jit_solution(13356889022441313213)
XLA Ops:
  0.6 4.5 %collective-permute-start = (bf16[128,512]{1,0:T(8,128)(2,1)}, bf16[128,512]{1,0:T(8,128)(2,1)S(1)}, u32[]{:S(2)}, u32[]{:S(2)}) collective-permute-start(bf16[128,512]{1,0:T(8,128)(2,1)} %param.6), channel_id=1, source_target_pairs={{0,0},{1,65},{2,130},{3,195},{4,260},{5,325},{6,390},{7,455},{64,1... | collective-permute-start | bytes 393224 | tf_op jit(solution)/shard_map/ppermute | solution.py:199
  5.1 2.7 %gate_cotangent.1.refs_2_ = bf16[128,896]{1,0:T(8,128)(2,1)} custom-call(s32[1]{0:T(128)} %bitcast.2.place_ref, s32[64]{0:T(128)} %lengths_ref.1, bf16[128,896]{1,0:T(8,128)(2,1)} %gate_in.1, bf16[128,896]{1,0:T(8,128)(2,1)} %up_in.1, bf16[128,896]{1,0:T(8,128)(2,1)} %cotangent_in.1), custom_call_target="tpu_custom_call" | custom-call | flops 1376256 | bytes 917504 | tf_op jit(solution)/shard_map/gate_cotangent/pallas_call | solution.py:55
  7.9 0.0 copy-start
  7.9 7.6 %collective-permute-done = bf16[128,512]{1,0:T(8,128)(2,1)S(1)} collective-permute-done((bf16[128,512]{1,0:T(8,128)(2,1)}, bf16[128,512]{1,0:T(8,128)(2,1)S(1)}, u32[]{:S(2)}, u32[]{:S(2)}) %collective-permute-start) | collective-permute-done | bytes 131104 | tf_op jit(solution)/shard_map/ppermute | solution.py:199
  15.5 1.9 %collective-permute-start.1 = (bf16[128,512]{1,0:T(8,128)(2,1)S(1)}, bf16[128,512]{1,0:T(8,128)(2,1)S(1)}, u32[]{:S(2)}, u32[]{:S(2)}) collective-permute-start(bf16[128,512]{1,0:T(8,128)(2,1)S(1)} %collective-permute-done), channel_id=1, source_target_pairs={{0,2},{1,3},{2,0},{3,1},{4,6},{5,7},{6,4},{7,5},{8,10},{9,11},{10,... | collective-permute-start | bytes 393224 | tf_op jit(solution)/shard_map/ppermute | solution.py:206
  17.4 1.9 %collective-permute-start.4 = (bf16[128,896]{1,0:T(8,128)(2,1)}, bf16[128,896]{1,0:T(8,128)(2,1)S(1)}, u32[]{:S(2)}, u32[]{:S(2)}) collective-permute-start(bf16[128,896]{1,0:T(8,128)(2,1)} %gate_cotangent.1.refs_2_), channel_id=1, source_target_pairs={{0,64},{64,128},{128,192},{192,256},{256,320},{320,384},{384,448},... | collective-permute-start | bytes 688136 | tf_op jit(solution)/shard_map/ppermute | solution.py:214
  19.3 3.0 %collective-permute-done.1 = bf16[128,512]{1,0:T(8,128)(2,1)S(1)} collective-permute-done((bf16[128,512]{1,0:T(8,128)(2,1)S(1)}, bf16[128,512]{1,0:T(8,128)(2,1)S(1)}, u32[]{:S(2)}, u32[]{:S(2)}) %collective-permute-start.1) | collective-permute-done | bytes 131104 | tf_op jit(solution)/shard_map/ppermute | solution.py:206
  22.4 5.0 %collective-permute-start.2 = (bf16[256,512]{1,0:T(8,128)(2,1)S(1)}, bf16[256,512]{1,0:T(8,128)(2,1)S(1)}, u32[]{:S(2)}, u32[]{:S(2)}) collective-permute-start(bf16[256,512]{1,0:T(8,128)(2,1)S(1)} %pad_maximum_fusion), channel_id=1, source_target_pairs={{0,6},{1,7},{2,4},{3,5},{4,2},{5,3},{6,0},{7,1},{8,14},{9,15},{10,... | collective-permute-start | bytes 786440 | tf_op jit(solution)/shard_map/ppermute | solution.py:206
  27.4 0.0 copy-done
  27.4 4.2 %collective-permute-start.5 = (bf16[128,896]{1,0:T(8,128)(2,1)S(1)}, bf16[128,896]{1,0:T(8,128)(2,1)S(1)}, u32[]{:S(2)}, u32[]{:S(2)}) collective-permute-start(bf16[128,896]{1,0:T(8,128)(2,1)S(1)} %copy-done), channel_id=1, source_target_pairs={{0,448},{64,0},{128,64},{192,128},{256,192},{320,256},{384,320},{4... | collective-permute-start | bytes 688136 | tf_op jit(solution)/shard_map/ppermute | solution.py:218
  31.7 0.0 collective-permute-done.4.refs_3_
  31.7 2.1 %collective-permute-start.6 = (bf16[128,896]{1,0:T(8,128)(2,1)S(1)}, bf16[128,896]{1,0:T(8,128)(2,1)S(1)}, u32[]{:S(2)}, u32[]{:S(2)}) collective-permute-start(bf16[128,896]{1,0:T(8,128)(2,1)S(1)} %collective-permute-done.4.refs_3_), channel_id=1, source_target_pairs={{0,64},{64,128},{128,192},{192,256},{256,320},{320,384},{384,448},... | collective-permute-start | bytes 688136 | tf_op jit(solution)/shard_map/ppermute | solution.py:214
  33.8 0.0 collective-permute-done.2
  33.9 1.9 %collective-permute-start.3 = (bf16[512,512]{1,0:T(8,128)(2,1)S(1)}, bf16[512,512]{1,0:T(8,128)(2,1)S(1)}, u32[]{:S(2)}, u32[]{:S(2)}) collective-permute-start(bf16[512,512]{1,0:T(8,128)(2,1)S(1)} %constant_dynamic-update-slice_fusion.refs_0_), channel_id=1, source_target_pairs={{0,1},{1,0},{2,3},{3,2},{4,5},{5,4},{6,7},{7,6},{8,9},{9,8},{10,11... | collective-permute-start | bytes 1572872 | tf_op jit(solution)/shard_map/ppermute | solution.py:206
  35.8 0.0 collective-permute-done.5.refs_4_
  35.9 4.9 %collective-permute-start.7 = (bf16[128,896]{1,0:T(8,128)(2,1)S(1)}, bf16[128,896]{1,0:T(8,128)(2,1)S(1)}, u32[]{:S(2)}, u32[]{:S(2)}) collective-permute-start(bf16[128,896]{1,0:T(8,128)(2,1)S(1)} %collective-permute-done.5.refs_4_), channel_id=1, source_target_pairs={{0,448},{64,0},{128,64},{192,128},{256,192},{320,256},{384,320},{4... | collective-permute-start | bytes 688136 | tf_op jit(solution)/shard_map/ppermute | solution.py:218
  40.8 0.0 collective-permute-done.6.refs_5_
  40.8 1.9 %collective-permute-start.8 = (bf16[128,896]{1,0:T(8,128)(2,1)S(1)}, bf16[128,896]{1,0:T(8,128)(2,1)S(1)}, u32[]{:S(2)}, u32[]{:S(2)}) collective-permute-start(bf16[128,896]{1,0:T(8,128)(2,1)S(1)} %collective-permute-done.6.refs_5_), channel_id=1, source_target_pairs={{0,64},{64,128},{128,192},{192,256},{256,320},{320,384},{384,448},... | collective-permute-start | bytes 688136 | tf_op jit(solution)/shard_map/ppermute | solution.py:214
  42.7 3.5 %collective-permute-done.7.refs_6_ = bf16[128,896]{1,0:T(8,128)(2,1)S(1)} collective-permute-done((bf16[128,896]{1,0:T(8,128)(2,1)S(1)}, bf16[128,896]{1,0:T(8,128)(2,1)S(1)}, u32[]{:S(2)}, u32[]{:S(2)}) %collective-permute-start.7) | collective-permute-done | bytes 229408 | tf_op jit(solution)/shard_map/ppermute | solution.py:218
  46.2 5.6 %collective-permute-start.9 = (bf16[128,896]{1,0:T(8,128)(2,1)S(1)}, bf16[128,896]{1,0:T(8,128)(2,1)S(1)}, u32[]{:S(2)}, u32[]{:S(2)}) collective-permute-start(bf16[128,896]{1,0:T(8,128)(2,1)S(1)} %collective-permute-done.7.refs_6_), channel_id=1, source_target_pairs={{0,448},{64,0},{128,64},{192,128},{256,192},{320,256},{384,320},{4... | collective-permute-start | bytes 688136 | tf_op jit(solution)/shard_map/ppermute | solution.py:218
  51.8 0.0 collective-permute-done.8.refs_7_
  51.9 1.9 %collective-permute-start.10 = (bf16[128,896]{1,0:T(8,128)(2,1)S(1)}, bf16[128,896]{1,0:T(8,128)(2,1)S(1)}, u32[]{:S(2)}, u32[]{:S(2)}) collective-permute-start(bf16[128,896]{1,0:T(8,128)(2,1)S(1)} %collective-permute-done.8.refs_7_), channel_id=1, source_target_pairs={{0,64},{64,128},{128,192},{192,256},{256,320},{320,384},{384,448},... | collective-permute-start | bytes 688136 | tf_op jit(solution)/shard_map/ppermute | solution.py:214
  53.8 2.8 %collective-permute-done.9.refs_8_ = bf16[128,896]{1,0:T(8,128)(2,1)S(1)} collective-permute-done((bf16[128,896]{1,0:T(8,128)(2,1)S(1)}, bf16[128,896]{1,0:T(8,128)(2,1)S(1)}, u32[]{:S(2)}, u32[]{:S(2)}) %collective-permute-start.9) | collective-permute-done | bytes 229408 | tf_op jit(solution)/shard_map/ppermute | solution.py:218
  56.5 5.3 %collective-permute-done.10.refs_9_ = bf16[128,896]{1,0:T(8,128)(2,1)S(1)} collective-permute-done((bf16[128,896]{1,0:T(8,128)(2,1)S(1)}, bf16[128,896]{1,0:T(8,128)(2,1)S(1)}, u32[]{:S(2)}, u32[]{:S(2)}) %collective-permute-start.10) | collective-permute-done | bytes 229408 | tf_op jit(solution)/shard_map/ppermute | solution.py:214
  61.9 0.0 collective-permute-done.3.refs_1_
  61.9 1.5 %partial_product.1 = bf16[512,896]{1,0:T(8,128)(2,1)S(1)} custom-call(s32[1]{0:T(128)} %bitcast.y_ref, s32[1]{0:T(128)} %bitcast.1.t_ref, bf16[512,512]{1,0:T(8,128)(2,1)S(1)} %constant_dynamic-update-slice_fusion.refs_0_, bf16[512,512]{1,0:T(8,128)(2,1)S(1)} %collective-permute-done.3.refs_1_, bf16[128,896]{1,0:T(8,128)(2,1)S(1)} %copy-done, ...), custom_call_target="tpu_custom_call" | custom-call | flops 939524096 | bytes 6000000 | tf_op jit(solution)/shard_map/partial_product/pallas_call | solution.py:103
  63.4 0.0 copy-start.1
  63.4 34.8 %all_to_all.20.parts_ref = bf16[8,64,896]{2,1,0:T(8,128)(2,1)S(1)} all-to-all(bf16[8,64,896]{2,1,0:T(8,128)(2,1)S(1)} %bitcast.10), channel_id=1, replica_groups=mesh['y'=8,'z'=8,'t'=8] {'z'}, dimensions={0} | all-to-all | bytes 1835008 | tf_op jit(solution)/shard_map/all_to_all | solution.py:224
  98.2 0.0 copy-done.1
  98.2 0.9 momentum_step.1
  99.1 9.8 %all_to_all.21.grams_ref = f32[8,32,128]{2,1,0:T(8,128)S(1)} all-to-all(f32[8,32,128]{2,1,0:T(8,128)S(1)} %get-tuple-element.7), channel_id=1, replica_groups=mesh['y'=8,'z'=8,'t'=8] {'t'}, dimensions={0} | all-to-all | bytes 262144 | tf_op jit(solution)/shard_map/all_to_all | solution.py:226
  108.9 3.0 %polar_update.1 = bf16[8,64,112]{2,1,0:T(8,128)(2,1)S(1)} custom-call(f32[8,32,128]{2,1,0:T(8,128)S(1)} %all_to_all.21.grams_ref, f32[64,896]{1,0:T(8,128)S(1)} %get-tuple-element.8.block_ref), custom_call_target="tpu_custom_call" | custom-call | flops 100000000 | bytes 600000 | tf_op jit(solution)/shard_map/polar_update/pallas_call | solution.py:185
  111.9 13.0 %all_to_all.22 = bf16[8,64,112]{2,1,0:T(8,128)(2,1)S(1)} all-to-all(bf16[8,64,112]{2,1,0:T(8,128)(2,1)S(1)} %polar_update.1), channel_id=1, replica_groups=mesh['y'=8,'z'=8,'t'=8] {'y'}, dimensions={0} | all-to-all | bytes 229376 | tf_op jit(solution)/shard_map/all_to_all | solution.py:228
  124.9 0.2 copy.10
  125.1 0.2 reshape.28
  125.3 11.3 %all_to_all.23 = bf16[8,2,3584]{2,1,0:T(2,128)(2,1)S(1)} all-to-all(bf16[8,2,3584]{2,1,0:T(2,128)(2,1)S(1)} %reshape.28), channel_id=1, replica_groups=mesh['y'=8,'z'=8,'t'=8] {'z'}, dimensions={0} | all-to-all | bytes 229376 | tf_op jit(solution)/shard_map/all_to_all | solution.py:231
  136.6 0.2 reshape.29
  136.7 0.1 copy.11
  136.8 0.9 reshape.27
  (4 shorter events, 0.1 us)
Async XLA Ops:
  0.6 14.9 %collective-permute-start = (bf16[128,512]{1,0:T(8,128)(2,1)}, bf16[128,512]{1,0:T(8,128)(2,1)S(1)}, u32[]{:S(2)}, u32[]{:S(2)}) collective-permute-start(bf16[128,512]{1,0:T(8,128)(2,1)} %param.6), channel_id=1, source_target_pairs={{0,0},{1,65},{2,130},{3,195},{4,260},{5,325},{6,390},{7,455},{64,1... | collective-permute-start | bytes 393224 | tf_op jit(solution)/shard_map/ppermute | solution.py:199
  7.9 19.5 %copy-start = (bf16[128,896]{1,0:T(8,128)(2,1)S(1)}, bf16[128,896]{1,0:T(8,128)(2,1)}, u32[]{:S(2)}) copy-start(bf16[128,896]{1,0:T(8,128)(2,1)} %gate_cotangent.1.refs_2_) | copy-start | bytes 688132
  15.5 6.8 %collective-permute-start.1 = (bf16[128,512]{1,0:T(8,128)(2,1)S(1)}, bf16[128,512]{1,0:T(8,128)(2,1)S(1)}, u32[]{:S(2)}, u32[]{:S(2)}) collective-permute-start(bf16[128,512]{1,0:T(8,128)(2,1)S(1)} %collective-permute-done), channel_id=1, source_target_pairs={{0,2},{1,3},{2,0},{3,1},{4,6},{5,7},{6,4},{7,5},{8,10},{9,11},{10,... | collective-permute-start | bytes 393224 | tf_op jit(solution)/shard_map/ppermute | solution.py:206
  17.4 14.3 %collective-permute-start.4 = (bf16[128,896]{1,0:T(8,128)(2,1)}, bf16[128,896]{1,0:T(8,128)(2,1)S(1)}, u32[]{:S(2)}, u32[]{:S(2)}) collective-permute-start(bf16[128,896]{1,0:T(8,128)(2,1)} %gate_cotangent.1.refs_2_), channel_id=1, source_target_pairs={{0,64},{64,128},{128,192},{192,256},{256,320},{320,384},{384,448},... | collective-permute-start | bytes 688136 | tf_op jit(solution)/shard_map/ppermute | solution.py:214
  22.4 11.5 %collective-permute-start.2 = (bf16[256,512]{1,0:T(8,128)(2,1)S(1)}, bf16[256,512]{1,0:T(8,128)(2,1)S(1)}, u32[]{:S(2)}, u32[]{:S(2)}) collective-permute-start(bf16[256,512]{1,0:T(8,128)(2,1)S(1)} %pad_maximum_fusion), channel_id=1, source_target_pairs={{0,6},{1,7},{2,4},{3,5},{4,2},{5,3},{6,0},{7,1},{8,14},{9,15},{10,... | collective-permute-start | bytes 786440 | tf_op jit(solution)/shard_map/ppermute | solution.py:206
  27.4 8.4 %collective-permute-start.5 = (bf16[128,896]{1,0:T(8,128)(2,1)S(1)}, bf16[128,896]{1,0:T(8,128)(2,1)S(1)}, u32[]{:S(2)}, u32[]{:S(2)}) collective-permute-start(bf16[128,896]{1,0:T(8,128)(2,1)S(1)} %copy-done), channel_id=1, source_target_pairs={{0,448},{64,0},{128,64},{192,128},{256,192},{320,256},{384,320},{4... | collective-permute-start | bytes 688136 | tf_op jit(solution)/shard_map/ppermute | solution.py:218
  31.7 9.1 %collective-permute-start.6 = (bf16[128,896]{1,0:T(8,128)(2,1)S(1)}, bf16[128,896]{1,0:T(8,128)(2,1)S(1)}, u32[]{:S(2)}, u32[]{:S(2)}) collective-permute-start(bf16[128,896]{1,0:T(8,128)(2,1)S(1)} %collective-permute-done.4.refs_3_), channel_id=1, source_target_pairs={{0,64},{64,128},{128,192},{192,256},{256,320},{320,384},{384,448},... | collective-permute-start | bytes 688136 | tf_op jit(solution)/shard_map/ppermute | solution.py:214
  33.9 28.0 %collective-permute-start.3 = (bf16[512,512]{1,0:T(8,128)(2,1)S(1)}, bf16[512,512]{1,0:T(8,128)(2,1)S(1)}, u32[]{:S(2)}, u32[]{:S(2)}) collective-permute-start(bf16[512,512]{1,0:T(8,128)(2,1)S(1)} %constant_dynamic-update-slice_fusion.refs_0_), channel_id=1, source_target_pairs={{0,1},{1,0},{2,3},{3,2},{4,5},{5,4},{6,7},{7,6},{8,9},{9,8},{10,11... | collective-permute-start | bytes 1572872 | tf_op jit(solution)/shard_map/ppermute | solution.py:206
  35.9 10.4 %collective-permute-start.7 = (bf16[128,896]{1,0:T(8,128)(2,1)S(1)}, bf16[128,896]{1,0:T(8,128)(2,1)S(1)}, u32[]{:S(2)}, u32[]{:S(2)}) collective-permute-start(bf16[128,896]{1,0:T(8,128)(2,1)S(1)} %collective-permute-done.5.refs_4_), channel_id=1, source_target_pairs={{0,448},{64,0},{128,64},{192,128},{256,192},{320,256},{384,320},{4... | collective-permute-start | bytes 688136 | tf_op jit(solution)/shard_map/ppermute | solution.py:218
  40.8 11.0 %collective-permute-start.8 = (bf16[128,896]{1,0:T(8,128)(2,1)S(1)}, bf16[128,896]{1,0:T(8,128)(2,1)S(1)}, u32[]{:S(2)}, u32[]{:S(2)}) collective-permute-start(bf16[128,896]{1,0:T(8,128)(2,1)S(1)} %collective-permute-done.6.refs_5_), channel_id=1, source_target_pairs={{0,64},{64,128},{128,192},{192,256},{256,320},{320,384},{384,448},... | collective-permute-start | bytes 688136 | tf_op jit(solution)/shard_map/ppermute | solution.py:214
  46.2 10.3 %collective-permute-start.9 = (bf16[128,896]{1,0:T(8,128)(2,1)S(1)}, bf16[128,896]{1,0:T(8,128)(2,1)S(1)}, u32[]{:S(2)}, u32[]{:S(2)}) collective-permute-start(bf16[128,896]{1,0:T(8,128)(2,1)S(1)} %collective-permute-done.7.refs_6_), channel_id=1, source_target_pairs={{0,448},{64,0},{128,64},{192,128},{256,192},{320,256},{384,320},{4... | collective-permute-start | bytes 688136 | tf_op jit(solution)/shard_map/ppermute | solution.py:218
  51.9 10.0 %collective-permute-start.10 = (bf16[128,896]{1,0:T(8,128)(2,1)S(1)}, bf16[128,896]{1,0:T(8,128)(2,1)S(1)}, u32[]{:S(2)}, u32[]{:S(2)}) collective-permute-start(bf16[128,896]{1,0:T(8,128)(2,1)S(1)} %collective-permute-done.8.refs_7_), channel_id=1, source_target_pairs={{0,64},{64,128},{128,192},{192,256},{256,320},{320,384},{384,448},... | collective-permute-start | bytes 688136 | tf_op jit(solution)/shard_map/ppermute | solution.py:214
  63.4 34.8 %copy-start.1 = (f32[64,896]{1,0:T(8,128)S(1)}, f32[64,896]{1,0:T(8,128)}, u32[]{:S(2)}) copy-start(f32[64,896]{1,0:T(8,128)} %momentum_ref.1) | copy-start | bytes 688132

commit v7 on v3

--- a/solution.py
+++ b/solution.py
@@ -78,14 +78,14 @@
     return (y * NZ + z) * NT + t
 
 
-def ring_pairs(step):
-    pairs = []
-    for y in range(NY):
-        for z in range(NZ):
-            for t in range(NT):
-                target = (y, (z + step) % NZ, t) if t % 2 else ((y + step) % NY, z, t)
-                pairs.append((device_number(y, z, t), device_number(*target)))
-    return pairs
+def line_groups(even_axis):
+    groups = []
+    for t in range(NT):
+        along_y = (t % 2 == 0) == (even_axis == "y")
+        for fixed in range(NZ if along_y else NY):
+            line = [(i, fixed) if along_y else (fixed, i) for i in range(NY if along_y else NZ)]
+            groups.append([device_number(y, z, t) for y, z in line])
+    return groups
 
 
 def tensor_pairs(masks):
@@ -97,68 +97,51 @@
     ]
 
 
-def cross_groups():
-    along_z = [[device_number(y, z, t) for z in range(NZ)] for y in range(NY) for t in range(0, NT, 2)]
-    along_y = [[device_number(y, z, t) for y in range(NY)] for z in range(NZ) for t in range(1, NT, 2)]
-    return along_z + along_y
-
-
-def partial_kernel(orders, grad_offsets, y_ref, z_ref, t_ref, *refs):
-    feature_refs, grad_refs = refs[:2], refs[2 : 2 + NY]
-    out_ref, features, grads = refs[2 + NY :]
-    tokens = grad_refs[0].shape[0]
+def partial_kernel(orders, t_ref, first_ref, second_ref, grads_ref, out_ref, features):
     rows = out_ref.shape[0]
+    tokens = first_ref.shape[1]
     t = t_ref[0]
-    odd = lax.rem(t, 2)
-    blocks = [(ref, start) for ref in feature_refs for start in range(0, ref.shape[0], rows)]
-
-    @pl.when(odd == 0)
+    blocks = [(ref, start) for ref in (first_ref, second_ref) for start in range(0, ref.shape[0], rows)]
+
+    @pl.when(lax.rem(t, 2) == 0)
     def _():
         for offset, (ref, start) in zip(orders[0], blocks):
             group = lax.bitwise_xor(t, offset)
             features[:, pl.ds(pl.multiple_of(group * tokens, tokens), tokens)] = ref[start : start + rows, :]
 
-    @pl.when(odd == 1)
+    @pl.when(lax.rem(t, 2) == 1)
     def _():
         for offset, (ref, start) in zip(orders[1], blocks):
-            group = lax.bitwise_xor(t, offset)
+            block_rows = pl.ds(pl.multiple_of(lax.bitwise_xor(t, offset) * BLK, BLK), BLK)
             for z in range(NZ):
-                features[pl.ds(pl.multiple_of(group * BLK, BLK), BLK), z * tokens : (z + 1) * tokens] = ref[
+                features[block_rows, z * tokens : (z + 1) * tokens] = ref[
                     start + z * BLK : start + (z + 1) * BLK, :
                 ]
 
-    own = jnp.where(odd == 0, y_ref[0], z_ref[0])
-    for offset, ref in zip(grad_offsets, grad_refs):
-        group = lax.rem(own + (NY + offset), NY)
-        grads[pl.ds(pl.multiple_of(group * tokens, tokens), tokens), :] = ref[...]
     step = 128
     for start in range(0, rows, step):
         product = jnp.dot(
-            features[start : start + step, :], grads[...], preferred_element_type=jnp.float32
+            features[start : start + step, :], grads_ref[...], preferred_element_type=jnp.float32
         )
         out_ref[start : start + step, :] = product.astype(out_ref.dtype)
 
 
-def partial_product(y, z, t, orders, grad_offsets, feature_halves, grad_blocks):
-    tokens, columns = grad_blocks[0].shape
+def partial_product(t, orders, feature_halves, grads):
+    tokens, columns = grads.shape
     rows = NZ * BLK
     vmem = pl.BlockSpec(memory_space=pltpu.VMEM)
-    smem = pl.BlockSpec(memory_space=pltpu.SMEM)
-    return pl.pallas_call(
-        functools.partial(partial_kernel, orders, tuple(grad_offsets)),
+    return pl.pallas_call(
+        functools.partial(partial_kernel, orders),
         out_shape=jax.ShapeDtypeStruct((rows, columns), jnp.bfloat16),
-        in_specs=[smem] * 3 + [vmem] * (2 + NY),
+        in_specs=[pl.BlockSpec(memory_space=pltpu.SMEM), vmem, vmem, vmem],
         out_specs=vmem,
-        scratch_shapes=[
-            pltpu.VMEM((rows, NY * tokens), jnp.bfloat16),
-            pltpu.VMEM((NY * tokens, columns), jnp.bfloat16),
-        ],
+        scratch_shapes=[pltpu.VMEM((rows, tokens), jnp.bfloat16)],
         compiler_params=pltpu.CompilerParams(vmem_limit_bytes=32 * 1024 * 1024),
         cost_estimate=pl.CostEstimate(
-            flops=2 * NY * tokens * rows * columns, bytes_accessed=6_000_000, transcendentals=0
+            flops=2 * tokens * rows * columns, bytes_accessed=6_000_000, transcendentals=0
         ),
         name="partial_product",
-    )(*(jnp.reshape(i, (1,)) for i in (y, z, t)), *feature_halves, *grad_blocks)
+    )(jnp.reshape(t, (1,)), *feature_halves, grads)
 
 
 def momentum_kernel(parts_ref, momentum_ref, moment_ref, nesterov_ref, grams_ref):
@@ -242,8 +225,8 @@
     turned, gate_grad = prepare(y * NZ + z, lengths, features, gate_pre, up_pre, hidden_grad)
 
     swap = [(a * NT + b, b * NT + a) for a in range(NY) for b in range(NT)]
-    by_tokens = lax.ppermute(turned, ("y", "t"), swap)
-    up, down = (lax.ppermute(gate_grad, AXES, ring_pairs(step)) for step in (1, -1))
+    by_tokens = lax.ppermute(features, ("y", "t"), swap).T
+    grads = lax.all_gather(gate_grad, AXES, axis_index_groups=line_groups("y"), axis=0, tiled=True)
     by_blocks = lax.all_to_all(
         turned.reshape(NZ, BLK, turned.shape[1]), "z", split_axis=0, concat_axis=0, tiled=True
     ).reshape(turned.shape)
@@ -257,22 +240,10 @@
         halves = (kept, arrived)
         kept = jnp.concatenate(halves, axis=0)
 
-    grad_blocks, grad_offsets = [gate_grad], [0]
-    for step in range(1, NY // 2 + 1):
-        if step > 1:
-            up = lax.ppermute(up, AXES, ring_pairs(1))
-        grad_blocks.append(up)
-        grad_offsets.append(-step)
-        if 2 * step < NY:
-            if step > 1:
-                down = lax.ppermute(down, AXES, ring_pairs(-1))
-            grad_blocks.append(down)
-            grad_offsets.append(step)
-
-    partial_value = partial_product(y, z, t, orders, grad_offsets, halves, grad_blocks)
+    partial_value = partial_product(t, orders, halves, grads)
     pieces = partial_value.reshape(NZ, BLK, partial_value.shape[1])
     received = lax.all_to_all(
-        pieces, AXES, split_axis=0, concat_axis=0, axis_index_groups=cross_groups(), tiled=True
+        pieces, AXES, split_axis=0, concat_axis=0, axis_index_groups=line_groups("z"), tiled=True
     )
     new_moment, nesterov, grams = momentum_step(received, momentum)
     grams = lax.all_to_all(grams, "t", split_axis=0, concat_axis=0, tiled=True)

time: 140 us -> 138 us (0.986)
  starting transfers between devices: 47.2 us -> 21.3 us
  between operations: 0.85 us -> 14.2 us
  waiting for transfers between devices: 22.9 us -> 27.6 us
  blocking collectives: 58.6 us -> 61.7 us
  local copies, waits for them, and re-layouts: 1.51 us -> 4.01 us
    ppermute x8 -> x1, starting transfers between devices: 29.4 us -> 4.47 us  [per_device(): by_tokens = lax.ppermute(features, ('y', 't'), swap).T]
    ppermute x3, waiting for transfers between devices: 1.32 us -> 16.1 us  [per_device(): lax.ppermute(given if halves is None else kept, AXES, tensor_pairs(masks))]
    ppermute x8 -> x1, waiting for transfers between devices: 21.6 us -> 11.4 us  [per_device(): by_tokens = lax.ppermute(features, ('y', 't'), swap).T]
    unnamed x8 -> x7, local copies, waits for them, and re-layouts: 0.38 us -> 2.89 us
    all_to_all x1, blocking collectives: 8.98 us -> 11 us  [per_device(): grams = lax.all_to_all(grams, 't', split_axis=0, concat_axis=0, tiled=True)]
  transfers between devices with their start and end apart: 12 -> 6, of which waited for: 6 -> 4; matrix products, arithmetic and copies ran while one was open for 0% -> 1% of each run, Pallas kernels for 0% -> 0%
where the time goes in v7:
time: 138 us; the launch traced here: 137 us
  blocking collectives  61.7 us (45%)
  waiting for transfers between devices  27.6 us (20%)
  starting transfers between devices  21.3 us (15%)
  between operations  14.2 us (10%)
  Pallas kernels  8.26 us (6%)
  local copies, waits for them, and re-layouts  4.01 us (3%)
    all_to_all x1, blocking collectives, per_device(): lax.all_to_all(pieces, AXES, split_axis=0, concat_axis=0, axis_index_grou...  24.2 us
    ppermute x3, waiting for transfers between devices, per_device(): lax.ppermute(given if halves is None else kept, AXES, tensor_pairs(masks))  16.1 us
    all_to_all x1, blocking collectives, per_device(): by_y = lax.all_to_all(by_y, 'y', split_axis=0, concat_axis=0, tiled=True)  15.3 us
    ppermute x1, waiting for transfers between devices, per_device(): by_tokens = lax.ppermute(features, ('y', 't'), swap).T  11.4 us
    all_to_all x1, blocking collectives, per_device(): by_z = lax.all_to_all(by_z, 'z', split_axis=0, concat_axis=0, tiled=True)  11.3 us
    all_to_all x1, blocking collectives, per_device(): grams = lax.all_to_all(grams, 't', split_axis=0, concat_axis=0, tiled=True)  11 us
    all_to_all x1, starting transfers between devices, per_device(): lax.all_to_all(turned.reshape(NZ, BLK, turned.shape[1]), 'z', split_axis=...  10.3 us
    ppermute x3, starting transfers between devices, per_device(): lax.ppermute(given if halves is None else kept, AXES, tensor_pairs(masks))  6.44 us
  transfers between devices with their start and end apart: 6, of which 4 were waited for; matrix products, arithmetic and copies ran while one was open for 1% of the time, Pallas kernels for 0%

profile of v7, /device:TPU:2, one launch (start us, length us, event | category | flops | bytes accessed | tf_op | source)
XLA Modules:
  0.0 137.1 jit_solution(8773687796876627923)
XLA Ops:
  7.2 0.0 all-gather.2.cloned.1.call-start
  7.2 2.8 %prepare.1 = (bf16[512,128]{1,0:T(8,128)(2,1)}, bf16[128,896]{1,0:T(8,128)(2,1)}) custom-call(s32[1]{0:T(128)} %bitcast.2.place_ref, s32[64]{0:T(128)} %lengths_ref.1, bf16[128,512]{1,0:T(8,128)(2,1)} %features_in.1, bf16[128,896]{1,0:T(8,128)(2,1)} %gate_in.1, bf16[128,896]{1,0:T(8,128)(2,1)} %up_in.1, bf16[128,896]{1,0:T(8,128)(2,1)} %cotangent_in.1), custom_call_target="tpu_custom_call" | custom-call | flops 1376256 | bytes 917504 | tf_op jit(solution)/shard_map/prepare/pallas_call | solution.py:59
  10.0 0.0 all-gather.2.cloned.1.call-update
  10.1 10.3 %all-to-all-start = ((bf16[8,64,128]{2,1,0:T(8,128)(2,1)}), bf16[8,64,128]{2,1,0:T(8,128)(2,1)S(1)}, u32[]{:S(2)}, u32[]{:S(2)}) async-start(bf16[8,64,128]{2,1,0:T(8,128)(2,1)} %bitcast.19), calls=%async_computation | async-start | bytes 262144 | tf_op jit(solution)/shard_map/all_to_all | solution.py:230
  20.4 1.0 copy.12
  21.4 4.5 %collective-permute-start = (bf16[128,512]{0,1:T(8,128)(2,1)S(1)}, bf16[128,512]{0,1:T(8,128)(2,1)S(1)}, u32[]{:S(2)}, u32[]{:S(2)}) collective-permute-start(bf16[128,512]{0,1:T(8,128)(2,1)S(1)} %copy.12), channel_id=1, source_target_pairs={{0,0},{1,64},{2,128},{3,192},{4,256},{5,320},{6,384},{7,448},{64,1... | collective-permute-start | bytes 393224 | tf_op jit(solution)/shard_map/ppermute | solution.py:228
  25.9 11.4 %collective-permute-done = bf16[128,512]{0,1:T(8,128)(2,1)S(1)} collective-permute-done((bf16[128,512]{0,1:T(8,128)(2,1)S(1)}, bf16[128,512]{0,1:T(8,128)(2,1)S(1)}, u32[]{:S(2)}, u32[]{:S(2)}) %collective-permute-start) | collective-permute-done | bytes 131104 | tf_op jit(solution)/shard_map/ppermute | solution.py:228
  37.3 0.0 all-to-all-done
  37.4 1.9 %collective-permute-start.1 = (bf16[512,128]{1,0:T(8,128)(2,1)S(1)}, bf16[512,128]{1,0:T(8,128)(2,1)S(1)}, u32[]{:S(2)}, u32[]{:S(2)}) collective-permute-start(bf16[512,128]{1,0:T(8,128)(2,1)S(1)} %get-tuple-element.13), channel_id=1, source_target_pairs={{0,1},{1,0},{2,3},{3,2},{4,5},{5,4},{6,7},{7,6},{8,9},{9,8},{10,11... | collective-permute-start | bytes 393224 | tf_op jit(solution)/shard_map/ppermute | solution.py:238
  39.3 1.3 collective-permute-done.1
  40.6 1.9 %collective-permute-start.2 = (bf16[1024,128]{1,0:T(8,128)(2,1)S(1)}, bf16[1024,128]{1,0:T(8,128)(2,1)S(1)}, u32[]{:S(2)}, u32[]{:S(2)}) collective-permute-start(bf16[1024,128]{1,0:T(8,128)(2,1)S(1)} %pad_maximum_fusion.1), channel_id=1, source_target_pairs={{0,2},{1,7},{2,0},{3,5},{4,6},{5,3},{6,4},{7,1},{8,10},{9,15},{10,... | collective-permute-start | bytes 786440 | tf_op jit(solution)/shard_map/ppermute | solution.py:238
  42.5 6.3 %collective-permute-done.2 = bf16[1024,128]{1,0:T(8,128)(2,1)S(1)} collective-permute-done((bf16[1024,128]{1,0:T(8,128)(2,1)S(1)}, bf16[1024,128]{1,0:T(8,128)(2,1)S(1)}, u32[]{:S(2)}, u32[]{:S(2)}) %collective-permute-start.2) | collective-permute-done | bytes 262176 | tf_op jit(solution)/shard_map/ppermute | solution.py:238
  48.9 2.6 %collective-permute-start.3 = (bf16[2048,128]{1,0:T(8,128)(2,1)S(1)}, bf16[2048,128]{1,0:T(8,128)(2,1)S(1)}, u32[]{:S(2)}, u32[]{:S(2)}) collective-permute-start(bf16[2048,128]{1,0:T(8,128)(2,1)S(1)} %pad_maximum_fusion.first_ref), channel_id=1, source_target_pairs={{0,6},{1,3},{2,4},{3,1},{4,2},{5,7},{6,0},{7,5},{8,14},{9,11},{10,... | collective-permute-start | bytes 1572872 | tf_op jit(solution)/shard_map/ppermute | solution.py:238
  51.5 8.5 %collective-permute-done.3.second_ref = bf16[2048,128]{1,0:T(8,128)(2,1)S(1)} collective-permute-done((bf16[2048,128]{1,0:T(8,128)(2,1)S(1)}, bf16[2048,128]{1,0:T(8,128)(2,1)S(1)}, u32[]{:S(2)}, u32[]{:S(2)}) %collective-permute-start.3) | collective-permute-done | bytes 524320 | tf_op jit(solution)/shard_map/ppermute | solution.py:238
  60.0 0.0 all-gather.2.cloned.1.call-done.grads_ref
  60.0 0.0 copy-start
  60.0 1.5 %copy-done = bf16[1024,896]{1,0:T(8,128)(2,1)S(1)} copy-done((bf16[1024,896]{1,0:T(8,128)(2,1)S(1)}, bf16[1024,896]{1,0:T(8,128)(2,1)}, u32[]{:S(2)}) %copy-start) | copy-done | bytes 1835032
  61.5 1.6 %partial_product.1 = bf16[512,896]{1,0:T(8,128)(2,1)S(1)} custom-call(s32[1]{0:T(128)} %bitcast.t_ref, bf16[2048,128]{1,0:T(8,128)(2,1)S(1)} %pad_maximum_fusion.first_ref, bf16[2048,128]{1,0:T(8,128)(2,1)S(1)} %collective-permute-done.3.second_ref, bf16[1024,896]{1,0:T(8,128)(2,1)S(1)} %copy-done), custom_call_target="tpu_custom_call" | custom-call | flops 939524096 | bytes 6000000 | tf_op jit(solution)/shard_map/partial_product/pallas_call | solution.py:133
  63.1 0.0 copy-start.1
  63.1 24.2 %all_to_all.25.parts_ref = bf16[8,64,896]{2,1,0:T(8,128)(2,1)S(1)} all-to-all(bf16[8,64,896]{2,1,0:T(8,128)(2,1)S(1)} %bitcast.16), channel_id=1, replica_groups={{0,8,16,24,32,40,48,56},{64,72,80,88,96,104,112,120},{128,136,144,152,1..., dimensions={0} | all-to-all | bytes 1835008 | tf_op jit(solution)/shard_map/all_to_all | solution.py:245
  87.3 0.0 copy-done.1
  87.3 0.9 momentum_step.1
  88.2 11.0 %all_to_all.26.grams_ref = f32[8,32,128]{2,1,0:T(8,128)S(1)} all-to-all(f32[8,32,128]{2,1,0:T(8,128)S(1)} %get-tuple-element.9), channel_id=1, replica_groups=mesh['y'=8,'z'=8,'t'=8] {'t'}, dimensions={0} | all-to-all | bytes 262144 | tf_op jit(solution)/shard_map/all_to_all | solution.py:249
  99.1 3.0 %polar_update.1 = bf16[8,64,112]{2,1,0:T(8,128)(2,1)S(1)} custom-call(f32[8,32,128]{2,1,0:T(8,128)S(1)} %all_to_all.26.grams_ref, f32[64,896]{1,0:T(8,128)S(1)} %get-tuple-element.10.block_ref), custom_call_target="tpu_custom_call" | custom-call | flops 100000000 | bytes 600000 | tf_op jit(solution)/shard_map/polar_update/pallas_call | solution.py:212
  102.1 15.3 %all_to_all.27 = bf16[8,64,112]{2,1,0:T(8,128)(2,1)S(1)} all-to-all(bf16[8,64,112]{2,1,0:T(8,128)(2,1)S(1)} %polar_update.1), channel_id=1, replica_groups=mesh['y'=8,'z'=8,'t'=8] {'y'}, dimensions={0} | all-to-all | bytes 229376 | tf_op jit(solution)/shard_map/all_to_all | solution.py:251
  117.4 0.2 copy.13
  117.6 0.2 reshape.32
  117.8 11.3 %all_to_all.28 = bf16[8,2,3584]{2,1,0:T(2,128)(2,1)S(1)} all-to-all(bf16[8,2,3584]{2,1,0:T(2,128)(2,1)S(1)} %reshape.32), channel_id=1, replica_groups=mesh['y'=8,'z'=8,'t'=8] {'z'}, dimensions={0} | all-to-all | bytes 229376 | tf_op jit(solution)/shard_map/all_to_all | solution.py:254
  129.1 0.2 reshape.33
  129.3 0.1 copy.14
  129.4 0.9 reshape.31
  (3 shorter events, 0.1 us)
Async XLA Ops:
  7.2 52.8 %all-gather.2.cloned.1.call-start = ((), (), s32[]{:S(2)}) async-start(), calls=%async_computation.5 | async-start | bytes 2064384 | tf_op jit(solution)/shard_map/all_gather | solution.py:229
  10.1 27.3 %all-to-all-start = ((bf16[8,64,128]{2,1,0:T(8,128)(2,1)}), bf16[8,64,128]{2,1,0:T(8,128)(2,1)S(1)}, u32[]{:S(2)}, u32[]{:S(2)}) async-start(bf16[8,64,128]{2,1,0:T(8,128)(2,1)} %bitcast.19), calls=%async_computation | async-start | bytes 262144 | tf_op jit(solution)/shard_map/all_to_all | solution.py:230
  21.4 15.9 %collective-permute-start = (bf16[128,512]{0,1:T(8,128)(2,1)S(1)}, bf16[128,512]{0,1:T(8,128)(2,1)S(1)}, u32[]{:S(2)}, u32[]{:S(2)}) collective-permute-start(bf16[128,512]{0,1:T(8,128)(2,1)S(1)} %copy.12), channel_id=1, source_target_pairs={{0,0},{1,64},{2,128},{3,192},{4,256},{5,320},{6,384},{7,448},{64,1... | collective-permute-start | bytes 393224 | tf_op jit(solution)/shard_map/ppermute | solution.py:228
  37.4 3.2 %collective-permute-start.1 = (bf16[512,128]{1,0:T(8,128)(2,1)S(1)}, bf16[512,128]{1,0:T(8,128)(2,1)S(1)}, u32[]{:S(2)}, u32[]{:S(2)}) collective-permute-start(bf16[512,128]{1,0:T(8,128)(2,1)S(1)} %get-tuple-element.13), channel_id=1, source_target_pairs={{0,1},{1,0},{2,3},{3,2},{4,5},{5,4},{6,7},{7,6},{8,9},{9,8},{10,11... | collective-permute-start | bytes 393224 | tf_op jit(solution)/shard_map/ppermute | solution.py:238
  40.6 8.3 %collective-permute-start.2 = (bf16[1024,128]{1,0:T(8,128)(2,1)S(1)}, bf16[1024,128]{1,0:T(8,128)(2,1)S(1)}, u32[]{:S(2)}, u32[]{:S(2)}) collective-permute-start(bf16[1024,128]{1,0:T(8,128)(2,1)S(1)} %pad_maximum_fusion.1), channel_id=1, source_target_pairs={{0,2},{1,7},{2,0},{3,5},{4,6},{5,3},{6,4},{7,1},{8,10},{9,15},{10,... | collective-permute-start | bytes 786440 | tf_op jit(solution)/shard_map/ppermute | solution.py:238
  48.9 11.1 %collective-permute-start.3 = (bf16[2048,128]{1,0:T(8,128)(2,1)S(1)}, bf16[2048,128]{1,0:T(8,128)(2,1)S(1)}, u32[]{:S(2)}, u32[]{:S(2)}) collective-permute-start(bf16[2048,128]{1,0:T(8,128)(2,1)S(1)} %pad_maximum_fusion.first_ref), channel_id=1, source_target_pairs={{0,6},{1,3},{2,4},{3,1},{4,2},{5,7},{6,0},{7,5},{8,14},{9,11},{10,... | collective-permute-start | bytes 1572872 | tf_op jit(solution)/shard_map/ppermute | solution.py:238
  60.0 1.5 %copy-start = (bf16[1024,896]{1,0:T(8,128)(2,1)S(1)}, bf16[1024,896]{1,0:T(8,128)(2,1)}, u32[]{:S(2)}) copy-start(bf16[1024,896]{1,0:T(8,128)(2,1)} %all-gather.2.cloned.1.call-done.grads_ref) | copy-start | bytes 5505028
  63.1 24.2 %copy-start.1 = (f32[64,896]{1,0:T(8,128)S(1)}, f32[64,896]{1,0:T(8,128)}, u32[]{:S(2)}) copy-start(f32[64,896]{1,0:T(8,128)} %momentum_ref.1) | copy-start | bytes 688132
Sparse Core Ops, SparseCore 0:
  10.7 47.9 all-gather.1

commit v8 on v7

--- a/solution.py
+++ b/solution.py
@@ -28,7 +28,7 @@
 AXES = ("y", "z", "t")
 
 
-def prepare_kernel(place_ref, lengths_ref, features_in, gate_in, up_in, cotangent_in, turned_ref, grad_ref, *scratch):
+def prepare_kernel(place_ref, lengths_ref, features_in, gate_in, up_in, cotangent_in, turned_ref, copies_ref, *scratch):
     buffers, arrived = scratch[:4], scratch[4]
     sources = (features_in, gate_in, up_in, cotangent_in)
     copies = [
@@ -46,7 +46,9 @@
     gate_grad = cotangent * up_value * sigmoid_gate * (1.0 + gate_value * (1.0 - sigmoid_gate))
     position = lax.broadcasted_iota(jnp.int32, gate_value.shape, 0)
     trained = position < lengths_ref[place_ref[0]]
-    grad_ref[...] = jnp.where(trained, gate_grad, 0.0).astype(grad_ref.dtype)
+    gate_grad = jnp.where(trained, gate_grad, 0.0).astype(copies_ref.dtype)
+    for part in range(copies_ref.shape[0]):
+        copies_ref[part] = gate_grad
 
 
 def prepare(place, lengths, features, gate_pre, up_pre, hidden_grad):
@@ -60,7 +62,7 @@
         prepare_kernel,
         out_shape=(
             jax.ShapeDtypeStruct((rows, tokens), jnp.bfloat16),
-            jax.ShapeDtypeStruct((tokens, columns), jnp.bfloat16),
+            jax.ShapeDtypeStruct((NZ, tokens, columns), jnp.bfloat16),
         ),
         in_specs=[smem, smem] + [hbm] * 4,
         out_specs=(vmem, vmem),
@@ -72,6 +74,24 @@
         ),
         name="prepare",
     )(jnp.reshape(place, (1,)), lengths, *arrays)
+
+
+def turn_kernel(value_ref, turned_ref):
+    turned_ref[...] = value_ref[...].T
+
+
+def turn(value):
+    rows, columns = value.shape
+    vmem = pl.BlockSpec(memory_space=pltpu.VMEM)
+    return pl.pallas_call(
+        turn_kernel,
+        out_shape=jax.ShapeDtypeStruct((columns, rows), value.dtype),
+        in_specs=[vmem],
+        out_specs=vmem,
+        compiler_params=pltpu.CompilerParams(vmem_limit_bytes=8 * 1024 * 1024),
+        cost_estimate=pl.CostEstimate(flops=rows * columns, bytes_accessed=4 * rows * columns, transcendentals=0),
+        name="turn",
+    )(value)
 
 
 def device_number(y, z, t):
@@ -222,14 +242,18 @@
 
 def per_device(features, gate_pre, up_pre, hidden_grad, lengths, momentum):
     y, z, t = (lax.axis_index(name) for name in AXES)
-    turned, gate_grad = prepare(y * NZ + z, lengths, features, gate_pre, up_pre, hidden_grad)
-
     swap = [(a * NT + b, b * NT + a) for a in range(NY) for b in range(NT)]
-    by_tokens = lax.ppermute(features, ("y", "t"), swap).T
-    grads = lax.all_gather(gate_grad, AXES, axis_index_groups=line_groups("y"), axis=0, tiled=True)
+    swapped = lax.ppermute(features, ("y", "t"), swap)
+    turned, copies = prepare(y * NZ + z, lengths, features, gate_pre, up_pre, hidden_grad)
+
     by_blocks = lax.all_to_all(
         turned.reshape(NZ, BLK, turned.shape[1]), "z", split_axis=0, concat_axis=0, tiled=True
     ).reshape(turned.shape)
+    copies, swapped, by_blocks = lax.optimization_barrier((copies, swapped, by_blocks))
+    grads = lax.all_to_all(
+        copies, AXES, split_axis=0, concat_axis=0, axis_index_groups=line_groups("y"), tiled=True
+    ).reshape(-1, copies.shape[2])
+    by_tokens = turn(swapped)
     even = lax.rem(t, 2) == 0
     kept = jnp.where(even, by_tokens, by_blocks)
     given = jnp.where(even, by_blocks, by_tokens)

time: 138 us -> 128 us (0.928)
  between operations: 14.2 us -> 0.75 us
  starting transfers between devices: 21.3 us -> 30 us
  blocking collectives: 61.7 us -> 57.9 us
  local copies, waits for them, and re-layouts: 4.01 us -> 1.5 us
    all_to_all x0 -> x1, starting transfers between devices: none -> 5.7 us  [per_device(): lax.all_to_all(copies, AXES, split_axis=0, concat_axis=0, axis_index_grou...]
    all_to_all x0 -> x1, waiting for transfers between devices: none -> 4.66 us  [per_device(): lax.all_to_all(copies, AXES, split_axis=0, concat_axis=0, axis_index_grou...]
    ppermute x3, starting transfers between devices: 6.44 us -> 9.5 us  [per_device(): lax.ppermute(given if halves is None else kept, AXES, tensor_pairs(masks))]
    ppermute x3, waiting for transfers between devices: 16.1 us -> 13.1 us  [per_device(): lax.ppermute(given if halves is None else kept, AXES, tensor_pairs(masks))]
    all_to_all x1, blocking collectives: 15.3 us -> 12.6 us  [per_device(): by_y = lax.all_to_all(by_y, 'y', split_axis=0, concat_axis=0, tiled=True)]
    unnamed x7 -> x4, local copies, waits for them, and re-layouts: 2.89 us -> 0.37 us
    all_to_all x1, blocking collectives: 11 us -> 9.41 us  [per_device(): grams = lax.all_to_all(grams, 't', split_axis=0, concat_axis=0, tiled=True)]
  transfers between devices with their start and end apart: 6 -> 6, of which waited for: 4 -> 5; matrix products, arithmetic and copies ran while one was open for 1% -> 0% of each run, Pallas kernels for 0% -> 0%
where the time goes in v8:
time: 128 us
  blocking collectives  57.9 us (45%)
  starting transfers between devices  30 us (23%)
  waiting for transfers between devices  28.7 us (22%)
  Pallas kernels  8.92 us (7%)
  local copies, waits for them, and re-layouts  1.5 us (1%)
    all_to_all x1, blocking collectives, per_device(): lax.all_to_all(pieces, AXES, split_axis=0, concat_axis=0, axis_index_grou...  24.5 us
    ppermute x3, waiting for transfers between devices, per_device(): lax.ppermute(given if halves is None else kept, AXES, tensor_pairs(masks))  13.1 us
    all_to_all x1, blocking collectives, per_device(): by_y = lax.all_to_all(by_y, 'y', split_axis=0, concat_axis=0, tiled=True)  12.6 us
    all_to_all x1, blocking collectives, per_device(): by_z = lax.all_to_all(by_z, 'z', split_axis=0, concat_axis=0, tiled=True)  11.3 us
    ppermute x1, waiting for transfers between devices, per_device(): swapped = lax.ppermute(features, ('y', 't'), swap)  11 us
    all_to_all x1, starting transfers between devices, per_device(): lax.all_to_all(turned.reshape(NZ, BLK, turned.shape[1]), 'z', split_axis=...  10.3 us
    ppermute x3, starting transfers between devices, per_device(): lax.ppermute(given if halves is None else kept, AXES, tensor_pairs(masks))  9.5 us
    all_to_all x1, blocking collectives, per_device(): grams = lax.all_to_all(grams, 't', split_axis=0, concat_axis=0, tiled=True)  9.41 us
  transfers between devices with their start and end apart: 6, of which 5 were waited for; matrix products, arithmetic and copies ran while one was open for 0% of the time, Pallas kernels for 0%

profile of v8, /device:TPU:2, one launch (start us, length us, event | category | flops | bytes accessed | tf_op | source)
XLA Modules:
  0.0 127.8 jit_solution(13376393118544199859)
XLA Ops:
  0.6 3.4 %prepare.1 = (bf16[512,128]{1,0:T(8,128)(2,1)}, bf16[8,128,896]{2,1,0:T(8,128)(2,1)}) custom-call(s32[1]{0:T(128)} %bitcast.1.place_ref, s32[64]{0:T(128)} %lengths_ref.1, bf16[128,512]{1,0:T(8,128)(2,1)} %features_in.1, bf16[128,896]{1,0:T(8,128)(2,1)} %gate_in.1, bf16[128,896]{1,0:T(8,128)(2,1)} %up_in.1, bf16[128,896]{1,0:T(8,128)(2,1)} %cotangent_in.1), custom_call_target="tpu_custom_call" | custom-call | flops 1376256 | bytes 917504 | tf_op jit(solution)/shard_map/prepare/pallas_call | solution.py:61
  4.0 10.3 %all-to-all-start = ((bf16[8,64,128]{2,1,0:T(8,128)(2,1)}), bf16[8,64,128]{2,1,0:T(8,128)(2,1)S(1)}, u32[]{:S(2)}, u32[]{:S(2)}) async-start(bf16[8,64,128]{2,1,0:T(8,128)(2,1)} %bitcast.17), calls=%async_computation | async-start | bytes 262144 | tf_op jit(solution)/shard_map/all_to_all | solution.py:249
  14.4 4.5 %collective-permute-start = (bf16[128,512]{1,0:T(8,128)(2,1)}, bf16[128,512]{1,0:T(8,128)(2,1)S(1)}, u32[]{:S(2)}, u32[]{:S(2)}) collective-permute-start(bf16[128,512]{1,0:T(8,128)(2,1)} %features_in.1), channel_id=1, source_target_pairs={{0,0},{1,64},{2,128},{3,192},{4,256},{5,320},{6,384},{7,448},{64,1... | collective-permute-start | bytes 393224 | tf_op jit(solution)/shard_map/ppermute | solution.py:246
  18.8 11.0 %collective-permute-done.value_ref = bf16[128,512]{1,0:T(8,128)(2,1)S(1)} collective-permute-done((bf16[128,512]{1,0:T(8,128)(2,1)}, bf16[128,512]{1,0:T(8,128)(2,1)S(1)}, u32[]{:S(2)}, u32[]{:S(2)}) %collective-permute-start) | collective-permute-done | bytes 131104 | tf_op jit(solution)/shard_map/ppermute | solution.py:246
  29.8 0.0 all-to-all-done
  29.8 5.7 %all-to-all-start.1 = ((bf16[8,128,896]{2,1,0:T(8,128)(2,1)}), bf16[8,128,896]{2,1,0:T(8,128)(2,1)S(1)}, u32[]{:S(2)}, u32[]{:S(2)}) async-start(bf16[8,128,896]{2,1,0:T(8,128)(2,1)} %get-tuple-element.14), calls=%async_computation.1 | async-start | bytes 3670016 | tf_op jit(solution)/shard_map/all_to_all | solution.py:253
  35.5 0.1 turn.1
  35.6 1.9 %collective-permute-start.1 = (bf16[512,128]{1,0:T(8,128)(2,1)S(1)}, bf16[512,128]{1,0:T(8,128)(2,1)S(1)}, u32[]{:S(2)}, u32[]{:S(2)}) collective-permute-start(bf16[512,128]{1,0:T(8,128)(2,1)S(1)} %get-tuple-element.19), channel_id=1, source_target_pairs={{0,1},{1,0},{2,3},{3,2},{4,5},{5,4},{6,7},{7,6},{8,9},{9,8},{10,11... | collective-permute-start | bytes 393224 | tf_op jit(solution)/shard_map/ppermute | solution.py:262
  37.5 1.3 %collective-permute-done.1 = bf16[512,128]{1,0:T(8,128)(2,1)S(1)} collective-permute-done((bf16[512,128]{1,0:T(8,128)(2,1)S(1)}, bf16[512,128]{1,0:T(8,128)(2,1)S(1)}, u32[]{:S(2)}, u32[]{:S(2)}) %collective-permute-start.1) | collective-permute-done | bytes 131104 | tf_op jit(solution)/shard_map/ppermute | solution.py:262
  38.9 3.8 %collective-permute-start.2 = (bf16[1024,128]{1,0:T(8,128)(2,1)S(1)}, bf16[1024,128]{1,0:T(8,128)(2,1)S(1)}, u32[]{:S(2)}, u32[]{:S(2)}) collective-permute-start(bf16[1024,128]{1,0:T(8,128)(2,1)S(1)} %pad_maximum_fusion.1), channel_id=1, source_target_pairs={{0,2},{1,7},{2,0},{3,5},{4,6},{5,3},{6,4},{7,1},{8,10},{9,15},{10,... | collective-permute-start | bytes 786440 | tf_op jit(solution)/shard_map/ppermute | solution.py:262
  42.7 4.5 %collective-permute-done.2 = bf16[1024,128]{1,0:T(8,128)(2,1)S(1)} collective-permute-done((bf16[1024,128]{1,0:T(8,128)(2,1)S(1)}, bf16[1024,128]{1,0:T(8,128)(2,1)S(1)}, u32[]{:S(2)}, u32[]{:S(2)}) %collective-permute-start.2) | collective-permute-done | bytes 262176 | tf_op jit(solution)/shard_map/ppermute | solution.py:262
  47.2 3.8 %collective-permute-start.3 = (bf16[2048,128]{1,0:T(8,128)(2,1)S(1)}, bf16[2048,128]{1,0:T(8,128)(2,1)S(1)}, u32[]{:S(2)}, u32[]{:S(2)}) collective-permute-start(bf16[2048,128]{1,0:T(8,128)(2,1)S(1)} %pad_maximum_fusion.first_ref), channel_id=1, source_target_pairs={{0,6},{1,3},{2,4},{3,1},{4,2},{5,7},{6,0},{7,5},{8,14},{9,11},{10,... | collective-permute-start | bytes 1572872 | tf_op jit(solution)/shard_map/ppermute | solution.py:262
  51.0 7.3 %collective-permute-done.3.second_ref = bf16[2048,128]{1,0:T(8,128)(2,1)S(1)} collective-permute-done((bf16[2048,128]{1,0:T(8,128)(2,1)S(1)}, bf16[2048,128]{1,0:T(8,128)(2,1)S(1)}, u32[]{:S(2)}, u32[]{:S(2)}) %collective-permute-start.3) | collective-permute-done | bytes 524320 | tf_op jit(solution)/shard_map/ppermute | solution.py:262
  58.2 4.7 %all-to-all-done.1 = bf16[8,128,896]{2,1,0:T(8,128)(2,1)S(1)} async-done(((bf16[8,128,896]{2,1,0:T(8,128)(2,1)}), bf16[8,128,896]{2,1,0:T(8,128)(2,1)S(1)}, u32[]{:S(2)}, u32[]{:S(2)}) %all-to-all-start.1) | async-done | bytes 1835040 | tf_op jit(solution)/shard_map/all_to_all | solution.py:253
  62.9 1.6 %partial_product.1 = bf16[512,896]{1,0:T(8,128)(2,1)S(1)} custom-call(s32[1]{0:T(128)} %bitcast.t_ref, bf16[2048,128]{1,0:T(8,128)(2,1)S(1)} %pad_maximum_fusion.first_ref, bf16[2048,128]{1,0:T(8,128)(2,1)S(1)} %collective-permute-done.3.second_ref, bf16[1024,896]{1,0:T(8,128)(2,1)S(1)} %bitcast.12), custom_call_target="tpu_custom_call" | custom-call | flops 939524096 | bytes 6000000 | tf_op jit(solution)/shard_map/partial_product/pallas_call | solution.py:153
  64.5 0.0 copy-start
  64.5 24.5 %all_to_all.30.parts_ref = bf16[8,64,896]{2,1,0:T(8,128)(2,1)S(1)} all-to-all(bf16[8,64,896]{2,1,0:T(8,128)(2,1)S(1)} %bitcast.13), channel_id=1, replica_groups={{0,8,16,24,32,40,48,56},{64,72,80,88,96,104,112,120},{128,136,144,152,1..., dimensions={0} | all-to-all | bytes 1835008 | tf_op jit(solution)/shard_map/all_to_all | solution.py:269
  89.0 0.0 copy-done
  89.0 0.9 momentum_step.1
  89.9 9.4 %all_to_all.31.grams_ref = f32[8,32,128]{2,1,0:T(8,128)S(1)} all-to-all(f32[8,32,128]{2,1,0:T(8,128)S(1)} %get-tuple-element.15), channel_id=1, replica_groups=mesh['y'=8,'z'=8,'t'=8] {'t'}, dimensions={0} | all-to-all | bytes 262144 | tf_op jit(solution)/shard_map/all_to_all | solution.py:273
  99.3 3.0 %polar_update.1 = bf16[8,64,112]{2,1,0:T(8,128)(2,1)S(1)} custom-call(f32[8,32,128]{2,1,0:T(8,128)S(1)} %all_to_all.31.grams_ref, f32[64,896]{1,0:T(8,128)S(1)} %get-tuple-element.16.block_ref), custom_call_target="tpu_custom_call" | custom-call | flops 100000000 | bytes 600000 | tf_op jit(solution)/shard_map/polar_update/pallas_call | solution.py:232
  102.4 12.6 %all_to_all.32 = bf16[8,64,112]{2,1,0:T(8,128)(2,1)S(1)} all-to-all(bf16[8,64,112]{2,1,0:T(8,128)(2,1)S(1)} %polar_update.1), channel_id=1, replica_groups=mesh['y'=8,'z'=8,'t'=8] {'y'}, dimensions={0} | all-to-all | bytes 229376 | tf_op jit(solution)/shard_map/all_to_all | solution.py:275
  115.0 0.2 copy.10
  115.2 0.2 reshape.36
  115.4 11.3 %all_to_all.33 = bf16[8,2,3584]{2,1,0:T(2,128)(2,1)S(1)} all-to-all(bf16[8,2,3584]{2,1,0:T(2,128)(2,1)S(1)} %reshape.36), channel_id=1, replica_groups=mesh['y'=8,'z'=8,'t'=8] {'z'}, dimensions={0} | all-to-all | bytes 229376 | tf_op jit(solution)/shard_map/all_to_all | solution.py:278
  126.6 0.2 reshape.37
  126.8 0.1 copy.11
  126.9 0.9 reshape.35
  (3 shorter events, 0.1 us)
Async XLA Ops:
  4.0 25.8 %all-to-all-start = ((bf16[8,64,128]{2,1,0:T(8,128)(2,1)}), bf16[8,64,128]{2,1,0:T(8,128)(2,1)S(1)}, u32[]{:S(2)}, u32[]{:S(2)}) async-start(bf16[8,64,128]{2,1,0:T(8,128)(2,1)} %bitcast.17), calls=%async_computation | async-start | bytes 262144 | tf_op jit(solution)/shard_map/all_to_all | solution.py:249
  14.4 15.4 %collective-permute-start = (bf16[128,512]{1,0:T(8,128)(2,1)}, bf16[128,512]{1,0:T(8,128)(2,1)S(1)}, u32[]{:S(2)}, u32[]{:S(2)}) collective-permute-start(bf16[128,512]{1,0:T(8,128)(2,1)} %features_in.1), channel_id=1, source_target_pairs={{0,0},{1,64},{2,128},{3,192},{4,256},{5,320},{6,384},{7,448},{64,1... | collective-permute-start | bytes 393224 | tf_op jit(solution)/shard_map/ppermute | solution.py:246
  29.8 33.1 %all-to-all-start.1 = ((bf16[8,128,896]{2,1,0:T(8,128)(2,1)}), bf16[8,128,896]{2,1,0:T(8,128)(2,1)S(1)}, u32[]{:S(2)}, u32[]{:S(2)}) async-start(bf16[8,128,896]{2,1,0:T(8,128)(2,1)} %get-tuple-element.14), calls=%async_computation.1 | async-start | bytes 3670016 | tf_op jit(solution)/shard_map/all_to_all | solution.py:253
  35.6 3.2 %collective-permute-start.1 = (bf16[512,128]{1,0:T(8,128)(2,1)S(1)}, bf16[512,128]{1,0:T(8,128)(2,1)S(1)}, u32[]{:S(2)}, u32[]{:S(2)}) collective-permute-start(bf16[512,128]{1,0:T(8,128)(2,1)S(1)} %get-tuple-element.19), channel_id=1, source_target_pairs={{0,1},{1,0},{2,3},{3,2},{4,5},{5,4},{6,7},{7,6},{8,9},{9,8},{10,11... | collective-permute-start | bytes 393224 | tf_op jit(solution)/shard_map/ppermute | solution.py:262
  38.9 8.3 %collective-permute-start.2 = (bf16[1024,128]{1,0:T(8,128)(2,1)S(1)}, bf16[1024,128]{1,0:T(8,128)(2,1)S(1)}, u32[]{:S(2)}, u32[]{:S(2)}) collective-permute-start(bf16[1024,128]{1,0:T(8,128)(2,1)S(1)} %pad_maximum_fusion.1), channel_id=1, source_target_pairs={{0,2},{1,7},{2,0},{3,5},{4,6},{5,3},{6,4},{7,1},{8,10},{9,15},{10,... | collective-permute-start | bytes 786440 | tf_op jit(solution)/shard_map/ppermute | solution.py:262
  47.2 11.1 %collective-permute-start.3 = (bf16[2048,128]{1,0:T(8,128)(2,1)S(1)}, bf16[2048,128]{1,0:T(8,128)(2,1)S(1)}, u32[]{:S(2)}, u32[]{:S(2)}) collective-permute-start(bf16[2048,128]{1,0:T(8,128)(2,1)S(1)} %pad_maximum_fusion.first_ref), channel_id=1, source_target_pairs={{0,6},{1,3},{2,4},{3,1},{4,2},{5,7},{6,0},{7,5},{8,14},{9,11},{10,... | collective-permute-start | bytes 1572872 | tf_op jit(solution)/shard_map/ppermute | solution.py:262
  64.5 24.6 %copy-start = (f32[64,896]{1,0:T(8,128)S(1)}, f32[64,896]{1,0:T(8,128)}, u32[]{:S(2)}) copy-start(f32[64,896]{1,0:T(8,128)} %momentum_ref.1) | copy-start | bytes 688132

commit v9 on v8

--- a/solution.py
+++ b/solution.py
@@ -28,20 +28,18 @@
 AXES = ("y", "z", "t")
 
 
-def prepare_kernel(place_ref, lengths_ref, features_in, gate_in, up_in, cotangent_in, turned_ref, copies_ref, *scratch):
-    buffers, arrived = scratch[:4], scratch[4]
-    sources = (features_in, gate_in, up_in, cotangent_in)
+def gate_kernel(place_ref, lengths_ref, gate_in, up_in, cotangent_in, copies_ref, *scratch):
+    buffers, arrived = scratch[:3], scratch[3]
+    sources = (gate_in, up_in, cotangent_in)
     copies = [
         pltpu.make_async_copy(source, buffer, arrived.at[i])
         for i, (source, buffer) in enumerate(zip(sources, buffers))
     ]
     for copy in copies:
         copy.start()
-    copies[0].wait()
-    turned_ref[...] = buffers[0][...].T
-    for copy in copies[1:]:
+    for copy in copies:
         copy.wait()
-    gate_value, up_value, cotangent = (buffer[...].astype(jnp.float32) for buffer in buffers[1:])
+    gate_value, up_value, cotangent = (buffer[...].astype(jnp.float32) for buffer in buffers)
     sigmoid_gate = jax.nn.sigmoid(gate_value)
     gate_grad = cotangent * up_value * sigmoid_gate * (1.0 + gate_value * (1.0 - sigmoid_gate))
     position = lax.broadcasted_iota(jnp.int32, gate_value.shape, 0)
@@ -51,29 +49,46 @@
         copies_ref[part] = gate_grad
 
 
-def prepare(place, lengths, features, gate_pre, up_pre, hidden_grad):
+def gate_cotangent(place, lengths, gate_pre, up_pre, hidden_grad):
     tokens, columns = gate_pre.shape
-    rows = features.shape[1]
     hbm = pl.BlockSpec(memory_space=pltpu.HBM)
     vmem = pl.BlockSpec(memory_space=pltpu.VMEM)
     smem = pl.BlockSpec(memory_space=pltpu.SMEM)
-    arrays = (features, gate_pre, up_pre, hidden_grad)
-    return pl.pallas_call(
-        prepare_kernel,
-        out_shape=(
-            jax.ShapeDtypeStruct((rows, tokens), jnp.bfloat16),
-            jax.ShapeDtypeStruct((NZ, tokens, columns), jnp.bfloat16),
-        ),
-        in_specs=[smem, smem] + [hbm] * 4,
-        out_specs=(vmem, vmem),
+    arrays = (gate_pre, up_pre, hidden_grad)
+    return pl.pallas_call(
+        gate_kernel,
+        out_shape=jax.ShapeDtypeStruct((NZ, tokens, columns), jnp.bfloat16),
+        in_specs=[smem, smem] + [hbm] * 3,
+        out_specs=vmem,
         scratch_shapes=[pltpu.VMEM(array.shape, array.dtype) for array in arrays]
-        + [pltpu.SemaphoreType.DMA((4,))],
+        + [pltpu.SemaphoreType.DMA((3,))],
         compiler_params=pltpu.CompilerParams(vmem_limit_bytes=60 * 1024 * 1024),
         cost_estimate=pl.CostEstimate(
-            flops=12 * tokens * columns, bytes_accessed=8 * tokens * columns, transcendentals=tokens * columns
+            flops=64 * tokens * columns, bytes_accessed=400 * tokens * columns, transcendentals=tokens * columns
         ),
-        name="prepare",
+        name="gate_cotangent",
     )(jnp.reshape(place, (1,)), lengths, *arrays)
+
+
+def turn_first_kernel(value_in, turned_ref, buffer, arrived):
+    copy = pltpu.make_async_copy(value_in, buffer, arrived)
+    copy.start()
+    copy.wait()
+    turned_ref[...] = buffer[...].T
+
+
+def turn_first(value):
+    rows, columns = value.shape
+    return pl.pallas_call(
+        turn_first_kernel,
+        out_shape=jax.ShapeDtypeStruct((columns, rows), value.dtype),
+        in_specs=[pl.BlockSpec(memory_space=pltpu.HBM)],
+        out_specs=pl.BlockSpec(memory_space=pltpu.VMEM),
+        scratch_shapes=[pltpu.VMEM(value.shape, value.dtype), pltpu.SemaphoreType.DMA],
+        compiler_params=pltpu.CompilerParams(vmem_limit_bytes=60 * 1024 * 1024),
+        cost_estimate=pl.CostEstimate(flops=rows * columns, bytes_accessed=4 * rows * columns, transcendentals=0),
+        name="turn_first",
+    )(value)
 
 
 def turn_kernel(value_ref, turned_ref):
@@ -244,7 +259,8 @@
     y, z, t = (lax.axis_index(name) for name in AXES)
     swap = [(a * NT + b, b * NT + a) for a in range(NY) for b in range(NT)]
     swapped = lax.ppermute(features, ("y", "t"), swap)
-    turned, copies = prepare(y * NZ + z, lengths, features, gate_pre, up_pre, hidden_grad)
+    turned = turn_first(features)
+    copies = gate_cotangent(y * NZ + z, lengths, gate_pre, up_pre, hidden_grad)
 
     by_blocks = lax.all_to_all(
         turned.reshape(NZ, BLK, turned.shape[1]), "z", split_axis=0, concat_axis=0, tiled=True

time: 128 us -> 127 us (level)
  waiting for transfers between devices: 28.7 us -> 25.4 us
  Pallas kernels: 8.92 us -> 10.5 us
    ppermute x1, waiting for transfers between devices: 11 us -> 7.63 us  [per_device(): swapped = lax.ppermute(features, ('y', 't'), swap)]
    pallas_call x1 -> x2, Pallas kernels: 3.38 us -> 4.96 us  [the longest x1 3.31 us: gate_cotangent(): pl.pallas_call(gate_kernel, out_shape=jax.ShapeDtypeStruct((NZ, tokens, c...]
  transfers between devices with their start and end apart: 6 -> 6, of which waited for: 5 -> 5; matrix products, arithmetic and copies ran while one was open for 0% -> 0% of each run, Pallas kernels for 0% -> 3%
where the time goes in v9:
time: 127 us; the launch traced here: 126 us
  blocking collectives  57.9 us (46%)
  starting transfers between devices  30 us (24%)
  waiting for transfers between devices  25.4 us (20%)
  Pallas kernels  10.5 us (8%)
  local copies, waits for them, and re-layouts  1.5 us (1%)
    all_to_all x1, blocking collectives, per_device(): lax.all_to_all(pieces, AXES, split_axis=0, concat_axis=0, axis_index_grou...  24.6 us
    ppermute x3, waiting for transfers between devices, per_device(): lax.ppermute(given if halves is None else kept, AXES, tensor_pairs(masks))  13.1 us
    all_to_all x1, blocking collectives, per_device(): by_y = lax.all_to_all(by_y, 'y', split_axis=0, concat_axis=0, tiled=True)  12.6 us
    all_to_all x1, blocking collectives, per_device(): by_z = lax.all_to_all(by_z, 'z', split_axis=0, concat_axis=0, tiled=True)  11.3 us
    all_to_all x1, starting transfers between devices, per_device(): lax.all_to_all(turned.reshape(NZ, BLK, turned.shape[1]), 'z', split_axis=...  10.3 us
    ppermute x3, starting transfers between devices, per_device(): lax.ppermute(given if halves is None else kept, AXES, tensor_pairs(masks))  9.5 us
    all_to_all x1, blocking collectives, per_device(): grams = lax.all_to_all(grams, 't', split_axis=0, concat_axis=0, tiled=True)  9.4 us
    ppermute x1, waiting for transfers between devices, per_device(): swapped = lax.ppermute(features, ('y', 't'), swap)  7.63 us
  transfers between devices with their start and end apart: 6, of which 5 were waited for; matrix products, arithmetic and copies ran while one was open for 0% of the time, Pallas kernels for 3%

profile of v9, /device:TPU:2, one launch (start us, length us, event | category | flops | bytes accessed | tf_op | source)
XLA Modules:
  0.0 126.1 jit_solution(6188119426596907662)
XLA Ops:
  0.6 1.7 %turn_first.1 = bf16[512,128]{1,0:T(8,128)(2,1)} custom-call(bf16[128,512]{1,0:T(8,128)(2,1)} %value_in.1), custom_call_target="tpu_custom_call" | custom-call | flops 65536 | bytes 262144 | tf_op jit(solution)/shard_map/turn_first/pallas_call | solution.py:82
  2.3 10.3 %all-to-all-start = ((bf16[8,64,128]{2,1,0:T(8,128)(2,1)}), bf16[8,64,128]{2,1,0:T(8,128)(2,1)S(1)}, u32[]{:S(2)}, u32[]{:S(2)}) async-start(bf16[8,64,128]{2,1,0:T(8,128)(2,1)} %bitcast.17), calls=%async_computation | async-start | bytes 262144 | tf_op jit(solution)/shard_map/all_to_all | solution.py:265
  12.6 4.5 %collective-permute-start = (bf16[128,512]{1,0:T(8,128)(2,1)}, bf16[128,512]{1,0:T(8,128)(2,1)S(1)}, u32[]{:S(2)}, u32[]{:S(2)}) collective-permute-start(bf16[128,512]{1,0:T(8,128)(2,1)} %value_in.1), channel_id=1, source_target_pairs={{0,0},{1,64},{2,128},{3,192},{4,256},{5,320},{6,384},{7,448},{64,1... | collective-permute-start | bytes 393224 | tf_op jit(solution)/shard_map/ppermute | solution.py:261
  17.1 3.3 %gate_cotangent.1 = bf16[8,128,896]{2,1,0:T(8,128)(2,1)} custom-call(s32[1]{0:T(128)} %bitcast.1.place_ref, s32[64]{0:T(128)} %lengths_ref.1, bf16[128,896]{1,0:T(8,128)(2,1)} %gate_in.1, bf16[128,896]{1,0:T(8,128)(2,1)} %up_in.1, bf16[128,896]{1,0:T(8,128)(2,1)} %cotangent_in.1), custom_call_target="tpu_custom_call" | custom-call | flops 7340032 | bytes 45875200 | tf_op jit(solution)/shard_map/gate_cotangent/pallas_call | solution.py:58
  20.4 7.6 %collective-permute-done.value_ref = bf16[128,512]{1,0:T(8,128)(2,1)S(1)} collective-permute-done((bf16[128,512]{1,0:T(8,128)(2,1)}, bf16[128,512]{1,0:T(8,128)(2,1)S(1)}, u32[]{:S(2)}, u32[]{:S(2)}) %collective-permute-start) | collective-permute-done | bytes 131104 | tf_op jit(solution)/shard_map/ppermute | solution.py:261
  28.0 0.0 all-to-all-done
  28.0 5.7 %all-to-all-start.1 = ((bf16[8,128,896]{2,1,0:T(8,128)(2,1)}), bf16[8,128,896]{2,1,0:T(8,128)(2,1)S(1)}, u32[]{:S(2)}, u32[]{:S(2)}) async-start(bf16[8,128,896]{2,1,0:T(8,128)(2,1)} %gate_cotangent.1), calls=%async_computation.1 | async-start | bytes 3670016 | tf_op jit(solution)/shard_map/all_to_all | solution.py:269
  33.7 0.1 turn.1
  33.9 1.9 %collective-permute-start.1 = (bf16[512,128]{1,0:T(8,128)(2,1)S(1)}, bf16[512,128]{1,0:T(8,128)(2,1)S(1)}, u32[]{:S(2)}, u32[]{:S(2)}) collective-permute-start(bf16[512,128]{1,0:T(8,128)(2,1)S(1)} %get-tuple-element.15), channel_id=1, source_target_pairs={{0,1},{1,0},{2,3},{3,2},{4,5},{5,4},{6,7},{7,6},{8,9},{9,8},{10,11... | collective-permute-start | bytes 393224 | tf_op jit(solution)/shard_map/ppermute | solution.py:278
  35.8 1.3 %collective-permute-done.1 = bf16[512,128]{1,0:T(8,128)(2,1)S(1)} collective-permute-done((bf16[512,128]{1,0:T(8,128)(2,1)S(1)}, bf16[512,128]{1,0:T(8,128)(2,1)S(1)}, u32[]{:S(2)}, u32[]{:S(2)}) %collective-permute-start.1) | collective-permute-done | bytes 131104 | tf_op jit(solution)/shard_map/ppermute | solution.py:278
  37.1 3.8 %collective-permute-start.2 = (bf16[1024,128]{1,0:T(8,128)(2,1)S(1)}, bf16[1024,128]{1,0:T(8,128)(2,1)S(1)}, u32[]{:S(2)}, u32[]{:S(2)}) collective-permute-start(bf16[1024,128]{1,0:T(8,128)(2,1)S(1)} %pad_maximum_fusion.1), channel_id=1, source_target_pairs={{0,2},{1,7},{2,0},{3,5},{4,6},{5,3},{6,4},{7,1},{8,10},{9,15},{10,... | collective-permute-start | bytes 786440 | tf_op jit(solution)/shard_map/ppermute | solution.py:278
  40.9 4.5 %collective-permute-done.2 = bf16[1024,128]{1,0:T(8,128)(2,1)S(1)} collective-permute-done((bf16[1024,128]{1,0:T(8,128)(2,1)S(1)}, bf16[1024,128]{1,0:T(8,128)(2,1)S(1)}, u32[]{:S(2)}, u32[]{:S(2)}) %collective-permute-start.2) | collective-permute-done | bytes 262176 | tf_op jit(solution)/shard_map/ppermute | solution.py:278
  45.4 3.8 %collective-permute-start.3 = (bf16[2048,128]{1,0:T(8,128)(2,1)S(1)}, bf16[2048,128]{1,0:T(8,128)(2,1)S(1)}, u32[]{:S(2)}, u32[]{:S(2)}) collective-permute-start(bf16[2048,128]{1,0:T(8,128)(2,1)S(1)} %pad_maximum_fusion.first_ref), channel_id=1, source_target_pairs={{0,6},{1,3},{2,4},{3,1},{4,2},{5,7},{6,0},{7,5},{8,14},{9,11},{10,... | collective-permute-start | bytes 1572872 | tf_op jit(solution)/shard_map/ppermute | solution.py:278
  49.2 7.3 %collective-permute-done.3.second_ref = bf16[2048,128]{1,0:T(8,128)(2,1)S(1)} collective-permute-done((bf16[2048,128]{1,0:T(8,128)(2,1)S(1)}, bf16[2048,128]{1,0:T(8,128)(2,1)S(1)}, u32[]{:S(2)}, u32[]{:S(2)}) %collective-permute-start.3) | collective-permute-done | bytes 524320 | tf_op jit(solution)/shard_map/ppermute | solution.py:278
  56.5 4.7 %all-to-all-done.1 = bf16[8,128,896]{2,1,0:T(8,128)(2,1)S(1)} async-done(((bf16[8,128,896]{2,1,0:T(8,128)(2,1)}), bf16[8,128,896]{2,1,0:T(8,128)(2,1)S(1)}, u32[]{:S(2)}, u32[]{:S(2)}) %all-to-all-start.1) | async-done | bytes 1835040 | tf_op jit(solution)/shard_map/all_to_all | solution.py:269
  61.2 1.6 %partial_product.1 = bf16[512,896]{1,0:T(8,128)(2,1)S(1)} custom-call(s32[1]{0:T(128)} %bitcast.t_ref, bf16[2048,128]{1,0:T(8,128)(2,1)S(1)} %pad_maximum_fusion.first_ref, bf16[2048,128]{1,0:T(8,128)(2,1)S(1)} %collective-permute-done.3.second_ref, bf16[1024,896]{1,0:T(8,128)(2,1)S(1)} %bitcast.12), custom_call_target="tpu_custom_call" | custom-call | flops 939524096 | bytes 6000000 | tf_op jit(solution)/shard_map/partial_product/pallas_call | solution.py:168
  62.7 0.0 copy-start
  62.8 24.6 %all_to_all.30.parts_ref = bf16[8,64,896]{2,1,0:T(8,128)(2,1)S(1)} all-to-all(bf16[8,64,896]{2,1,0:T(8,128)(2,1)S(1)} %bitcast.13), channel_id=1, replica_groups={{0,8,16,24,32,40,48,56},{64,72,80,88,96,104,112,120},{128,136,144,152,1..., dimensions={0} | all-to-all | bytes 1835008 | tf_op jit(solution)/shard_map/all_to_all | solution.py:285
  87.3 0.0 copy-done
  87.3 0.9 momentum_step.1
  88.2 9.4 %all_to_all.31.grams_ref = f32[8,32,128]{2,1,0:T(8,128)S(1)} all-to-all(f32[8,32,128]{2,1,0:T(8,128)S(1)} %get-tuple-element.11), channel_id=1, replica_groups=mesh['y'=8,'z'=8,'t'=8] {'t'}, dimensions={0} | all-to-all | bytes 262144 | tf_op jit(solution)/shard_map/all_to_all | solution.py:289
  97.6 3.0 %polar_update.1 = bf16[8,64,112]{2,1,0:T(8,128)(2,1)S(1)} custom-call(f32[8,32,128]{2,1,0:T(8,128)S(1)} %all_to_all.31.grams_ref, f32[64,896]{1,0:T(8,128)S(1)} %get-tuple-element.12.block_ref), custom_call_target="tpu_custom_call" | custom-call | flops 100000000 | bytes 600000 | tf_op jit(solution)/shard_map/polar_update/pallas_call | solution.py:247
  100.6 12.6 %all_to_all.32 = bf16[8,64,112]{2,1,0:T(8,128)(2,1)S(1)} all-to-all(bf16[8,64,112]{2,1,0:T(8,128)(2,1)S(1)} %polar_update.1), channel_id=1, replica_groups=mesh['y'=8,'z'=8,'t'=8] {'y'}, dimensions={0} | all-to-all | bytes 229376 | tf_op jit(solution)/shard_map/all_to_all | solution.py:291
  113.3 0.2 copy.10
  113.4 0.2 reshape.36
  113.6 11.3 %all_to_all.33 = bf16[8,2,3584]{2,1,0:T(2,128)(2,1)S(1)} all-to-all(bf16[8,2,3584]{2,1,0:T(2,128)(2,1)S(1)} %reshape.36), channel_id=1, replica_groups=mesh['y'=8,'z'=8,'t'=8] {'z'}, dimensions={0} | all-to-all | bytes 229376 | tf_op jit(solution)/shard_map/all_to_all | solution.py:294
  124.9 0.2 reshape.37
  125.1 0.1 copy.11
  125.2 0.9 reshape.35
  (3 shorter events, 0.1 us)
Async XLA Ops:
  2.3 25.8 %all-to-all-start = ((bf16[8,64,128]{2,1,0:T(8,128)(2,1)}), bf16[8,64,128]{2,1,0:T(8,128)(2,1)S(1)}, u32[]{:S(2)}, u32[]{:S(2)}) async-start(bf16[8,64,128]{2,1,0:T(8,128)(2,1)} %bitcast.17), calls=%async_computation | async-start | bytes 262144 | tf_op jit(solution)/shard_map/all_to_all | solution.py:265
  12.6 15.4 %collective-permute-start = (bf16[128,512]{1,0:T(8,128)(2,1)}, bf16[128,512]{1,0:T(8,128)(2,1)S(1)}, u32[]{:S(2)}, u32[]{:S(2)}) collective-permute-start(bf16[128,512]{1,0:T(8,128)(2,1)} %value_in.1), channel_id=1, source_target_pairs={{0,0},{1,64},{2,128},{3,192},{4,256},{5,320},{6,384},{7,448},{64,1... | collective-permute-start | bytes 393224 | tf_op jit(solution)/shard_map/ppermute | solution.py:261
  28.0 33.1 %all-to-all-start.1 = ((bf16[8,128,896]{2,1,0:T(8,128)(2,1)}), bf16[8,128,896]{2,1,0:T(8,128)(2,1)S(1)}, u32[]{:S(2)}, u32[]{:S(2)}) async-start(bf16[8,128,896]{2,1,0:T(8,128)(2,1)} %gate_cotangent.1), calls=%async_computation.1 | async-start | bytes 3670016 | tf_op jit(solution)/shard_map/all_to_all | solution.py:269
  33.9 3.2 %collective-permute-start.1 = (bf16[512,128]{1,0:T(8,128)(2,1)S(1)}, bf16[512,128]{1,0:T(8,128)(2,1)S(1)}, u32[]{:S(2)}, u32[]{:S(2)}) collective-permute-start(bf16[512,128]{1,0:T(8,128)(2,1)S(1)} %get-tuple-element.15), channel_id=1, source_target_pairs={{0,1},{1,0},{2,3},{3,2},{4,5},{5,4},{6,7},{7,6},{8,9},{9,8},{10,11... | collective-permute-start | bytes 393224 | tf_op jit(solution)/shard_map/ppermute | solution.py:278
  37.1 8.3 %collective-permute-start.2 = (bf16[1024,128]{1,0:T(8,128)(2,1)S(1)}, bf16[1024,128]{1,0:T(8,128)(2,1)S(1)}, u32[]{:S(2)}, u32[]{:S(2)}) collective-permute-start(bf16[1024,128]{1,0:T(8,128)(2,1)S(1)} %pad_maximum_fusion.1), channel_id=1, source_target_pairs={{0,2},{1,7},{2,0},{3,5},{4,6},{5,3},{6,4},{7,1},{8,10},{9,15},{10,... | collective-permute-start | bytes 786440 | tf_op jit(solution)/shard_map/ppermute | solution.py:278
  45.4 11.1 %collective-permute-start.3 = (bf16[2048,128]{1,0:T(8,128)(2,1)S(1)}, bf16[2048,128]{1,0:T(8,128)(2,1)S(1)}, u32[]{:S(2)}, u32[]{:S(2)}) collective-permute-start(bf16[2048,128]{1,0:T(8,128)(2,1)S(1)} %pad_maximum_fusion.first_ref), channel_id=1, source_target_pairs={{0,6},{1,3},{2,4},{3,1},{4,2},{5,7},{6,0},{7,5},{8,14},{9,11},{10,... | collective-permute-start | bytes 1572872 | tf_op jit(solution)/shard_map/ppermute | solution.py:278
  62.7 24.6 %copy-start = (f32[64,896]{1,0:T(8,128)S(1)}, f32[64,896]{1,0:T(8,128)}, u32[]{:S(2)}) copy-start(f32[64,896]{1,0:T(8,128)} %momentum_ref.1) | copy-start | bytes 688132

commit v10 on v9

--- a/solution.py
+++ b/solution.py
@@ -104,7 +104,7 @@
         in_specs=[vmem],
         out_specs=vmem,
         compiler_params=pltpu.CompilerParams(vmem_limit_bytes=8 * 1024 * 1024),
-        cost_estimate=pl.CostEstimate(flops=rows * columns, bytes_accessed=4 * rows * columns, transcendentals=0),
+        cost_estimate=pl.CostEstimate(flops=rows * columns, bytes_accessed=3000 * rows * columns, transcendentals=0),
         name="turn",
     )(value)
 
@@ -265,7 +265,7 @@
     by_blocks = lax.all_to_all(
         turned.reshape(NZ, BLK, turned.shape[1]), "z", split_axis=0, concat_axis=0, tiled=True
     ).reshape(turned.shape)
-    copies, swapped, by_blocks = lax.optimization_barrier((copies, swapped, by_blocks))
+    copies, by_blocks = lax.optimization_barrier((copies, by_blocks))
     grads = lax.all_to_all(
         copies, AXES, split_axis=0, concat_axis=0, axis_index_groups=line_groups("y"), tiled=True
     ).reshape(-1, copies.shape[2])

time: 127 us -> 147 us (1.16)
  waiting for transfers between devices: 25.4 us -> 48.4 us
  blocking collectives: 57.9 us -> 56.2 us
    ppermute x1, waiting for transfers between devices: 7.63 us -> 26.6 us  [per_device(): swapped = lax.ppermute(features, ('y', 't'), swap)]
    all_to_all x1, waiting for transfers between devices: 0.01 us -> 5.79 us  [per_device(): lax.all_to_all(turned.reshape(NZ, BLK, turned.shape[1]), 'z', split_axis=...]
    all_to_all x1, waiting for transfers between devices: 4.66 us -> 0.01 us  [per_device(): lax.all_to_all(copies, AXES, split_axis=0, concat_axis=0, axis_index_grou...]
    all_to_all x1, blocking collectives: 24.6 us -> 20.7 us  [per_device(): lax.all_to_all(pieces, AXES, split_axis=0, concat_axis=0, axis_index_grou...]
    ppermute x3, starting transfers between devices: 9.5 us -> 6.5 us  [per_device(): lax.ppermute(given if halves is None else kept, AXES, tensor_pairs(masks))]
    ppermute x3, waiting for transfers between devices: 13.1 us -> 16.1 us  [per_device(): lax.ppermute(given if halves is None else kept, AXES, tensor_pairs(masks))]
    all_to_all x1, blocking collectives: 12.6 us -> 14.3 us  [per_device(): by_y = lax.all_to_all(by_y, 'y', split_axis=0, concat_axis=0, tiled=True)]
    all_to_all x1, starting transfers between devices: 5.7 us -> 7.23 us  [per_device(): lax.all_to_all(copies, AXES, split_axis=0, concat_axis=0, axis_index_grou...]
  transfers between devices with their start and end apart: 6 -> 6, of which waited for: 5 -> 5; matrix products, arithmetic and copies ran while one was open for 0% -> 0% of each run, Pallas kernels for 3% -> 2%
where the time goes in v10:
time: 147 us; the launch traced here: 146 us
  blocking collectives  56.2 us (38%)
  waiting for transfers between devices  48.4 us (33%)
  starting transfers between devices  28.8 us (20%)
  Pallas kernels  10.5 us (7%)
  local copies, waits for them, and re-layouts  1.5 us (1%)
    ppermute x1, waiting for transfers between devices, per_device(): swapped = lax.ppermute(features, ('y', 't'), swap)  26.6 us
    all_to_all x1, blocking collectives, per_device(): lax.all_to_all(pieces, AXES, split_axis=0, concat_axis=0, axis_index_grou...  20.7 us
    ppermute x3, waiting for transfers between devices, per_device(): lax.ppermute(given if halves is None else kept, AXES, tensor_pairs(masks))  16.1 us
    all_to_all x1, blocking collectives, per_device(): by_y = lax.all_to_all(by_y, 'y', split_axis=0, concat_axis=0, tiled=True)  14.3 us
    all_to_all x1, blocking collectives, per_device(): by_z = lax.all_to_all(by_z, 'z', split_axis=0, concat_axis=0, tiled=True)  11.3 us
    all_to_all x1, starting transfers between devices, per_device(): lax.all_to_all(turned.reshape(NZ, BLK, turned.shape[1]), 'z', split_axis=...  10.3 us
    all_to_all x1, blocking collectives, per_device(): grams = lax.all_to_all(grams, 't', split_axis=0, concat_axis=0, tiled=True)  9.91 us
    all_to_all x1, starting transfers between devices, per_device(): lax.all_to_all(copies, AXES, split_axis=0, concat_axis=0, axis_index_grou...  7.23 us
  transfers between devices with their start and end apart: 6, of which 5 were waited for; matrix products, arithmetic and copies ran while one was open for 0% of the time, Pallas kernels for 2%

profile of v10, /device:TPU:2, one launch (start us, length us, event | category | flops | bytes accessed | tf_op | source)
XLA Modules:
  0.0 146.3 jit_solution(9862400377966077202)
XLA Ops:
  0.6 1.7 %turn_first.1 = bf16[512,128]{1,0:T(8,128)(2,1)} custom-call(bf16[128,512]{1,0:T(8,128)(2,1)} %value_in.1), custom_call_target="tpu_custom_call" | custom-call | flops 65536 | bytes 262144 | tf_op jit(solution)/shard_map/turn_first/pallas_call | solution.py:82
  2.3 10.3 %all-to-all-start = ((bf16[8,64,128]{2,1,0:T(8,128)(2,1)}), bf16[8,64,128]{2,1,0:T(8,128)(2,1)S(1)}, u32[]{:S(2)}, u32[]{:S(2)}) async-start(bf16[8,64,128]{2,1,0:T(8,128)(2,1)} %bitcast.17), calls=%async_computation | async-start | bytes 262144 | tf_op jit(solution)/shard_map/all_to_all | solution.py:265
  12.6 3.3 %gate_cotangent.1 = bf16[8,128,896]{2,1,0:T(8,128)(2,1)} custom-call(s32[1]{0:T(128)} %bitcast.1.place_ref, s32[64]{0:T(128)} %lengths_ref.1, bf16[128,896]{1,0:T(8,128)(2,1)} %gate_in.1, bf16[128,896]{1,0:T(8,128)(2,1)} %up_in.1, bf16[128,896]{1,0:T(8,128)(2,1)} %cotangent_in.1), custom_call_target="tpu_custom_call" | custom-call | flops 7340032 | bytes 45875200 | tf_op jit(solution)/shard_map/gate_cotangent/pallas_call | solution.py:58
  15.9 5.8 %all-to-all-done = bf16[8,64,128]{2,1,0:T(8,128)(2,1)S(1)} async-done(((bf16[8,64,128]{2,1,0:T(8,128)(2,1)}), bf16[8,64,128]{2,1,0:T(8,128)(2,1)S(1)}, u32[]{:S(2)}, u32[]{:S(2)}) %all-to-all-start) | async-done | bytes 131104 | tf_op jit(solution)/shard_map/all_to_all | solution.py:265
  21.7 0.0 copy-start.1
  21.7 7.2 %all-to-all-start.1 = ((bf16[8,128,896]{2,1,0:T(8,128)(2,1)}), bf16[8,128,896]{2,1,0:T(8,128)(2,1)S(1)}, u32[]{:S(2)}, u32[]{:S(2)}) async-start(bf16[8,128,896]{2,1,0:T(8,128)(2,1)} %gate_cotangent.1), calls=%async_computation.1 | async-start | bytes 3670016 | tf_op jit(solution)/shard_map/all_to_all | solution.py:269
  29.0 0.0 copy-done.1
  29.0 4.8 %collective-permute-start = (bf16[128,512]{1,0:T(8,128)(2,1)S(1)}, bf16[128,512]{1,0:T(8,128)(2,1)S(1)}, u32[]{:S(2)}, u32[]{:S(2)}) collective-permute-start(bf16[128,512]{1,0:T(8,128)(2,1)S(1)} %copy-done.1), channel_id=1, source_target_pairs={{0,0},{1,64},{2,128},{3,192},{4,256},{5,320},{6,384},{7,448},{64,1... | collective-permute-start | bytes 393224 | tf_op jit(solution)/shard_map/ppermute | solution.py:261
  33.8 26.6 %collective-permute-done.value_ref = bf16[128,512]{1,0:T(8,128)(2,1)S(1)} collective-permute-done((bf16[128,512]{1,0:T(8,128)(2,1)S(1)}, bf16[128,512]{1,0:T(8,128)(2,1)S(1)}, u32[]{:S(2)}, u32[]{:S(2)}) %collective-permute-start) | collective-permute-done | bytes 131104 | tf_op jit(solution)/shard_map/ppermute | solution.py:261
  60.3 0.1 turn.1
  60.4 1.9 %collective-permute-start.1 = (bf16[512,128]{1,0:T(8,128)(2,1)S(1)}, bf16[512,128]{1,0:T(8,128)(2,1)S(1)}, u32[]{:S(2)}, u32[]{:S(2)}) collective-permute-start(bf16[512,128]{1,0:T(8,128)(2,1)S(1)} %get-tuple-element.13), channel_id=1, source_target_pairs={{0,1},{1,0},{2,3},{3,2},{4,5},{5,4},{6,7},{7,6},{8,9},{9,8},{10,11... | collective-permute-start | bytes 393224 | tf_op jit(solution)/shard_map/ppermute | solution.py:278
  62.4 1.3 collective-permute-done.1
  63.7 1.9 %collective-permute-start.2 = (bf16[1024,128]{1,0:T(8,128)(2,1)S(1)}, bf16[1024,128]{1,0:T(8,128)(2,1)S(1)}, u32[]{:S(2)}, u32[]{:S(2)}) collective-permute-start(bf16[1024,128]{1,0:T(8,128)(2,1)S(1)} %pad_maximum_fusion.1), channel_id=1, source_target_pairs={{0,2},{1,7},{2,0},{3,5},{4,6},{5,3},{6,4},{7,1},{8,10},{9,15},{10,... | collective-permute-start | bytes 786440 | tf_op jit(solution)/shard_map/ppermute | solution.py:278
  65.6 6.3 %collective-permute-done.2 = bf16[1024,128]{1,0:T(8,128)(2,1)S(1)} collective-permute-done((bf16[1024,128]{1,0:T(8,128)(2,1)S(1)}, bf16[1024,128]{1,0:T(8,128)(2,1)S(1)}, u32[]{:S(2)}, u32[]{:S(2)}) %collective-permute-start.2) | collective-permute-done | bytes 262176 | tf_op jit(solution)/shard_map/ppermute | solution.py:278
  72.0 2.7 %collective-permute-start.3 = (bf16[2048,128]{1,0:T(8,128)(2,1)S(1)}, bf16[2048,128]{1,0:T(8,128)(2,1)S(1)}, u32[]{:S(2)}, u32[]{:S(2)}) collective-permute-start(bf16[2048,128]{1,0:T(8,128)(2,1)S(1)} %pad_maximum_fusion.first_ref), channel_id=1, source_target_pairs={{0,6},{1,3},{2,4},{3,1},{4,2},{5,7},{6,0},{7,5},{8,14},{9,11},{10,... | collective-permute-start | bytes 1572872 | tf_op jit(solution)/shard_map/ppermute | solution.py:278
  74.7 8.4 %collective-permute-done.3.second_ref = bf16[2048,128]{1,0:T(8,128)(2,1)S(1)} collective-permute-done((bf16[2048,128]{1,0:T(8,128)(2,1)S(1)}, bf16[2048,128]{1,0:T(8,128)(2,1)S(1)}, u32[]{:S(2)}, u32[]{:S(2)}) %collective-permute-start.3) | collective-permute-done | bytes 524320 | tf_op jit(solution)/shard_map/ppermute | solution.py:278
  83.1 0.0 all-to-all-done.1
  83.1 1.6 %partial_product.1 = bf16[512,896]{1,0:T(8,128)(2,1)S(1)} custom-call(s32[1]{0:T(128)} %bitcast.t_ref, bf16[2048,128]{1,0:T(8,128)(2,1)S(1)} %pad_maximum_fusion.first_ref, bf16[2048,128]{1,0:T(8,128)(2,1)S(1)} %collective-permute-done.3.second_ref, bf16[1024,896]{1,0:T(8,128)(2,1)S(1)} %bitcast.12), custom_call_target="tpu_custom_call" | custom-call | flops 939524096 | bytes 6000000 | tf_op jit(solution)/shard_map/partial_product/pallas_call | solution.py:168
  84.7 0.0 copy-start
  84.7 20.7 %all_to_all.30.parts_ref = bf16[8,64,896]{2,1,0:T(8,128)(2,1)S(1)} all-to-all(bf16[8,64,896]{2,1,0:T(8,128)(2,1)S(1)} %bitcast.13), channel_id=1, replica_groups={{0,8,16,24,32,40,48,56},{64,72,80,88,96,104,112,120},{128,136,144,152,1..., dimensions={0} | all-to-all | bytes 1835008 | tf_op jit(solution)/shard_map/all_to_all | solution.py:285
  105.3 0.0 copy-done
  105.3 0.9 momentum_step.1
  106.2 9.9 %all_to_all.31.grams_ref = f32[8,32,128]{2,1,0:T(8,128)S(1)} all-to-all(f32[8,32,128]{2,1,0:T(8,128)S(1)} %get-tuple-element.9), channel_id=1, replica_groups=mesh['y'=8,'z'=8,'t'=8] {'t'}, dimensions={0} | all-to-all | bytes 262144 | tf_op jit(solution)/shard_map/all_to_all | solution.py:289
  116.1 3.0 %polar_update.1 = bf16[8,64,112]{2,1,0:T(8,128)(2,1)S(1)} custom-call(f32[8,32,128]{2,1,0:T(8,128)S(1)} %all_to_all.31.grams_ref, f32[64,896]{1,0:T(8,128)S(1)} %get-tuple-element.10.block_ref), custom_call_target="tpu_custom_call" | custom-call | flops 100000000 | bytes 600000 | tf_op jit(solution)/shard_map/polar_update/pallas_call | solution.py:247
  119.1 14.3 %all_to_all.32 = bf16[8,64,112]{2,1,0:T(8,128)(2,1)S(1)} all-to-all(bf16[8,64,112]{2,1,0:T(8,128)(2,1)S(1)} %polar_update.1), channel_id=1, replica_groups=mesh['y'=8,'z'=8,'t'=8] {'y'}, dimensions={0} | all-to-all | bytes 229376 | tf_op jit(solution)/shard_map/all_to_all | solution.py:291
  133.5 0.2 copy.10
  133.6 0.2 reshape.36
  133.8 11.3 %all_to_all.33 = bf16[8,2,3584]{2,1,0:T(2,128)(2,1)S(1)} all-to-all(bf16[8,2,3584]{2,1,0:T(2,128)(2,1)S(1)} %reshape.36), channel_id=1, replica_groups=mesh['y'=8,'z'=8,'t'=8] {'z'}, dimensions={0} | all-to-all | bytes 229376 | tf_op jit(solution)/shard_map/all_to_all | solution.py:294
  145.1 0.2 reshape.37
  145.3 0.1 copy.11
  145.4 0.9 reshape.35
  (3 shorter events, 0.1 us)
Async XLA Ops:
  2.3 19.4 %all-to-all-start = ((bf16[8,64,128]{2,1,0:T(8,128)(2,1)}), bf16[8,64,128]{2,1,0:T(8,128)(2,1)S(1)}, u32[]{:S(2)}, u32[]{:S(2)}) async-start(bf16[8,64,128]{2,1,0:T(8,128)(2,1)} %bitcast.17), calls=%async_computation | async-start | bytes 262144 | tf_op jit(solution)/shard_map/all_to_all | solution.py:265
  21.7 7.2 %copy-start.1 = (bf16[128,512]{1,0:T(8,128)(2,1)S(1)}, bf16[128,512]{1,0:T(8,128)(2,1)}, u32[]{:S(2)}) copy-start(bf16[128,512]{1,0:T(8,128)(2,1)} %value_in.1) | copy-start | bytes 393220
  21.7 61.4 %all-to-all-start.1 = ((bf16[8,128,896]{2,1,0:T(8,128)(2,1)}), bf16[8,128,896]{2,1,0:T(8,128)(2,1)S(1)}, u32[]{:S(2)}, u32[]{:S(2)}) async-start(bf16[8,128,896]{2,1,0:T(8,128)(2,1)} %gate_cotangent.1), calls=%async_computation.1 | async-start | bytes 3670016 | tf_op jit(solution)/shard_map/all_to_all | solution.py:269
  29.0 31.4 %collective-permute-start = (bf16[128,512]{1,0:T(8,128)(2,1)S(1)}, bf16[128,512]{1,0:T(8,128)(2,1)S(1)}, u32[]{:S(2)}, u32[]{:S(2)}) collective-permute-start(bf16[128,512]{1,0:T(8,128)(2,1)S(1)} %copy-done.1), channel_id=1, source_target_pairs={{0,0},{1,64},{2,128},{3,192},{4,256},{5,320},{6,384},{7,448},{64,1... | collective-permute-start | bytes 393224 | tf_op jit(solution)/shard_map/ppermute | solution.py:261
  60.4 3.2 %collective-permute-start.1 = (bf16[512,128]{1,0:T(8,128)(2,1)S(1)}, bf16[512,128]{1,0:T(8,128)(2,1)S(1)}, u32[]{:S(2)}, u32[]{:S(2)}) collective-permute-start(bf16[512,128]{1,0:T(8,128)(2,1)S(1)} %get-tuple-element.13), channel_id=1, source_target_pairs={{0,1},{1,0},{2,3},{3,2},{4,5},{5,4},{6,7},{7,6},{8,9},{9,8},{10,11... | collective-permute-start | bytes 393224 | tf_op jit(solution)/shard_map/ppermute | solution.py:278
  63.7 8.3 %collective-permute-start.2 = (bf16[1024,128]{1,0:T(8,128)(2,1)S(1)}, bf16[1024,128]{1,0:T(8,128)(2,1)S(1)}, u32[]{:S(2)}, u32[]{:S(2)}) collective-permute-start(bf16[1024,128]{1,0:T(8,128)(2,1)S(1)} %pad_maximum_fusion.1), channel_id=1, source_target_pairs={{0,2},{1,7},{2,0},{3,5},{4,6},{5,3},{6,4},{7,1},{8,10},{9,15},{10,... | collective-permute-start | bytes 786440 | tf_op jit(solution)/shard_map/ppermute | solution.py:278
  72.0 11.1 %collective-permute-start.3 = (bf16[2048,128]{1,0:T(8,128)(2,1)S(1)}, bf16[2048,128]{1,0:T(8,128)(2,1)S(1)}, u32[]{:S(2)}, u32[]{:S(2)}) collective-permute-start(bf16[2048,128]{1,0:T(8,128)(2,1)S(1)} %pad_maximum_fusion.first_ref), channel_id=1, source_target_pairs={{0,6},{1,3},{2,4},{3,1},{4,2},{5,7},{6,0},{7,5},{8,14},{9,11},{10,... | collective-permute-start | bytes 1572872 | tf_op jit(solution)/shard_map/ppermute | solution.py:278
  84.7 20.7 %copy-start = (f32[64,896]{1,0:T(8,128)S(1)}, f32[64,896]{1,0:T(8,128)}, u32[]{:S(2)}) copy-start(f32[64,896]{1,0:T(8,128)} %momentum_ref.1) | copy-start | bytes 688132

commit v11 on v10

--- a/solution.py
+++ b/solution.py
@@ -104,7 +104,7 @@
         in_specs=[vmem],
         out_specs=vmem,
         compiler_params=pltpu.CompilerParams(vmem_limit_bytes=8 * 1024 * 1024),
-        cost_estimate=pl.CostEstimate(flops=rows * columns, bytes_accessed=3000 * rows * columns, transcendentals=0),
+        cost_estimate=pl.CostEstimate(flops=rows * columns, bytes_accessed=4 * rows * columns, transcendentals=0),
         name="turn",
     )(value)
 
@@ -259,7 +259,7 @@
     y, z, t = (lax.axis_index(name) for name in AXES)
     swap = [(a * NT + b, b * NT + a) for a in range(NY) for b in range(NT)]
     swapped = lax.ppermute(features, ("y", "t"), swap)
-    turned = turn_first(features)
+    turned, swapped = lax.optimization_barrier((turn_first(features), swapped))
     copies = gate_cotangent(y * NZ + z, lengths, gate_pre, up_pre, hidden_grad)
 
     by_blocks = lax.all_to_all(

time: 147 us -> 130 us (0.88)
  waiting for transfers between devices: 48.4 us -> 35.7 us
  blocking collectives: 56.2 us -> 52.4 us
    ppermute x1, waiting for transfers between devices: 26.6 us -> 9.28 us  [per_device(): swapped = lax.ppermute(features, ('y', 't'), swap)]
    all_to_all x1, waiting for transfers between devices: 0.01 us -> 4.66 us  [per_device(): lax.all_to_all(copies, AXES, split_axis=0, concat_axis=0, axis_index_grou...]
    all_to_all x1, blocking collectives: 14.3 us -> 12.6 us  [per_device(): by_y = lax.all_to_all(by_y, 'y', split_axis=0, concat_axis=0, tiled=True)]
    all_to_all x1, blocking collectives: 9.91 us -> 8.41 us  [per_device(): grams = lax.all_to_all(grams, 't', split_axis=0, concat_axis=0, tiled=True)]
  transfers between devices with their start and end apart: 6 -> 6, of which waited for: 5 -> 6; matrix products, arithmetic and copies ran while one was open for 0% -> 0% of each run, Pallas kernels for 2% -> 4%
where the time goes in v11:
time: 130 us; the launch traced here: 129 us
  blocking collectives  52.4 us (40%)
  waiting for transfers between devices  35.7 us (27%)
  starting transfers between devices  28.2 us (22%)
  Pallas kernels  10.5 us (8%)
  local copies, waits for them, and re-layouts  1.5 us (1%)
    all_to_all x1, blocking collectives, per_device(): lax.all_to_all(pieces, AXES, split_axis=0, concat_axis=0, axis_index_grou...  20 us
    ppermute x3, waiting for transfers between devices, per_device(): lax.ppermute(given if halves is None else kept, AXES, tensor_pairs(masks))  16 us
    all_to_all x1, blocking collectives, per_device(): by_y = lax.all_to_all(by_y, 'y', split_axis=0, concat_axis=0, tiled=True)  12.6 us
    all_to_all x1, blocking collectives, per_device(): by_z = lax.all_to_all(by_z, 'z', split_axis=0, concat_axis=0, tiled=True)  11.3 us
    all_to_all x1, starting transfers between devices, per_device(): lax.all_to_all(turned.reshape(NZ, BLK, turned.shape[1]), 'z', split_axis=...  10.3 us
    ppermute x1, waiting for transfers between devices, per_device(): swapped = lax.ppermute(features, ('y', 't'), swap)  9.28 us
    all_to_all x1, blocking collectives, per_device(): grams = lax.all_to_all(grams, 't', split_axis=0, concat_axis=0, tiled=True)  8.41 us
    all_to_all x1, starting transfers between devices, per_device(): lax.all_to_all(copies, AXES, split_axis=0, concat_axis=0, axis_index_grou...  6.83 us
  transfers between devices with their start and end apart: 6, of which 6 were waited for; matrix products, arithmetic and copies ran while one was open for 0% of the time, Pallas kernels for 4%

profile of v11, /device:TPU:2, one launch (start us, length us, event | category | flops | bytes accessed | tf_op | source)
XLA Modules:
  0.0 129.1 jit_solution(15559811870595084488)
XLA Ops:
  0.6 4.5 %collective-permute-start = (bf16[128,512]{1,0:T(8,128)(2,1)}, bf16[128,512]{1,0:T(8,128)(2,1)S(1)}, u32[]{:S(2)}, u32[]{:S(2)}) collective-permute-start(bf16[128,512]{1,0:T(8,128)(2,1)} %value_in.1), channel_id=1, source_target_pairs={{0,0},{1,64},{2,128},{3,192},{4,256},{5,320},{6,384},{7,448},{64,1... | collective-permute-start | bytes 393224 | tf_op jit(solution)/shard_map/ppermute | solution.py:261
  5.1 1.7 %turn_first.1 = bf16[512,128]{1,0:T(8,128)(2,1)} custom-call(bf16[128,512]{1,0:T(8,128)(2,1)} %value_in.1), custom_call_target="tpu_custom_call" | custom-call | flops 65536 | bytes 262144 | tf_op jit(solution)/shard_map/turn_first/pallas_call | solution.py:82
  6.8 9.3 %collective-permute-done.value_ref = bf16[128,512]{1,0:T(8,128)(2,1)S(1)} collective-permute-done((bf16[128,512]{1,0:T(8,128)(2,1)}, bf16[128,512]{1,0:T(8,128)(2,1)S(1)}, u32[]{:S(2)}, u32[]{:S(2)}) %collective-permute-start) | collective-permute-done | bytes 131104 | tf_op jit(solution)/shard_map/ppermute | solution.py:261
  16.1 10.3 %all-to-all-start = ((bf16[8,64,128]{2,1,0:T(8,128)(2,1)}), bf16[8,64,128]{2,1,0:T(8,128)(2,1)S(1)}, u32[]{:S(2)}, u32[]{:S(2)}) async-start(bf16[8,64,128]{2,1,0:T(8,128)(2,1)} %bitcast.17), calls=%async_computation | async-start | bytes 262144 | tf_op jit(solution)/shard_map/all_to_all | solution.py:265
  26.4 3.3 %gate_cotangent.1 = bf16[8,128,896]{2,1,0:T(8,128)(2,1)} custom-call(s32[1]{0:T(128)} %bitcast.1.place_ref, s32[64]{0:T(128)} %lengths_ref.1, bf16[128,896]{1,0:T(8,128)(2,1)} %gate_in.1, bf16[128,896]{1,0:T(8,128)(2,1)} %up_in.1, bf16[128,896]{1,0:T(8,128)(2,1)} %cotangent_in.1), custom_call_target="tpu_custom_call" | custom-call | flops 7340032 | bytes 45875200 | tf_op jit(solution)/shard_map/gate_cotangent/pallas_call | solution.py:58
  29.7 5.8 %all-to-all-done = bf16[8,64,128]{2,1,0:T(8,128)(2,1)S(1)} async-done(((bf16[8,64,128]{2,1,0:T(8,128)(2,1)}), bf16[8,64,128]{2,1,0:T(8,128)(2,1)S(1)}, u32[]{:S(2)}, u32[]{:S(2)}) %all-to-all-start) | async-done | bytes 131104 | tf_op jit(solution)/shard_map/all_to_all | solution.py:265
  35.5 6.8 %all-to-all-start.1 = ((bf16[8,128,896]{2,1,0:T(8,128)(2,1)}), bf16[8,128,896]{2,1,0:T(8,128)(2,1)S(1)}, u32[]{:S(2)}, u32[]{:S(2)}) async-start(bf16[8,128,896]{2,1,0:T(8,128)(2,1)} %gate_cotangent.1), calls=%async_computation.1 | async-start | bytes 3670016 | tf_op jit(solution)/shard_map/all_to_all | solution.py:269
  42.3 0.1 turn.1
  42.4 1.9 %collective-permute-start.1 = (bf16[512,128]{1,0:T(8,128)(2,1)S(1)}, bf16[512,128]{1,0:T(8,128)(2,1)S(1)}, u32[]{:S(2)}, u32[]{:S(2)}) collective-permute-start(bf16[512,128]{1,0:T(8,128)(2,1)S(1)} %get-tuple-element.17), channel_id=1, source_target_pairs={{0,1},{1,0},{2,3},{3,2},{4,5},{5,4},{6,7},{7,6},{8,9},{9,8},{10,11... | collective-permute-start | bytes 393224 | tf_op jit(solution)/shard_map/ppermute | solution.py:278
  44.3 1.3 %collective-permute-done.1 = bf16[512,128]{1,0:T(8,128)(2,1)S(1)} collective-permute-done((bf16[512,128]{1,0:T(8,128)(2,1)S(1)}, bf16[512,128]{1,0:T(8,128)(2,1)S(1)}, u32[]{:S(2)}, u32[]{:S(2)}) %collective-permute-start.1) | collective-permute-done | bytes 131104 | tf_op jit(solution)/shard_map/ppermute | solution.py:278
  45.7 2.7 %collective-permute-start.2 = (bf16[1024,128]{1,0:T(8,128)(2,1)S(1)}, bf16[1024,128]{1,0:T(8,128)(2,1)S(1)}, u32[]{:S(2)}, u32[]{:S(2)}) collective-permute-start(bf16[1024,128]{1,0:T(8,128)(2,1)S(1)} %pad_maximum_fusion.1), channel_id=1, source_target_pairs={{0,2},{1,7},{2,0},{3,5},{4,6},{5,3},{6,4},{7,1},{8,10},{9,15},{10,... | collective-permute-start | bytes 786440 | tf_op jit(solution)/shard_map/ppermute | solution.py:278
  48.3 5.6 %collective-permute-done.2 = bf16[1024,128]{1,0:T(8,128)(2,1)S(1)} collective-permute-done((bf16[1024,128]{1,0:T(8,128)(2,1)S(1)}, bf16[1024,128]{1,0:T(8,128)(2,1)S(1)}, u32[]{:S(2)}, u32[]{:S(2)}) %collective-permute-start.2) | collective-permute-done | bytes 262176 | tf_op jit(solution)/shard_map/ppermute | solution.py:278
  54.0 2.0 %collective-permute-start.3 = (bf16[2048,128]{1,0:T(8,128)(2,1)S(1)}, bf16[2048,128]{1,0:T(8,128)(2,1)S(1)}, u32[]{:S(2)}, u32[]{:S(2)}) collective-permute-start(bf16[2048,128]{1,0:T(8,128)(2,1)S(1)} %pad_maximum_fusion.first_ref), channel_id=1, source_target_pairs={{0,6},{1,3},{2,4},{3,1},{4,2},{5,7},{6,0},{7,5},{8,14},{9,11},{10,... | collective-permute-start | bytes 1572872 | tf_op jit(solution)/shard_map/ppermute | solution.py:278
  55.9 9.1 %collective-permute-done.3.second_ref = bf16[2048,128]{1,0:T(8,128)(2,1)S(1)} collective-permute-done((bf16[2048,128]{1,0:T(8,128)(2,1)S(1)}, bf16[2048,128]{1,0:T(8,128)(2,1)S(1)}, u32[]{:S(2)}, u32[]{:S(2)}) %collective-permute-start.3) | collective-permute-done | bytes 524320 | tf_op jit(solution)/shard_map/ppermute | solution.py:278
  65.0 4.7 %all-to-all-done.1 = bf16[8,128,896]{2,1,0:T(8,128)(2,1)S(1)} async-done(((bf16[8,128,896]{2,1,0:T(8,128)(2,1)}), bf16[8,128,896]{2,1,0:T(8,128)(2,1)S(1)}, u32[]{:S(2)}, u32[]{:S(2)}) %all-to-all-start.1) | async-done | bytes 1835040 | tf_op jit(solution)/shard_map/all_to_all | solution.py:269
  69.7 1.6 %partial_product.1 = bf16[512,896]{1,0:T(8,128)(2,1)S(1)} custom-call(s32[1]{0:T(128)} %bitcast.t_ref, bf16[2048,128]{1,0:T(8,128)(2,1)S(1)} %pad_maximum_fusion.first_ref, bf16[2048,128]{1,0:T(8,128)(2,1)S(1)} %collective-permute-done.3.second_ref, bf16[1024,896]{1,0:T(8,128)(2,1)S(1)} %bitcast.12), custom_call_target="tpu_custom_call" | custom-call | flops 939524096 | bytes 6000000 | tf_op jit(solution)/shard_map/partial_product/pallas_call | solution.py:168
  71.3 0.0 copy-start
  71.3 20.0 %all_to_all.30.parts_ref = bf16[8,64,896]{2,1,0:T(8,128)(2,1)S(1)} all-to-all(bf16[8,64,896]{2,1,0:T(8,128)(2,1)S(1)} %bitcast.13), channel_id=1, replica_groups={{0,8,16,24,32,40,48,56},{64,72,80,88,96,104,112,120},{128,136,144,152,1..., dimensions={0} | all-to-all | bytes 1835008 | tf_op jit(solution)/shard_map/all_to_all | solution.py:285
  91.3 0.0 copy-done
  91.3 0.9 momentum_step.1
  92.2 8.4 %all_to_all.31.grams_ref = f32[8,32,128]{2,1,0:T(8,128)S(1)} all-to-all(f32[8,32,128]{2,1,0:T(8,128)S(1)} %get-tuple-element.13), channel_id=1, replica_groups=mesh['y'=8,'z'=8,'t'=8] {'t'}, dimensions={0} | all-to-all | bytes 262144 | tf_op jit(solution)/shard_map/all_to_all | solution.py:289
  100.6 3.0 %polar_update.1 = bf16[8,64,112]{2,1,0:T(8,128)(2,1)S(1)} custom-call(f32[8,32,128]{2,1,0:T(8,128)S(1)} %all_to_all.31.grams_ref, f32[64,896]{1,0:T(8,128)S(1)} %get-tuple-element.14.block_ref), custom_call_target="tpu_custom_call" | custom-call | flops 100000000 | bytes 600000 | tf_op jit(solution)/shard_map/polar_update/pallas_call | solution.py:247
  103.6 12.6 %all_to_all.32 = bf16[8,64,112]{2,1,0:T(8,128)(2,1)S(1)} all-to-all(bf16[8,64,112]{2,1,0:T(8,128)(2,1)S(1)} %polar_update.1), channel_id=1, replica_groups=mesh['y'=8,'z'=8,'t'=8] {'y'}, dimensions={0} | all-to-all | bytes 229376 | tf_op jit(solution)/shard_map/all_to_all | solution.py:291
  116.3 0.2 copy.10
  116.5 0.2 reshape.36
  116.6 11.3 %all_to_all.33 = bf16[8,2,3584]{2,1,0:T(2,128)(2,1)S(1)} all-to-all(bf16[8,2,3584]{2,1,0:T(2,128)(2,1)S(1)} %reshape.36), channel_id=1, replica_groups=mesh['y'=8,'z'=8,'t'=8] {'z'}, dimensions={0} | all-to-all | bytes 229376 | tf_op jit(solution)/shard_map/all_to_all | solution.py:294
  127.9 0.2 reshape.37
  128.1 0.1 copy.11
  128.2 0.9 reshape.35
  (3 shorter events, 0.1 us)
Async XLA Ops:
  0.6 15.4 %collective-permute-start = (bf16[128,512]{1,0:T(8,128)(2,1)}, bf16[128,512]{1,0:T(8,128)(2,1)S(1)}, u32[]{:S(2)}, u32[]{:S(2)}) collective-permute-start(bf16[128,512]{1,0:T(8,128)(2,1)} %value_in.1), channel_id=1, source_target_pairs={{0,0},{1,64},{2,128},{3,192},{4,256},{5,320},{6,384},{7,448},{64,1... | collective-permute-start | bytes 393224 | tf_op jit(solution)/shard_map/ppermute | solution.py:261
  16.1 19.4 %all-to-all-start = ((bf16[8,64,128]{2,1,0:T(8,128)(2,1)}), bf16[8,64,128]{2,1,0:T(8,128)(2,1)S(1)}, u32[]{:S(2)}, u32[]{:S(2)}) async-start(bf16[8,64,128]{2,1,0:T(8,128)(2,1)} %bitcast.17), calls=%async_computation | async-start | bytes 262144 | tf_op jit(solution)/shard_map/all_to_all | solution.py:265
  35.5 34.3 %all-to-all-start.1 = ((bf16[8,128,896]{2,1,0:T(8,128)(2,1)}), bf16[8,128,896]{2,1,0:T(8,128)(2,1)S(1)}, u32[]{:S(2)}, u32[]{:S(2)}) async-start(bf16[8,128,896]{2,1,0:T(8,128)(2,1)} %gate_cotangent.1), calls=%async_computation.1 | async-start | bytes 3670016 | tf_op jit(solution)/shard_map/all_to_all | solution.py:269
  42.4 3.2 %collective-permute-start.1 = (bf16[512,128]{1,0:T(8,128)(2,1)S(1)}, bf16[512,128]{1,0:T(8,128)(2,1)S(1)}, u32[]{:S(2)}, u32[]{:S(2)}) collective-permute-start(bf16[512,128]{1,0:T(8,128)(2,1)S(1)} %get-tuple-element.17), channel_id=1, source_target_pairs={{0,1},{1,0},{2,3},{3,2},{4,5},{5,4},{6,7},{7,6},{8,9},{9,8},{10,11... | collective-permute-start | bytes 393224 | tf_op jit(solution)/shard_map/ppermute | solution.py:278
  45.7 8.3 %collective-permute-start.2 = (bf16[1024,128]{1,0:T(8,128)(2,1)S(1)}, bf16[1024,128]{1,0:T(8,128)(2,1)S(1)}, u32[]{:S(2)}, u32[]{:S(2)}) collective-permute-start(bf16[1024,128]{1,0:T(8,128)(2,1)S(1)} %pad_maximum_fusion.1), channel_id=1, source_target_pairs={{0,2},{1,7},{2,0},{3,5},{4,6},{5,3},{6,4},{7,1},{8,10},{9,15},{10,... | collective-permute-start | bytes 786440 | tf_op jit(solution)/shard_map/ppermute | solution.py:278
  54.0 11.1 %collective-permute-start.3 = (bf16[2048,128]{1,0:T(8,128)(2,1)S(1)}, bf16[2048,128]{1,0:T(8,128)(2,1)S(1)}, u32[]{:S(2)}, u32[]{:S(2)}) collective-permute-start(bf16[2048,128]{1,0:T(8,128)(2,1)S(1)} %pad_maximum_fusion.first_ref), channel_id=1, source_target_pairs={{0,6},{1,3},{2,4},{3,1},{4,2},{5,7},{6,0},{7,5},{8,14},{9,11},{10,... | collective-permute-start | bytes 1572872 | tf_op jit(solution)/shard_map/ppermute | solution.py:278
  71.3 20.0 %copy-start = (f32[64,896]{1,0:T(8,128)S(1)}, f32[64,896]{1,0:T(8,128)}, u32[]{:S(2)}) copy-start(f32[64,896]{1,0:T(8,128)} %momentum_ref.1) | copy-start | bytes 688132

commit v12 on v9

--- a/solution.py
+++ b/solution.py
@@ -64,7 +64,7 @@
         + [pltpu.SemaphoreType.DMA((3,))],
         compiler_params=pltpu.CompilerParams(vmem_limit_bytes=60 * 1024 * 1024),
         cost_estimate=pl.CostEstimate(
-            flops=64 * tokens * columns, bytes_accessed=400 * tokens * columns, transcendentals=tokens * columns
+            flops=64 * tokens * columns, bytes_accessed=8000 * tokens * columns, transcendentals=tokens * columns
         ),
         name="gate_cotangent",
     )(jnp.reshape(place, (1,)), lengths, *arrays)
@@ -265,14 +265,14 @@
     by_blocks = lax.all_to_all(
         turned.reshape(NZ, BLK, turned.shape[1]), "z", split_axis=0, concat_axis=0, tiled=True
     ).reshape(turned.shape)
-    copies, swapped, by_blocks = lax.optimization_barrier((copies, swapped, by_blocks))
+    by_blocks, swapped, copies = lax.optimization_barrier((by_blocks, swapped, copies))
     grads = lax.all_to_all(
         copies, AXES, split_axis=0, concat_axis=0, axis_index_groups=line_groups("y"), tiled=True
     ).reshape(-1, copies.shape[2])
     by_tokens = turn(swapped)
-    even = lax.rem(t, 2) == 0
-    kept = jnp.where(even, by_tokens, by_blocks)
-    given = jnp.where(even, by_blocks, by_tokens)
+    odd = lax.rem(t, 2) == 1
+    kept = jnp.where(odd, by_blocks, by_tokens)
+    given = jnp.where(odd, by_tokens, by_blocks)
     orders, halves = ([0], [0]), None
     for masks in [m for m in ((1, 1), (2, 6), (6, 2)) if max(m) < NT]:
         arrived = lax.ppermute(given if halves is None else kept, AXES, tensor_pairs(masks))

time: 127 us -> 127 us (level)
  no operation moved by 1% of the time
where the time goes in v12:
time: 127 us; the launch traced here: 126 us
  blocking collectives  57.9 us (46%)
  starting transfers between devices  30 us (24%)
  waiting for transfers between devices  25.4 us (20%)
  Pallas kernels  10.5 us (8%)
  local copies, waits for them, and re-layouts  1.5 us (1%)
    all_to_all x1, blocking collectives, per_device(): lax.all_to_all(pieces, AXES, split_axis=0, concat_axis=0, axis_index_grou...  24.6 us
    ppermute x3, waiting for transfers between devices, per_device(): lax.ppermute(given if halves is None else kept, AXES, tensor_pairs(masks))  13.1 us
    all_to_all x1, blocking collectives, per_device(): by_y = lax.all_to_all(by_y, 'y', split_axis=0, concat_axis=0, tiled=True)  12.6 us
    all_to_all x1, blocking collectives, per_device(): by_z = lax.all_to_all(by_z, 'z', split_axis=0, concat_axis=0, tiled=True)  11.3 us
    all_to_all x1, starting transfers between devices, per_device(): lax.all_to_all(turned.reshape(NZ, BLK, turned.shape[1]), 'z', split_axis=...  10.3 us
    ppermute x3, starting transfers between devices, per_device(): lax.ppermute(given if halves is None else kept, AXES, tensor_pairs(masks))  9.5 us
    all_to_all x1, blocking collectives, per_device(): grams = lax.all_to_all(grams, 't', split_axis=0, concat_axis=0, tiled=True)  9.4 us
    ppermute x1, waiting for transfers between devices, per_device(): swapped = lax.ppermute(features, ('y', 't'), swap)  7.63 us
  transfers between devices with their start and end apart: 6, of which 5 were waited for; matrix products, arithmetic and copies ran while one was open for 0% of the time, Pallas kernels for 3%

profile of v12, /device:TPU:2, one launch (start us, length us, event | category | flops | bytes accessed | tf_op | source)
XLA Modules:
  0.0 126.1 jit_solution(7220633269158000995)
XLA Ops:
  0.6 1.7 %turn_first.1 = bf16[512,128]{1,0:T(8,128)(2,1)} custom-call(bf16[128,512]{1,0:T(8,128)(2,1)} %value_in.1), custom_call_target="tpu_custom_call" | custom-call | flops 65536 | bytes 262144 | tf_op jit(solution)/shard_map/turn_first/pallas_call | solution.py:82
  2.3 10.3 %all-to-all-start = ((bf16[8,64,128]{2,1,0:T(8,128)(2,1)}), bf16[8,64,128]{2,1,0:T(8,128)(2,1)S(1)}, u32[]{:S(2)}, u32[]{:S(2)}) async-start(bf16[8,64,128]{2,1,0:T(8,128)(2,1)} %bitcast.17), calls=%async_computation | async-start | bytes 262144 | tf_op jit(solution)/shard_map/all_to_all | solution.py:265
  12.6 4.5 %collective-permute-start = (bf16[128,512]{1,0:T(8,128)(2,1)}, bf16[128,512]{1,0:T(8,128)(2,1)S(1)}, u32[]{:S(2)}, u32[]{:S(2)}) collective-permute-start(bf16[128,512]{1,0:T(8,128)(2,1)} %value_in.1), channel_id=1, source_target_pairs={{0,0},{1,64},{2,128},{3,192},{4,256},{5,320},{6,384},{7,448},{64,1... | collective-permute-start | bytes 393224 | tf_op jit(solution)/shard_map/ppermute | solution.py:261
  17.1 3.3 %gate_cotangent.1 = bf16[8,128,896]{2,1,0:T(8,128)(2,1)} custom-call(s32[1]{0:T(128)} %bitcast.3.place_ref, s32[64]{0:T(128)} %lengths_ref.1, bf16[128,896]{1,0:T(8,128)(2,1)} %gate_in.1, bf16[128,896]{1,0:T(8,128)(2,1)} %up_in.1, bf16[128,896]{1,0:T(8,128)(2,1)} %cotangent_in.1), custom_call_target="tpu_custom_call" | custom-call | flops 7340032 | bytes 917504000 | tf_op jit(solution)/shard_map/gate_cotangent/pallas_call | solution.py:58
  20.4 7.6 %collective-permute-done.value_ref = bf16[128,512]{1,0:T(8,128)(2,1)S(1)} collective-permute-done((bf16[128,512]{1,0:T(8,128)(2,1)}, bf16[128,512]{1,0:T(8,128)(2,1)S(1)}, u32[]{:S(2)}, u32[]{:S(2)}) %collective-permute-start) | collective-permute-done | bytes 131104 | tf_op jit(solution)/shard_map/ppermute | solution.py:261
  28.0 0.0 all-to-all-done
  28.0 5.7 %all-to-all-start.1 = ((bf16[8,128,896]{2,1,0:T(8,128)(2,1)}), bf16[8,128,896]{2,1,0:T(8,128)(2,1)S(1)}, u32[]{:S(2)}, u32[]{:S(2)}) async-start(bf16[8,128,896]{2,1,0:T(8,128)(2,1)} %gate_cotangent.1), calls=%async_computation.1 | async-start | bytes 3670016 | tf_op jit(solution)/shard_map/all_to_all | solution.py:269
  33.7 0.1 turn.1
  33.9 1.9 %collective-permute-start.1 = (bf16[512,128]{1,0:T(8,128)(2,1)S(1)}, bf16[512,128]{1,0:T(8,128)(2,1)S(1)}, u32[]{:S(2)}, u32[]{:S(2)}) collective-permute-start(bf16[512,128]{1,0:T(8,128)(2,1)S(1)} %get-tuple-element.15), channel_id=1, source_target_pairs={{0,1},{1,0},{2,3},{3,2},{4,5},{5,4},{6,7},{7,6},{8,9},{9,8},{10,11... | collective-permute-start | bytes 393224 | tf_op jit(solution)/shard_map/ppermute | solution.py:278
  35.8 1.3 %collective-permute-done.1 = bf16[512,128]{1,0:T(8,128)(2,1)S(1)} collective-permute-done((bf16[512,128]{1,0:T(8,128)(2,1)S(1)}, bf16[512,128]{1,0:T(8,128)(2,1)S(1)}, u32[]{:S(2)}, u32[]{:S(2)}) %collective-permute-start.1) | collective-permute-done | bytes 131104 | tf_op jit(solution)/shard_map/ppermute | solution.py:278
  37.1 3.8 %collective-permute-start.2 = (bf16[1024,128]{1,0:T(8,128)(2,1)S(1)}, bf16[1024,128]{1,0:T(8,128)(2,1)S(1)}, u32[]{:S(2)}, u32[]{:S(2)}) collective-permute-start(bf16[1024,128]{1,0:T(8,128)(2,1)S(1)} %pad_maximum_fusion.1), channel_id=1, source_target_pairs={{0,2},{1,7},{2,0},{3,5},{4,6},{5,3},{6,4},{7,1},{8,10},{9,15},{10,... | collective-permute-start | bytes 786440 | tf_op jit(solution)/shard_map/ppermute | solution.py:278
  40.9 4.5 %collective-permute-done.2 = bf16[1024,128]{1,0:T(8,128)(2,1)S(1)} collective-permute-done((bf16[1024,128]{1,0:T(8,128)(2,1)S(1)}, bf16[1024,128]{1,0:T(8,128)(2,1)S(1)}, u32[]{:S(2)}, u32[]{:S(2)}) %collective-permute-start.2) | collective-permute-done | bytes 262176 | tf_op jit(solution)/shard_map/ppermute | solution.py:278
  45.4 3.8 %collective-permute-start.3 = (bf16[2048,128]{1,0:T(8,128)(2,1)S(1)}, bf16[2048,128]{1,0:T(8,128)(2,1)S(1)}, u32[]{:S(2)}, u32[]{:S(2)}) collective-permute-start(bf16[2048,128]{1,0:T(8,128)(2,1)S(1)} %pad_maximum_fusion.first_ref), channel_id=1, source_target_pairs={{0,6},{1,3},{2,4},{3,1},{4,2},{5,7},{6,0},{7,5},{8,14},{9,11},{10,... | collective-permute-start | bytes 1572872 | tf_op jit(solution)/shard_map/ppermute | solution.py:278
  49.2 7.3 %collective-permute-done.3.second_ref = bf16[2048,128]{1,0:T(8,128)(2,1)S(1)} collective-permute-done((bf16[2048,128]{1,0:T(8,128)(2,1)S(1)}, bf16[2048,128]{1,0:T(8,128)(2,1)S(1)}, u32[]{:S(2)}, u32[]{:S(2)}) %collective-permute-start.3) | collective-permute-done | bytes 524320 | tf_op jit(solution)/shard_map/ppermute | solution.py:278
  56.5 4.7 %all-to-all-done.1 = bf16[8,128,896]{2,1,0:T(8,128)(2,1)S(1)} async-done(((bf16[8,128,896]{2,1,0:T(8,128)(2,1)}), bf16[8,128,896]{2,1,0:T(8,128)(2,1)S(1)}, u32[]{:S(2)}, u32[]{:S(2)}) %all-to-all-start.1) | async-done | bytes 1835040 | tf_op jit(solution)/shard_map/all_to_all | solution.py:269
  61.2 1.6 %partial_product.1 = bf16[512,896]{1,0:T(8,128)(2,1)S(1)} custom-call(s32[1]{0:T(128)} %bitcast.t_ref, bf16[2048,128]{1,0:T(8,128)(2,1)S(1)} %pad_maximum_fusion.first_ref, bf16[2048,128]{1,0:T(8,128)(2,1)S(1)} %collective-permute-done.3.second_ref, bf16[1024,896]{1,0:T(8,128)(2,1)S(1)} %bitcast.12), custom_call_target="tpu_custom_call" | custom-call | flops 939524096 | bytes 6000000 | tf_op jit(solution)/shard_map/partial_product/pallas_call | solution.py:168
  62.7 0.0 copy-start
  62.8 24.6 %all_to_all.30.parts_ref = bf16[8,64,896]{2,1,0:T(8,128)(2,1)S(1)} all-to-all(bf16[8,64,896]{2,1,0:T(8,128)(2,1)S(1)} %bitcast.13), channel_id=1, replica_groups={{0,8,16,24,32,40,48,56},{64,72,80,88,96,104,112,120},{128,136,144,152,1..., dimensions={0} | all-to-all | bytes 1835008 | tf_op jit(solution)/shard_map/all_to_all | solution.py:285
  87.3 0.0 copy-done
  87.3 0.9 momentum_step.1
  88.2 9.4 %all_to_all.31.grams_ref = f32[8,32,128]{2,1,0:T(8,128)S(1)} all-to-all(f32[8,32,128]{2,1,0:T(8,128)S(1)} %get-tuple-element.11), channel_id=1, replica_groups=mesh['y'=8,'z'=8,'t'=8] {'t'}, dimensions={0} | all-to-all | bytes 262144 | tf_op jit(solution)/shard_map/all_to_all | solution.py:289
  97.6 3.0 %polar_update.1 = bf16[8,64,112]{2,1,0:T(8,128)(2,1)S(1)} custom-call(f32[8,32,128]{2,1,0:T(8,128)S(1)} %all_to_all.31.grams_ref, f32[64,896]{1,0:T(8,128)S(1)} %get-tuple-element.12.block_ref), custom_call_target="tpu_custom_call" | custom-call | flops 100000000 | bytes 600000 | tf_op jit(solution)/shard_map/polar_update/pallas_call | solution.py:247
  100.6 12.6 %all_to_all.32 = bf16[8,64,112]{2,1,0:T(8,128)(2,1)S(1)} all-to-all(bf16[8,64,112]{2,1,0:T(8,128)(2,1)S(1)} %polar_update.1), channel_id=1, replica_groups=mesh['y'=8,'z'=8,'t'=8] {'y'}, dimensions={0} | all-to-all | bytes 229376 | tf_op jit(solution)/shard_map/all_to_all | solution.py:291
  113.3 0.2 copy.10
  113.4 0.2 reshape.36
  113.6 11.3 %all_to_all.33 = bf16[8,2,3584]{2,1,0:T(2,128)(2,1)S(1)} all-to-all(bf16[8,2,3584]{2,1,0:T(2,128)(2,1)S(1)} %reshape.36), channel_id=1, replica_groups=mesh['y'=8,'z'=8,'t'=8] {'z'}, dimensions={0} | all-to-all | bytes 229376 | tf_op jit(solution)/shard_map/all_to_all | solution.py:294
  124.9 0.2 reshape.37
  125.1 0.1 copy.11
  125.2 0.9 reshape.35
  (3 shorter events, 0.1 us)
Async XLA Ops:
  2.3 25.8 %all-to-all-start = ((bf16[8,64,128]{2,1,0:T(8,128)(2,1)}), bf16[8,64,128]{2,1,0:T(8,128)(2,1)S(1)}, u32[]{:S(2)}, u32[]{:S(2)}) async-start(bf16[8,64,128]{2,1,0:T(8,128)(2,1)} %bitcast.17), calls=%async_computation | async-start | bytes 262144 | tf_op jit(solution)/shard_map/all_to_all | solution.py:265
  12.6 15.4 %collective-permute-start = (bf16[128,512]{1,0:T(8,128)(2,1)}, bf16[128,512]{1,0:T(8,128)(2,1)S(1)}, u32[]{:S(2)}, u32[]{:S(2)}) collective-permute-start(bf16[128,512]{1,0:T(8,128)(2,1)} %value_in.1), channel_id=1, source_target_pairs={{0,0},{1,64},{2,128},{3,192},{4,256},{5,320},{6,384},{7,448},{64,1... | collective-permute-start | bytes 393224 | tf_op jit(solution)/shard_map/ppermute | solution.py:261
  28.0 33.1 %all-to-all-start.1 = ((bf16[8,128,896]{2,1,0:T(8,128)(2,1)}), bf16[8,128,896]{2,1,0:T(8,128)(2,1)S(1)}, u32[]{:S(2)}, u32[]{:S(2)}) async-start(bf16[8,128,896]{2,1,0:T(8,128)(2,1)} %gate_cotangent.1), calls=%async_computation.1 | async-start | bytes 3670016 | tf_op jit(solution)/shard_map/all_to_all | solution.py:269
  33.9 3.2 %collective-permute-start.1 = (bf16[512,128]{1,0:T(8,128)(2,1)S(1)}, bf16[512,128]{1,0:T(8,128)(2,1)S(1)}, u32[]{:S(2)}, u32[]{:S(2)}) collective-permute-start(bf16[512,128]{1,0:T(8,128)(2,1)S(1)} %get-tuple-element.15), channel_id=1, source_target_pairs={{0,1},{1,0},{2,3},{3,2},{4,5},{5,4},{6,7},{7,6},{8,9},{9,8},{10,11... | collective-permute-start | bytes 393224 | tf_op jit(solution)/shard_map/ppermute | solution.py:278
  37.1 8.3 %collective-permute-start.2 = (bf16[1024,128]{1,0:T(8,128)(2,1)S(1)}, bf16[1024,128]{1,0:T(8,128)(2,1)S(1)}, u32[]{:S(2)}, u32[]{:S(2)}) collective-permute-start(bf16[1024,128]{1,0:T(8,128)(2,1)S(1)} %pad_maximum_fusion.1), channel_id=1, source_target_pairs={{0,2},{1,7},{2,0},{3,5},{4,6},{5,3},{6,4},{7,1},{8,10},{9,15},{10,... | collective-permute-start | bytes 786440 | tf_op jit(solution)/shard_map/ppermute | solution.py:278
  45.4 11.1 %collective-permute-start.3 = (bf16[2048,128]{1,0:T(8,128)(2,1)S(1)}, bf16[2048,128]{1,0:T(8,128)(2,1)S(1)}, u32[]{:S(2)}, u32[]{:S(2)}) collective-permute-start(bf16[2048,128]{1,0:T(8,128)(2,1)S(1)} %pad_maximum_fusion.first_ref), channel_id=1, source_target_pairs={{0,6},{1,3},{2,4},{3,1},{4,2},{5,7},{6,0},{7,5},{8,14},{9,11},{10,... | collective-permute-start | bytes 1572872 | tf_op jit(solution)/shard_map/ppermute | solution.py:278
  62.7 24.6 %copy-start = (f32[64,896]{1,0:T(8,128)S(1)}, f32[64,896]{1,0:T(8,128)}, u32[]{:S(2)}) copy-start(f32[64,896]{1,0:T(8,128)} %momentum_ref.1) | copy-start | bytes 688132

commit v13 on v11

--- a/solution.py
+++ b/solution.py
@@ -70,43 +70,39 @@
     )(jnp.reshape(place, (1,)), lengths, *arrays)
 
 
-def turn_first_kernel(value_in, turned_ref, buffer, arrived):
-    copy = pltpu.make_async_copy(value_in, buffer, arrived)
-    copy.start()
-    copy.wait()
-    turned_ref[...] = buffer[...].T
-
-
-def turn_first(value):
-    rows, columns = value.shape
-    return pl.pallas_call(
-        turn_first_kernel,
-        out_shape=jax.ShapeDtypeStruct((columns, rows), value.dtype),
-        in_specs=[pl.BlockSpec(memory_space=pltpu.HBM)],
-        out_specs=pl.BlockSpec(memory_space=pltpu.VMEM),
-        scratch_shapes=[pltpu.VMEM(value.shape, value.dtype), pltpu.SemaphoreType.DMA],
-        compiler_params=pltpu.CompilerParams(vmem_limit_bytes=60 * 1024 * 1024),
-        cost_estimate=pl.CostEstimate(flops=rows * columns, bytes_accessed=4 * rows * columns, transcendentals=0),
-        name="turn_first",
-    )(value)
-
-
-def turn_kernel(value_ref, turned_ref):
-    turned_ref[...] = value_ref[...].T
-
-
-def turn(value):
-    rows, columns = value.shape
-    vmem = pl.BlockSpec(memory_space=pltpu.VMEM)
-    return pl.pallas_call(
-        turn_kernel,
-        out_shape=jax.ShapeDtypeStruct((columns, rows), value.dtype),
-        in_specs=[vmem],
-        out_specs=vmem,
-        compiler_params=pltpu.CompilerParams(vmem_limit_bytes=8 * 1024 * 1024),
-        cost_estimate=pl.CostEstimate(flops=rows * columns, bytes_accessed=4 * rows * columns, transcendentals=0),
-        name="turn",
-    )(value)
+def arrange_kernel(orders, t_ref, first_ref, second_ref, out_ref):
+    tokens = out_ref.shape[2]
+    t = t_ref[0]
+    blocks = [(ref, start) for ref in (first_ref, second_ref) for start in range(0, ref.shape[0], tokens)]
+
+    @pl.when(lax.rem(t, 2) == 0)
+    def _():
+        for offset, (ref, start) in zip(orders[0], blocks):
+            out_ref[lax.bitwise_xor(t, offset)] = ref[start : start + tokens, :].T
+
+    @pl.when(lax.rem(t, 2) == 1)
+    def _():
+        for offset, (ref, start) in zip(orders[1], blocks):
+            turned = ref[start : start + tokens, :].T
+            rows = pl.ds(pl.multiple_of(lax.bitwise_xor(t, offset) * BLK, BLK), BLK)
+            for z in range(NZ):
+                out_ref[z, rows, :] = turned[z * BLK : (z + 1) * BLK, :]
+
+
+def arrange(t, orders, halves, tokens):
+    rows = halves[0].shape[1]
+    vmem = pl.BlockSpec(memory_space=pltpu.VMEM)
+    return pl.pallas_call(
+        functools.partial(arrange_kernel, orders),
+        out_shape=jax.ShapeDtypeStruct((NZ, rows, tokens), jnp.bfloat16),
+        in_specs=[pl.BlockSpec(memory_space=pltpu.SMEM), vmem, vmem],
+        out_specs=vmem,
+        compiler_params=pltpu.CompilerParams(vmem_limit_bytes=16 * 1024 * 1024),
+        cost_estimate=pl.CostEstimate(
+            flops=NZ * rows * tokens, bytes_accessed=4 * NZ * rows * tokens, transcendentals=0
+        ),
+        name="arrange",
+    )(jnp.reshape(t, (1,)), *halves)
 
 
 def device_number(y, z, t):
@@ -132,27 +128,11 @@
     ]
 
 
-def partial_kernel(orders, t_ref, first_ref, second_ref, grads_ref, out_ref, features):
+def partial_kernel(pieces_ref, grads_ref, out_ref, features):
     rows = out_ref.shape[0]
-    tokens = first_ref.shape[1]
-    t = t_ref[0]
-    blocks = [(ref, start) for ref in (first_ref, second_ref) for start in range(0, ref.shape[0], rows)]
-
-    @pl.when(lax.rem(t, 2) == 0)
-    def _():
-        for offset, (ref, start) in zip(orders[0], blocks):
-            group = lax.bitwise_xor(t, offset)
-            features[:, pl.ds(pl.multiple_of(group * tokens, tokens), tokens)] = ref[start : start + rows, :]
-
-    @pl.when(lax.rem(t, 2) == 1)
-    def _():
-        for offset, (ref, start) in zip(orders[1], blocks):
-            block_rows = pl.ds(pl.multiple_of(lax.bitwise_xor(t, offset) * BLK, BLK), BLK)
-            for z in range(NZ):
-                features[block_rows, z * tokens : (z + 1) * tokens] = ref[
-                    start + z * BLK : start + (z + 1) * BLK, :
-                ]
-
+    tokens = pieces_ref.shape[2]
+    for group in range(pieces_ref.shape[0]):
+        features[:, group * tokens : (group + 1) * tokens] = pieces_ref[group]
     step = 128
     for start in range(0, rows, step):
         product = jnp.dot(
@@ -161,14 +141,14 @@
         out_ref[start : start + step, :] = product.astype(out_ref.dtype)
 
 
-def partial_product(t, orders, feature_halves, grads):
+def partial_product(pieces, grads):
     tokens, columns = grads.shape
-    rows = NZ * BLK
-    vmem = pl.BlockSpec(memory_space=pltpu.VMEM)
-    return pl.pallas_call(
-        functools.partial(partial_kernel, orders),
+    rows = pieces.shape[1]
+    vmem = pl.BlockSpec(memory_space=pltpu.VMEM)
+    return pl.pallas_call(
+        partial_kernel,
         out_shape=jax.ShapeDtypeStruct((rows, columns), jnp.bfloat16),
-        in_specs=[pl.BlockSpec(memory_space=pltpu.SMEM), vmem, vmem, vmem],
+        in_specs=[vmem, vmem],
         out_specs=vmem,
         scratch_shapes=[pltpu.VMEM((rows, tokens), jnp.bfloat16)],
         compiler_params=pltpu.CompilerParams(vmem_limit_bytes=32 * 1024 * 1024),
@@ -176,7 +156,7 @@
             flops=2 * tokens * rows * columns, bytes_accessed=6_000_000, transcendentals=0
         ),
         name="partial_product",
-    )(jnp.reshape(t, (1,)), *feature_halves, grads)
+    )(pieces, grads)
 
 
 def momentum_kernel(parts_ref, momentum_ref, moment_ref, nesterov_ref, grams_ref):
@@ -257,30 +237,23 @@
 
 def per_device(features, gate_pre, up_pre, hidden_grad, lengths, momentum):
     y, z, t = (lax.axis_index(name) for name in AXES)
-    swap = [(a * NT + b, b * NT + a) for a in range(NY) for b in range(NT)]
-    swapped = lax.ppermute(features, ("y", "t"), swap)
-    turned, swapped = lax.optimization_barrier((turn_first(features), swapped))
     copies = gate_cotangent(y * NZ + z, lengths, gate_pre, up_pre, hidden_grad)
 
-    by_blocks = lax.all_to_all(
-        turned.reshape(NZ, BLK, turned.shape[1]), "z", split_axis=0, concat_axis=0, tiled=True
-    ).reshape(turned.shape)
-    copies, by_blocks = lax.optimization_barrier((copies, by_blocks))
-    grads = lax.all_to_all(
-        copies, AXES, split_axis=0, concat_axis=0, axis_index_groups=line_groups("y"), tiled=True
-    ).reshape(-1, copies.shape[2])
-    by_tokens = turn(swapped)
-    even = lax.rem(t, 2) == 0
-    kept = jnp.where(even, by_tokens, by_blocks)
-    given = jnp.where(even, by_blocks, by_tokens)
-    orders, halves = ([0], [0]), None
-    for masks in [m for m in ((1, 1), (2, 6), (6, 2)) if max(m) < NT]:
-        arrived = lax.ppermute(given if halves is None else kept, AXES, tensor_pairs(masks))
-        orders = tuple(order + [o ^ mask for o in order] for order, mask in zip(orders, masks))
-        halves = (kept, arrived)
-        kept = jnp.concatenate(halves, axis=0)
-
-    partial_value = partial_product(t, orders, halves, grads)
+    held, halves, orders, first = features, None, ([0], [0]), None
+    for masks in [m for m in ((2, 6), (6, 2), (1, 1)) if max(m) < NT]:
+        arrived = lax.ppermute(held, AXES, tensor_pairs(masks))
+        orders = tuple(orders[p] + [o ^ masks[p] for o in orders[p ^ (masks[p] & 1)]] for p in (0, 1))
+        halves = (held, arrived)
+        held = jnp.concatenate(halves, axis=0)
+        first = arrived if first is None else first
+
+    lines = functools.partial(
+        lax.all_to_all, axis_name=AXES, split_axis=0, concat_axis=0, axis_index_groups=line_groups("y"), tiled=True
+    )
+    copies, _ = lax.optimization_barrier((copies, first))
+    grads = lines(copies).reshape(-1, copies.shape[2])
+    inputs = lines(arrange(t, orders, halves, features.shape[0]))
+    partial_value = partial_product(inputs, grads)
     pieces = partial_value.reshape(NZ, BLK, partial_value.shape[1])
     received = lax.all_to_all(
         pieces, AXES, split_axis=0, concat_axis=0, axis_index_groups=line_groups("z"), tiled=True

time: 130 us -> 147 us (1.13)
  blocking collectives: 52.4 us -> 91.4 us
  starting transfers between devices: 28.2 us -> 15.2 us
  waiting for transfers between devices: 35.7 us -> 26 us
    all_to_all x0 -> x1, blocking collectives: none -> 30.8 us  [per_device(): grads = lines(copies).reshape(-1, copies.shape[2])]
    ppermute x4 -> x3, waiting for transfers between devices: 25.3 us -> 10.4 us  [per_device(): arrived = lax.ppermute(held, AXES, tensor_pairs(masks))]
    all_to_all x2 -> x1, starting transfers between devices: 17.1 us -> 3.56 us  [per_device(): inputs = lines(arrange(t, orders, halves, features.shape[0]))]
    all_to_all x1, blocking collectives: 20 us -> 27.5 us  [per_device(): lax.all_to_all(pieces, AXES, split_axis=0, concat_axis=0, axis_index_grou...]
    all_to_all x2 -> x1, waiting for transfers between devices: 10.4 us -> 15.6 us  [per_device(): inputs = lines(arrange(t, orders, halves, features.shape[0]))]
    all_to_all x1, blocking collectives: 8.41 us -> 10.2 us  [per_device(): grams = lax.all_to_all(grams, 't', split_axis=0, concat_axis=0, tiled=True)]
    pallas_call x3 -> x2, Pallas kernels: 3.31 us -> 2.56 us  [the longest x1 1.3 us: arrange(): pl.pallas_call(functools.partial(arrange_kernel, orders), out_shape=jax.S...]
    ppermute x4 -> x3, starting transfers between devices: 11 us -> 11.7 us  [per_device(): arrived = lax.ppermute(held, AXES, tensor_pairs(masks))]
  transfers between devices with their start and end apart: 6 -> 4, of which waited for: 6 -> 4; matrix products, arithmetic and copies ran while one was open for 0% -> 1% of each run, Pallas kernels for 4% -> 2%
where the time goes in v13:
time: 147 us; the launch traced here: 146 us
  blocking collectives  91.4 us (62%)
  waiting for transfers between devices  26 us (18%)
  starting transfers between devices  15.2 us (10%)
  Pallas kernels  9.75 us (7%)
  local copies, waits for them, and re-layouts  2.44 us (2%)
    all_to_all x1, blocking collectives, per_device(): grads = lines(copies).reshape(-1, copies.shape[2])  30.8 us
    all_to_all x1, blocking collectives, per_device(): lax.all_to_all(pieces, AXES, split_axis=0, concat_axis=0, axis_index_grou...  27.5 us
    all_to_all x1, waiting for transfers between devices, per_device(): inputs = lines(arrange(t, orders, halves, features.shape[0]))  15.6 us
    ppermute x3, starting transfers between devices, per_device(): arrived = lax.ppermute(held, AXES, tensor_pairs(masks))  11.7 us
    all_to_all x1, blocking collectives, per_device(): by_y = lax.all_to_all(by_y, 'y', split_axis=0, concat_axis=0, tiled=True)  11.5 us
    all_to_all x1, blocking collectives, per_device(): by_z = lax.all_to_all(by_z, 'z', split_axis=0, concat_axis=0, tiled=True)  11.3 us
    ppermute x3, waiting for transfers between devices, per_device(): arrived = lax.ppermute(held, AXES, tensor_pairs(masks))  10.4 us
    all_to_all x1, blocking collectives, per_device(): grams = lax.all_to_all(grams, 't', split_axis=0, concat_axis=0, tiled=True)  10.2 us
  transfers between devices with their start and end apart: 4, of which 4 were waited for; matrix products, arithmetic and copies ran while one was open for 1% of the time, Pallas kernels for 2%

profile of v13, /device:TPU:2, one launch (start us, length us, event | category | flops | bytes accessed | tf_op | source)
XLA Modules:
  0.0 146.4 jit_solution(945501731523294170)
XLA Ops:
  0.6 7.8 %collective-permute-start = (bf16[128,512]{1,0:T(8,128)(2,1)}, bf16[128,512]{1,0:T(8,128)(2,1)S(1)}, u32[]{:S(2)}, u32[]{:S(2)}) collective-permute-start(bf16[128,512]{1,0:T(8,128)(2,1)} %param.6), channel_id=1, source_target_pairs={{0,2},{1,7},{2,0},{3,5},{4,6},{5,3},{6,4},{7,1},{8,10},{9,15},{10,... | collective-permute-start | bytes 393224 | tf_op jit(solution)/shard_map/ppermute | solution.py:244
  8.5 3.1 %collective-permute-done = bf16[128,512]{1,0:T(8,128)(2,1)S(1)} collective-permute-done((bf16[128,512]{1,0:T(8,128)(2,1)}, bf16[128,512]{1,0:T(8,128)(2,1)S(1)}, u32[]{:S(2)}, u32[]{:S(2)}) %collective-permute-start) | collective-permute-done | bytes 131104 | tf_op jit(solution)/shard_map/ppermute | solution.py:244
  11.6 0.9 pad_maximum_fusion
  12.5 1.9 %collective-permute-start.1 = (bf16[256,512]{1,0:T(8,128)(2,1)S(1)}, bf16[256,512]{1,0:T(8,128)(2,1)S(1)}, u32[]{:S(2)}, u32[]{:S(2)}) collective-permute-start(bf16[256,512]{1,0:T(8,128)(2,1)S(1)} %pad_maximum_fusion), channel_id=1, source_target_pairs={{0,6},{1,3},{2,4},{3,1},{4,2},{5,7},{6,0},{7,5},{8,14},{9,11},{10,... | collective-permute-start | bytes 786440 | tf_op jit(solution)/shard_map/ppermute | solution.py:244
  14.5 0.9 constant_dynamic-update-slice_fusion.2
  15.4 5.4 %collective-permute-done.1 = bf16[256,512]{1,0:T(8,128)(2,1)S(1)} collective-permute-done((bf16[256,512]{1,0:T(8,128)(2,1)S(1)}, bf16[256,512]{1,0:T(8,128)(2,1)S(1)}, u32[]{:S(2)}, u32[]{:S(2)}) %collective-permute-start.1) | collective-permute-done | bytes 262176 | tf_op jit(solution)/shard_map/ppermute | solution.py:244
  20.8 1.9 %collective-permute-start.2 = (bf16[512,512]{1,0:T(8,128)(2,1)S(1)}, bf16[512,512]{1,0:T(8,128)(2,1)S(1)}, u32[]{:S(2)}, u32[]{:S(2)}) collective-permute-start(bf16[512,512]{1,0:T(8,128)(2,1)S(1)} %constant_dynamic-update-slice_fusion.first_ref), channel_id=1, source_target_pairs={{0,1},{1,0},{2,3},{3,2},{4,5},{5,4},{6,7},{7,6},{8,9},{9,8},{10,11... | collective-permute-start | bytes 1572872 | tf_op jit(solution)/shard_map/ppermute | solution.py:244
  22.7 1.9 %collective-permute-done.2.second_ref = bf16[512,512]{1,0:T(8,128)(2,1)S(1)} collective-permute-done((bf16[512,512]{1,0:T(8,128)(2,1)S(1)}, bf16[512,512]{1,0:T(8,128)(2,1)S(1)}, u32[]{:S(2)}, u32[]{:S(2)}) %collective-permute-start.2) | collective-permute-done | bytes 524320 | tf_op jit(solution)/shard_map/ppermute | solution.py:244
  24.6 1.3 arrange.1
  25.9 3.6 %all-to-all-start = ((bf16[8,512,128]{2,1,0:T(8,128)(2,1)}), bf16[8,512,128]{2,1,0:T(8,128)(2,1)S(1)}, u32[]{:S(2)}, u32[]{:S(2)}) async-start(bf16[8,512,128]{2,1,0:T(8,128)(2,1)} %arrange.1), calls=%async_computation | async-start | bytes 2097152 | tf_op jit(solution)/shard_map/all_to_all | solution.py:255
  29.5 3.3 %gate_cotangent.1 = bf16[8,128,896]{2,1,0:T(8,128)(2,1)} custom-call(s32[1]{0:T(128)} %bitcast.1.place_ref, s32[64]{0:T(128)} %lengths_ref.1, bf16[128,896]{1,0:T(8,128)(2,1)} %gate_in.1, bf16[128,896]{1,0:T(8,128)(2,1)} %up_in.1, bf16[128,896]{1,0:T(8,128)(2,1)} %cotangent_in.1), custom_call_target="tpu_custom_call" | custom-call | flops 7340032 | bytes 45875200 | tf_op jit(solution)/shard_map/gate_cotangent/pallas_call | solution.py:58
  32.8 15.6 %all-to-all-done.pieces_ref = bf16[8,512,128]{2,1,0:T(8,128)(2,1)S(1)} async-done(((bf16[8,512,128]{2,1,0:T(8,128)(2,1)}), bf16[8,512,128]{2,1,0:T(8,128)(2,1)S(1)}, u32[]{:S(2)}, u32[]{:S(2)}) %all-to-all-start) | async-done | bytes 1048608 | tf_op jit(solution)/shard_map/all_to_all | solution.py:255
  48.3 30.8 %all_to_all.30 = bf16[8,128,896]{2,1,0:T(8,128)(2,1)S(1)} all-to-all(bf16[8,128,896]{2,1,0:T(8,128)(2,1)} %gate_cotangent.1), channel_id=1, replica_groups={{0,64,128,192,256,320,384,448},{8,72,136,200,264,328,392,456},{16,80,14..., dimensions={0} | all-to-all | bytes 3670016 | tf_op jit(solution)/shard_map/all_to_all | solution.py:254
  79.2 1.3 partial_product.1
  80.4 0.0 copy-start
  80.4 27.5 %all_to_all.31.parts_ref = bf16[8,64,896]{2,1,0:T(8,128)(2,1)S(1)} all-to-all(bf16[8,64,896]{2,1,0:T(8,128)(2,1)S(1)} %bitcast.11), channel_id=1, replica_groups={{0,8,16,24,32,40,48,56},{64,72,80,88,96,104,112,120},{128,136,144,152,1..., dimensions={0} | all-to-all | bytes 1835008 | tf_op jit(solution)/shard_map/all_to_all | solution.py:258
  107.9 0.0 copy-done
  107.9 0.9 momentum_step.1
  108.8 10.2 %all_to_all.32.grams_ref = f32[8,32,128]{2,1,0:T(8,128)S(1)} all-to-all(f32[8,32,128]{2,1,0:T(8,128)S(1)} %get-tuple-element.7), channel_id=1, replica_groups=mesh['y'=8,'z'=8,'t'=8] {'t'}, dimensions={0} | all-to-all | bytes 262144 | tf_op jit(solution)/shard_map/all_to_all | solution.py:262
  119.1 3.0 %polar_update.1 = bf16[8,64,112]{2,1,0:T(8,128)(2,1)S(1)} custom-call(f32[8,32,128]{2,1,0:T(8,128)S(1)} %all_to_all.32.grams_ref, f32[64,896]{1,0:T(8,128)S(1)} %get-tuple-element.8.block_ref), custom_call_target="tpu_custom_call" | custom-call | flops 100000000 | bytes 600000 | tf_op jit(solution)/shard_map/polar_update/pallas_call | solution.py:227
  122.1 11.5 %all_to_all.33 = bf16[8,64,112]{2,1,0:T(8,128)(2,1)S(1)} all-to-all(bf16[8,64,112]{2,1,0:T(8,128)(2,1)S(1)} %polar_update.1), channel_id=1, replica_groups=mesh['y'=8,'z'=8,'t'=8] {'y'}, dimensions={0} | all-to-all | bytes 229376 | tf_op jit(solution)/shard_map/all_to_all | solution.py:264
  133.6 0.2 copy.10
  133.8 0.2 reshape.28
  134.0 11.3 %all_to_all.34 = bf16[8,2,3584]{2,1,0:T(2,128)(2,1)S(1)} all-to-all(bf16[8,2,3584]{2,1,0:T(2,128)(2,1)S(1)} %reshape.28), channel_id=1, replica_groups=mesh['y'=8,'z'=8,'t'=8] {'z'}, dimensions={0} | all-to-all | bytes 229376 | tf_op jit(solution)/shard_map/all_to_all | solution.py:267
  145.3 0.2 reshape.29
  145.5 0.1 copy.11
  145.5 0.9 reshape.27
  (2 shorter events, 0.0 us)
Async XLA Ops:
  0.6 11.0 %collective-permute-start = (bf16[128,512]{1,0:T(8,128)(2,1)}, bf16[128,512]{1,0:T(8,128)(2,1)S(1)}, u32[]{:S(2)}, u32[]{:S(2)}) collective-permute-start(bf16[128,512]{1,0:T(8,128)(2,1)} %param.6), channel_id=1, source_target_pairs={{0,2},{1,7},{2,0},{3,5},{4,6},{5,3},{6,4},{7,1},{8,10},{9,15},{10,... | collective-permute-start | bytes 393224 | tf_op jit(solution)/shard_map/ppermute | solution.py:244
  12.5 8.3 %collective-permute-start.1 = (bf16[256,512]{1,0:T(8,128)(2,1)S(1)}, bf16[256,512]{1,0:T(8,128)(2,1)S(1)}, u32[]{:S(2)}, u32[]{:S(2)}) collective-permute-start(bf16[256,512]{1,0:T(8,128)(2,1)S(1)} %pad_maximum_fusion), channel_id=1, source_target_pairs={{0,6},{1,3},{2,4},{3,1},{4,2},{5,7},{6,0},{7,5},{8,14},{9,11},{10,... | collective-permute-start | bytes 786440 | tf_op jit(solution)/shard_map/ppermute | solution.py:244
  20.8 3.8 %collective-permute-start.2 = (bf16[512,512]{1,0:T(8,128)(2,1)S(1)}, bf16[512,512]{1,0:T(8,128)(2,1)S(1)}, u32[]{:S(2)}, u32[]{:S(2)}) collective-permute-start(bf16[512,512]{1,0:T(8,128)(2,1)S(1)} %constant_dynamic-update-slice_fusion.first_ref), channel_id=1, source_target_pairs={{0,1},{1,0},{2,3},{3,2},{4,5},{5,4},{6,7},{7,6},{8,9},{9,8},{10,11... | collective-permute-start | bytes 1572872 | tf_op jit(solution)/shard_map/ppermute | solution.py:244
  25.9 22.4 %all-to-all-start = ((bf16[8,512,128]{2,1,0:T(8,128)(2,1)}), bf16[8,512,128]{2,1,0:T(8,128)(2,1)S(1)}, u32[]{:S(2)}, u32[]{:S(2)}) async-start(bf16[8,512,128]{2,1,0:T(8,128)(2,1)} %arrange.1), calls=%async_computation | async-start | bytes 2097152 | tf_op jit(solution)/shard_map/all_to_all | solution.py:255
  80.4 27.5 %copy-start = (f32[64,896]{1,0:T(8,128)S(1)}, f32[64,896]{1,0:T(8,128)}, u32[]{:S(2)}) copy-start(f32[64,896]{1,0:T(8,128)} %momentum_ref.1) | copy-start | bytes 688132

commit v14 on v13

--- a/solution.py
+++ b/solution.py
@@ -64,7 +64,7 @@
         + [pltpu.SemaphoreType.DMA((3,))],
         compiler_params=pltpu.CompilerParams(vmem_limit_bytes=60 * 1024 * 1024),
         cost_estimate=pl.CostEstimate(
-            flops=64 * tokens * columns, bytes_accessed=400 * tokens * columns, transcendentals=tokens * columns
+            flops=64 * tokens * columns, bytes_accessed=24 * tokens * columns, transcendentals=tokens * columns
         ),
         name="gate_cotangent",
     )(jnp.reshape(place, (1,)), lengths, *arrays)
@@ -239,18 +239,18 @@
     y, z, t = (lax.axis_index(name) for name in AXES)
     copies = gate_cotangent(y * NZ + z, lengths, gate_pre, up_pre, hidden_grad)
 
-    held, halves, orders, first = features, None, ([0], [0]), None
+    held, halves, orders = features, None, ([0], [0])
     for masks in [m for m in ((2, 6), (6, 2), (1, 1)) if max(m) < NT]:
         arrived = lax.ppermute(held, AXES, tensor_pairs(masks))
+        if halves is None:
+            arrived, copies = lax.optimization_barrier((arrived, copies))
         orders = tuple(orders[p] + [o ^ masks[p] for o in orders[p ^ (masks[p] & 1)]] for p in (0, 1))
         halves = (held, arrived)
         held = jnp.concatenate(halves, axis=0)
-        first = arrived if first is None else first
 
     lines = functools.partial(
         lax.all_to_all, axis_name=AXES, split_axis=0, concat_axis=0, axis_index_groups=line_groups("y"), tiled=True
     )
-    copies, _ = lax.optimization_barrier((copies, first))
     grads = lines(copies).reshape(-1, copies.shape[2])
     inputs = lines(arrange(t, orders, halves, features.shape[0]))
     partial_value = partial_product(inputs, grads)

time: 147 us -> 144 us (0.980)
  blocking collectives: 91.4 us -> 112 us
  waiting for transfers between devices: 26 us -> 8.17 us
  starting transfers between devices: 15.2 us -> 11.8 us
    all_to_all x0 -> x1, blocking collectives: none -> 21.9 us  [per_device(): inputs = lines(arrange(t, orders, halves, features.shape[0]))]
    all_to_all x1 -> x0, waiting for transfers between devices: 15.6 us -> none  [per_device(): inputs = lines(arrange(t, orders, halves, features.shape[0]))]
    all_to_all x1 -> x0, starting transfers between devices: 3.56 us -> none  [per_device(): inputs = lines(arrange(t, orders, halves, features.shape[0]))]
    ppermute x3, waiting for transfers between devices: 10.4 us -> 8.17 us  [per_device(): arrived = lax.ppermute(held, AXES, tensor_pairs(masks))]
  transfers between devices with their start and end apart: 4 -> 3, of which waited for: 4 -> 2; matrix products, arithmetic and copies ran while one was open for 1% -> 0% of each run, Pallas kernels for 2% -> 2%
where the time goes in v14:
time: 144 us
  blocking collectives  112 us (78%)
  starting transfers between devices  11.8 us (8%)
  Pallas kernels  8.77 us (6%)
  waiting for transfers between devices  8.17 us (6%)
  local copies, waits for them, and re-layouts  1.54 us (1%)
    all_to_all x1, blocking collectives, per_device(): grads = lines(copies).reshape(-1, copies.shape[2])  29.8 us
    all_to_all x1, blocking collectives, per_device(): lax.all_to_all(pieces, AXES, split_axis=0, concat_axis=0, axis_index_grou...  27.8 us
    all_to_all x1, blocking collectives, per_device(): inputs = lines(arrange(t, orders, halves, features.shape[0]))  21.9 us
    ppermute x3, starting transfers between devices, per_device(): arrived = lax.ppermute(held, AXES, tensor_pairs(masks))  11.8 us
    all_to_all x1, blocking collectives, per_device(): by_y = lax.all_to_all(by_y, 'y', split_axis=0, concat_axis=0, tiled=True)  11.5 us
    all_to_all x1, blocking collectives, per_device(): by_z = lax.all_to_all(by_z, 'z', split_axis=0, concat_axis=0, tiled=True)  11.3 us
    all_to_all x1, blocking collectives, per_device(): grams = lax.all_to_all(grams, 't', split_axis=0, concat_axis=0, tiled=True)  10.2 us
    ppermute x3, waiting for transfers between devices, per_device(): arrived = lax.ppermute(held, AXES, tensor_pairs(masks))  8.17 us
  transfers between devices with their start and end apart: 3, of which 2 were waited for; matrix products, arithmetic and copies ran while one was open for 0% of the time, Pallas kernels for 2%

profile of v14, /device:TPU:2, one launch (start us, length us, event | category | flops | bytes accessed | tf_op | source)
XLA Modules:
  0.0 143.5 jit_solution(3337538314156298741)
XLA Ops:
  0.6 0.0 copy-start.2
  0.6 7.9 %collective-permute-start = (bf16[128,512]{1,0:T(8,128)(2,1)}, bf16[128,512]{1,0:T(8,128)(2,1)S(1)}, u32[]{:S(2)}, u32[]{:S(2)}) collective-permute-start(bf16[128,512]{1,0:T(8,128)(2,1)} %param.6), channel_id=1, source_target_pairs={{0,2},{1,7},{2,0},{3,5},{4,6},{5,3},{6,4},{7,1},{8,10},{9,15},{10,... | collective-permute-start | bytes 393224 | tf_op jit(solution)/shard_map/ppermute | solution.py:244
  8.6 3.3 %gate_cotangent.1 = bf16[8,128,896]{2,1,0:T(8,128)(2,1)} custom-call(s32[1]{0:T(128)} %bitcast.1.place_ref, s32[64]{0:T(128)} %lengths_ref.1, bf16[128,896]{1,0:T(8,128)(2,1)} %gate_in.1, bf16[128,896]{1,0:T(8,128)(2,1)} %up_in.1, bf16[128,896]{1,0:T(8,128)(2,1)} %cotangent_in.1), custom_call_target="tpu_custom_call" | custom-call | flops 7340032 | bytes 2752512 | tf_op jit(solution)/shard_map/gate_cotangent/pallas_call | solution.py:58
  11.9 0.0 collective-permute-done
  11.9 0.0 copy-done.2
  11.9 1.9 %collective-permute-start.1 = (bf16[256,512]{1,0:T(8,128)(2,1)S(1)}, bf16[256,512]{1,0:T(8,128)(2,1)S(1)}, u32[]{:S(2)}, u32[]{:S(2)}) collective-permute-start(bf16[256,512]{1,0:T(8,128)(2,1)S(1)} %pad_maximum_fusion), channel_id=1, source_target_pairs={{0,6},{1,3},{2,4},{3,1},{4,2},{5,7},{6,0},{7,5},{8,14},{9,11},{10,... | collective-permute-start | bytes 786440 | tf_op jit(solution)/shard_map/ppermute | solution.py:244
  13.9 6.3 %collective-permute-done.1 = bf16[256,512]{1,0:T(8,128)(2,1)S(1)} collective-permute-done((bf16[256,512]{1,0:T(8,128)(2,1)S(1)}, bf16[256,512]{1,0:T(8,128)(2,1)S(1)}, u32[]{:S(2)}, u32[]{:S(2)}) %collective-permute-start.1) | collective-permute-done | bytes 262176 | tf_op jit(solution)/shard_map/ppermute | solution.py:244
  20.2 1.9 %collective-permute-start.2 = (bf16[512,512]{1,0:T(8,128)(2,1)S(1)}, bf16[512,512]{1,0:T(8,128)(2,1)S(1)}, u32[]{:S(2)}, u32[]{:S(2)}) collective-permute-start(bf16[512,512]{1,0:T(8,128)(2,1)S(1)} %constant_dynamic-update-slice_fusion.first_ref), channel_id=1, source_target_pairs={{0,1},{1,0},{2,3},{3,2},{4,5},{5,4},{6,7},{7,6},{8,9},{9,8},{10,11... | collective-permute-start | bytes 1572872 | tf_op jit(solution)/shard_map/ppermute | solution.py:244
  22.2 1.9 %collective-permute-done.2.second_ref = bf16[512,512]{1,0:T(8,128)(2,1)S(1)} collective-permute-done((bf16[512,512]{1,0:T(8,128)(2,1)S(1)}, bf16[512,512]{1,0:T(8,128)(2,1)S(1)}, u32[]{:S(2)}, u32[]{:S(2)}) %collective-permute-start.2) | collective-permute-done | bytes 524320 | tf_op jit(solution)/shard_map/ppermute | solution.py:244
  24.0 0.0 copy-start.1
  24.0 0.3 arrange.1
  24.4 21.9 %all_to_all.30.pieces_ref = bf16[8,512,128]{2,1,0:T(8,128)(2,1)S(1)} all-to-all(bf16[8,512,128]{2,1,0:T(8,128)(2,1)S(1)} %arrange.1), channel_id=1, replica_groups={{0,64,128,192,256,320,384,448},{8,72,136,200,264,328,392,456},{16,80,14..., dimensions={0} | all-to-all | bytes 2097152 | tf_op jit(solution)/shard_map/all_to_all | solution.py:255
  46.2 0.0 copy-done.1
  46.2 29.8 %all_to_all.31 = bf16[8,128,896]{2,1,0:T(8,128)(2,1)S(1)} all-to-all(bf16[8,128,896]{2,1,0:T(8,128)(2,1)S(1)} %copy-done.1), channel_id=1, replica_groups={{0,64,128,192,256,320,384,448},{8,72,136,200,264,328,392,456},{16,80,14..., dimensions={0} | all-to-all | bytes 3670016 | tf_op jit(solution)/shard_map/all_to_all | solution.py:254
  76.0 1.3 partial_product.1
  77.3 0.0 copy-start
  77.3 27.8 %all_to_all.32.parts_ref = bf16[8,64,896]{2,1,0:T(8,128)(2,1)S(1)} all-to-all(bf16[8,64,896]{2,1,0:T(8,128)(2,1)S(1)} %bitcast.11), channel_id=1, replica_groups={{0,8,16,24,32,40,48,56},{64,72,80,88,96,104,112,120},{128,136,144,152,1..., dimensions={0} | all-to-all | bytes 1835008 | tf_op jit(solution)/shard_map/all_to_all | solution.py:258
  105.0 0.0 copy-done
  105.0 0.9 momentum_step.1
  105.9 10.2 %all_to_all.33.grams_ref = f32[8,32,128]{2,1,0:T(8,128)S(1)} all-to-all(f32[8,32,128]{2,1,0:T(8,128)S(1)} %get-tuple-element.9), channel_id=1, replica_groups=mesh['y'=8,'z'=8,'t'=8] {'t'}, dimensions={0} | all-to-all | bytes 262144 | tf_op jit(solution)/shard_map/all_to_all | solution.py:262
  116.2 3.0 %polar_update.1 = bf16[8,64,112]{2,1,0:T(8,128)(2,1)S(1)} custom-call(f32[8,32,128]{2,1,0:T(8,128)S(1)} %all_to_all.33.grams_ref, f32[64,896]{1,0:T(8,128)S(1)} %get-tuple-element.10.block_ref), custom_call_target="tpu_custom_call" | custom-call | flops 100000000 | bytes 600000 | tf_op jit(solution)/shard_map/polar_update/pallas_call | solution.py:227
  119.2 11.5 %all_to_all.34 = bf16[8,64,112]{2,1,0:T(8,128)(2,1)S(1)} all-to-all(bf16[8,64,112]{2,1,0:T(8,128)(2,1)S(1)} %polar_update.1), channel_id=1, replica_groups=mesh['y'=8,'z'=8,'t'=8] {'y'}, dimensions={0} | all-to-all | bytes 229376 | tf_op jit(solution)/shard_map/all_to_all | solution.py:264
  130.7 0.2 copy.10
  130.9 0.2 reshape.28
  131.1 11.3 %all_to_all.35 = bf16[8,2,3584]{2,1,0:T(2,128)(2,1)S(1)} all-to-all(bf16[8,2,3584]{2,1,0:T(2,128)(2,1)S(1)} %reshape.28), channel_id=1, replica_groups=mesh['y'=8,'z'=8,'t'=8] {'z'}, dimensions={0} | all-to-all | bytes 229376 | tf_op jit(solution)/shard_map/all_to_all | solution.py:267
  142.4 0.2 reshape.29
  142.6 0.1 copy.11
  142.6 0.9 reshape.27
  (4 shorter events, 0.1 us)
Async XLA Ops:
  0.6 11.3 %copy-start.2 = (bf16[128,512]{1,0:T(8,128)(2,1)S(1)}, bf16[128,512]{1,0:T(8,128)(2,1)}, u32[]{:S(2)}) copy-start(bf16[128,512]{1,0:T(8,128)(2,1)} %param.6) | copy-start | bytes 393220
  0.6 11.3 %collective-permute-start = (bf16[128,512]{1,0:T(8,128)(2,1)}, bf16[128,512]{1,0:T(8,128)(2,1)S(1)}, u32[]{:S(2)}, u32[]{:S(2)}) collective-permute-start(bf16[128,512]{1,0:T(8,128)(2,1)} %param.6), channel_id=1, source_target_pairs={{0,2},{1,7},{2,0},{3,5},{4,6},{5,3},{6,4},{7,1},{8,10},{9,15},{10,... | collective-permute-start | bytes 393224 | tf_op jit(solution)/shard_map/ppermute | solution.py:244
  11.9 8.3 %collective-permute-start.1 = (bf16[256,512]{1,0:T(8,128)(2,1)S(1)}, bf16[256,512]{1,0:T(8,128)(2,1)S(1)}, u32[]{:S(2)}, u32[]{:S(2)}) collective-permute-start(bf16[256,512]{1,0:T(8,128)(2,1)S(1)} %pad_maximum_fusion), channel_id=1, source_target_pairs={{0,6},{1,3},{2,4},{3,1},{4,2},{5,7},{6,0},{7,5},{8,14},{9,11},{10,... | collective-permute-start | bytes 786440 | tf_op jit(solution)/shard_map/ppermute | solution.py:244
  20.2 3.8 %collective-permute-start.2 = (bf16[512,512]{1,0:T(8,128)(2,1)S(1)}, bf16[512,512]{1,0:T(8,128)(2,1)S(1)}, u32[]{:S(2)}, u32[]{:S(2)}) collective-permute-start(bf16[512,512]{1,0:T(8,128)(2,1)S(1)} %constant_dynamic-update-slice_fusion.first_ref), channel_id=1, source_target_pairs={{0,1},{1,0},{2,3},{3,2},{4,5},{5,4},{6,7},{7,6},{8,9},{9,8},{10,11... | collective-permute-start | bytes 1572872 | tf_op jit(solution)/shard_map/ppermute | solution.py:244
  24.0 22.2 %copy-start.1 = (bf16[8,128,896]{2,1,0:T(8,128)(2,1)S(1)}, bf16[8,128,896]{2,1,0:T(8,128)(2,1)}, u32[]{:S(2)}) copy-start(bf16[8,128,896]{2,1,0:T(8,128)(2,1)} %gate_cotangent.1) | copy-start | bytes 5505028
  77.3 27.8 %copy-start = (f32[64,896]{1,0:T(8,128)S(1)}, f32[64,896]{1,0:T(8,128)}, u32[]{:S(2)}) copy-start(f32[64,896]{1,0:T(8,128)} %momentum_ref.1) | copy-start | bytes 688132

commit v15 on v11

--- a/solution.py
+++ b/solution.py
@@ -259,7 +259,8 @@
     y, z, t = (lax.axis_index(name) for name in AXES)
     swap = [(a * NT + b, b * NT + a) for a in range(NY) for b in range(NT)]
     swapped = lax.ppermute(features, ("y", "t"), swap)
-    turned, swapped = lax.optimization_barrier((turn_first(features), swapped))
+    turned = turn_first(features)
+    lengths, swapped = lax.optimization_barrier((lengths, swapped))
     copies = gate_cotangent(y * NZ + z, lengths, gate_pre, up_pre, hidden_grad)
 
     by_blocks = lax.all_to_all(

time: 130 us -> 130 us (level)
  waiting for transfers between devices: 35.7 us -> 28.7 us
  blocking collectives: 52.4 us -> 57.9 us
  starting transfers between devices: 28.2 us -> 30 us
    all_to_all x1, waiting for transfers between devices: 5.77 us -> 0.01 us  [per_device(): lax.all_to_all(turned.reshape(NZ, BLK, turned.shape[1]), 'z', split_axis=...]
    all_to_all x1, blocking collectives: 20 us -> 24.5 us  [per_device(): lax.all_to_all(pieces, AXES, split_axis=0, concat_axis=0, axis_index_grou...]
    ppermute x3, waiting for transfers between devices: 16 us -> 13.1 us  [per_device(): lax.ppermute(given if halves is None else kept, AXES, tensor_pairs(masks))]
    ppermute x3, starting transfers between devices: 6.55 us -> 9.5 us  [per_device(): lax.ppermute(given if halves is None else kept, AXES, tensor_pairs(masks))]
    ppermute x1, waiting for transfers between devices: 9.28 us -> 10.9 us  [per_device(): swapped = lax.ppermute(features, ('y', 't'), swap)]
  transfers between devices with their start and end apart: 6 -> 6, of which waited for: 6 -> 5; matrix products, arithmetic and copies ran while one was open for 0% -> 0% of each run, Pallas kernels for 4% -> 3%
where the time goes in v15:
time: 130 us; the launch traced here: 129 us
  blocking collectives  57.9 us (45%)
  starting transfers between devices  30 us (23%)
  waiting for transfers between devices  28.7 us (22%)
  Pallas kernels  10.5 us (8%)
  local copies, waits for them, and re-layouts  1.5 us (1%)
    all_to_all x1, blocking collectives, per_device(): lax.all_to_all(pieces, AXES, split_axis=0, concat_axis=0, axis_index_grou...  24.5 us
    ppermute x3, waiting for transfers between devices, per_device(): lax.ppermute(given if halves is None else kept, AXES, tensor_pairs(masks))  13.1 us
    all_to_all x1, blocking collectives, per_device(): by_y = lax.all_to_all(by_y, 'y', split_axis=0, concat_axis=0, tiled=True)  12.6 us
    all_to_all x1, blocking collectives, per_device(): by_z = lax.all_to_all(by_z, 'z', split_axis=0, concat_axis=0, tiled=True)  11.3 us
    ppermute x1, waiting for transfers between devices, per_device(): swapped = lax.ppermute(features, ('y', 't'), swap)  10.9 us
    all_to_all x1, starting transfers between devices, per_device(): lax.all_to_all(turned.reshape(NZ, BLK, turned.shape[1]), 'z', split_axis=...  10.3 us
    ppermute x3, starting transfers between devices, per_device(): lax.ppermute(given if halves is None else kept, AXES, tensor_pairs(masks))  9.5 us
    all_to_all x1, blocking collectives, per_device(): grams = lax.all_to_all(grams, 't', split_axis=0, concat_axis=0, tiled=True)  9.4 us
  transfers between devices with their start and end apart: 6, of which 5 were waited for; matrix products, arithmetic and copies ran while one was open for 0% of the time, Pallas kernels for 3%

profile of v15, /device:TPU:2, one launch (start us, length us, event | category | flops | bytes accessed | tf_op | source)
XLA Modules:
  0.0 129.4 jit_solution(4965392976189050341)
XLA Ops:
  0.6 1.7 %turn_first.1 = bf16[512,128]{1,0:T(8,128)(2,1)} custom-call(bf16[128,512]{1,0:T(8,128)(2,1)} %value_in.1), custom_call_target="tpu_custom_call" | custom-call | flops 65536 | bytes 262144 | tf_op jit(solution)/shard_map/turn_first/pallas_call | solution.py:82
  2.3 10.3 %all-to-all-start = ((bf16[8,64,128]{2,1,0:T(8,128)(2,1)}), bf16[8,64,128]{2,1,0:T(8,128)(2,1)S(1)}, u32[]{:S(2)}, u32[]{:S(2)}) async-start(bf16[8,64,128]{2,1,0:T(8,128)(2,1)} %bitcast.17), calls=%async_computation | async-start | bytes 262144 | tf_op jit(solution)/shard_map/all_to_all | solution.py:266
  12.6 4.5 %collective-permute-start = (bf16[128,512]{1,0:T(8,128)(2,1)}, bf16[128,512]{1,0:T(8,128)(2,1)S(1)}, u32[]{:S(2)}, u32[]{:S(2)}) collective-permute-start(bf16[128,512]{1,0:T(8,128)(2,1)} %value_in.1), channel_id=1, source_target_pairs={{0,0},{1,64},{2,128},{3,192},{4,256},{5,320},{6,384},{7,448},{64,1... | collective-permute-start | bytes 393224 | tf_op jit(solution)/shard_map/ppermute | solution.py:261
  17.1 10.9 %collective-permute-done.value_ref = bf16[128,512]{1,0:T(8,128)(2,1)S(1)} collective-permute-done((bf16[128,512]{1,0:T(8,128)(2,1)}, bf16[128,512]{1,0:T(8,128)(2,1)S(1)}, u32[]{:S(2)}, u32[]{:S(2)}) %collective-permute-start) | collective-permute-done | bytes 131104 | tf_op jit(solution)/shard_map/ppermute | solution.py:261
  28.0 3.3 %gate_cotangent.1 = bf16[8,128,896]{2,1,0:T(8,128)(2,1)} custom-call(s32[1]{0:T(128)} %bitcast.1.place_ref, s32[64]{0:T(128)} %lengths_ref, bf16[128,896]{1,0:T(8,128)(2,1)} %gate_in.1, bf16[128,896]{1,0:T(8,128)(2,1)} %up_in.1, bf16[128,896]{1,0:T(8,128)(2,1)} %cotangent_in.1), custom_call_target="tpu_custom_call" | custom-call | flops 7340032 | bytes 45875200 | tf_op jit(solution)/shard_map/gate_cotangent/pallas_call | solution.py:58
  31.4 0.0 all-to-all-done
  31.4 5.7 %all-to-all-start.1 = ((bf16[8,128,896]{2,1,0:T(8,128)(2,1)}), bf16[8,128,896]{2,1,0:T(8,128)(2,1)S(1)}, u32[]{:S(2)}, u32[]{:S(2)}) async-start(bf16[8,128,896]{2,1,0:T(8,128)(2,1)} %gate_cotangent.1), calls=%async_computation.1 | async-start | bytes 3670016 | tf_op jit(solution)/shard_map/all_to_all | solution.py:270
  37.1 0.1 turn.1
  37.2 1.9 %collective-permute-start.1 = (bf16[512,128]{1,0:T(8,128)(2,1)S(1)}, bf16[512,128]{1,0:T(8,128)(2,1)S(1)}, u32[]{:S(2)}, u32[]{:S(2)}) collective-permute-start(bf16[512,128]{1,0:T(8,128)(2,1)S(1)} %get-tuple-element.17), channel_id=1, source_target_pairs={{0,1},{1,0},{2,3},{3,2},{4,5},{5,4},{6,7},{7,6},{8,9},{9,8},{10,11... | collective-permute-start | bytes 393224 | tf_op jit(solution)/shard_map/ppermute | solution.py:279
  39.1 1.3 %collective-permute-done.1 = bf16[512,128]{1,0:T(8,128)(2,1)S(1)} collective-permute-done((bf16[512,128]{1,0:T(8,128)(2,1)S(1)}, bf16[512,128]{1,0:T(8,128)(2,1)S(1)}, u32[]{:S(2)}, u32[]{:S(2)}) %collective-permute-start.1) | collective-permute-done | bytes 131104 | tf_op jit(solution)/shard_map/ppermute | solution.py:279
  40.5 3.8 %collective-permute-start.2 = (bf16[1024,128]{1,0:T(8,128)(2,1)S(1)}, bf16[1024,128]{1,0:T(8,128)(2,1)S(1)}, u32[]{:S(2)}, u32[]{:S(2)}) collective-permute-start(bf16[1024,128]{1,0:T(8,128)(2,1)S(1)} %pad_maximum_fusion.1), channel_id=1, source_target_pairs={{0,2},{1,7},{2,0},{3,5},{4,6},{5,3},{6,4},{7,1},{8,10},{9,15},{10,... | collective-permute-start | bytes 786440 | tf_op jit(solution)/shard_map/ppermute | solution.py:279
  44.3 4.5 %collective-permute-done.2 = bf16[1024,128]{1,0:T(8,128)(2,1)S(1)} collective-permute-done((bf16[1024,128]{1,0:T(8,128)(2,1)S(1)}, bf16[1024,128]{1,0:T(8,128)(2,1)S(1)}, u32[]{:S(2)}, u32[]{:S(2)}) %collective-permute-start.2) | collective-permute-done | bytes 262176 | tf_op jit(solution)/shard_map/ppermute | solution.py:279
  48.8 3.8 %collective-permute-start.3 = (bf16[2048,128]{1,0:T(8,128)(2,1)S(1)}, bf16[2048,128]{1,0:T(8,128)(2,1)S(1)}, u32[]{:S(2)}, u32[]{:S(2)}) collective-permute-start(bf16[2048,128]{1,0:T(8,128)(2,1)S(1)} %pad_maximum_fusion.first_ref), channel_id=1, source_target_pairs={{0,6},{1,3},{2,4},{3,1},{4,2},{5,7},{6,0},{7,5},{8,14},{9,11},{10,... | collective-permute-start | bytes 1572872 | tf_op jit(solution)/shard_map/ppermute | solution.py:279
  52.5 7.3 %collective-permute-done.3.second_ref = bf16[2048,128]{1,0:T(8,128)(2,1)S(1)} collective-permute-done((bf16[2048,128]{1,0:T(8,128)(2,1)S(1)}, bf16[2048,128]{1,0:T(8,128)(2,1)S(1)}, u32[]{:S(2)}, u32[]{:S(2)}) %collective-permute-start.3) | collective-permute-done | bytes 524320 | tf_op jit(solution)/shard_map/ppermute | solution.py:279
  59.8 4.7 %all-to-all-done.1 = bf16[8,128,896]{2,1,0:T(8,128)(2,1)S(1)} async-done(((bf16[8,128,896]{2,1,0:T(8,128)(2,1)}), bf16[8,128,896]{2,1,0:T(8,128)(2,1)S(1)}, u32[]{:S(2)}, u32[]{:S(2)}) %all-to-all-start.1) | async-done | bytes 1835040 | tf_op jit(solution)/shard_map/all_to_all | solution.py:270
  64.5 1.6 %partial_product.1 = bf16[512,896]{1,0:T(8,128)(2,1)S(1)} custom-call(s32[1]{0:T(128)} %bitcast.t_ref, bf16[2048,128]{1,0:T(8,128)(2,1)S(1)} %pad_maximum_fusion.first_ref, bf16[2048,128]{1,0:T(8,128)(2,1)S(1)} %collective-permute-done.3.second_ref, bf16[1024,896]{1,0:T(8,128)(2,1)S(1)} %bitcast.12), custom_call_target="tpu_custom_call" | custom-call | flops 939524096 | bytes 6000000 | tf_op jit(solution)/shard_map/partial_product/pallas_call | solution.py:168
  66.1 0.0 copy-start
  66.1 24.5 %all_to_all.30.parts_ref = bf16[8,64,896]{2,1,0:T(8,128)(2,1)S(1)} all-to-all(bf16[8,64,896]{2,1,0:T(8,128)(2,1)S(1)} %bitcast.13), channel_id=1, replica_groups={{0,8,16,24,32,40,48,56},{64,72,80,88,96,104,112,120},{128,136,144,152,1..., dimensions={0} | all-to-all | bytes 1835008 | tf_op jit(solution)/shard_map/all_to_all | solution.py:286
  90.6 0.0 copy-done
  90.6 0.9 momentum_step.1
  91.5 9.4 %all_to_all.31.grams_ref = f32[8,32,128]{2,1,0:T(8,128)S(1)} all-to-all(f32[8,32,128]{2,1,0:T(8,128)S(1)} %get-tuple-element.13), channel_id=1, replica_groups=mesh['y'=8,'z'=8,'t'=8] {'t'}, dimensions={0} | all-to-all | bytes 262144 | tf_op jit(solution)/shard_map/all_to_all | solution.py:290
  100.9 3.0 %polar_update.1 = bf16[8,64,112]{2,1,0:T(8,128)(2,1)S(1)} custom-call(f32[8,32,128]{2,1,0:T(8,128)S(1)} %all_to_all.31.grams_ref, f32[64,896]{1,0:T(8,128)S(1)} %get-tuple-element.14.block_ref), custom_call_target="tpu_custom_call" | custom-call | flops 100000000 | bytes 600000 | tf_op jit(solution)/shard_map/polar_update/pallas_call | solution.py:247
  104.0 12.6 %all_to_all.32 = bf16[8,64,112]{2,1,0:T(8,128)(2,1)S(1)} all-to-all(bf16[8,64,112]{2,1,0:T(8,128)(2,1)S(1)} %polar_update.1), channel_id=1, replica_groups=mesh['y'=8,'z'=8,'t'=8] {'y'}, dimensions={0} | all-to-all | bytes 229376 | tf_op jit(solution)/shard_map/all_to_all | solution.py:292
  116.6 0.2 copy.10
  116.8 0.2 reshape.36
  117.0 11.3 %all_to_all.33 = bf16[8,2,3584]{2,1,0:T(2,128)(2,1)S(1)} all-to-all(bf16[8,2,3584]{2,1,0:T(2,128)(2,1)S(1)} %reshape.36), channel_id=1, replica_groups=mesh['y'=8,'z'=8,'t'=8] {'z'}, dimensions={0} | all-to-all | bytes 229376 | tf_op jit(solution)/shard_map/all_to_all | solution.py:295
  128.2 0.2 reshape.37
  128.4 0.1 copy.11
  128.5 0.9 reshape.35
  (3 shorter events, 0.1 us)
Async XLA Ops:
  2.3 29.1 %all-to-all-start = ((bf16[8,64,128]{2,1,0:T(8,128)(2,1)}), bf16[8,64,128]{2,1,0:T(8,128)(2,1)S(1)}, u32[]{:S(2)}, u32[]{:S(2)}) async-start(bf16[8,64,128]{2,1,0:T(8,128)(2,1)} %bitcast.17), calls=%async_computation | async-start | bytes 262144 | tf_op jit(solution)/shard_map/all_to_all | solution.py:266
  12.6 15.4 %collective-permute-start = (bf16[128,512]{1,0:T(8,128)(2,1)}, bf16[128,512]{1,0:T(8,128)(2,1)S(1)}, u32[]{:S(2)}, u32[]{:S(2)}) collective-permute-start(bf16[128,512]{1,0:T(8,128)(2,1)} %value_in.1), channel_id=1, source_target_pairs={{0,0},{1,64},{2,128},{3,192},{4,256},{5,320},{6,384},{7,448},{64,1... | collective-permute-start | bytes 393224 | tf_op jit(solution)/shard_map/ppermute | solution.py:261
  31.4 33.1 %all-to-all-start.1 = ((bf16[8,128,896]{2,1,0:T(8,128)(2,1)}), bf16[8,128,896]{2,1,0:T(8,128)(2,1)S(1)}, u32[]{:S(2)}, u32[]{:S(2)}) async-start(bf16[8,128,896]{2,1,0:T(8,128)(2,1)} %gate_cotangent.1), calls=%async_computation.1 | async-start | bytes 3670016 | tf_op jit(solution)/shard_map/all_to_all | solution.py:270
  37.2 3.2 %collective-permute-start.1 = (bf16[512,128]{1,0:T(8,128)(2,1)S(1)}, bf16[512,128]{1,0:T(8,128)(2,1)S(1)}, u32[]{:S(2)}, u32[]{:S(2)}) collective-permute-start(bf16[512,128]{1,0:T(8,128)(2,1)S(1)} %get-tuple-element.17), channel_id=1, source_target_pairs={{0,1},{1,0},{2,3},{3,2},{4,5},{5,4},{6,7},{7,6},{8,9},{9,8},{10,11... | collective-permute-start | bytes 393224 | tf_op jit(solution)/shard_map/ppermute | solution.py:279
  40.5 8.3 %collective-permute-start.2 = (bf16[1024,128]{1,0:T(8,128)(2,1)S(1)}, bf16[1024,128]{1,0:T(8,128)(2,1)S(1)}, u32[]{:S(2)}, u32[]{:S(2)}) collective-permute-start(bf16[1024,128]{1,0:T(8,128)(2,1)S(1)} %pad_maximum_fusion.1), channel_id=1, source_target_pairs={{0,2},{1,7},{2,0},{3,5},{4,6},{5,3},{6,4},{7,1},{8,10},{9,15},{10,... | collective-permute-start | bytes 786440 | tf_op jit(solution)/shard_map/ppermute | solution.py:279
  48.8 11.1 %collective-permute-start.3 = (bf16[2048,128]{1,0:T(8,128)(2,1)S(1)}, bf16[2048,128]{1,0:T(8,128)(2,1)S(1)}, u32[]{:S(2)}, u32[]{:S(2)}) collective-permute-start(bf16[2048,128]{1,0:T(8,128)(2,1)S(1)} %pad_maximum_fusion.first_ref), channel_id=1, source_target_pairs={{0,6},{1,3},{2,4},{3,1},{4,2},{5,7},{6,0},{7,5},{8,14},{9,11},{10,... | collective-permute-start | bytes 1572872 | tf_op jit(solution)/shard_map/ppermute | solution.py:279
  66.1 24.6 %copy-start = (f32[64,896]{1,0:T(8,128)S(1)}, f32[64,896]{1,0:T(8,128)}, u32[]{:S(2)}) copy-start(f32[64,896]{1,0:T(8,128)} %momentum_ref.1) | copy-start | bytes 688132

commit v16 on v9

--- a/solution.py
+++ b/solution.py
@@ -70,27 +70,6 @@
     )(jnp.reshape(place, (1,)), lengths, *arrays)
 
 
-def turn_first_kernel(value_in, turned_ref, buffer, arrived):
-    copy = pltpu.make_async_copy(value_in, buffer, arrived)
-    copy.start()
-    copy.wait()
-    turned_ref[...] = buffer[...].T
-
-
-def turn_first(value):
-    rows, columns = value.shape
-    return pl.pallas_call(
-        turn_first_kernel,
-        out_shape=jax.ShapeDtypeStruct((columns, rows), value.dtype),
-        in_specs=[pl.BlockSpec(memory_space=pltpu.HBM)],
-        out_specs=pl.BlockSpec(memory_space=pltpu.VMEM),
-        scratch_shapes=[pltpu.VMEM(value.shape, value.dtype), pltpu.SemaphoreType.DMA],
-        compiler_params=pltpu.CompilerParams(vmem_limit_bytes=60 * 1024 * 1024),
-        cost_estimate=pl.CostEstimate(flops=rows * columns, bytes_accessed=4 * rows * columns, transcendentals=0),
-        name="turn_first",
-    )(value)
-
-
 def turn_kernel(value_ref, turned_ref):
     turned_ref[...] = value_ref[...].T
 
@@ -231,12 +210,12 @@
     for iteration in range(ITERS):
         square = mul(gram, gram)
         poly = linear_coeff * eye + cubic_coeff * gram + quintic_coeff * square
-        mapping = poly if iteration == 0 else mul(poly, mapping)
         if iteration < ITERS - 1:
+            mapping = poly if iteration == 0 else mul(poly, mapping)
             gram = mul(mul(poly, gram), poly)
-    mapping = mapping * (inverse * (update_gain * math.sqrt(HID)))
+    scaled = mul(mapping * (inverse * (update_gain * math.sqrt(HID))), block_ref[...])
     units = out_ref.shape[2]
-    rows = mul(mapping, block_ref[...]).astype(out_ref.dtype)
+    rows = mul(poly, scaled).astype(out_ref.dtype)
     for part in range(out_ref.shape[0]):
         out_ref[part] = rows[:, part * units : (part + 1) * units]
 
@@ -259,7 +238,7 @@
     y, z, t = (lax.axis_index(name) for name in AXES)
     swap = [(a * NT + b, b * NT + a) for a in range(NY) for b in range(NT)]
     swapped = lax.ppermute(features, ("y", "t"), swap)
-    turned = turn_first(features)
+    turned = turn(features)
     copies = gate_cotangent(y * NZ + z, lengths, gate_pre, up_pre, hidden_grad)
 
     by_blocks = lax.all_to_all(

time: 127 us -> 126 us (level)
    pallas_call x1 -> x0, Pallas kernels: 1.66 us -> none  [turn_first(): pl.pallas_call(turn_first_kernel, out_shape=jax.ShapeDtypeStruct((columns...]
where the time goes in v16:
time: 126 us
  blocking collectives  57.9 us (46%)
  starting transfers between devices  30 us (24%)
  waiting for transfers between devices  25.4 us (20%)
  Pallas kernels  9.44 us (7%)
  local copies, waits for them, and re-layouts  2.4 us (2%)
    all_to_all x1, blocking collectives, per_device(): lax.all_to_all(pieces, AXES, split_axis=0, concat_axis=0, axis_index_grou...  24.6 us
    ppermute x3, waiting for transfers between devices, per_device(): lax.ppermute(given if halves is None else kept, AXES, tensor_pairs(masks))  13.1 us
    all_to_all x1, blocking collectives, per_device(): by_y = lax.all_to_all(by_y, 'y', split_axis=0, concat_axis=0, tiled=True)  12.6 us
    all_to_all x1, blocking collectives, per_device(): by_z = lax.all_to_all(by_z, 'z', split_axis=0, concat_axis=0, tiled=True)  11.3 us
    all_to_all x1, starting transfers between devices, per_device(): lax.all_to_all(turned.reshape(NZ, BLK, turned.shape[1]), 'z', split_axis=...  10.3 us
    ppermute x3, starting transfers between devices, per_device(): lax.ppermute(given if halves is None else kept, AXES, tensor_pairs(masks))  9.5 us
    all_to_all x1, blocking collectives, per_device(): grams = lax.all_to_all(grams, 't', split_axis=0, concat_axis=0, tiled=True)  9.4 us
    ppermute x1, waiting for transfers between devices, per_device(): swapped = lax.ppermute(features, ('y', 't'), swap)  7.64 us
  transfers between devices with their start and end apart: 6, of which 5 were waited for; matrix products, arithmetic and copies ran while one was open for 0% of the time, Pallas kernels for 3%

profile of v16, /device:TPU:2, one launch (start us, length us, event | category | flops | bytes accessed | tf_op | source)
XLA Modules:
  0.0 125.9 jit_solution(2579443421552035107)
XLA Ops:
  0.6 0.0 copy-start.1
  0.6 0.9 copy-done.1
  1.5 0.7 turn.2
  2.3 10.3 %all-to-all-start = ((bf16[8,64,128]{2,1,0:T(8,128)(2,1)}), bf16[8,64,128]{2,1,0:T(8,128)(2,1)S(1)}, u32[]{:S(2)}, u32[]{:S(2)}) async-start(bf16[8,64,128]{2,1,0:T(8,128)(2,1)} %bitcast.2), calls=%async_computation | async-start | bytes 262144 | tf_op jit(solution)/shard_map/all_to_all | solution.py:244
  12.6 4.5 %collective-permute-start = (bf16[128,512]{1,0:T(8,128)(2,1)}, bf16[128,512]{1,0:T(8,128)(2,1)S(1)}, u32[]{:S(2)}, u32[]{:S(2)}) collective-permute-start(bf16[128,512]{1,0:T(8,128)(2,1)} %value_ref.1), channel_id=1, source_target_pairs={{0,0},{1,64},{2,128},{3,192},{4,256},{5,320},{6,384},{7,448},{64,1... | collective-permute-start | bytes 393224 | tf_op jit(solution)/shard_map/ppermute | solution.py:240
  17.1 3.3 %gate_cotangent.1 = bf16[8,128,896]{2,1,0:T(8,128)(2,1)} custom-call(s32[1]{0:T(128)} %bitcast.1.place_ref, s32[64]{0:T(128)} %lengths_ref.1, bf16[128,896]{1,0:T(8,128)(2,1)} %gate_in.1, bf16[128,896]{1,0:T(8,128)(2,1)} %up_in.1, bf16[128,896]{1,0:T(8,128)(2,1)} %cotangent_in.1), custom_call_target="tpu_custom_call" | custom-call | flops 7340032 | bytes 45875200 | tf_op jit(solution)/shard_map/gate_cotangent/pallas_call | solution.py:58
  20.4 7.6 %collective-permute-done.value_ref = bf16[128,512]{1,0:T(8,128)(2,1)S(1)} collective-permute-done((bf16[128,512]{1,0:T(8,128)(2,1)}, bf16[128,512]{1,0:T(8,128)(2,1)S(1)}, u32[]{:S(2)}, u32[]{:S(2)}) %collective-permute-start) | collective-permute-done | bytes 131104 | tf_op jit(solution)/shard_map/ppermute | solution.py:240
  28.0 0.0 all-to-all-done
  28.0 5.7 %all-to-all-start.1 = ((bf16[8,128,896]{2,1,0:T(8,128)(2,1)}), bf16[8,128,896]{2,1,0:T(8,128)(2,1)S(1)}, u32[]{:S(2)}, u32[]{:S(2)}) async-start(bf16[8,128,896]{2,1,0:T(8,128)(2,1)} %gate_cotangent.1), calls=%async_computation.1 | async-start | bytes 3670016 | tf_op jit(solution)/shard_map/all_to_all | solution.py:248
  33.7 0.1 turn.3
  33.8 1.9 %collective-permute-start.1 = (bf16[512,128]{1,0:T(8,128)(2,1)S(1)}, bf16[512,128]{1,0:T(8,128)(2,1)S(1)}, u32[]{:S(2)}, u32[]{:S(2)}) collective-permute-start(bf16[512,128]{1,0:T(8,128)(2,1)S(1)} %get-tuple-element.15), channel_id=1, source_target_pairs={{0,1},{1,0},{2,3},{3,2},{4,5},{5,4},{6,7},{7,6},{8,9},{9,8},{10,11... | collective-permute-start | bytes 393224 | tf_op jit(solution)/shard_map/ppermute | solution.py:257
  35.8 1.3 %collective-permute-done.1 = bf16[512,128]{1,0:T(8,128)(2,1)S(1)} collective-permute-done((bf16[512,128]{1,0:T(8,128)(2,1)S(1)}, bf16[512,128]{1,0:T(8,128)(2,1)S(1)}, u32[]{:S(2)}, u32[]{:S(2)}) %collective-permute-start.1) | collective-permute-done | bytes 131104 | tf_op jit(solution)/shard_map/ppermute | solution.py:257
  37.1 3.8 %collective-permute-start.2 = (bf16[1024,128]{1,0:T(8,128)(2,1)S(1)}, bf16[1024,128]{1,0:T(8,128)(2,1)S(1)}, u32[]{:S(2)}, u32[]{:S(2)}) collective-permute-start(bf16[1024,128]{1,0:T(8,128)(2,1)S(1)} %pad_maximum_fusion.1), channel_id=1, source_target_pairs={{0,2},{1,7},{2,0},{3,5},{4,6},{5,3},{6,4},{7,1},{8,10},{9,15},{10,... | collective-permute-start | bytes 786440 | tf_op jit(solution)/shard_map/ppermute | solution.py:257
  40.9 4.5 %collective-permute-done.2 = bf16[1024,128]{1,0:T(8,128)(2,1)S(1)} collective-permute-done((bf16[1024,128]{1,0:T(8,128)(2,1)S(1)}, bf16[1024,128]{1,0:T(8,128)(2,1)S(1)}, u32[]{:S(2)}, u32[]{:S(2)}) %collective-permute-start.2) | collective-permute-done | bytes 262176 | tf_op jit(solution)/shard_map/ppermute | solution.py:257
  45.4 3.8 %collective-permute-start.3 = (bf16[2048,128]{1,0:T(8,128)(2,1)S(1)}, bf16[2048,128]{1,0:T(8,128)(2,1)S(1)}, u32[]{:S(2)}, u32[]{:S(2)}) collective-permute-start(bf16[2048,128]{1,0:T(8,128)(2,1)S(1)} %pad_maximum_fusion.first_ref), channel_id=1, source_target_pairs={{0,6},{1,3},{2,4},{3,1},{4,2},{5,7},{6,0},{7,5},{8,14},{9,11},{10,... | collective-permute-start | bytes 1572872 | tf_op jit(solution)/shard_map/ppermute | solution.py:257
  49.2 7.3 %collective-permute-done.3.second_ref = bf16[2048,128]{1,0:T(8,128)(2,1)S(1)} collective-permute-done((bf16[2048,128]{1,0:T(8,128)(2,1)S(1)}, bf16[2048,128]{1,0:T(8,128)(2,1)S(1)}, u32[]{:S(2)}, u32[]{:S(2)}) %collective-permute-start.3) | collective-permute-done | bytes 524320 | tf_op jit(solution)/shard_map/ppermute | solution.py:257
  56.5 4.7 %all-to-all-done.1 = bf16[8,128,896]{2,1,0:T(8,128)(2,1)S(1)} async-done(((bf16[8,128,896]{2,1,0:T(8,128)(2,1)}), bf16[8,128,896]{2,1,0:T(8,128)(2,1)S(1)}, u32[]{:S(2)}, u32[]{:S(2)}) %all-to-all-start.1) | async-done | bytes 1835040 | tf_op jit(solution)/shard_map/all_to_all | solution.py:248
  61.1 1.6 %partial_product.1 = bf16[512,896]{1,0:T(8,128)(2,1)S(1)} custom-call(s32[1]{0:T(128)} %bitcast.t_ref, bf16[2048,128]{1,0:T(8,128)(2,1)S(1)} %pad_maximum_fusion.first_ref, bf16[2048,128]{1,0:T(8,128)(2,1)S(1)} %collective-permute-done.3.second_ref, bf16[1024,896]{1,0:T(8,128)(2,1)S(1)} %bitcast.12), custom_call_target="tpu_custom_call" | custom-call | flops 939524096 | bytes 6000000 | tf_op jit(solution)/shard_map/partial_product/pallas_call | solution.py:147
  62.7 0.0 copy-start
  62.7 24.6 %all_to_all.30.parts_ref = bf16[8,64,896]{2,1,0:T(8,128)(2,1)S(1)} all-to-all(bf16[8,64,896]{2,1,0:T(8,128)(2,1)S(1)} %bitcast.13), channel_id=1, replica_groups={{0,8,16,24,32,40,48,56},{64,72,80,88,96,104,112,120},{128,136,144,152,1..., dimensions={0} | all-to-all | bytes 1835008 | tf_op jit(solution)/shard_map/all_to_all | solution.py:264
  87.3 0.0 copy-done
  87.3 0.9 momentum_step.1
  88.2 9.4 %all_to_all.31.grams_ref = f32[8,32,128]{2,1,0:T(8,128)S(1)} all-to-all(f32[8,32,128]{2,1,0:T(8,128)S(1)} %get-tuple-element.11), channel_id=1, replica_groups=mesh['y'=8,'z'=8,'t'=8] {'t'}, dimensions={0} | all-to-all | bytes 262144 | tf_op jit(solution)/shard_map/all_to_all | solution.py:268
  97.6 2.9 %polar_update.1 = bf16[8,64,112]{2,1,0:T(8,128)(2,1)S(1)} custom-call(f32[8,32,128]{2,1,0:T(8,128)S(1)} %all_to_all.31.grams_ref, f32[64,896]{1,0:T(8,128)S(1)} %get-tuple-element.12.block_ref), custom_call_target="tpu_custom_call" | custom-call | flops 100000000 | bytes 600000 | tf_op jit(solution)/shard_map/polar_update/pallas_call | solution.py:226
  100.4 12.6 %all_to_all.32 = bf16[8,64,112]{2,1,0:T(8,128)(2,1)S(1)} all-to-all(bf16[8,64,112]{2,1,0:T(8,128)(2,1)S(1)} %polar_update.1), channel_id=1, replica_groups=mesh['y'=8,'z'=8,'t'=8] {'y'}, dimensions={0} | all-to-all | bytes 229376 | tf_op jit(solution)/shard_map/all_to_all | solution.py:270
  113.1 0.2 copy.10
  113.3 0.2 reshape.36
  113.5 11.3 %all_to_all.33 = bf16[8,2,3584]{2,1,0:T(2,128)(2,1)S(1)} all-to-all(bf16[8,2,3584]{2,1,0:T(2,128)(2,1)S(1)} %reshape.36), channel_id=1, replica_groups=mesh['y'=8,'z'=8,'t'=8] {'z'}, dimensions={0} | all-to-all | bytes 229376 | tf_op jit(solution)/shard_map/all_to_all | solution.py:273
  124.7 0.2 reshape.37
  124.9 0.1 copy.11
  125.0 0.9 reshape.35
  (3 shorter events, 0.1 us)
Async XLA Ops:
  0.6 0.9 copy-start.1
  2.3 25.7 %all-to-all-start = ((bf16[8,64,128]{2,1,0:T(8,128)(2,1)}), bf16[8,64,128]{2,1,0:T(8,128)(2,1)S(1)}, u32[]{:S(2)}, u32[]{:S(2)}) async-start(bf16[8,64,128]{2,1,0:T(8,128)(2,1)} %bitcast.2), calls=%async_computation | async-start | bytes 262144 | tf_op jit(solution)/shard_map/all_to_all | solution.py:244
  12.6 15.4 %collective-permute-start = (bf16[128,512]{1,0:T(8,128)(2,1)}, bf16[128,512]{1,0:T(8,128)(2,1)S(1)}, u32[]{:S(2)}, u32[]{:S(2)}) collective-permute-start(bf16[128,512]{1,0:T(8,128)(2,1)} %value_ref.1), channel_id=1, source_target_pairs={{0,0},{1,64},{2,128},{3,192},{4,256},{5,320},{6,384},{7,448},{64,1... | collective-permute-start | bytes 393224 | tf_op jit(solution)/shard_map/ppermute | solution.py:240
  28.0 33.1 %all-to-all-start.1 = ((bf16[8,128,896]{2,1,0:T(8,128)(2,1)}), bf16[8,128,896]{2,1,0:T(8,128)(2,1)S(1)}, u32[]{:S(2)}, u32[]{:S(2)}) async-start(bf16[8,128,896]{2,1,0:T(8,128)(2,1)} %gate_cotangent.1), calls=%async_computation.1 | async-start | bytes 3670016 | tf_op jit(solution)/shard_map/all_to_all | solution.py:248
  33.8 3.2 %collective-permute-start.1 = (bf16[512,128]{1,0:T(8,128)(2,1)S(1)}, bf16[512,128]{1,0:T(8,128)(2,1)S(1)}, u32[]{:S(2)}, u32[]{:S(2)}) collective-permute-start(bf16[512,128]{1,0:T(8,128)(2,1)S(1)} %get-tuple-element.15), channel_id=1, source_target_pairs={{0,1},{1,0},{2,3},{3,2},{4,5},{5,4},{6,7},{7,6},{8,9},{9,8},{10,11... | collective-permute-start | bytes 393224 | tf_op jit(solution)/shard_map/ppermute | solution.py:257
  37.1 8.3 %collective-permute-start.2 = (bf16[1024,128]{1,0:T(8,128)(2,1)S(1)}, bf16[1024,128]{1,0:T(8,128)(2,1)S(1)}, u32[]{:S(2)}, u32[]{:S(2)}) collective-permute-start(bf16[1024,128]{1,0:T(8,128)(2,1)S(1)} %pad_maximum_fusion.1), channel_id=1, source_target_pairs={{0,2},{1,7},{2,0},{3,5},{4,6},{5,3},{6,4},{7,1},{8,10},{9,15},{10,... | collective-permute-start | bytes 786440 | tf_op jit(solution)/shard_map/ppermute | solution.py:257
  45.4 11.1 %collective-permute-start.3 = (bf16[2048,128]{1,0:T(8,128)(2,1)S(1)}, bf16[2048,128]{1,0:T(8,128)(2,1)S(1)}, u32[]{:S(2)}, u32[]{:S(2)}) collective-permute-start(bf16[2048,128]{1,0:T(8,128)(2,1)S(1)} %pad_maximum_fusion.first_ref), channel_id=1, source_target_pairs={{0,6},{1,3},{2,4},{3,1},{4,2},{5,7},{6,0},{7,5},{8,14},{9,11},{10,... | collective-permute-start | bytes 1572872 | tf_op jit(solution)/shard_map/ppermute | solution.py:257
  62.7 24.6 %copy-start = (f32[64,896]{1,0:T(8,128)S(1)}, f32[64,896]{1,0:T(8,128)}, u32[]{:S(2)}) copy-start(f32[64,896]{1,0:T(8,128)} %momentum_ref.1) | copy-start | bytes 688132

commit v17 on v16

--- a/solution.py
+++ b/solution.py
@@ -234,6 +234,15 @@
     )(grams, block)
 
 
+def exchange_whole(pieces):
+    return lax.all_to_all(pieces, "z", split_axis=0, concat_axis=0, tiled=True)
+
+
+def exchange_halves(pieces):
+    half = pieces.shape[1] // 2
+    return jnp.concatenate([exchange_whole(pieces[:, :half]), exchange_whole(pieces[:, half:])], axis=1)
+
+
 def per_device(features, gate_pre, up_pre, hidden_grad, lengths, momentum):
     y, z, t = (lax.axis_index(name) for name in AXES)
     swap = [(a * NT + b, b * NT + a) for a in range(NY) for b in range(NT)]
@@ -241,8 +250,8 @@
     turned = turn(features)
     copies = gate_cotangent(y * NZ + z, lengths, gate_pre, up_pre, hidden_grad)
 
-    by_blocks = lax.all_to_all(
-        turned.reshape(NZ, BLK, turned.shape[1]), "z", split_axis=0, concat_axis=0, tiled=True
+    by_blocks = lax.cond(
+        z < 2 * NZ, exchange_whole, exchange_halves, turned.reshape(NZ, BLK, turned.shape[1])
     ).reshape(turned.shape)
     copies, swapped, by_blocks = lax.optimization_barrier((copies, swapped, by_blocks))
     grads = lax.all_to_all(

time: 126 us -> 123 us (0.976)
  blocking collectives: 57.9 us -> 72.8 us
  starting transfers between devices: 30 us -> 18.4 us
  waiting for transfers between devices: 25.4 us -> 18.8 us
    all_to_all x0 -> x1, blocking collectives: none -> 20.5 us  [exchange_whole(): return lax.all_to_all(pieces, 'z', split_axis=0, concat_axis=0, tiled=True)]
    all_to_all x1 -> x0, starting transfers between devices: 10.3 us -> none  [per_device(): lax.all_to_all(turned.reshape(NZ, BLK, turned.shape[1]), 'z', split_axis=...]
    ppermute x1, waiting for transfers between devices: 7.64 us -> 0.01 us  [per_device(): swapped = lax.ppermute(features, ('y', 't'), swap)]
    all_to_all x1, blocking collectives: 24.6 us -> 20 us  [per_device(): lax.all_to_all(pieces, AXES, split_axis=0, concat_axis=0, axis_index_grou...]
  transfers between devices with their start and end apart: 6 -> 5, of which waited for: 5 -> 4; matrix products, arithmetic and copies ran while one was open for 0% -> 0% of each run, Pallas kernels for 3% -> 3%
where the time goes in v17:
time: 123 us; the launch traced here: 122 us
  blocking collectives  72.8 us (59%)
  waiting for transfers between devices  18.8 us (15%)
  starting transfers between devices  18.4 us (15%)
  Pallas kernels  8.78 us (7%)
  local copies, waits for them, and re-layouts  2.4 us (2%)
    all_to_all x1, blocking collectives, exchange_whole(): return lax.all_to_all(pieces, 'z', split_axis=0, concat_axis=0, tiled=True)  20.5 us
    all_to_all x1, blocking collectives, per_device(): lax.all_to_all(pieces, AXES, split_axis=0, concat_axis=0, axis_index_grou...  20 us
    ppermute x3, waiting for transfers between devices, per_device(): lax.ppermute(given if halves is None else kept, AXES, tensor_pairs(masks))  14.1 us
    all_to_all x1, blocking collectives, per_device(): by_y = lax.all_to_all(by_y, 'y', split_axis=0, concat_axis=0, tiled=True)  11.8 us
    all_to_all x1, blocking collectives, per_device(): by_z = lax.all_to_all(by_z, 'z', split_axis=0, concat_axis=0, tiled=True)  11.3 us
    all_to_all x1, blocking collectives, per_device(): grams = lax.all_to_all(grams, 't', split_axis=0, concat_axis=0, tiled=True)  9.19 us
    ppermute x3, starting transfers between devices, per_device(): lax.ppermute(given if halves is None else kept, AXES, tensor_pairs(masks))  8.43 us
    all_to_all x1, starting transfers between devices, per_device(): lax.all_to_all(copies, AXES, split_axis=0, concat_axis=0, axis_index_grou...  5.55 us
  transfers between devices with their start and end apart: 5, of which 4 were waited for; matrix products, arithmetic and copies ran while one was open for 0% of the time, Pallas kernels for 3%

profile of v17, /device:TPU:2, one launch (start us, length us, event | category | flops | bytes accessed | tf_op | source)
XLA Modules:
  0.0 122.1 jit_solution(16867769679680029914)
XLA Ops:
  0.6 4.5 %collective-permute-start = (bf16[128,512]{1,0:T(8,128)(2,1)}, bf16[128,512]{1,0:T(8,128)(2,1)S(1)}, u32[]{:S(2)}, u32[]{:S(2)}) collective-permute-start(bf16[128,512]{1,0:T(8,128)(2,1)} %value_ref.1), channel_id=1, source_target_pairs={{0,0},{1,64},{2,128},{3,192},{4,256},{5,320},{6,384},{7,448},{64,1... | collective-permute-start | bytes 393224 | tf_op jit(solution)/shard_map/ppermute | solution.py:249
  5.1 0.0 copy-start.1
  5.1 0.9 copy-done.1
  6.0 0.1 turn.2
  6.1 20.5 %conditional.1 = (bf16[512,128]{1,0:T(8,128)(2,1)S(1)}) conditional(s32[]{:T(128)} %convert_element_type.3, bf16[512,128]{1,0:T(8,128)(2,1)S(1)} %turn.2, bf16[512,128]{1,0:T(8,128)(2,1)S(1)} %turn.2), branch_computations={%region_0.0_spmd, %region_1.0_spmd} | conditional | bytes 786440 | solution.py:253
  6.1 20.5 %all_to_all.39 = bf16[8,64,128]{2,1,0:T(8,128)(2,1)S(1)} all-to-all(bf16[8,64,128]{2,1,0:T(8,128)(2,1)S(1)} %bitcast.17), channel_id=1, replica_groups=mesh['y'=8,'z'=8,'t'=8] {'z'}, dimensions={0} | all-to-all | bytes 262144 | tf_op jit(solution)/shard_map/cond/branch_1_fun/all_to_all | solution.py:238
  26.6 3.3 %gate_cotangent.1 = bf16[8,128,896]{2,1,0:T(8,128)(2,1)} custom-call(s32[1]{0:T(128)} %bitcast.5.place_ref, s32[64]{0:T(128)} %lengths_ref.1, bf16[128,896]{1,0:T(8,128)(2,1)} %gate_in.1, bf16[128,896]{1,0:T(8,128)(2,1)} %up_in.1, bf16[128,896]{1,0:T(8,128)(2,1)} %cotangent_in.1), custom_call_target="tpu_custom_call" | custom-call | flops 7340032 | bytes 45875200 | tf_op jit(solution)/shard_map/gate_cotangent/pallas_call | solution.py:58
  29.9 0.0 collective-permute-done.value_ref
  29.9 5.5 %all-to-all-start.3 = ((bf16[8,128,896]{2,1,0:T(8,128)(2,1)}), bf16[8,128,896]{2,1,0:T(8,128)(2,1)S(1)}, u32[]{:S(2)}, u32[]{:S(2)}) async-start(bf16[8,128,896]{2,1,0:T(8,128)(2,1)} %gate_cotangent.1), calls=%async_computation.3 | async-start | bytes 3670016 | tf_op jit(solution)/shard_map/all_to_all | solution.py:257
  35.5 0.1 turn.3
  35.6 1.9 %collective-permute-start.1 = (bf16[512,128]{1,0:T(8,128)(2,1)S(1)}, bf16[512,128]{1,0:T(8,128)(2,1)S(1)}, u32[]{:S(2)}, u32[]{:S(2)}) collective-permute-start(bf16[512,128]{1,0:T(8,128)(2,1)S(1)} %get-tuple-element.25), channel_id=1, source_target_pairs={{0,1},{1,0},{2,3},{3,2},{4,5},{5,4},{6,7},{7,6},{8,9},{9,8},{10,11... | collective-permute-start | bytes 393224 | tf_op jit(solution)/shard_map/ppermute | solution.py:266
  37.5 1.3 %collective-permute-done.1 = bf16[512,128]{1,0:T(8,128)(2,1)S(1)} collective-permute-done((bf16[512,128]{1,0:T(8,128)(2,1)S(1)}, bf16[512,128]{1,0:T(8,128)(2,1)S(1)}, u32[]{:S(2)}, u32[]{:S(2)}) %collective-permute-start.1) | collective-permute-done | bytes 131104 | tf_op jit(solution)/shard_map/ppermute | solution.py:266
  38.9 3.1 %collective-permute-start.2 = (bf16[1024,128]{1,0:T(8,128)(2,1)S(1)}, bf16[1024,128]{1,0:T(8,128)(2,1)S(1)}, u32[]{:S(2)}, u32[]{:S(2)}) collective-permute-start(bf16[1024,128]{1,0:T(8,128)(2,1)S(1)} %pad_maximum_fusion.2), channel_id=1, source_target_pairs={{0,2},{1,7},{2,0},{3,5},{4,6},{5,3},{6,4},{7,1},{8,10},{9,15},{10,... | collective-permute-start | bytes 786440 | tf_op jit(solution)/shard_map/ppermute | solution.py:266
  42.0 5.1 %collective-permute-done.2 = bf16[1024,128]{1,0:T(8,128)(2,1)S(1)} collective-permute-done((bf16[1024,128]{1,0:T(8,128)(2,1)S(1)}, bf16[1024,128]{1,0:T(8,128)(2,1)S(1)}, u32[]{:S(2)}, u32[]{:S(2)}) %collective-permute-start.2) | collective-permute-done | bytes 262176 | tf_op jit(solution)/shard_map/ppermute | solution.py:266
  47.2 3.4 %collective-permute-start.3 = (bf16[2048,128]{1,0:T(8,128)(2,1)S(1)}, bf16[2048,128]{1,0:T(8,128)(2,1)S(1)}, u32[]{:S(2)}, u32[]{:S(2)}) collective-permute-start(bf16[2048,128]{1,0:T(8,128)(2,1)S(1)} %pad_maximum_fusion.1.first_ref), channel_id=1, source_target_pairs={{0,6},{1,3},{2,4},{3,1},{4,2},{5,7},{6,0},{7,5},{8,14},{9,11},{10,... | collective-permute-start | bytes 1572872 | tf_op jit(solution)/shard_map/ppermute | solution.py:266
  50.6 7.7 %collective-permute-done.3.second_ref = bf16[2048,128]{1,0:T(8,128)(2,1)S(1)} collective-permute-done((bf16[2048,128]{1,0:T(8,128)(2,1)S(1)}, bf16[2048,128]{1,0:T(8,128)(2,1)S(1)}, u32[]{:S(2)}, u32[]{:S(2)}) %collective-permute-start.3) | collective-permute-done | bytes 524320 | tf_op jit(solution)/shard_map/ppermute | solution.py:266
  58.2 4.7 %all-to-all-done.3 = bf16[8,128,896]{2,1,0:T(8,128)(2,1)S(1)} async-done(((bf16[8,128,896]{2,1,0:T(8,128)(2,1)}), bf16[8,128,896]{2,1,0:T(8,128)(2,1)S(1)}, u32[]{:S(2)}, u32[]{:S(2)}) %all-to-all-start.3) | async-done | bytes 1835040 | tf_op jit(solution)/shard_map/all_to_all | solution.py:257
  62.9 1.6 %partial_product.1 = bf16[512,896]{1,0:T(8,128)(2,1)S(1)} custom-call(s32[1]{0:T(128)} %bitcast.4.t_ref, bf16[2048,128]{1,0:T(8,128)(2,1)S(1)} %pad_maximum_fusion.1.first_ref, bf16[2048,128]{1,0:T(8,128)(2,1)S(1)} %collective-permute-done.3.second_ref, bf16[1024,896]{1,0:T(8,128)(2,1)S(1)} %bitcast.14), custom_call_target="tpu_custom_call" | custom-call | flops 939524096 | bytes 6000000 | tf_op jit(solution)/shard_map/partial_product/pallas_call | solution.py:147
  64.5 0.0 copy-start
  64.5 20.0 %all_to_all.40.parts_ref = bf16[8,64,896]{2,1,0:T(8,128)(2,1)S(1)} all-to-all(bf16[8,64,896]{2,1,0:T(8,128)(2,1)S(1)} %bitcast.15), channel_id=1, replica_groups={{0,8,16,24,32,40,48,56},{64,72,80,88,96,104,112,120},{128,136,144,152,1..., dimensions={0} | all-to-all | bytes 1835008 | tf_op jit(solution)/shard_map/all_to_all | solution.py:273
  84.5 0.0 copy-done
  84.5 0.9 momentum_step.1
  85.4 9.2 %all_to_all.41.grams_ref = f32[8,32,128]{2,1,0:T(8,128)S(1)} all-to-all(f32[8,32,128]{2,1,0:T(8,128)S(1)} %get-tuple-element.19), channel_id=1, replica_groups=mesh['y'=8,'z'=8,'t'=8] {'t'}, dimensions={0} | all-to-all | bytes 262144 | tf_op jit(solution)/shard_map/all_to_all | solution.py:277
  94.6 2.9 %polar_update.1 = bf16[8,64,112]{2,1,0:T(8,128)(2,1)S(1)} custom-call(f32[8,32,128]{2,1,0:T(8,128)S(1)} %all_to_all.41.grams_ref, f32[64,896]{1,0:T(8,128)S(1)} %get-tuple-element.20.block_ref), custom_call_target="tpu_custom_call" | custom-call | flops 100000000 | bytes 600000 | tf_op jit(solution)/shard_map/polar_update/pallas_call | solution.py:226
  97.5 11.8 %all_to_all.42 = bf16[8,64,112]{2,1,0:T(8,128)(2,1)S(1)} all-to-all(bf16[8,64,112]{2,1,0:T(8,128)(2,1)S(1)} %polar_update.1), channel_id=1, replica_groups=mesh['y'=8,'z'=8,'t'=8] {'y'}, dimensions={0} | all-to-all | bytes 229376 | tf_op jit(solution)/shard_map/all_to_all | solution.py:279
  109.3 0.2 copy.10
  109.5 0.2 reshape.46
  109.7 11.3 %all_to_all.43 = bf16[8,2,3584]{2,1,0:T(2,128)(2,1)S(1)} all-to-all(bf16[8,2,3584]{2,1,0:T(2,128)(2,1)S(1)} %reshape.46), channel_id=1, replica_groups=mesh['y'=8,'z'=8,'t'=8] {'z'}, dimensions={0} | all-to-all | bytes 229376 | tf_op jit(solution)/shard_map/all_to_all | solution.py:282
  120.9 0.2 reshape.47
  121.1 0.1 copy.11
  121.2 0.9 reshape.45
  (3 shorter events, 0.1 us)
Async XLA Ops:
  0.6 29.3 %collective-permute-start = (bf16[128,512]{1,0:T(8,128)(2,1)}, bf16[128,512]{1,0:T(8,128)(2,1)S(1)}, u32[]{:S(2)}, u32[]{:S(2)}) collective-permute-start(bf16[128,512]{1,0:T(8,128)(2,1)} %value_ref.1), channel_id=1, source_target_pairs={{0,0},{1,64},{2,128},{3,192},{4,256},{5,320},{6,384},{7,448},{64,1... | collective-permute-start | bytes 393224 | tf_op jit(solution)/shard_map/ppermute | solution.py:249
  5.1 0.9 copy-start.1
  29.9 33.0 %all-to-all-start.3 = ((bf16[8,128,896]{2,1,0:T(8,128)(2,1)}), bf16[8,128,896]{2,1,0:T(8,128)(2,1)S(1)}, u32[]{:S(2)}, u32[]{:S(2)}) async-start(bf16[8,128,896]{2,1,0:T(8,128)(2,1)} %gate_cotangent.1), calls=%async_computation.3 | async-start | bytes 3670016 | tf_op jit(solution)/shard_map/all_to_all | solution.py:257
  35.6 3.2 %collective-permute-start.1 = (bf16[512,128]{1,0:T(8,128)(2,1)S(1)}, bf16[512,128]{1,0:T(8,128)(2,1)S(1)}, u32[]{:S(2)}, u32[]{:S(2)}) collective-permute-start(bf16[512,128]{1,0:T(8,128)(2,1)S(1)} %get-tuple-element.25), channel_id=1, source_target_pairs={{0,1},{1,0},{2,3},{3,2},{4,5},{5,4},{6,7},{7,6},{8,9},{9,8},{10,11... | collective-permute-start | bytes 393224 | tf_op jit(solution)/shard_map/ppermute | solution.py:266
  38.9 8.3 %collective-permute-start.2 = (bf16[1024,128]{1,0:T(8,128)(2,1)S(1)}, bf16[1024,128]{1,0:T(8,128)(2,1)S(1)}, u32[]{:S(2)}, u32[]{:S(2)}) collective-permute-start(bf16[1024,128]{1,0:T(8,128)(2,1)S(1)} %pad_maximum_fusion.2), channel_id=1, source_target_pairs={{0,2},{1,7},{2,0},{3,5},{4,6},{5,3},{6,4},{7,1},{8,10},{9,15},{10,... | collective-permute-start | bytes 786440 | tf_op jit(solution)/shard_map/ppermute | solution.py:266
  47.2 11.1 %collective-permute-start.3 = (bf16[2048,128]{1,0:T(8,128)(2,1)S(1)}, bf16[2048,128]{1,0:T(8,128)(2,1)S(1)}, u32[]{:S(2)}, u32[]{:S(2)}) collective-permute-start(bf16[2048,128]{1,0:T(8,128)(2,1)S(1)} %pad_maximum_fusion.1.first_ref), channel_id=1, source_target_pairs={{0,6},{1,3},{2,4},{3,1},{4,2},{5,7},{6,0},{7,5},{8,14},{9,11},{10,... | collective-permute-start | bytes 1572872 | tf_op jit(solution)/shard_map/ppermute | solution.py:266
  64.5 20.0 %copy-start = (f32[64,896]{1,0:T(8,128)S(1)}, f32[64,896]{1,0:T(8,128)}, u32[]{:S(2)}) copy-start(f32[64,896]{1,0:T(8,128)} %momentum_ref.1) | copy-start | bytes 688132

commit v18 on v17

--- a/solution.py
+++ b/solution.py
@@ -247,8 +247,8 @@
     y, z, t = (lax.axis_index(name) for name in AXES)
     swap = [(a * NT + b, b * NT + a) for a in range(NY) for b in range(NT)]
     swapped = lax.ppermute(features, ("y", "t"), swap)
-    turned = turn(features)
     copies = gate_cotangent(y * NZ + z, lengths, gate_pre, up_pre, hidden_grad)
+    turned, copies = lax.optimization_barrier((turn(features), copies))
 
     by_blocks = lax.cond(
         z < 2 * NZ, exchange_whole, exchange_halves, turned.reshape(NZ, BLK, turned.shape[1])

time: 123 us -> 123 us (level)
  no operation moved by 1% of the time
where the time goes in v18:
time: 123 us; the launch traced here: 122 us
  blocking collectives  72.8 us (59%)
  waiting for transfers between devices  18.8 us (15%)
  starting transfers between devices  18.4 us (15%)
  Pallas kernels  8.78 us (7%)
  local copies, waits for them, and re-layouts  2.4 us (2%)
    all_to_all x1, blocking collectives, exchange_whole(): return lax.all_to_all(pieces, 'z', split_axis=0, concat_axis=0, tiled=True)  20.5 us
    all_to_all x1, blocking collectives, per_device(): lax.all_to_all(pieces, AXES, split_axis=0, concat_axis=0, axis_index_grou...  20 us
    ppermute x3, waiting for transfers between devices, per_device(): lax.ppermute(given if halves is None else kept, AXES, tensor_pairs(masks))  14.1 us
    all_to_all x1, blocking collectives, per_device(): by_y = lax.all_to_all(by_y, 'y', split_axis=0, concat_axis=0, tiled=True)  11.8 us
    all_to_all x1, blocking collectives, per_device(): by_z = lax.all_to_all(by_z, 'z', split_axis=0, concat_axis=0, tiled=True)  11.3 us
    all_to_all x1, blocking collectives, per_device(): grams = lax.all_to_all(grams, 't', split_axis=0, concat_axis=0, tiled=True)  9.2 us
    ppermute x3, starting transfers between devices, per_device(): lax.ppermute(given if halves is None else kept, AXES, tensor_pairs(masks))  8.43 us
    all_to_all x1, starting transfers between devices, per_device(): lax.all_to_all(copies, AXES, split_axis=0, concat_axis=0, axis_index_grou...  5.54 us
  transfers between devices with their start and end apart: 5, of which 4 were waited for; matrix products, arithmetic and copies ran while one was open for 0% of the time, Pallas kernels for 3%

profile of v18, /device:TPU:2, one launch (start us, length us, event | category | flops | bytes accessed | tf_op | source)
XLA Modules:
  0.0 122.1 jit_solution(7550819628006611289)
XLA Ops:
  0.6 4.5 %collective-permute-start = (bf16[128,512]{1,0:T(8,128)(2,1)}, bf16[128,512]{1,0:T(8,128)(2,1)S(1)}, u32[]{:S(2)}, u32[]{:S(2)}) collective-permute-start(bf16[128,512]{1,0:T(8,128)(2,1)} %value_ref.1), channel_id=1, source_target_pairs={{0,0},{1,64},{2,128},{3,192},{4,256},{5,320},{6,384},{7,448},{64,1... | collective-permute-start | bytes 393224 | tf_op jit(solution)/shard_map/ppermute | solution.py:249
  5.1 0.0 copy-start.1
  5.1 0.9 copy-done.1
  6.0 0.1 turn.2
  6.1 3.3 %gate_cotangent.1 = bf16[8,128,896]{2,1,0:T(8,128)(2,1)} custom-call(s32[1]{0:T(128)} %bitcast.3.place_ref, s32[64]{0:T(128)} %lengths_ref.1, bf16[128,896]{1,0:T(8,128)(2,1)} %gate_in.1, bf16[128,896]{1,0:T(8,128)(2,1)} %up_in.1, bf16[128,896]{1,0:T(8,128)(2,1)} %cotangent_in.1), custom_call_target="tpu_custom_call" | custom-call | flops 7340032 | bytes 45875200 | tf_op jit(solution)/shard_map/gate_cotangent/pallas_call | solution.py:58
  9.4 20.5 %conditional.1 = (bf16[512,128]{1,0:T(8,128)(2,1)S(1)}) conditional(s32[]{:T(128)} %convert_element_type.3, bf16[8,64,128]{2,1,0:T(8,128)(2,1)S(1)} %bitcast.15, bf16[8,64,128]{2,1,0:T(8,128)(2,1)S(1)} %bitcast.16), branch_computations={%region_0.0_spmd, %region_1.0_spmd} | conditional | bytes 786440 | solution.py:253
  9.4 20.5 %all_to_all.39 = bf16[8,64,128]{2,1,0:T(8,128)(2,1)S(1)} all-to-all(bf16[8,64,128]{2,1,0:T(8,128)(2,1)S(1)} %param.1), channel_id=1, replica_groups=mesh['y'=8,'z'=8,'t'=8] {'z'}, dimensions={0} | all-to-all | bytes 262144 | tf_op jit(solution)/shard_map/cond/branch_1_fun/all_to_all | solution.py:238
  29.9 0.0 collective-permute-done.value_ref
  29.9 5.5 %all-to-all-start.3 = ((bf16[8,128,896]{2,1,0:T(8,128)(2,1)}), bf16[8,128,896]{2,1,0:T(8,128)(2,1)S(1)}, u32[]{:S(2)}, u32[]{:S(2)}) async-start(bf16[8,128,896]{2,1,0:T(8,128)(2,1)} %gate_cotangent.1), calls=%async_computation.3 | async-start | bytes 3670016 | tf_op jit(solution)/shard_map/all_to_all | solution.py:257
  35.5 0.1 turn.3
  35.6 1.9 %collective-permute-start.1 = (bf16[512,128]{1,0:T(8,128)(2,1)S(1)}, bf16[512,128]{1,0:T(8,128)(2,1)S(1)}, u32[]{:S(2)}, u32[]{:S(2)}) collective-permute-start(bf16[512,128]{1,0:T(8,128)(2,1)S(1)} %get-tuple-element.27), channel_id=1, source_target_pairs={{0,1},{1,0},{2,3},{3,2},{4,5},{5,4},{6,7},{7,6},{8,9},{9,8},{10,11... | collective-permute-start | bytes 393224 | tf_op jit(solution)/shard_map/ppermute | solution.py:266
  37.5 1.3 %collective-permute-done.1 = bf16[512,128]{1,0:T(8,128)(2,1)S(1)} collective-permute-done((bf16[512,128]{1,0:T(8,128)(2,1)S(1)}, bf16[512,128]{1,0:T(8,128)(2,1)S(1)}, u32[]{:S(2)}, u32[]{:S(2)}) %collective-permute-start.1) | collective-permute-done | bytes 131104 | tf_op jit(solution)/shard_map/ppermute | solution.py:266
  38.8 3.1 %collective-permute-start.2 = (bf16[1024,128]{1,0:T(8,128)(2,1)S(1)}, bf16[1024,128]{1,0:T(8,128)(2,1)S(1)}, u32[]{:S(2)}, u32[]{:S(2)}) collective-permute-start(bf16[1024,128]{1,0:T(8,128)(2,1)S(1)} %pad_maximum_fusion.2), channel_id=1, source_target_pairs={{0,2},{1,7},{2,0},{3,5},{4,6},{5,3},{6,4},{7,1},{8,10},{9,15},{10,... | collective-permute-start | bytes 786440 | tf_op jit(solution)/shard_map/ppermute | solution.py:266
  42.0 5.1 %collective-permute-done.2 = bf16[1024,128]{1,0:T(8,128)(2,1)S(1)} collective-permute-done((bf16[1024,128]{1,0:T(8,128)(2,1)S(1)}, bf16[1024,128]{1,0:T(8,128)(2,1)S(1)}, u32[]{:S(2)}, u32[]{:S(2)}) %collective-permute-start.2) | collective-permute-done | bytes 262176 | tf_op jit(solution)/shard_map/ppermute | solution.py:266
  47.1 3.4 %collective-permute-start.3 = (bf16[2048,128]{1,0:T(8,128)(2,1)S(1)}, bf16[2048,128]{1,0:T(8,128)(2,1)S(1)}, u32[]{:S(2)}, u32[]{:S(2)}) collective-permute-start(bf16[2048,128]{1,0:T(8,128)(2,1)S(1)} %pad_maximum_fusion.1.first_ref), channel_id=1, source_target_pairs={{0,6},{1,3},{2,4},{3,1},{4,2},{5,7},{6,0},{7,5},{8,14},{9,11},{10,... | collective-permute-start | bytes 1572872 | tf_op jit(solution)/shard_map/ppermute | solution.py:266
  50.5 7.7 %collective-permute-done.3.second_ref = bf16[2048,128]{1,0:T(8,128)(2,1)S(1)} collective-permute-done((bf16[2048,128]{1,0:T(8,128)(2,1)S(1)}, bf16[2048,128]{1,0:T(8,128)(2,1)S(1)}, u32[]{:S(2)}, u32[]{:S(2)}) %collective-permute-start.3) | collective-permute-done | bytes 524320 | tf_op jit(solution)/shard_map/ppermute | solution.py:266
  58.2 4.7 %all-to-all-done.3 = bf16[8,128,896]{2,1,0:T(8,128)(2,1)S(1)} async-done(((bf16[8,128,896]{2,1,0:T(8,128)(2,1)}), bf16[8,128,896]{2,1,0:T(8,128)(2,1)S(1)}, u32[]{:S(2)}, u32[]{:S(2)}) %all-to-all-start.3) | async-done | bytes 1835040 | tf_op jit(solution)/shard_map/all_to_all | solution.py:257
  62.9 1.6 %partial_product.1 = bf16[512,896]{1,0:T(8,128)(2,1)S(1)} custom-call(s32[1]{0:T(128)} %bitcast.2.t_ref, bf16[2048,128]{1,0:T(8,128)(2,1)S(1)} %pad_maximum_fusion.1.first_ref, bf16[2048,128]{1,0:T(8,128)(2,1)S(1)} %collective-permute-done.3.second_ref, bf16[1024,896]{1,0:T(8,128)(2,1)S(1)} %bitcast.13), custom_call_target="tpu_custom_call" | custom-call | flops 939524096 | bytes 6000000 | tf_op jit(solution)/shard_map/partial_product/pallas_call | solution.py:147
  64.5 0.0 copy-start
  64.5 20.0 %all_to_all.40.parts_ref = bf16[8,64,896]{2,1,0:T(8,128)(2,1)S(1)} all-to-all(bf16[8,64,896]{2,1,0:T(8,128)(2,1)S(1)} %bitcast.14), channel_id=1, replica_groups={{0,8,16,24,32,40,48,56},{64,72,80,88,96,104,112,120},{128,136,144,152,1..., dimensions={0} | all-to-all | bytes 1835008 | tf_op jit(solution)/shard_map/all_to_all | solution.py:273
  84.5 0.0 copy-done
  84.5 0.9 momentum_step.1
  85.4 9.2 %all_to_all.41.grams_ref = f32[8,32,128]{2,1,0:T(8,128)S(1)} all-to-all(f32[8,32,128]{2,1,0:T(8,128)S(1)} %get-tuple-element.21), channel_id=1, replica_groups=mesh['y'=8,'z'=8,'t'=8] {'t'}, dimensions={0} | all-to-all | bytes 262144 | tf_op jit(solution)/shard_map/all_to_all | solution.py:277
  94.6 2.9 %polar_update.1 = bf16[8,64,112]{2,1,0:T(8,128)(2,1)S(1)} custom-call(f32[8,32,128]{2,1,0:T(8,128)S(1)} %all_to_all.41.grams_ref, f32[64,896]{1,0:T(8,128)S(1)} %get-tuple-element.22.block_ref), custom_call_target="tpu_custom_call" | custom-call | flops 100000000 | bytes 600000 | tf_op jit(solution)/shard_map/polar_update/pallas_call | solution.py:226
  97.5 11.8 %all_to_all.42 = bf16[8,64,112]{2,1,0:T(8,128)(2,1)S(1)} all-to-all(bf16[8,64,112]{2,1,0:T(8,128)(2,1)S(1)} %polar_update.1), channel_id=1, replica_groups=mesh['y'=8,'z'=8,'t'=8] {'y'}, dimensions={0} | all-to-all | bytes 229376 | tf_op jit(solution)/shard_map/all_to_all | solution.py:279
  109.3 0.2 copy.10
  109.5 0.2 reshape.45
  109.6 11.3 %all_to_all.43 = bf16[8,2,3584]{2,1,0:T(2,128)(2,1)S(1)} all-to-all(bf16[8,2,3584]{2,1,0:T(2,128)(2,1)S(1)} %reshape.45), channel_id=1, replica_groups=mesh['y'=8,'z'=8,'t'=8] {'z'}, dimensions={0} | all-to-all | bytes 229376 | tf_op jit(solution)/shard_map/all_to_all | solution.py:282
  120.9 0.2 reshape.46
  121.1 0.1 copy.11
  121.2 0.9 reshape.44
  (3 shorter events, 0.1 us)
Async XLA Ops:
  0.6 29.3 %collective-permute-start = (bf16[128,512]{1,0:T(8,128)(2,1)}, bf16[128,512]{1,0:T(8,128)(2,1)S(1)}, u32[]{:S(2)}, u32[]{:S(2)}) collective-permute-start(bf16[128,512]{1,0:T(8,128)(2,1)} %value_ref.1), channel_id=1, source_target_pairs={{0,0},{1,64},{2,128},{3,192},{4,256},{5,320},{6,384},{7,448},{64,1... | collective-permute-start | bytes 393224 | tf_op jit(solution)/shard_map/ppermute | solution.py:249
  5.1 0.9 copy-start.1
  29.9 33.0 %all-to-all-start.3 = ((bf16[8,128,896]{2,1,0:T(8,128)(2,1)}), bf16[8,128,896]{2,1,0:T(8,128)(2,1)S(1)}, u32[]{:S(2)}, u32[]{:S(2)}) async-start(bf16[8,128,896]{2,1,0:T(8,128)(2,1)} %gate_cotangent.1), calls=%async_computation.3 | async-start | bytes 3670016 | tf_op jit(solution)/shard_map/all_to_all | solution.py:257
  35.6 3.2 %collective-permute-start.1 = (bf16[512,128]{1,0:T(8,128)(2,1)S(1)}, bf16[512,128]{1,0:T(8,128)(2,1)S(1)}, u32[]{:S(2)}, u32[]{:S(2)}) collective-permute-start(bf16[512,128]{1,0:T(8,128)(2,1)S(1)} %get-tuple-element.27), channel_id=1, source_target_pairs={{0,1},{1,0},{2,3},{3,2},{4,5},{5,4},{6,7},{7,6},{8,9},{9,8},{10,11... | collective-permute-start | bytes 393224 | tf_op jit(solution)/shard_map/ppermute | solution.py:266
  38.8 8.3 %collective-permute-start.2 = (bf16[1024,128]{1,0:T(8,128)(2,1)S(1)}, bf16[1024,128]{1,0:T(8,128)(2,1)S(1)}, u32[]{:S(2)}, u32[]{:S(2)}) collective-permute-start(bf16[1024,128]{1,0:T(8,128)(2,1)S(1)} %pad_maximum_fusion.2), channel_id=1, source_target_pairs={{0,2},{1,7},{2,0},{3,5},{4,6},{5,3},{6,4},{7,1},{8,10},{9,15},{10,... | collective-permute-start | bytes 786440 | tf_op jit(solution)/shard_map/ppermute | solution.py:266
  47.1 11.1 %collective-permute-start.3 = (bf16[2048,128]{1,0:T(8,128)(2,1)S(1)}, bf16[2048,128]{1,0:T(8,128)(2,1)S(1)}, u32[]{:S(2)}, u32[]{:S(2)}) collective-permute-start(bf16[2048,128]{1,0:T(8,128)(2,1)S(1)} %pad_maximum_fusion.1.first_ref), channel_id=1, source_target_pairs={{0,6},{1,3},{2,4},{3,1},{4,2},{5,7},{6,0},{7,5},{8,14},{9,11},{10,... | collective-permute-start | bytes 1572872 | tf_op jit(solution)/shard_map/ppermute | solution.py:266
  64.5 20.0 %copy-start = (f32[64,896]{1,0:T(8,128)S(1)}, f32[64,896]{1,0:T(8,128)}, u32[]{:S(2)}) copy-start(f32[64,896]{1,0:T(8,128)} %momentum_ref.1) | copy-start | bytes 688132

commit v19 on v17

--- a/solution.py
+++ b/solution.py
@@ -28,40 +28,56 @@
 AXES = ("y", "z", "t")
 
 
-def gate_kernel(place_ref, lengths_ref, gate_in, up_in, cotangent_in, copies_ref, *scratch):
-    buffers, arrived = scratch[:3], scratch[3]
+def gate_kernel(place_ref, lengths_ref, gate_in, up_in, cotangent_in, copies_out, *scratch):
+    buffers, result, arrived, written = scratch[:3], scratch[3], scratch[4], scratch[5]
     sources = (gate_in, up_in, cotangent_in)
-    copies = [
-        pltpu.make_async_copy(source, buffer, arrived.at[i])
-        for i, (source, buffer) in enumerate(zip(sources, buffers))
+    half = result.shape[0] // 2
+    rows = [pl.ds(part * half, half) for part in range(2)]
+    loads = [
+        [
+            pltpu.make_async_copy(source.at[rows[part]], buffer.at[rows[part]], arrived.at[part, i])
+            for i, (source, buffer) in enumerate(zip(sources, buffers))
+        ]
+        for part in range(2)
     ]
-    for copy in copies:
-        copy.start()
-    for copy in copies:
-        copy.wait()
-    gate_value, up_value, cotangent = (buffer[...].astype(jnp.float32) for buffer in buffers)
-    sigmoid_gate = jax.nn.sigmoid(gate_value)
-    gate_grad = cotangent * up_value * sigmoid_gate * (1.0 + gate_value * (1.0 - sigmoid_gate))
-    position = lax.broadcasted_iota(jnp.int32, gate_value.shape, 0)
-    trained = position < lengths_ref[place_ref[0]]
-    gate_grad = jnp.where(trained, gate_grad, 0.0).astype(copies_ref.dtype)
-    for part in range(copies_ref.shape[0]):
-        copies_ref[part] = gate_grad
+    for load in loads[0] + loads[1]:
+        load.start()
+    limit = lengths_ref[place_ref[0]]
+    stores = []
+    for part in range(2):
+        for load in loads[part]:
+            load.wait()
+        gate_value, up_value, cotangent = (buffer[rows[part], :].astype(jnp.float32) for buffer in buffers)
+        sigmoid_gate = jax.nn.sigmoid(gate_value)
+        gate_grad = cotangent * up_value * sigmoid_gate * (1.0 + gate_value * (1.0 - sigmoid_gate))
+        position = lax.broadcasted_iota(jnp.int32, gate_value.shape, 0) + part * half
+        result[rows[part], :] = jnp.where(position < limit, gate_grad, 0.0).astype(result.dtype)
+        for peer in range(copies_out.shape[0]):
+            store = pltpu.make_async_copy(
+                result.at[rows[part]], copies_out.at[peer, rows[part]], written.at[part, peer]
+            )
+            store.start()
+            stores.append(store)
+    for store in stores:
+        store.wait()
 
 
 def gate_cotangent(place, lengths, gate_pre, up_pre, hidden_grad):
     tokens, columns = gate_pre.shape
     hbm = pl.BlockSpec(memory_space=pltpu.HBM)
-    vmem = pl.BlockSpec(memory_space=pltpu.VMEM)
     smem = pl.BlockSpec(memory_space=pltpu.SMEM)
     arrays = (gate_pre, up_pre, hidden_grad)
     return pl.pallas_call(
         gate_kernel,
         out_shape=jax.ShapeDtypeStruct((NZ, tokens, columns), jnp.bfloat16),
         in_specs=[smem, smem] + [hbm] * 3,
-        out_specs=vmem,
+        out_specs=hbm,
         scratch_shapes=[pltpu.VMEM(array.shape, array.dtype) for array in arrays]
-        + [pltpu.SemaphoreType.DMA((3,))],
+        + [
+            pltpu.VMEM((tokens, columns), jnp.bfloat16),
+            pltpu.SemaphoreType.DMA((2, 3)),
+            pltpu.SemaphoreType.DMA((2, NZ)),
+        ],
         compiler_params=pltpu.CompilerParams(vmem_limit_bytes=60 * 1024 * 1024),
         cost_estimate=pl.CostEstimate(
             flops=64 * tokens * columns, bytes_accessed=400 * tokens * columns, transcendentals=tokens * columns

time: 123 us -> 123 us (level)
  no operation moved by 1% of the time
where the time goes in v19:
time: 123 us; the launch traced here: 122 us
  blocking collectives  72.8 us (59%)
  waiting for transfers between devices  18.8 us (15%)
  starting transfers between devices  18.4 us (15%)
  Pallas kernels  8.68 us (7%)
  local copies, waits for them, and re-layouts  2.4 us (2%)
    all_to_all x1, blocking collectives, exchange_whole(): return lax.all_to_all(pieces, 'z', split_axis=0, concat_axis=0, tiled=True)  20.5 us
    all_to_all x1, blocking collectives, per_device(): lax.all_to_all(pieces, AXES, split_axis=0, concat_axis=0, axis_index_grou...  20 us
    ppermute x3, waiting for transfers between devices, per_device(): lax.ppermute(given if halves is None else kept, AXES, tensor_pairs(masks))  14.1 us
    all_to_all x1, blocking collectives, per_device(): by_y = lax.all_to_all(by_y, 'y', split_axis=0, concat_axis=0, tiled=True)  11.8 us
    all_to_all x1, blocking collectives, per_device(): by_z = lax.all_to_all(by_z, 'z', split_axis=0, concat_axis=0, tiled=True)  11.3 us
    all_to_all x1, blocking collectives, per_device(): grams = lax.all_to_all(grams, 't', split_axis=0, concat_axis=0, tiled=True)  9.19 us
    ppermute x3, starting transfers between devices, per_device(): lax.ppermute(given if halves is None else kept, AXES, tensor_pairs(masks))  8.43 us
    all_to_all x1, starting transfers between devices, per_device(): lax.all_to_all(copies, AXES, split_axis=0, concat_axis=0, axis_index_grou...  5.55 us
  transfers between devices with their start and end apart: 5, of which 4 were waited for; matrix products, arithmetic and copies ran while one was open for 0% of the time, Pallas kernels for 3%

profile of v19, /device:TPU:2, one launch (start us, length us, event | category | flops | bytes accessed | tf_op | source)
XLA Modules:
  0.0 122.0 jit_solution(14155832008071887554)
XLA Ops:
  0.6 4.5 %collective-permute-start = (bf16[128,512]{1,0:T(8,128)(2,1)}, bf16[128,512]{1,0:T(8,128)(2,1)S(1)}, u32[]{:S(2)}, u32[]{:S(2)}) collective-permute-start(bf16[128,512]{1,0:T(8,128)(2,1)} %value_ref.1), channel_id=1, source_target_pairs={{0,0},{1,64},{2,128},{3,192},{4,256},{5,320},{6,384},{7,448},{64,1... | collective-permute-start | bytes 393224 | tf_op jit(solution)/shard_map/ppermute | solution.py:265
  5.1 0.0 copy-start.1
  5.1 0.9 copy-done.1
  6.0 0.1 turn.2
  6.1 20.5 %conditional.1 = (bf16[512,128]{1,0:T(8,128)(2,1)S(1)}) conditional(s32[]{:T(128)} %convert_element_type.3, bf16[512,128]{1,0:T(8,128)(2,1)S(1)} %turn.2, bf16[512,128]{1,0:T(8,128)(2,1)S(1)} %turn.2), branch_computations={%region_0.0_spmd, %region_1.0_spmd} | conditional | bytes 786440 | solution.py:269
  6.1 20.5 %all_to_all.39 = bf16[8,64,128]{2,1,0:T(8,128)(2,1)S(1)} all-to-all(bf16[8,64,128]{2,1,0:T(8,128)(2,1)S(1)} %bitcast.17), channel_id=1, replica_groups=mesh['y'=8,'z'=8,'t'=8] {'z'}, dimensions={0} | all-to-all | bytes 262144 | tf_op jit(solution)/shard_map/cond/branch_1_fun/all_to_all | solution.py:254
  26.6 3.2 %gate_cotangent.1 = bf16[8,128,896]{2,1,0:T(8,128)(2,1)} custom-call(s32[1]{0:T(128)} %bitcast.5.place_ref, s32[64]{0:T(128)} %lengths_ref.1, bf16[128,896]{1,0:T(8,128)(2,1)} %gate_in.1, bf16[128,896]{1,0:T(8,128)(2,1)} %up_in.1, bf16[128,896]{1,0:T(8,128)(2,1)} %cotangent_in.1), custom_call_target="tpu_custom_call" | custom-call | flops 7340032 | bytes 45875200 | tf_op jit(solution)/shard_map/gate_cotangent/pallas_call | solution.py:70
  29.8 0.0 collective-permute-done.value_ref
  29.8 5.5 %all-to-all-start.3 = ((bf16[8,128,896]{2,1,0:T(8,128)(2,1)}), bf16[8,128,896]{2,1,0:T(8,128)(2,1)S(1)}, u32[]{:S(2)}, u32[]{:S(2)}) async-start(bf16[8,128,896]{2,1,0:T(8,128)(2,1)} %gate_cotangent.1), calls=%async_computation.3 | async-start | bytes 3670016 | tf_op jit(solution)/shard_map/all_to_all | solution.py:273
  35.4 0.1 turn.3
  35.5 1.9 %collective-permute-start.1 = (bf16[512,128]{1,0:T(8,128)(2,1)S(1)}, bf16[512,128]{1,0:T(8,128)(2,1)S(1)}, u32[]{:S(2)}, u32[]{:S(2)}) collective-permute-start(bf16[512,128]{1,0:T(8,128)(2,1)S(1)} %get-tuple-element.25), channel_id=1, source_target_pairs={{0,1},{1,0},{2,3},{3,2},{4,5},{5,4},{6,7},{7,6},{8,9},{9,8},{10,11... | collective-permute-start | bytes 393224 | tf_op jit(solution)/shard_map/ppermute | solution.py:282
  37.4 1.3 %collective-permute-done.1 = bf16[512,128]{1,0:T(8,128)(2,1)S(1)} collective-permute-done((bf16[512,128]{1,0:T(8,128)(2,1)S(1)}, bf16[512,128]{1,0:T(8,128)(2,1)S(1)}, u32[]{:S(2)}, u32[]{:S(2)}) %collective-permute-start.1) | collective-permute-done | bytes 131104 | tf_op jit(solution)/shard_map/ppermute | solution.py:282
  38.8 3.1 %collective-permute-start.2 = (bf16[1024,128]{1,0:T(8,128)(2,1)S(1)}, bf16[1024,128]{1,0:T(8,128)(2,1)S(1)}, u32[]{:S(2)}, u32[]{:S(2)}) collective-permute-start(bf16[1024,128]{1,0:T(8,128)(2,1)S(1)} %pad_maximum_fusion.2), channel_id=1, source_target_pairs={{0,2},{1,7},{2,0},{3,5},{4,6},{5,3},{6,4},{7,1},{8,10},{9,15},{10,... | collective-permute-start | bytes 786440 | tf_op jit(solution)/shard_map/ppermute | solution.py:282
  41.9 5.1 %collective-permute-done.2 = bf16[1024,128]{1,0:T(8,128)(2,1)S(1)} collective-permute-done((bf16[1024,128]{1,0:T(8,128)(2,1)S(1)}, bf16[1024,128]{1,0:T(8,128)(2,1)S(1)}, u32[]{:S(2)}, u32[]{:S(2)}) %collective-permute-start.2) | collective-permute-done | bytes 262176 | tf_op jit(solution)/shard_map/ppermute | solution.py:282
  47.1 3.4 %collective-permute-start.3 = (bf16[2048,128]{1,0:T(8,128)(2,1)S(1)}, bf16[2048,128]{1,0:T(8,128)(2,1)S(1)}, u32[]{:S(2)}, u32[]{:S(2)}) collective-permute-start(bf16[2048,128]{1,0:T(8,128)(2,1)S(1)} %pad_maximum_fusion.1.first_ref), channel_id=1, source_target_pairs={{0,6},{1,3},{2,4},{3,1},{4,2},{5,7},{6,0},{7,5},{8,14},{9,11},{10,... | collective-permute-start | bytes 1572872 | tf_op jit(solution)/shard_map/ppermute | solution.py:282
  50.5 7.7 %collective-permute-done.3.second_ref = bf16[2048,128]{1,0:T(8,128)(2,1)S(1)} collective-permute-done((bf16[2048,128]{1,0:T(8,128)(2,1)S(1)}, bf16[2048,128]{1,0:T(8,128)(2,1)S(1)}, u32[]{:S(2)}, u32[]{:S(2)}) %collective-permute-start.3) | collective-permute-done | bytes 524320 | tf_op jit(solution)/shard_map/ppermute | solution.py:282
  58.1 4.7 %all-to-all-done.3 = bf16[8,128,896]{2,1,0:T(8,128)(2,1)S(1)} async-done(((bf16[8,128,896]{2,1,0:T(8,128)(2,1)}), bf16[8,128,896]{2,1,0:T(8,128)(2,1)S(1)}, u32[]{:S(2)}, u32[]{:S(2)}) %all-to-all-start.3) | async-done | bytes 1835040 | tf_op jit(solution)/shard_map/all_to_all | solution.py:273
  62.8 1.6 %partial_product.1 = bf16[512,896]{1,0:T(8,128)(2,1)S(1)} custom-call(s32[1]{0:T(128)} %bitcast.4.t_ref, bf16[2048,128]{1,0:T(8,128)(2,1)S(1)} %pad_maximum_fusion.1.first_ref, bf16[2048,128]{1,0:T(8,128)(2,1)S(1)} %collective-permute-done.3.second_ref, bf16[1024,896]{1,0:T(8,128)(2,1)S(1)} %bitcast.14), custom_call_target="tpu_custom_call" | custom-call | flops 939524096 | bytes 6000000 | tf_op jit(solution)/shard_map/partial_product/pallas_call | solution.py:163
  64.4 0.0 copy-start
  64.4 20.0 %all_to_all.40.parts_ref = bf16[8,64,896]{2,1,0:T(8,128)(2,1)S(1)} all-to-all(bf16[8,64,896]{2,1,0:T(8,128)(2,1)S(1)} %bitcast.15), channel_id=1, replica_groups={{0,8,16,24,32,40,48,56},{64,72,80,88,96,104,112,120},{128,136,144,152,1..., dimensions={0} | all-to-all | bytes 1835008 | tf_op jit(solution)/shard_map/all_to_all | solution.py:289
  84.4 0.0 copy-done
  84.4 0.9 momentum_step.1
  85.3 9.2 %all_to_all.41.grams_ref = f32[8,32,128]{2,1,0:T(8,128)S(1)} all-to-all(f32[8,32,128]{2,1,0:T(8,128)S(1)} %get-tuple-element.19), channel_id=1, replica_groups=mesh['y'=8,'z'=8,'t'=8] {'t'}, dimensions={0} | all-to-all | bytes 262144 | tf_op jit(solution)/shard_map/all_to_all | solution.py:293
  94.5 2.9 %polar_update.1 = bf16[8,64,112]{2,1,0:T(8,128)(2,1)S(1)} custom-call(f32[8,32,128]{2,1,0:T(8,128)S(1)} %all_to_all.41.grams_ref, f32[64,896]{1,0:T(8,128)S(1)} %get-tuple-element.20.block_ref), custom_call_target="tpu_custom_call" | custom-call | flops 100000000 | bytes 600000 | tf_op jit(solution)/shard_map/polar_update/pallas_call | solution.py:242
  97.4 11.8 %all_to_all.42 = bf16[8,64,112]{2,1,0:T(8,128)(2,1)S(1)} all-to-all(bf16[8,64,112]{2,1,0:T(8,128)(2,1)S(1)} %polar_update.1), channel_id=1, replica_groups=mesh['y'=8,'z'=8,'t'=8] {'y'}, dimensions={0} | all-to-all | bytes 229376 | tf_op jit(solution)/shard_map/all_to_all | solution.py:295
  109.2 0.2 copy.10
  109.4 0.2 reshape.46
  109.6 11.3 %all_to_all.43 = bf16[8,2,3584]{2,1,0:T(2,128)(2,1)S(1)} all-to-all(bf16[8,2,3584]{2,1,0:T(2,128)(2,1)S(1)} %reshape.46), channel_id=1, replica_groups=mesh['y'=8,'z'=8,'t'=8] {'z'}, dimensions={0} | all-to-all | bytes 229376 | tf_op jit(solution)/shard_map/all_to_all | solution.py:298
  120.8 0.2 reshape.47
  121.0 0.1 copy.11
  121.1 0.9 reshape.45
  (3 shorter events, 0.1 us)
Async XLA Ops:
  0.6 29.2 %collective-permute-start = (bf16[128,512]{1,0:T(8,128)(2,1)}, bf16[128,512]{1,0:T(8,128)(2,1)S(1)}, u32[]{:S(2)}, u32[]{:S(2)}) collective-permute-start(bf16[128,512]{1,0:T(8,128)(2,1)} %value_ref.1), channel_id=1, source_target_pairs={{0,0},{1,64},{2,128},{3,192},{4,256},{5,320},{6,384},{7,448},{64,1... | collective-permute-start | bytes 393224 | tf_op jit(solution)/shard_map/ppermute | solution.py:265
  5.1 0.9 copy-start.1
  29.8 33.0 %all-to-all-start.3 = ((bf16[8,128,896]{2,1,0:T(8,128)(2,1)}), bf16[8,128,896]{2,1,0:T(8,128)(2,1)S(1)}, u32[]{:S(2)}, u32[]{:S(2)}) async-start(bf16[8,128,896]{2,1,0:T(8,128)(2,1)} %gate_cotangent.1), calls=%async_computation.3 | async-start | bytes 3670016 | tf_op jit(solution)/shard_map/all_to_all | solution.py:273
  35.5 3.2 %collective-permute-start.1 = (bf16[512,128]{1,0:T(8,128)(2,1)S(1)}, bf16[512,128]{1,0:T(8,128)(2,1)S(1)}, u32[]{:S(2)}, u32[]{:S(2)}) collective-permute-start(bf16[512,128]{1,0:T(8,128)(2,1)S(1)} %get-tuple-element.25), channel_id=1, source_target_pairs={{0,1},{1,0},{2,3},{3,2},{4,5},{5,4},{6,7},{7,6},{8,9},{9,8},{10,11... | collective-permute-start | bytes 393224 | tf_op jit(solution)/shard_map/ppermute | solution.py:282
  38.8 8.3 %collective-permute-start.2 = (bf16[1024,128]{1,0:T(8,128)(2,1)S(1)}, bf16[1024,128]{1,0:T(8,128)(2,1)S(1)}, u32[]{:S(2)}, u32[]{:S(2)}) collective-permute-start(bf16[1024,128]{1,0:T(8,128)(2,1)S(1)} %pad_maximum_fusion.2), channel_id=1, source_target_pairs={{0,2},{1,7},{2,0},{3,5},{4,6},{5,3},{6,4},{7,1},{8,10},{9,15},{10,... | collective-permute-start | bytes 786440 | tf_op jit(solution)/shard_map/ppermute | solution.py:282
  47.1 11.1 %collective-permute-start.3 = (bf16[2048,128]{1,0:T(8,128)(2,1)S(1)}, bf16[2048,128]{1,0:T(8,128)(2,1)S(1)}, u32[]{:S(2)}, u32[]{:S(2)}) collective-permute-start(bf16[2048,128]{1,0:T(8,128)(2,1)S(1)} %pad_maximum_fusion.1.first_ref), channel_id=1, source_target_pairs={{0,6},{1,3},{2,4},{3,1},{4,2},{5,7},{6,0},{7,5},{8,14},{9,11},{10,... | collective-permute-start | bytes 1572872 | tf_op jit(solution)/shard_map/ppermute | solution.py:282
  64.4 20.0 %copy-start = (f32[64,896]{1,0:T(8,128)S(1)}, f32[64,896]{1,0:T(8,128)}, u32[]{:S(2)}) copy-start(f32[64,896]{1,0:T(8,128)} %momentum_ref.1) | copy-start | bytes 688132
